TPU v7x, 32 devices: a whole 2x2x4 slice. The times are simulated.
32 devices in a mesh: dp: 8 (over z, x), mp: 4 (over y, core).
Axes of the slice: x: 2, y: 2, z: 4, core: 2. Of those that a mesh axis runs over, the one named last changes fastest.
Arguments:
- tokens: bfloat16 [1024, 16384], P('dp', 'mp'), may hold values from -6 to 6
- cotangent: bfloat16 [1024, 16384], P('dp', 'mp'), may hold values from -6 to 6
- right_one: bfloat16 [128, 128, 128], P('mp', 'dp'), may hold values from -0.5 to 0.5
- left_one: bfloat16 [128, 128, 128], P('mp', 'dp'), may hold values from -0.5 to 0.5
- right_two: bfloat16 [128, 128, 128], P('mp', 'dp'), may hold values from -0.5 to 0.5
- left_two: bfloat16 [128, 128, 128], P('mp', 'dp'), may hold values from -0.5 to 0.5
Outputs:
- tokens_grad: bfloat16 [1024, 16384], P('dp', 'mp')
- right_one_grad: float32 [128, 128, 128], P('mp', 'dp')
- left_one_grad: float32 [128, 128, 128], P('mp', 'dp')
- right_two_grad: float32 [128, 128, 128], P('mp', 'dp')
- left_two_grad: float32 [128, 128, 128], P('mp', 'dp')
All inputs are finite; a program needn't handle non-finite values.
Results may differ from a plain program's by a relative error of at most 0.0072.
Values may be sent and summed in bfloat16 or wider, within the bound.
No kernel may reach another device: no remote copies, remote signals or barrier semaphores. Data moves between devices by JAX's collectives and lax.ppermute only.
A program may use at most 64 MiB of HBM per device.

v0:
```python
import math

import jax
import jax.numpy as jnp
from jax import lax
from jax.sharding import PartitionSpec as P

half_root = 0.7071067811865476
inv_root_tau = 0.3989422804014327


def gelu_parts(values):
    normal_cdf = 0.5 * (1.0 + lax.erf(values * half_root))
    return (
        values * normal_cdf,
        normal_cdf + values * jnp.exp(-0.5 * values * values) * inv_root_tau,
    )


def to_blocks(source):
    return lax.all_to_all(source, "mp", split_axis=0, concat_axis=1, tiled=True)


def to_rows(source):
    return lax.all_to_all(source, "mp", split_axis=1, concat_axis=0, tiled=True)


def grad_columns(source, left_full):
    received = lax.all_to_all(source, "mp", split_axis=0, concat_axis=1, tiled=True)
    passed = jnp.einsum(
        "jkt,jbk->jbt", received, left_full, preferred_element_type=jnp.float32
    ).astype(jnp.bfloat16)
    return (received, passed)


def on_device(tokens, cotangent, right_one, left_one, right_two, left_two):
    rows = tokens.shape[0]
    local_blocks = right_one.shape[0]
    block_size = right_one.shape[2]
    scale = 1.0 / math.sqrt(rows * lax.axis_size("dp"))
    inputs = tokens.reshape(rows, local_blocks, block_size)
    right_first, left_first, right_second, left_second = (
        lax.all_gather(right_one, "dp", axis=1, tiled=True),
        lax.all_gather(left_one, "dp", axis=1, tiled=True),
        lax.all_gather(right_two, "dp", axis=1, tiled=True),
        lax.all_gather(left_two, "dp", axis=1, tiled=True),
    )
    first_mixed = jnp.einsum(
        "tbi,bij->jbt", inputs, right_first, preferred_element_type=jnp.float32
    ).astype(jnp.bfloat16)
    first_columns = to_blocks(first_mixed)
    first_outer = jnp.einsum(
        "jbt,jbk->kjt", first_columns, left_first, preferred_element_type=jnp.float32
    ).astype(jnp.bfloat16)
    preact = to_blocks(first_outer)
    activated, slope = gelu_parts(preact.astype(jnp.float32))
    hidden = activated.astype(jnp.bfloat16)
    second_mixed = jnp.einsum(
        "bit,bij->jbt", hidden, right_second, preferred_element_type=jnp.float32
    ).astype(jnp.bfloat16)
    upstream = jnp.transpose(cotangent.reshape(rows, local_blocks, block_size), (2, 1, 0))
    second_columns = to_blocks(second_mixed)
    upstream_columns, second_back = grad_columns(upstream, left_second)
    grad_left_two = jnp.einsum(
        "jbt,jkt->jbk", second_columns, upstream_columns, preferred_element_type=jnp.float32
    )
    second_rows = to_rows(second_back)
    grad_right_two = jnp.einsum(
        "bit,jbt->bij", hidden, second_rows, preferred_element_type=jnp.float32
    )
    back_hidden = jnp.einsum(
        "jbt,bij->bit", second_rows, right_second, preferred_element_type=jnp.float32
    )
    grad_preact = jnp.transpose((back_hidden * slope).astype(jnp.bfloat16), (1, 0, 2))
    first_upstream, first_back = grad_columns(grad_preact, left_first)
    grad_left_one = jnp.einsum(
        "jbt,jkt->jbk", first_columns, first_upstream, preferred_element_type=jnp.float32
    )
    first_rows = to_rows(first_back)
    grad_right_one = jnp.einsum(
        "tbi,jbt->bij", inputs, first_rows, preferred_element_type=jnp.float32
    )
    tokens_grad = jnp.einsum(
        "jbt,bij->tbi", first_rows, right_first, preferred_element_type=jnp.float32
    ).astype(jnp.bfloat16)
    tokens_grad = tokens_grad.reshape(rows, local_blocks * block_size)
    summed = (
        lax.psum_scatter(grad_right_one, "dp", scatter_dimension=1, tiled=True),
        lax.psum_scatter(grad_left_one, "dp", scatter_dimension=1, tiled=True),
        lax.psum_scatter(grad_right_two, "dp", scatter_dimension=1, tiled=True),
        lax.psum_scatter(grad_left_two, "dp", scatter_dimension=1, tiled=True),
    )
    return (tokens_grad, summed[0] * scale, summed[1] * scale, summed[2] * scale, summed[3] * scale)


def solution(mesh):
    placed = (
        P("dp", "mp"),
        P("dp", "mp"),
        P("mp", "dp", None),
        P("mp", "dp", None),
        P("mp", "dp", None),
        P("mp", "dp", None),
    )
    return jax.shard_map(
        on_device,
        mesh=mesh,
        in_specs=placed,
        out_specs=(
            P("dp", "mp"),
            P("mp", "dp", None),
            P("mp", "dp", None),
            P("mp", "dp", None),
            P("mp", "dp", None),
        ),
        check_vma=False,
    )
```

profile of v0, /device:TPU:0, one launch (start us, length us, event | category | flops | bytes accessed | tf_op | source)
XLA Modules:
  0.0 463.2 jit_solution(11806618659608898693)
XLA Ops:
  8.7 1.6 copy.130
  10.3 1.7 copy.131
  12.0 4.2 all-to-all-start
  17.0 35.4 %all-gather.9.cloned.1.call-done = bf16[32,128,128]{2,1,0:T(8,128)(2,1)} async-done(((bf16[32,16,128]{2,1,0:T(8,128)(2,1)}), bf16[32,128,128]{2,1,0:T(8,128)(2,1)}) %all-gather.9.cloned.1.call-update) | async-done | bytes 1048592 | tf_op jit(solution)/shard_map/all_gather | solution.py:43
  52.3 2.1 fusion.6
  54.4 1.7 copy.138
  56.1 3.5 all-to-all-start.2
  59.6 1.4 copy.132
  61.0 31.8 %all-gather.5.cloned.1.call-done = bf16[32,128,128]{2,1,0:T(8,128)(2,1)} async-done(((bf16[32,16,128]{2,1,0:T(8,128)(2,1)}), bf16[32,128,128]{2,1,0:T(8,128)(2,1)}) %all-gather.5.cloned.1.call-update) | async-done | bytes 1048592 | tf_op jit(solution)/shard_map/all_gather | solution.py:46
  92.8 1.6 convolution_convert_fusion.5
  94.5 1.7 copy.133
  96.2 4.2 all-to-all-start.1
  101.1 1.4 copy.139
  102.5 30.9 %all-gather.11.cloned.1.call-done = bf16[32,128,128]{2,1,0:T(8,128)(2,1)} async-done(((bf16[32,16,128]{2,1,0:T(8,128)(2,1)}), bf16[32,128,128]{2,1,0:T(8,128)(2,1)}) %all-gather.11.cloned.1.call-update) | async-done | bytes 1048592 | tf_op jit(solution)/shard_map/all_gather | solution.py:44
  133.3 2.7 fusion.7
  136.1 2.7 copy.141
  138.7 3.5 all-to-all-start.3
  142.3 2.6 copy.135
  144.9 11.8 %all-to-all-done.3 = bf16[128,32,128]{2,1,0:T(8,128)(2,1)S(1)} async-done(((bf16[128,32,128]{2,1,0:T(8,128)(2,1)}), bf16[128,32,128]{2,1,0:T(8,128)(2,1)S(1)}, u32[]{:S(2)}, u32[]{:S(2)}) %all-to-all-start.3) | async-done | bytes 1048608 | tf_op jit(solution)/shard_map/all_to_all | solution.py:21
  157.0 1.6 copy.142
  158.6 2.9 copy.143
  161.5 2.1 multiply_convert_fusion
  164.5 2.6 copy.159
  167.2 6.5 %all-gather.7.cloned.1.call-done = bf16[32,128,128]{2,1,0:T(8,128)(2,1)} async-done(((bf16[32,16,128]{2,1,0:T(8,128)(2,1)}), bf16[32,128,128]{2,1,0:T(8,128)(2,1)}) %all-gather.7.cloned.1.call-update) | async-done | bytes 1048592 | tf_op jit(solution)/shard_map/all_gather | solution.py:45
  173.7 4.5 fusion.10
  178.2 2.6 copy.147
  180.9 18.1 %all_to_all.117 = bf16[128,32,128]{2,1,0:T(8,128)(2,1)S(1)} all-to-all(bf16[128,32,128]{2,1,0:T(8,128)(2,1)} %copy.147), channel_id=1, replica_groups=mesh['dp'=8,'mp'=4] {'mp'}, dimensions={0} | all-to-all | bytes 2097152 | tf_op jit(solution)/shard_map/all_to_all | solution.py:29
  200.9 2.5 copy.155
  203.5 2.6 fusion.9
  206.1 1.9 copy.160
  208.1 16.9 %all_to_all.118 = bf16[128,32,128]{2,1,0:T(8,128)(2,1)S(1)} all-to-all(bf16[128,32,128]{2,1,0:T(8,128)(2,1)S(1)} %copy.160), channel_id=1, replica_groups=mesh['dp'=8,'mp'=4] {'mp'}, dimensions={0} | all-to-all | bytes 2097152 | tf_op jit(solution)/shard_map/all_to_all | solution.py:21
  225.9 2.6 copy.162
  228.6 1.3 copy-done.4
  230.2 1.9 fusion.8
  232.1 1.9 copy.150
  234.0 16.9 %all_to_all.119 = bf16[32,128,128]{2,0,1:T(8,128)(2,1)S(1)} all-to-all(bf16[32,128,128]{2,0,1:T(8,128)(2,1)S(1)} %copy.150), channel_id=1, replica_groups=mesh['dp'=8,'mp'=4] {'mp'}, dimensions={1} | all-to-all | bytes 2097152 | tf_op jit(solution)/shard_map/all_to_all | solution.py:25
  251.0 1.8 convolution_bitcast_fusion
  252.8 3.2 copy.154
  256.1 1.2 copy-done.5
  257.3 1.5 convolution_convert_fusion
  258.8 2.3 copy.163
  261.0 1.0 broadcast_multiply_fusion.1
  262.8 51.0 %reduce-scatter.7.cloned.1.call-done = f32[32,16,128]{2,0,1:T(8,128)} async-done(((f32[32,128,128]{2,0,1:T(8,128)}), f32[32,16,128]{2,0,1:T(8,128)}) %reduce-scatter.7.cloned.1.call-update) | async-done | bytes 262160 | tf_op jit(solution)/shard_map/reduce_scatter | solution.py:89
  313.9 1.0 broadcast_multiply_fusion.2
  315.7 68.5 %reduce-scatter.11.cloned.1.call-done = f32[32,16,128]{2,0,1:T(8,128)} async-done(((f32[32,128,128]{2,0,1:T(8,128)}), f32[32,16,128]{2,0,1:T(8,128)}) %reduce-scatter.11.cloned.1.call-update) | async-done | bytes 262160 | tf_op jit(solution)/shard_map/reduce_scatter | solution.py:91
  384.3 1.0 broadcast_multiply_fusion
  386.1 68.4 %reduce-scatter.5.cloned.1.call-done = f32[32,16,128]{2,0,1:T(8,128)} async-done(((f32[32,128,128]{2,0,1:T(8,128)}), f32[32,16,128]{2,0,1:T(8,128)}) %reduce-scatter.5.cloned.1.call-update) | async-done | bytes 262160 | tf_op jit(solution)/shard_map/reduce_scatter | solution.py:88
  454.5 1.0 broadcast_multiply_fusion.3
  (49 shorter events, 11.0 us)
Async XLA Ops:
  7.2 45.2 %copy-start = (bf16[128,4096]{1,0:T(8,128)(2,1)S(1)}, bf16[128,4096]{1,0:T(8,128)(2,1)}, u32[]{:S(2)}) copy-start(bf16[128,4096]{1,0:T(8,128)(2,1)} %param.6) | copy-start | bytes 3145732
  7.2 45.1 %all-gather.9.cloned.1.call-start = ((), (), s32[]{:S(2)}) async-start(), calls=%async_computation.13 | async-start | bytes 1179648 | tf_op jit(solution)/shard_map/all_gather | solution.py:43
  7.9 84.9 %all-gather.5.cloned.1.call-start = ((), (), s32[]{:S(2)}) async-start(), calls=%async_computation.11 | async-start | bytes 1179648 | tf_op jit(solution)/shard_map/all_gather | solution.py:46
  12.0 44.1 %all-to-all-start = ((bf16[128,32,128]{2,1,0:T(8,128)(2,1)}), bf16[128,32,128]{2,1,0:T(8,128)(2,1)S(1)}, u32[]{:S(2)}, u32[]{:S(2)}) async-start(bf16[128,32,128]{2,1,0:T(8,128)(2,1)} %copy.131), calls=%async_computation | async-start | bytes 2097152 | tf_op jit(solution)/shard_map/all_to_all | solution.py:29
  16.3 117.1 %all-gather.11.cloned.1.call-start = ((), (), s32[]{:S(2)}) async-start(), calls=%async_computation.14 | async-start | bytes 1179648 | tf_op jit(solution)/shard_map/all_gather | solution.py:44
  56.1 3.5 copy-start.8
  56.1 40.1 %all-to-all-start.2 = ((bf16[128,32,128]{2,1,0:T(8,128)(2,1)}), bf16[128,32,128]{2,1,0:T(8,128)(2,1)S(1)}, u32[]{:S(2)}, u32[]{:S(2)}) async-start(bf16[128,32,128]{2,1,0:T(8,128)(2,1)} %copy.138), calls=%async_computation.2 | async-start | bytes 2097152 | tf_op jit(solution)/shard_map/all_to_all | solution.py:21
  96.2 4.8 %copy-start.7 = (bf16[128,32,128]{2,1,0:T(8,128)(2,1)}, bf16[128,32,128]{2,1,0:T(8,128)(2,1)S(1)}, u32[]{:S(2)}) copy-start(bf16[128,32,128]{2,1,0:T(8,128)(2,1)S(1)} %all-to-all-done.2) | copy-start | bytes 3145732
  96.2 42.5 %all-to-all-start.1 = ((bf16[32,128,128]{2,0,1:T(8,128)(2,1)}), bf16[32,128,128]{2,0,1:T(8,128)(2,1)}, u32[]{:S(2)}, u32[]{:S(2)}) async-start(bf16[32,128,128]{2,0,1:T(8,128)(2,1)} %copy.133), calls=%async_computation.1 | async-start | bytes 2097152 | tf_op jit(solution)/shard_map/all_to_all | solution.py:25
  100.5 73.2 %all-gather.7.cloned.1.call-start = ((), (), s32[]{:S(2)}) async-start(), calls=%async_computation.12 | async-start | bytes 1179648 | tf_op jit(solution)/shard_map/all_gather | solution.py:45
  102.4 36.3 %copy-start.1 = (bf16[32,4,32,128]{3,2,1,0:T(8,128)(2,1)}, bf16[32,4,32,128]{3,2,1,0:T(8,128)(2,1)S(1)}, u32[]{:S(2)}) copy-start(bf16[32,4,32,128]{3,2,1,0:T(8,128)(2,1)S(1)} %copy.139) | copy-start | bytes 3145732
  138.7 18.0 %all-to-all-start.3 = ((bf16[128,32,128]{2,1,0:T(8,128)(2,1)}), bf16[128,32,128]{2,1,0:T(8,128)(2,1)S(1)}, u32[]{:S(2)}, u32[]{:S(2)}) async-start(bf16[128,32,128]{2,1,0:T(8,128)(2,1)} %copy.141), calls=%async_computation.3 | async-start | bytes 2097152 | tf_op jit(solution)/shard_map/all_to_all | solution.py:21
  142.3 118.7 %reduce-scatter.9.cloned.1.call-start = ((), (), s32[]{:S(2)}) async-start(), calls=%async_computation.17 | async-start | bytes 2359296 | tf_op jit(solution)/shard_map/reduce_scatter | solution.py:90
  161.5 2.1 copy-start.9
  167.1 146.7 %reduce-scatter.7.cloned.1.call-start = ((), (), s32[]{:S(2)}) async-start(), calls=%async_computation.16 | async-start | bytes 2359296 | tf_op jit(solution)/shard_map/reduce_scatter | solution.py:89
  180.9 19.2 %copy-start.2 = (bf16[32,4,32,128]{3,2,1,0:T(8,128)(2,1)S(1)}, bf16[32,4,32,128]{3,2,1,0:T(8,128)(2,1)}, u32[]{:S(2)}) copy-start(bf16[32,4,32,128]{3,2,1,0:T(8,128)(2,1)} %copy-done.1) | copy-start | bytes 3145732
  199.1 1.0 copy-start.3
  203.4 180.8 %reduce-scatter.11.cloned.1.call-start = ((), (), s32[]{:S(2)}) async-start(), calls=%async_computation.18 | async-start | bytes 2359296 | tf_op jit(solution)/shard_map/reduce_scatter | solution.py:91
  228.5 1.4 copy-start.4
  228.5 1.7 copy-start.6
  228.5 226.0 %reduce-scatter.5.cloned.1.call-start = ((), (), s32[]{:S(2)}) async-start(), calls=%async_computation.15 | async-start | bytes 2359296 | tf_op jit(solution)/shard_map/reduce_scatter | solution.py:88
  256.1 1.2 copy-start.5
Sparse Core Ops, SparseCore 0:
  10.1 42.2 all-gather.8
  54.4 38.4 all-gather.4
  94.9 38.4 all-gather.10
  135.2 38.4 all-gather.6
  177.1 66.6 reduce-scatter.8
  247.2 66.6 reduce-scatter.6
  317.4 66.8 reduce-scatter.10
  387.8 66.6 reduce-scatter.4
where the time goes:
time: 464 us; the launch traced here: 463 us
  waiting for transfers between devices  307 us (66%)
  blocking collectives  51.9 us (11%)
  local copies, waits for them, and re-layouts  46.5 us (10%)
  matrix products  21.4 us (5%)
  starting transfers between devices  15.8 us (3%)
  between operations  14.3 us (3%)
  other arithmetic  6.28 us (1%)
    reduce_scatter x1, waiting for transfers between devices, on_device(): lax.psum_scatter(grad_left_two, 'dp', scatter_dimension=1, tiled=True)  68.5 us
    reduce_scatter x1, waiting for transfers between devices, on_device(): lax.psum_scatter(grad_right_one, 'dp', scatter_dimension=1, tiled=True)  68.4 us
    reduce_scatter x1, waiting for transfers between devices, on_device(): lax.psum_scatter(grad_left_one, 'dp', scatter_dimension=1, tiled=True)  51 us
    all_gather x1, waiting for transfers between devices, on_device(): lax.all_gather(right_one, 'dp', axis=1, tiled=True)  35.4 us
    all_gather x1, waiting for transfers between devices, on_device(): lax.all_gather(left_two, 'dp', axis=1, tiled=True)  31.8 us
    all_gather x1, waiting for transfers between devices, on_device(): lax.all_gather(left_one, 'dp', axis=1, tiled=True)  30.9 us
    all_to_all x1, blocking collectives, grad_columns(): lax.all_to_all(source, 'mp', split_axis=0, concat_axis=1, tiled=True)  18.1 us
    all_to_all x1, blocking collectives, to_blocks(): return lax.all_to_all(source, 'mp', split_axis=0, concat_axis=1, tiled=True)  16.9 us
  transfers between devices with their start and end apart: 12, of which 8 were waited for; matrix products, arithmetic and copies ran while one was open for 15% of the time, Pallas kernels for 0%

commit v1 on v0

--- a/solution.py
+++ b/solution.py
@@ -33,6 +33,45 @@
     return (received, passed)
 
 
+def hop(source, axis, offset):
+    size = lax.axis_size(axis)
+    return lax.ppermute(source, axis, [(i, i ^ offset) for i in range(size)])
+
+
+def reorder(pieces):
+    size = pieces.shape[0]
+    me = lax.axis_index("dp")
+    bits = size.bit_length() - 1
+    rest = pieces.shape[1:]
+    pieces = pieces.reshape((2,) * bits + rest)
+    for bit in range(bits):
+        axis = bits - 1 - bit
+        pieces = jnp.where((me >> bit) & 1 == 1, jnp.flip(pieces, axis), pieces)
+    return pieces.reshape((size,) + rest)
+
+
+def gather_rows(shard):
+    size = lax.axis_size("dp")
+    held = jnp.stack([shard] + [hop(shard, "dp", r) for r in range(2, size, 2)])
+    other = hop(held, "dp", 1)
+    pieces = jnp.stack([held, other], axis=1).reshape((size,) + shard.shape)
+    blocks, rows, width = shard.shape
+    return jnp.transpose(reorder(pieces), (1, 0, 2, 3)).reshape(blocks, size * rows, width)
+
+
+def scatter_rows(grad, scale):
+    size = lax.axis_size("dp")
+    blocks, rows, width = grad.shape
+    pieces = reorder(jnp.transpose(grad.reshape(blocks, size, rows // size, width), (1, 0, 2, 3)))
+    pieces = pieces.reshape(size // 2, 2, blocks, rows // size, width)
+    arrived = hop(pieces[:, 1].astype(jnp.bfloat16), "dp", 1)
+    held = pieces[:, 0] + arrived.astype(jnp.float32)
+    total = held[0]
+    for q in range(1, size // 2):
+        total = total + hop(held[q].astype(jnp.bfloat16), "dp", 2 * q).astype(jnp.float32)
+    return total * scale
+
+
 def on_device(tokens, cotangent, right_one, left_one, right_two, left_two):
     rows = tokens.shape[0]
     local_blocks = right_one.shape[0]
@@ -40,10 +79,10 @@
     scale = 1.0 / math.sqrt(rows * lax.axis_size("dp"))
     inputs = tokens.reshape(rows, local_blocks, block_size)
     right_first, left_first, right_second, left_second = (
-        lax.all_gather(right_one, "dp", axis=1, tiled=True),
-        lax.all_gather(left_one, "dp", axis=1, tiled=True),
-        lax.all_gather(right_two, "dp", axis=1, tiled=True),
-        lax.all_gather(left_two, "dp", axis=1, tiled=True),
+        gather_rows(right_one),
+        gather_rows(left_one),
+        gather_rows(right_two),
+        gather_rows(left_two),
     )
     first_mixed = jnp.einsum(
         "tbi,bij->jbt", inputs, right_first, preferred_element_type=jnp.float32
@@ -85,12 +124,12 @@
     ).astype(jnp.bfloat16)
     tokens_grad = tokens_grad.reshape(rows, local_blocks * block_size)
     summed = (
-        lax.psum_scatter(grad_right_one, "dp", scatter_dimension=1, tiled=True),
-        lax.psum_scatter(grad_left_one, "dp", scatter_dimension=1, tiled=True),
-        lax.psum_scatter(grad_right_two, "dp", scatter_dimension=1, tiled=True),
-        lax.psum_scatter(grad_left_two, "dp", scatter_dimension=1, tiled=True),
+        scatter_rows(grad_right_one, scale),
+        scatter_rows(grad_left_one, scale),
+        scatter_rows(grad_right_two, scale),
+        scatter_rows(grad_left_two, scale),
     )
-    return (tokens_grad, summed[0] * scale, summed[1] * scale, summed[2] * scale, summed[3] * scale)
+    return (tokens_grad, summed[0], summed[1], summed[2], summed[3])
 
 
 def solution(mesh):

time: 464 us -> 265 us (0.57)
  waiting for transfers between devices: 307 us -> 127 us
  starting transfers between devices: 15.8 us -> 68.5 us
  blocking collectives: 51.9 us -> 0 us
  other arithmetic: 6.28 us -> 21.9 us
  between operations: 14.3 us -> 1.34 us
  matrix products: 21.4 us -> 9.51 us
  local copies, waits for them, and re-layouts: 46.5 us -> 35.3 us
    reduce_scatter x4 -> x0, waiting for transfers between devices: 188 us -> none  [the longest x1 68.5 us: on_device(): lax.psum_scatter(grad_left_two, 'dp', scatter_dimension=1, tiled=True)]
    all_gather x4 -> x0, waiting for transfers between devices: 105 us -> none  [the longest x1 35.4 us: on_device(): lax.all_gather(right_one, 'dp', axis=1, tiled=True)]
    ppermute x0 -> x32, waiting for transfers between devices: none -> 92.3 us  [hop(): return lax.ppermute(source, axis, [(i, i ^ offset) for i in range(size)])]
    all_to_all x3 -> x0, blocking collectives: 51.9 us -> none  [the longest x1 18.1 us: grad_columns(): lax.all_to_all(source, 'mp', split_axis=0, concat_axis=1, tiled=True)]
    ppermute x0 -> x32, starting transfers between devices: none -> 39.6 us  [hop(): return lax.ppermute(source, axis, [(i, i ^ offset) for i in range(size)])]
    all_to_all x1 -> x2, waiting for transfers between devices: 0.01 us -> 11.1 us  [grad_columns(): lax.all_to_all(source, 'mp', split_axis=0, concat_axis=1, tiled=True)]
    dot_general x4 -> x0, local copies, waits for them, and re-layouts: 10.9 us -> none  [the longest x1 3.2 us: on_device(): jnp.einsum('tbi,jbt->bij', inputs, first_rows, preferred_element_type=jnp...]
    another operation x0 -> x12, other arithmetic: none -> 10.3 us  [the longest x4 5.64 us: gather_rows(): held = jnp.stack([shard] + [hop(shard, 'dp', r) for r in range(2, size, 2)])]
  transfers between devices with their start and end apart: 12 -> 39, of which waited for: 8 -> 23; matrix products, arithmetic and copies ran while one was open for 15% -> 18% of each run, Pallas kernels for 0% -> 0%
where the time goes in v1:
time: 265 us; the launch traced here: 264 us
  waiting for transfers between devices  127 us (48%)
  starting transfers between devices  68.5 us (26%)
  local copies, waits for them, and re-layouts  35.3 us (13%)
  other arithmetic  21.9 us (8%)
  matrix products  9.51 us (4%)
    ppermute x32, waiting for transfers between devices, hop(): return lax.ppermute(source, axis, [(i, i ^ offset) for i in range(size)])  92.3 us
    ppermute x32, starting transfers between devices, hop(): return lax.ppermute(source, axis, [(i, i ^ offset) for i in range(size)])  39.6 us
    all_to_all x3, waiting for transfers between devices, to_blocks(): return lax.all_to_all(source, 'mp', split_axis=0, concat_axis=1, tiled=True)  16 us
    all_to_all x3, starting transfers between devices, to_blocks(): return lax.all_to_all(source, 'mp', split_axis=0, concat_axis=1, tiled=True)  13 us
    all_to_all x2, waiting for transfers between devices, grad_columns(): lax.all_to_all(source, 'mp', split_axis=0, concat_axis=1, tiled=True)  11.1 us
    unnamed x34, local copies, waits for them, and re-layouts  8.58 us
    all_to_all x2, starting transfers between devices, to_rows(): return lax.all_to_all(source, 'mp', split_axis=1, concat_axis=0, tiled=True)  7.99 us
    all_to_all x2, waiting for transfers between devices, to_rows(): return lax.all_to_all(source, 'mp', split_axis=1, concat_axis=0, tiled=True)  7.93 us
  transfers between devices with their start and end apart: 39, of which 23 were waited for; matrix products, arithmetic and copies ran while one was open for 18% of the time, Pallas kernels for 0%

profile of v1, /device:TPU:0, one launch (start us, length us, event | category | flops | bytes accessed | tf_op | source)
XLA Modules:
  0.0 263.8 jit_solution(14449628069671337302)
XLA Ops:
  0.6 3.1 %collective-permute-start = (bf16[32,16,128]{2,1,0:T(8,128)(2,1)}, bf16[32,16,128]{2,1,0:T(8,128)(2,1)S(1)}, u32[]{:S(2)}, u32[]{:S(2)}) collective-permute-start(bf16[32,16,128]{2,1,0:T(8,128)(2,1)} %param.8), channel_id=1, source_target_pairs={{0,8},{4,12},{8,0},{12,4},{16,24},{20,28},{24,16},{28,20},{1,9},{5... | collective-permute-start | bytes 393224 | tf_op jit(solution)/shard_map/ppermute | solution.py:38
  3.7 2.5 collective-permute-start.2
  6.3 1.8 collective-permute-start.8
  8.1 5.6 %collective-permute-done.2 = bf16[32,16,128]{2,1,0:T(8,128)(2,1)S(1)} collective-permute-done((bf16[32,16,128]{2,1,0:T(8,128)(2,1)}, bf16[32,16,128]{2,1,0:T(8,128)(2,1)S(1)}, u32[]{:S(2)}, u32[]{:S(2)}) %collective-permute-start.2) | collective-permute-done | bytes 131104 | tf_op jit(solution)/shard_map/ppermute | solution.py:38
  13.7 4.5 %collective-permute-done.1 = bf16[32,16,128]{2,1,0:T(8,128)(2,1)S(1)} collective-permute-done((bf16[32,16,128]{2,1,0:T(8,128)(2,1)}, bf16[32,16,128]{2,1,0:T(8,128)(2,1)S(1)}, u32[]{:S(2)}, u32[]{:S(2)}) %collective-permute-start.1) | collective-permute-done | bytes 131104 | tf_op jit(solution)/shard_map/ppermute | solution.py:38
  18.2 1.8 pad_maximum_fusion.4
  21.4 2.6 collective-permute-start.10
  25.3 2.3 collective-permute-start.13
  27.6 2.5 collective-permute-done.10
  32.3 1.7 copy.93
  34.0 3.6 %all-to-all-start = ((bf16[128,32,128]{2,1,0:T(8,128)(2,1)}), bf16[128,32,128]{2,1,0:T(8,128)(2,1)S(1)}, u32[]{:S(2)}, u32[]{:S(2)}) async-start(bf16[128,32,128]{2,1,0:T(8,128)(2,1)} %copy.93), calls=%async_computation | async-start | bytes 2097152 | tf_op jit(solution)/shard_map/all_to_all | solution.py:29
  38.4 3.2 %collective-permute-start.4 = (bf16[32,16,128]{2,1,0:T(8,128)(2,1)S(1)}, bf16[32,16,128]{2,1,0:T(8,128)(2,1)S(1)}, u32[]{:S(2)}, u32[]{:S(2)}) collective-permute-start(bf16[32,16,128]{2,1,0:T(8,128)(2,1)S(1)} %copy-done.13), channel_id=1, source_target_pairs={{0,8},{4,12},{8,0},{12,4},{16,24},{20,28},{24,16},{28,20},{1,9},{5... | collective-permute-start | bytes 393224 | tf_op jit(solution)/shard_map/ppermute | solution.py:38
  44.9 1.9 collective-permute-done.9
  47.4 1.9 pad_maximum_fusion.6
  49.3 1.9 collective-permute-done.4
  51.8 5.1 %collective-permute-done.5 = bf16[32,16,128]{2,1,0:T(8,128)(2,1)S(1)} collective-permute-done((bf16[32,16,128]{2,1,0:T(8,128)(2,1)S(1)}, bf16[32,16,128]{2,1,0:T(8,128)(2,1)S(1)}, u32[]{:S(2)}, u32[]{:S(2)}) %collective-permute-start.5) | collective-permute-done | bytes 131104 | tf_op jit(solution)/shard_map/ppermute | solution.py:38
  61.1 1.6 copy.99
  63.3 4.3 %all-to-all-start.2 = ((bf16[128,32,128]{2,1,0:T(8,128)(2,1)}), bf16[128,32,128]{2,1,0:T(8,128)(2,1)}, u32[]{:S(2)}, u32[]{:S(2)}) async-start(bf16[128,32,128]{2,1,0:T(8,128)(2,1)} %copy.99), calls=%async_computation.2 | async-start | bytes 2097152 | tf_op jit(solution)/shard_map/all_to_all | solution.py:21
  68.1 13.4 %collective-permute-done.7 = bf16[4,32,16,128]{3,2,1,0:T(8,128)(2,1)} collective-permute-done((bf16[4,32,16,128]{3,2,1,0:T(8,128)(2,1)}, bf16[4,32,16,128]{3,2,1,0:T(8,128)(2,1)}, u32[]{:S(2)}, u32[]{:S(2)}) %collective-permute-start.7) | collective-permute-done | bytes 524320 | tf_op jit(solution)/shard_map/ppermute | solution.py:38
  84.5 1.7 copy.95
  86.2 4.2 %all-to-all-start.1 = ((bf16[32,128,128]{2,0,1:T(8,128)(2,1)}), bf16[32,128,128]{2,0,1:T(8,128)(2,1)}, u32[]{:S(2)}, u32[]{:S(2)}) async-start(bf16[32,128,128]{2,0,1:T(8,128)(2,1)} %copy.95), calls=%async_computation.1 | async-start | bytes 2097152 | tf_op jit(solution)/shard_map/all_to_all | solution.py:25
  95.4 1.6 copy.102
  97.0 7.9 %all-to-all-done.1 = bf16[32,128,128]{2,0,1:T(8,128)(2,1)} async-done(((bf16[32,128,128]{2,0,1:T(8,128)(2,1)}), bf16[32,128,128]{2,0,1:T(8,128)(2,1)}, u32[]{:S(2)}, u32[]{:S(2)}) %all-to-all-start.1) | async-done | bytes 1048608 | tf_op jit(solution)/shard_map/all_to_all | solution.py:25
  105.0 4.4 %all-to-all-start.3 = ((bf16[128,32,128]{2,1,0:T(8,128)(2,1)}), bf16[128,32,128]{2,1,0:T(8,128)(2,1)}, u32[]{:S(2)}, u32[]{:S(2)}) async-start(bf16[128,32,128]{2,1,0:T(8,128)(2,1)} %copy.102), calls=%async_computation.3 | async-start | bytes 2097152 | tf_op jit(solution)/shard_map/all_to_all | solution.py:21
  110.3 2.3 copy.96
  112.7 11.0 %all-to-all-done.3 = bf16[128,32,128]{2,1,0:T(8,128)(2,1)} async-done(((bf16[128,32,128]{2,1,0:T(8,128)(2,1)}), bf16[128,32,128]{2,1,0:T(8,128)(2,1)}, u32[]{:S(2)}, u32[]{:S(2)}) %all-to-all-start.3) | async-done | bytes 1048608 | tf_op jit(solution)/shard_map/all_to_all | solution.py:21
  129.2 4.2 %all-to-all-start.4 = ((bf16[128,32,128]{2,1,0:T(8,128)(2,1)}), bf16[128,32,128]{2,1,0:T(8,128)(2,1)}, u32[]{:S(2)}, u32[]{:S(2)}) async-start(bf16[128,32,128]{2,1,0:T(8,128)(2,1)} %copy.104), calls=%async_computation.4 | async-start | bytes 2097152 | tf_op jit(solution)/shard_map/all_to_all | solution.py:29
  133.5 1.7 fusion.12
  135.2 1.7 copy.119
  136.9 11.1 %all-to-all-done.4 = bf16[128,32,128]{2,1,0:T(8,128)(2,1)} async-done(((bf16[128,32,128]{2,1,0:T(8,128)(2,1)}), bf16[128,32,128]{2,1,0:T(8,128)(2,1)}, u32[]{:S(2)}, u32[]{:S(2)}) %all-to-all-start.4) | async-done | bytes 1048608 | tf_op jit(solution)/shard_map/all_to_all | solution.py:29
  148.0 4.3 %all-to-all-start.6 = ((bf16[128,32,128]{2,1,0:T(8,128)(2,1)}), bf16[128,32,128]{2,1,0:T(8,128)(2,1)}, u32[]{:S(2)}, u32[]{:S(2)}) async-start(bf16[128,32,128]{2,1,0:T(8,128)(2,1)} %copy.119), calls=%async_computation.6 | async-start | bytes 2097152 | tf_op jit(solution)/shard_map/all_to_all | solution.py:21
  152.3 2.1 fusion.49
  161.8 4.9 %all-to-all-done.6 = bf16[128,32,128]{2,1,0:T(8,128)(2,1)} async-done(((bf16[128,32,128]{2,1,0:T(8,128)(2,1)}), bf16[128,32,128]{2,1,0:T(8,128)(2,1)}, u32[]{:S(2)}, u32[]{:S(2)}) %all-to-all-start.6) | async-done | bytes 1048608 | tf_op jit(solution)/shard_map/all_to_all | solution.py:21
  166.8 3.7 %all-to-all-start.5 = ((bf16[32,128,128]{2,0,1:T(8,128)(2,1)}), bf16[32,128,128]{2,0,1:T(8,128)(2,1)S(1)}, u32[]{:S(2)}, u32[]{:S(2)}) async-start(bf16[32,128,128]{2,0,1:T(8,128)(2,1)} %copy.106), calls=%async_computation.5 | async-start | bytes 2097152 | tf_op jit(solution)/shard_map/all_to_all | solution.py:25
  177.8 12.2 %collective-permute-done.28 = bf16[4,32,16,128]{3,2,1,0:T(8,128)(2,1)S(1)} collective-permute-done((bf16[4,32,16,128]{3,2,1,0:T(8,128)(2,1)S(1)}, bf16[4,32,16,128]{3,2,1,0:T(8,128)(2,1)S(1)}, u32[]{:S(2)}, u32[]{:S(2)}) %collective-permute-start.28) | collective-permute-done | bytes 524320 | tf_op jit(solution)/shard_map/ppermute | solution.py:38
  190.2 1.9 collective-permute-start.29
  193.8 6.8 %collective-permute-done.24 = bf16[4,32,16,128]{3,2,1,0:T(8,128)(2,1)S(1)} collective-permute-done((bf16[4,32,16,128]{3,2,1,0:T(8,128)(2,1)S(1)}, bf16[4,32,16,128]{3,2,1,0:T(8,128)(2,1)S(1)}, u32[]{:S(2)}, u32[]{:S(2)}) %collective-permute-start.24) | collective-permute-done | bytes 524320 | tf_op jit(solution)/shard_map/ppermute | solution.py:38
  200.8 1.9 collective-permute-start.25
  206.1 3.6 %collective-permute-done.25 = bf16[32,16,128]{2,1,0:T(8,128)(2,1)S(1)} collective-permute-done((bf16[32,16,128]{2,1,0:T(8,128)(2,1)S(1)}, bf16[32,16,128]{2,1,0:T(8,128)(2,1)S(1)}, u32[]{:S(2)}, u32[]{:S(2)}) %collective-permute-start.25) | collective-permute-done | bytes 131104 | tf_op jit(solution)/shard_map/ppermute | solution.py:38
  210.9 5.1 %collective-permute-done.26 = bf16[32,16,128]{2,1,0:T(8,128)(2,1)S(1)} collective-permute-done((bf16[32,16,128]{2,1,0:T(8,128)(2,1)S(1)}, bf16[32,16,128]{2,1,0:T(8,128)(2,1)S(1)}, u32[]{:S(2)}, u32[]{:S(2)}) %collective-permute-start.26) | collective-permute-done | bytes 131104 | tf_op jit(solution)/shard_map/ppermute | solution.py:38
  222.5 2.6 reverse_select_fusion.8
  228.2 12.3 %collective-permute-done.20 = bf16[4,32,16,128]{3,2,1,0:T(8,128)(2,1)S(1)} collective-permute-done((bf16[4,32,16,128]{3,2,1,0:T(8,128)(2,1)S(1)}, bf16[4,32,16,128]{3,2,1,0:T(8,128)(2,1)S(1)}, u32[]{:S(2)}, u32[]{:S(2)}) %collective-permute-start.20) | collective-permute-done | bytes 524320 | tf_op jit(solution)/shard_map/ppermute | solution.py:38
  240.8 1.7 collective-permute-start.23
  242.5 1.7 collective-permute-start.22
  244.3 5.4 %collective-permute-done.16 = bf16[4,32,16,128]{3,2,1,0:T(8,128)(2,1)S(1)} collective-permute-done((bf16[4,32,16,128]{3,2,1,0:T(8,128)(2,1)S(1)}, bf16[4,32,16,128]{3,2,1,0:T(8,128)(2,1)S(1)}, u32[]{:S(2)}, u32[]{:S(2)}) %collective-permute-start.16) | collective-permute-done | bytes 524320 | tf_op jit(solution)/shard_map/ppermute | solution.py:38
  250.0 1.9 collective-permute-start.19
  254.2 2.6 collective-permute-done.17
  258.1 5.0 %collective-permute-done.18 = bf16[32,16,128]{2,1,0:T(8,128)(2,1)S(1)} collective-permute-done((bf16[32,16,128]{2,1,0:T(8,128)(2,1)S(1)}, bf16[32,16,128]{2,1,0:T(8,128)(2,1)S(1)}, u32[]{:S(2)}, u32[]{:S(2)}) %collective-permute-start.18) | collective-permute-done | bytes 131104 | tf_op jit(solution)/shard_map/ppermute | solution.py:38
  (145 shorter events, 65.5 us)
Async XLA Ops:
  0.6 7.5 %collective-permute-start = (bf16[32,16,128]{2,1,0:T(8,128)(2,1)}, bf16[32,16,128]{2,1,0:T(8,128)(2,1)S(1)}, u32[]{:S(2)}, u32[]{:S(2)}) collective-permute-start(bf16[32,16,128]{2,1,0:T(8,128)(2,1)} %param.8), channel_id=1, source_target_pairs={{0,8},{4,12},{8,0},{12,4},{16,24},{20,28},{24,16},{28,20},{1,9},{5... | collective-permute-start | bytes 393224 | tf_op jit(solution)/shard_map/ppermute | solution.py:38
  3.7 10.0 %collective-permute-start.2 = (bf16[32,16,128]{2,1,0:T(8,128)(2,1)}, bf16[32,16,128]{2,1,0:T(8,128)(2,1)S(1)}, u32[]{:S(2)}, u32[]{:S(2)}) collective-permute-start(bf16[32,16,128]{2,1,0:T(8,128)(2,1)} %param.8), channel_id=1, source_target_pairs={{0,24},{4,28},{8,16},{12,20},{16,8},{20,12},{24,0},{28,4},{1,25},{... | collective-permute-start | bytes 393224 | tf_op jit(solution)/shard_map/ppermute | solution.py:38
  6.2 12.0 %collective-permute-start.1 = (bf16[32,16,128]{2,1,0:T(8,128)(2,1)}, bf16[32,16,128]{2,1,0:T(8,128)(2,1)S(1)}, u32[]{:S(2)}, u32[]{:S(2)}) collective-permute-start(bf16[32,16,128]{2,1,0:T(8,128)(2,1)} %param.8), channel_id=1, source_target_pairs={{0,16},{4,20},{8,24},{12,28},{16,0},{20,4},{24,8},{28,12},{1,17},{... | collective-permute-start | bytes 393224 | tf_op jit(solution)/shard_map/ppermute | solution.py:38
  6.3 19.0 %collective-permute-start.8 = (bf16[32,16,128]{2,1,0:T(8,128)(2,1)}, bf16[32,16,128]{2,1,0:T(8,128)(2,1)S(1)}, u32[]{:S(2)}, u32[]{:S(2)}) collective-permute-start(bf16[32,16,128]{2,1,0:T(8,128)(2,1)} %param.10), channel_id=1, source_target_pairs={{0,8},{4,12},{8,0},{12,4},{16,24},{20,28},{24,16},{28,20},{1,9},{5... | collective-permute-start | bytes 393224 | tf_op jit(solution)/shard_map/ppermute | solution.py:38
  20.0 38.3 %collective-permute-start.3 = (bf16[4,32,16,128]{3,2,1,0:T(8,128)(2,1)}, bf16[4,32,16,128]{3,2,1,0:T(8,128)(2,1)}, u32[]{:S(2)}, u32[]{:S(2)}) collective-permute-start(bf16[4,32,16,128]{3,2,1,0:T(8,128)(2,1)} %pad_maximum_fusion.4), channel_id=1, source_target_pairs={{0,4},{4,0},{8,12},{12,8},{16,20},{20,16},{24,28},{28,24},{1,5},{5... | collective-permute-start | bytes 1572872 | tf_op jit(solution)/shard_map/ppermute | solution.py:38
  21.4 8.6 %collective-permute-start.10 = (bf16[32,16,128]{2,1,0:T(8,128)(2,1)}, bf16[32,16,128]{2,1,0:T(8,128)(2,1)S(1)}, u32[]{:S(2)}, u32[]{:S(2)}) collective-permute-start(bf16[32,16,128]{2,1,0:T(8,128)(2,1)} %param.10), channel_id=1, source_target_pairs={{0,24},{4,28},{8,16},{12,20},{16,8},{20,12},{24,0},{28,4},{1,25},{... | collective-permute-start | bytes 393224 | tf_op jit(solution)/shard_map/ppermute | solution.py:38
  24.1 14.4 %collective-permute-start.12 = (bf16[32,16,128]{2,1,0:T(8,128)(2,1)}, bf16[32,16,128]{2,1,0:T(8,128)(2,1)}, u32[]{:S(2)}, u32[]{:S(2)}) collective-permute-start(bf16[32,16,128]{2,1,0:T(8,128)(2,1)} %param.11), channel_id=1, source_target_pairs={{0,8},{4,12},{8,0},{12,4},{16,24},{20,28},{24,16},{28,20},{1,9},{5... | collective-permute-start | bytes 393224 | tf_op jit(solution)/shard_map/ppermute | solution.py:38
  24.1 17.6 %collective-permute-start.14 = (bf16[32,16,128]{2,1,0:T(8,128)(2,1)}, bf16[32,16,128]{2,1,0:T(8,128)(2,1)}, u32[]{:S(2)}, u32[]{:S(2)}) collective-permute-start(bf16[32,16,128]{2,1,0:T(8,128)(2,1)} %param.11), channel_id=1, source_target_pairs={{0,24},{4,28},{8,16},{12,20},{16,8},{20,12},{24,0},{28,4},{1,25},{... | collective-permute-start | bytes 393224 | tf_op jit(solution)/shard_map/ppermute | solution.py:38
  25.3 4.8 %copy-start.14 = (bf16[32,16,128]{2,1,0:T(8,128)(2,1)}, bf16[32,16,128]{2,1,0:T(8,128)(2,1)S(1)}, u32[]{:S(2)}) copy-start(bf16[32,16,128]{2,1,0:T(8,128)(2,1)S(1)} %collective-permute-done.8) | copy-start | bytes 393220
  25.3 18.6 %collective-permute-start.13 = (bf16[32,16,128]{2,1,0:T(8,128)(2,1)}, bf16[32,16,128]{2,1,0:T(8,128)(2,1)}, u32[]{:S(2)}, u32[]{:S(2)}) collective-permute-start(bf16[32,16,128]{2,1,0:T(8,128)(2,1)} %param.11), channel_id=1, source_target_pairs={{0,16},{4,20},{8,24},{12,28},{16,0},{20,4},{24,8},{28,12},{1,17},{... | collective-permute-start | bytes 393224 | tf_op jit(solution)/shard_map/ppermute | solution.py:38
  30.7 16.2 %collective-permute-start.9 = (bf16[32,16,128]{2,1,0:T(8,128)(2,1)}, bf16[32,16,128]{2,1,0:T(8,128)(2,1)}, u32[]{:S(2)}, u32[]{:S(2)}) collective-permute-start(bf16[32,16,128]{2,1,0:T(8,128)(2,1)} %param.10), channel_id=1, source_target_pairs={{0,16},{4,20},{8,24},{12,28},{16,0},{20,4},{24,8},{28,12},{1,17},{... | collective-permute-start | bytes 393224 | tf_op jit(solution)/shard_map/ppermute | solution.py:38
  34.0 3.7 %copy-start.10 = (bf16[128,4096]{1,0:T(8,128)(2,1)S(1)}, bf16[128,4096]{1,0:T(8,128)(2,1)}, u32[]{:S(2)}) copy-start(bf16[128,4096]{1,0:T(8,128)(2,1)} %param.6) | copy-start | bytes 3145732
  34.0 4.4 %copy-start.13 = (bf16[32,16,128]{2,1,0:T(8,128)(2,1)S(1)}, bf16[32,16,128]{2,1,0:T(8,128)(2,1)}, u32[]{:S(2)}) copy-start(bf16[32,16,128]{2,1,0:T(8,128)(2,1)} %param.9) | copy-start | bytes 393220
  34.0 9.8 %copy-start.11 = (bf16[32,16,128]{2,1,0:T(8,128)(2,1)S(1)}, bf16[32,16,128]{2,1,0:T(8,128)(2,1)}, u32[]{:S(2)}) copy-start(bf16[32,16,128]{2,1,0:T(8,128)(2,1)} %param.11) | copy-start | bytes 393220
  34.0 29.2 %all-to-all-start = ((bf16[128,32,128]{2,1,0:T(8,128)(2,1)}), bf16[128,32,128]{2,1,0:T(8,128)(2,1)S(1)}, u32[]{:S(2)}, u32[]{:S(2)}) async-start(bf16[128,32,128]{2,1,0:T(8,128)(2,1)} %copy.93), calls=%async_computation | async-start | bytes 2097152 | tf_op jit(solution)/shard_map/all_to_all | solution.py:29
  37.7 9.7 %copy-start.12 = (bf16[32,16,128]{2,1,0:T(8,128)(2,1)S(1)}, bf16[32,16,128]{2,1,0:T(8,128)(2,1)}, u32[]{:S(2)}) copy-start(bf16[32,16,128]{2,1,0:T(8,128)(2,1)} %param.10) | copy-start | bytes 393220
  38.4 22.2 %copy-start.1 = (bf16[128,4096]{0,1:T(8,128)(2,1)}, bf16[128,4096]{0,1:T(8,128)(2,1)S(1)}, u32[]{:S(2)}) copy-start(bf16[128,4096]{0,1:T(8,128)(2,1)S(1)} %copy.128) | copy-start | bytes 3145732
  38.4 12.8 %collective-permute-start.4 = (bf16[32,16,128]{2,1,0:T(8,128)(2,1)S(1)}, bf16[32,16,128]{2,1,0:T(8,128)(2,1)S(1)}, u32[]{:S(2)}, u32[]{:S(2)}) collective-permute-start(bf16[32,16,128]{2,1,0:T(8,128)(2,1)S(1)} %copy-done.13), channel_id=1, source_target_pairs={{0,8},{4,12},{8,0},{12,4},{16,24},{20,28},{24,16},{28,20},{1,9},{5... | collective-permute-start | bytes 393224 | tf_op jit(solution)/shard_map/ppermute | solution.py:38
  41.7 10.1 %collective-permute-start.6 = (bf16[32,16,128]{2,1,0:T(8,128)(2,1)S(1)}, bf16[32,16,128]{2,1,0:T(8,128)(2,1)S(1)}, u32[]{:S(2)}, u32[]{:S(2)}) collective-permute-start(bf16[32,16,128]{2,1,0:T(8,128)(2,1)S(1)} %copy-done.13), channel_id=1, source_target_pairs={{0,24},{4,28},{8,16},{12,20},{16,8},{20,12},{24,0},{28,4},{1,25},{... | collective-permute-start | bytes 393224 | tf_op jit(solution)/shard_map/ppermute | solution.py:38
  43.8 13.1 %collective-permute-start.5 = (bf16[32,16,128]{2,1,0:T(8,128)(2,1)S(1)}, bf16[32,16,128]{2,1,0:T(8,128)(2,1)S(1)}, u32[]{:S(2)}, u32[]{:S(2)}) collective-permute-start(bf16[32,16,128]{2,1,0:T(8,128)(2,1)S(1)} %copy-done.13), channel_id=1, source_target_pairs={{0,16},{4,20},{8,24},{12,28},{16,0},{20,4},{24,8},{28,12},{1,17},{... | collective-permute-start | bytes 393224 | tf_op jit(solution)/shard_map/ppermute | solution.py:38
  46.9 15.8 %collective-permute-start.15 = (bf16[4,32,16,128]{3,2,1,0:T(8,128)(2,1)S(1)}, bf16[4,32,16,128]{3,2,1,0:T(8,128)(2,1)S(1)}, u32[]{:S(2)}, u32[]{:S(2)}) collective-permute-start(bf16[4,32,16,128]{3,2,1,0:T(8,128)(2,1)S(1)} %pad_maximum_fusion.7), channel_id=1, source_target_pairs={{0,4},{4,0},{8,12},{12,8},{16,20},{20,16},{24,28},{28,24},{1,5},{5... | collective-permute-start | bytes 1572872 | tf_op jit(solution)/shard_map/ppermute | solution.py:38
  51.2 39.9 %collective-permute-start.11 = (bf16[4,32,16,128]{3,2,1,0:T(8,128)(2,1)}, bf16[4,32,16,128]{3,2,1,0:T(8,128)(2,1)}, u32[]{:S(2)}, u32[]{:S(2)}) collective-permute-start(bf16[4,32,16,128]{3,2,1,0:T(8,128)(2,1)} %pad_maximum_fusion.6), channel_id=1, source_target_pairs={{0,4},{4,0},{8,12},{12,8},{16,20},{20,16},{24,28},{28,24},{1,5},{5... | collective-permute-start | bytes 1572872 | tf_op jit(solution)/shard_map/ppermute | solution.py:38
  57.8 23.7 %collective-permute-start.7 = (bf16[4,32,16,128]{3,2,1,0:T(8,128)(2,1)}, bf16[4,32,16,128]{3,2,1,0:T(8,128)(2,1)}, u32[]{:S(2)}, u32[]{:S(2)}) collective-permute-start(bf16[4,32,16,128]{3,2,1,0:T(8,128)(2,1)} %pad_maximum_fusion.5), channel_id=1, source_target_pairs={{0,4},{4,0},{8,12},{12,8},{16,20},{20,16},{24,28},{28,24},{1,5},{5... | collective-permute-start | bytes 1572872 | tf_op jit(solution)/shard_map/ppermute | solution.py:38
  63.3 22.9 %all-to-all-start.2 = ((bf16[128,32,128]{2,1,0:T(8,128)(2,1)}), bf16[128,32,128]{2,1,0:T(8,128)(2,1)}, u32[]{:S(2)}, u32[]{:S(2)}) async-start(bf16[128,32,128]{2,1,0:T(8,128)(2,1)} %copy.99), calls=%async_computation.2 | async-start | bytes 2097152 | tf_op jit(solution)/shard_map/all_to_all | solution.py:21
  86.2 18.8 %all-to-all-start.1 = ((bf16[32,128,128]{2,0,1:T(8,128)(2,1)}), bf16[32,128,128]{2,0,1:T(8,128)(2,1)}, u32[]{:S(2)}, u32[]{:S(2)}) async-start(bf16[32,128,128]{2,0,1:T(8,128)(2,1)} %copy.95), calls=%async_computation.1 | async-start | bytes 2097152 | tf_op jit(solution)/shard_map/all_to_all | solution.py:25
  105.0 18.8 %all-to-all-start.3 = ((bf16[128,32,128]{2,1,0:T(8,128)(2,1)}), bf16[128,32,128]{2,1,0:T(8,128)(2,1)}, u32[]{:S(2)}, u32[]{:S(2)}) async-start(bf16[128,32,128]{2,1,0:T(8,128)(2,1)} %copy.102), calls=%async_computation.3 | async-start | bytes 2097152 | tf_op jit(solution)/shard_map/all_to_all | solution.py:21
  129.2 18.8 %all-to-all-start.4 = ((bf16[128,32,128]{2,1,0:T(8,128)(2,1)}), bf16[128,32,128]{2,1,0:T(8,128)(2,1)}, u32[]{:S(2)}, u32[]{:S(2)}) async-start(bf16[128,32,128]{2,1,0:T(8,128)(2,1)} %copy.104), calls=%async_computation.4 | async-start | bytes 2097152 | tf_op jit(solution)/shard_map/all_to_all | solution.py:29
  135.2 17.0 %copy-start = (bf16[32,128,128]{2,1,0:T(8,128)(2,1)S(1)}, bf16[32,128,128]{2,1,0:T(8,128)(2,1)}, u32[]{:S(2)}) copy-start(bf16[32,128,128]{2,1,0:T(8,128)(2,1)} %get-tuple-element.29) | copy-start | bytes 3145732
  148.0 18.8 %all-to-all-start.6 = ((bf16[128,32,128]{2,1,0:T(8,128)(2,1)}), bf16[128,32,128]{2,1,0:T(8,128)(2,1)}, u32[]{:S(2)}, u32[]{:S(2)}) async-start(bf16[128,32,128]{2,1,0:T(8,128)(2,1)} %copy.119), calls=%async_computation.6 | async-start | bytes 2097152 | tf_op jit(solution)/shard_map/all_to_all | solution.py:21
  161.8 10.0 %copy-start.4 = (bf16[32,4,32,128]{3,2,1,0:T(8,128)(2,1)S(1)}, bf16[32,4,32,128]{3,2,1,0:T(8,128)(2,1)}, u32[]{:S(2)}) copy-start(bf16[32,4,32,128]{3,2,1,0:T(8,128)(2,1)} %copy-done.3) | copy-start | bytes 3145732
  166.8 50.0 %all-to-all-start.5 = ((bf16[32,128,128]{2,0,1:T(8,128)(2,1)}), bf16[32,128,128]{2,0,1:T(8,128)(2,1)S(1)}, u32[]{:S(2)}, u32[]{:S(2)}) async-start(bf16[32,128,128]{2,0,1:T(8,128)(2,1)} %copy.106), calls=%async_computation.5 | async-start | bytes 2097152 | tf_op jit(solution)/shard_map/all_to_all | solution.py:25
  175.2 14.8 %collective-permute-start.28 = (bf16[4,32,16,128]{3,2,1,0:T(8,128)(2,1)S(1)}, bf16[4,32,16,128]{3,2,1,0:T(8,128)(2,1)S(1)}, u32[]{:S(2)}, u32[]{:S(2)}) collective-permute-start(bf16[4,32,16,128]{3,2,1,0:T(8,128)(2,1)S(1)} %fusion.21), channel_id=1, source_target_pairs={{0,4},{4,0},{8,12},{12,8},{16,20},{20,16},{24,28},{28,24},{1,5},{5... | collective-permute-start | bytes 1572872 | tf_op jit(solution)/shard_map/ppermute | solution.py:38
  176.3 24.3 %collective-permute-start.24 = (bf16[4,32,16,128]{3,2,1,0:T(8,128)(2,1)S(1)}, bf16[4,32,16,128]{3,2,1,0:T(8,128)(2,1)S(1)}, u32[]{:S(2)}, u32[]{:S(2)}) collective-permute-start(bf16[4,32,16,128]{3,2,1,0:T(8,128)(2,1)S(1)} %fusion.20), channel_id=1, source_target_pairs={{0,4},{4,0},{8,12},{12,8},{16,20},{20,16},{24,28},{28,24},{1,5},{5... | collective-permute-start | bytes 1572872 | tf_op jit(solution)/shard_map/ppermute | solution.py:38
  190.2 13.7 %collective-permute-start.29 = (bf16[32,16,128]{2,1,0:T(8,128)(2,1)S(1)}, bf16[32,16,128]{2,1,0:T(8,128)(2,1)S(1)}, u32[]{:S(2)}, u32[]{:S(2)}) collective-permute-start(bf16[32,16,128]{2,1,0:T(8,128)(2,1)S(1)} %get-tuple-element.35), channel_id=1, source_target_pairs={{0,8},{4,12},{8,0},{12,4},{16,24},{20,28},{24,16},{28,20},{1,9},{5... | collective-permute-start | bytes 393224 | tf_op jit(solution)/shard_map/ppermute | solution.py:38
  192.1 12.3 %collective-permute-start.31 = (bf16[32,16,128]{2,1,0:T(8,128)(2,1)S(1)}, bf16[32,16,128]{2,1,0:T(8,128)(2,1)S(1)}, u32[]{:S(2)}, u32[]{:S(2)}) collective-permute-start(bf16[32,16,128]{2,1,0:T(8,128)(2,1)S(1)} %get-tuple-element.36), channel_id=1, source_target_pairs={{0,24},{4,28},{8,16},{12,20},{16,8},{20,12},{24,0},{28,4},{1,25},{... | collective-permute-start | bytes 393224 | tf_op jit(solution)/shard_map/ppermute | solution.py:38
  193.3 12.0 %collective-permute-start.30 = (bf16[32,16,128]{2,1,0:T(8,128)(2,1)S(1)}, bf16[32,16,128]{2,1,0:T(8,128)(2,1)S(1)}, u32[]{:S(2)}, u32[]{:S(2)}) collective-permute-start(bf16[32,16,128]{2,1,0:T(8,128)(2,1)S(1)} %get-tuple-element.37), channel_id=1, source_target_pairs={{0,16},{4,20},{8,24},{12,28},{16,0},{20,4},{24,8},{28,12},{1,17},{... | collective-permute-start | bytes 393224 | tf_op jit(solution)/shard_map/ppermute | solution.py:38
  200.8 8.9 %collective-permute-start.25 = (bf16[32,16,128]{2,1,0:T(8,128)(2,1)S(1)}, bf16[32,16,128]{2,1,0:T(8,128)(2,1)S(1)}, u32[]{:S(2)}, u32[]{:S(2)}) collective-permute-start(bf16[32,16,128]{2,1,0:T(8,128)(2,1)S(1)} %get-tuple-element.38), channel_id=1, source_target_pairs={{0,8},{4,12},{8,0},{12,4},{16,24},{20,28},{24,16},{28,20},{1,9},{5... | collective-permute-start | bytes 393224 | tf_op jit(solution)/shard_map/ppermute | solution.py:38
  202.6 8.2 %collective-permute-start.27 = (bf16[32,16,128]{2,1,0:T(8,128)(2,1)S(1)}, bf16[32,16,128]{2,1,0:T(8,128)(2,1)S(1)}, u32[]{:S(2)}, u32[]{:S(2)}) collective-permute-start(bf16[32,16,128]{2,1,0:T(8,128)(2,1)S(1)} %get-tuple-element.39), channel_id=1, source_target_pairs={{0,24},{4,28},{8,16},{12,20},{16,8},{20,12},{24,0},{28,4},{1,25},{... | collective-permute-start | bytes 393224 | tf_op jit(solution)/shard_map/ppermute | solution.py:38
  203.9 12.2 %collective-permute-start.26 = (bf16[32,16,128]{2,1,0:T(8,128)(2,1)S(1)}, bf16[32,16,128]{2,1,0:T(8,128)(2,1)S(1)}, u32[]{:S(2)}, u32[]{:S(2)}) collective-permute-start(bf16[32,16,128]{2,1,0:T(8,128)(2,1)S(1)} %get-tuple-element.40), channel_id=1, source_target_pairs={{0,16},{4,20},{8,24},{12,28},{16,0},{20,4},{24,8},{28,12},{1,17},{... | collective-permute-start | bytes 393224 | tf_op jit(solution)/shard_map/ppermute | solution.py:38
  220.5 2.0 copy-start.8
  225.6 14.9 %collective-permute-start.20 = (bf16[4,32,16,128]{3,2,1,0:T(8,128)(2,1)S(1)}, bf16[4,32,16,128]{3,2,1,0:T(8,128)(2,1)S(1)}, u32[]{:S(2)}, u32[]{:S(2)}) collective-permute-start(bf16[4,32,16,128]{3,2,1,0:T(8,128)(2,1)S(1)} %fusion.19), channel_id=1, source_target_pairs={{0,4},{4,0},{8,12},{12,8},{16,20},{20,16},{24,28},{28,24},{1,5},{5... | collective-permute-start | bytes 1572872 | tf_op jit(solution)/shard_map/ppermute | solution.py:38
  226.7 23.0 %collective-permute-start.16 = (bf16[4,32,16,128]{3,2,1,0:T(8,128)(2,1)S(1)}, bf16[4,32,16,128]{3,2,1,0:T(8,128)(2,1)S(1)}, u32[]{:S(2)}, u32[]{:S(2)}) collective-permute-start(bf16[4,32,16,128]{3,2,1,0:T(8,128)(2,1)S(1)} %fusion.18), channel_id=1, source_target_pairs={{0,4},{4,0},{8,12},{12,8},{16,20},{20,16},{24,28},{28,24},{1,5},{5... | collective-permute-start | bytes 1572872 | tf_op jit(solution)/shard_map/ppermute | solution.py:38
  240.7 11.1 %collective-permute-start.21 = (bf16[32,16,128]{2,1,0:T(8,128)(2,1)S(1)}, bf16[32,16,128]{2,1,0:T(8,128)(2,1)S(1)}, u32[]{:S(2)}, u32[]{:S(2)}) collective-permute-start(bf16[32,16,128]{2,1,0:T(8,128)(2,1)S(1)} %get-tuple-element.41), channel_id=1, source_target_pairs={{0,8},{4,12},{8,0},{12,4},{16,24},{20,28},{24,16},{28,20},{1,9},{5... | collective-permute-start | bytes 393224 | tf_op jit(solution)/shard_map/ppermute | solution.py:38
  240.8 12.7 %collective-permute-start.23 = (bf16[32,16,128]{2,1,0:T(8,128)(2,1)S(1)}, bf16[32,16,128]{2,1,0:T(8,128)(2,1)S(1)}, u32[]{:S(2)}, u32[]{:S(2)}) collective-permute-start(bf16[32,16,128]{2,1,0:T(8,128)(2,1)S(1)} %get-tuple-element.42), channel_id=1, source_target_pairs={{0,24},{4,28},{8,16},{12,20},{16,8},{20,12},{24,0},{28,4},{1,25},{... | collective-permute-start | bytes 393224 | tf_op jit(solution)/shard_map/ppermute | solution.py:38
  242.5 10.9 %collective-permute-start.22 = (bf16[32,16,128]{2,1,0:T(8,128)(2,1)S(1)}, bf16[32,16,128]{2,1,0:T(8,128)(2,1)S(1)}, u32[]{:S(2)}, u32[]{:S(2)}) collective-permute-start(bf16[32,16,128]{2,1,0:T(8,128)(2,1)S(1)} %get-tuple-element.43), channel_id=1, source_target_pairs={{0,16},{4,20},{8,24},{12,28},{16,0},{20,4},{24,8},{28,12},{1,17},{... | collective-permute-start | bytes 393224 | tf_op jit(solution)/shard_map/ppermute | solution.py:38
  249.9 6.9 %collective-permute-start.17 = (bf16[32,16,128]{2,1,0:T(8,128)(2,1)S(1)}, bf16[32,16,128]{2,1,0:T(8,128)(2,1)S(1)}, u32[]{:S(2)}, u32[]{:S(2)}) collective-permute-start(bf16[32,16,128]{2,1,0:T(8,128)(2,1)S(1)} %get-tuple-element.44), channel_id=1, source_target_pairs={{0,8},{4,12},{8,0},{12,4},{16,24},{20,28},{24,16},{28,20},{1,9},{5... | collective-permute-start | bytes 393224 | tf_op jit(solution)/shard_map/ppermute | solution.py:38
  250.0 8.1 %collective-permute-start.19 = (bf16[32,16,128]{2,1,0:T(8,128)(2,1)S(1)}, bf16[32,16,128]{2,1,0:T(8,128)(2,1)S(1)}, u32[]{:S(2)}, u32[]{:S(2)}) collective-permute-start(bf16[32,16,128]{2,1,0:T(8,128)(2,1)S(1)} %get-tuple-element.45), channel_id=1, source_target_pairs={{0,24},{4,28},{8,16},{12,20},{16,8},{20,12},{24,0},{28,4},{1,25},{... | collective-permute-start | bytes 393224 | tf_op jit(solution)/shard_map/ppermute | solution.py:38
  251.9 11.2 %collective-permute-start.18 = (bf16[32,16,128]{2,1,0:T(8,128)(2,1)S(1)}, bf16[32,16,128]{2,1,0:T(8,128)(2,1)S(1)}, u32[]{:S(2)}, u32[]{:S(2)}) collective-permute-start(bf16[32,16,128]{2,1,0:T(8,128)(2,1)S(1)} %get-tuple-element.46), channel_id=1, source_target_pairs={{0,16},{4,20},{8,24},{12,28},{16,0},{20,4},{24,8},{28,12},{1,17},{... | collective-permute-start | bytes 393224 | tf_op jit(solution)/shard_map/ppermute | solution.py:38
  (7 other events, 8.5 us)

commit v2 on v0

v2 whole, which is shorter than its diff:
```python
import functools
import math

import jax
import jax.numpy as jnp
from jax import lax
from jax.experimental import pallas as pl
from jax.experimental.pallas import tpu as pltpu
from jax.sharding import PartitionSpec as P

half_root = 0.7071067811865476
inv_root_tau = 0.3989422804014327
lane_tile = 128
packed_rows = 16
vmem_bytes = 56 * 1024 * 1024


def gelu_parts(values):
    normal_cdf = 0.5 * (1.0 + lax.erf(values * half_root))
    return (
        values * normal_cdf,
        normal_cdf + values * jnp.exp(-0.5 * values * values) * inv_root_tau,
    )


def hop(source, axis, offset):
    size = lax.axis_size(axis)
    return lax.ppermute(source, axis, [(i, i ^ offset) for i in range(size)])


def exchange(sends):
    return [sends[0]] + [hop(sends[q], "mp", q) for q in range(1, len(sends))]


def gather_rows(shard):
    size = lax.axis_size("dp")
    held = [shard] + [hop(shard, "dp", r) for r in range(2, size, 2)]
    other = [hop(piece, "dp", 1) for piece in held]
    pieces = [piece for pair in zip(held, other) for piece in pair]
    if shard.shape[1] % packed_rows == 0:
        return [piece.reshape(-1, shard.shape[2]) for piece in pieces]
    return [reorder(jnp.stack(pieces))]


def reorder(pieces):
    size, local, rows, width = pieces.shape
    me = lax.axis_index("dp")
    bits = size.bit_length() - 1
    pieces = pieces.reshape((2,) * bits + (local, rows, width))
    for bit in range(bits):
        axis = bits - 1 - bit
        pieces = jnp.where((me >> bit) & 1 == 1, jnp.flip(pieces, axis), pieces)
    pieces = jnp.transpose(pieces.reshape(size, local, rows, width), (1, 0, 2, 3))
    return pieces.reshape(local * size * rows, width)


def scatter_rows(sent, kept, scale):
    held = kept + hop(sent, "dp", 1).astype(jnp.float32)
    total = held[0]
    for q in range(1, held.shape[0]):
        total = total + hop(held[q].astype(jnp.bfloat16), "dp", 2 * q).astype(jnp.float32)
    return total * scale


class Sizes:
    def __init__(self, tokens, right_one):
        self.tokens = tokens.shape[0]
        self.local, self.rows, self.block = right_one.shape
        self.dp = lax.axis_size("dp")
        self.mp = lax.axis_size("mp")


def matmul(left, right, left_dim, right_dim):
    return lax.dot_general(
        left, right, (((left_dim,), (right_dim,)), ((), ())), preferred_element_type=jnp.float32
    )


def place(full, pieces, index):
    local, block, width = full.shape
    rows = block // len(pieces)
    if len(pieces) == 1:
        full[...] = pieces[0][...].reshape(local, rows, width)
        return
    for q, piece in enumerate(pieces):
        start = pl.multiple_of((index ^ q) * rows, rows)
        full[:, pl.ds(start, rows), :] = piece[...].reshape(local, rows, width)


def spread(mixed, sends, index):
    size = sends[0].shape[0]
    for q, send in enumerate(sends):
        start = pl.multiple_of((index ^ q) * size, size)
        for h in range(mixed.shape[0]):
            lanes = slice(h * lane_tile, (h + 1) * lane_tile)
            send[:, lanes] = mixed[h, pl.ds(start, size), :].astype(jnp.bfloat16)


def split_grad(sums, sent, kept, index):
    pairs = sent.shape[0]
    local, block, width = sums.shape
    rows = block // (2 * pairs)
    for q in range(pairs):
        for target, offset in ((kept, 2 * q), (sent, 2 * q + 1)):
            start = pl.multiple_of((index ^ offset) * rows, rows)
            part = sums[:, pl.ds(start, rows), :].reshape(local * rows, width)
            target[q] = part.astype(target.dtype)


def column(mixed, c, local, value):
    for h in range(mixed.shape[0]):
        lanes = slice(h * lane_tile, (h + 1) * lane_tile)
        mixed[h, pl.ds(c, value.shape[0], stride=local), :] = value[:, lanes]


def turn_kernel(z, ids, cotangent, *refs):
    sends, (mixed,) = refs[: z.mp], refs[z.mp :]
    for c in range(z.local):
        part = cotangent[:, c * z.block : (c + 1) * z.block].astype(jnp.float32)
        column(mixed, c, z.local, part.T)
    spread(mixed, sends, ids[1])


def first_kernel(z, count, ids, tokens, *refs):
    pieces, refs = refs[:count], refs[count:]
    full, sends, mixed = refs[0], refs[1 : 1 + z.mp], refs[1 + z.mp]
    place(full, pieces, ids[0])
    for c in range(z.local):
        part = tokens[:, c * z.block : (c + 1) * z.block]
        column(mixed, c, z.local, matmul(full[c], part, 0, 1))
    spread(mixed, sends, ids[1])


def middle_kernel(z, count, side, ids, *refs):
    pieces, arrived, refs = refs[:count], refs[count : count + z.mp], refs[count + z.mp :]
    full, columns, sends, mixed = refs[0], refs[1], refs[2 : 2 + z.mp], refs[2 + z.mp]
    place(full, pieces, ids[0])
    place(columns, arrived, ids[1])
    for c in range(z.local):
        column(mixed, c, z.local, matmul(full[c], columns[c], side, 0))
    spread(mixed, sends, ids[1])


def gelu_kernel(z, count, ids, *refs):
    pieces, refs = refs[:count], refs[count:]
    preact, backs, refs = refs[: z.mp], refs[z.mp : 2 * z.mp], refs[2 * z.mp :]
    full, hidden, back, sends, mixed = refs[0], refs[1], refs[2], refs[3 : 3 + z.mp], refs[3 + z.mp]
    place(full, pieces, ids[0])
    place(hidden, preact, ids[1])
    place(back, backs, ids[1])
    for c in range(z.local):
        activated, slope = gelu_parts(hidden[c].astype(jnp.float32))
        hidden[c] = activated.astype(jnp.bfloat16)
        column(mixed, c, z.local, matmul(full[c], back[c], 1, 0) * slope)
    spread(mixed, sends, ids[1])


def second_kernel(z, ids, full, hidden, *refs):
    sends, (mixed,) = refs[: z.mp], refs[z.mp :]
    for c in range(z.local):
        column(mixed, c, z.local, matmul(full[c], hidden[c], 0, 0))
    spread(mixed, sends, ids[1])


def grad_kernel(z, ids, left, right, sent, kept, sums):
    for c in range(z.local):
        sums[c] = matmul(left[c], right[c], 1, 1)
    split_grad(sums, sent, kept, ids[0])


def placed_grad_kernel(z, ids, right, *refs):
    pieces, (sent, kept, left, sums) = refs[: z.mp], refs[z.mp :]
    place(left, pieces, ids[1])
    grad_kernel(z, ids, left, right, sent, kept, sums)


def last_grad_kernel(z, ids, tokens, *refs):
    pieces, (turned, sent, kept, back, sums) = refs[: z.mp], refs[z.mp :]
    place(back, pieces, ids[1])
    for c in range(z.local):
        block = back[c].T
        turned[c] = block
        sums[c] = matmul(tokens[:, c * z.block : (c + 1) * z.block], block, 0, 0)
    split_grad(sums, sent, kept, ids[0])


def tokens_kernel(z, full, turned, out):
    for c in range(z.local):
        part = matmul(turned[c], full[c], 1, 1)
        out[:, c * z.block : (c + 1) * z.block] = part.astype(jnp.bfloat16)


def shaped(kind, *shape):
    return jax.ShapeDtypeStruct(shape, kind)


def run(body, outs, scratch, inputs, products):
    specs = [
        pl.BlockSpec(memory_space=pltpu.SMEM if one.dtype == jnp.int32 else pltpu.VMEM) for one in inputs
    ]
    moved = sum(math.prod(one.shape) * one.dtype.itemsize for one in (*inputs, *outs))
    return pl.pallas_call(
        body,
        out_shape=outs,
        in_specs=specs,
        out_specs=[pl.BlockSpec(memory_space=pltpu.VMEM) for _ in outs],
        scratch_shapes=scratch,
        compiler_params=pltpu.CompilerParams(vmem_limit_bytes=vmem_bytes),
        cost_estimate=pl.CostEstimate(flops=2 * products, bytes_accessed=moved, transcendentals=0),
    )(*inputs)


def on_device(tokens, cotangent, right_one, left_one, right_two, left_two):
    z = Sizes(tokens, right_one)
    bf16, f32 = jnp.bfloat16, jnp.float32
    scale = 1.0 / math.sqrt(z.tokens * z.dp)
    ids = jnp.stack([lax.axis_index("dp"), lax.axis_index("mp")]).astype(jnp.int32)
    products = z.local * z.block * z.block * z.tokens
    weight = shaped(bf16, z.local, z.block, z.block)
    acts = shaped(bf16, z.local, z.block, z.tokens)
    sends = [shaped(bf16, z.local * z.local, z.tokens)] * z.mp
    halves = [
        shaped(bf16, z.dp // 2, z.local * z.rows, z.block),
        shaped(f32, z.dp // 2, z.local * z.rows, z.block),
    ]
    mixed = pltpu.VMEM((z.tokens // lane_tile, z.block * z.local, lane_tile), f32)
    sums = pltpu.VMEM((z.local, z.block, z.block), f32)
    held = pltpu.VMEM((z.local, z.block, z.tokens), bf16)

    part = functools.partial

    first_pieces = gather_rows(right_one)
    outer_pieces = gather_rows(left_two)
    inner_pieces = gather_rows(left_one)
    second_pieces = gather_rows(right_two)
    count = len(first_pieces)

    upstream = exchange(run(part(turn_kernel, z), sends, [mixed], [ids, cotangent], 0))
    right_first, *parts = run(
        part(first_kernel, z, count), [weight] + sends, [mixed], [ids, tokens, *first_pieces], products
    )
    first_columns = exchange(parts)
    _, upstream_columns, *parts = run(
        part(middle_kernel, z, count, 1),
        [weight, acts] + sends,
        [mixed],
        [ids, *outer_pieces, *upstream],
        products,
    )
    second_rows = exchange(parts)
    left_first, columns, *parts = run(
        part(middle_kernel, z, count, 0),
        [weight, acts] + sends,
        [mixed],
        [ids, *inner_pieces, *first_columns],
        products,
    )
    preact = exchange(parts)
    right_second, hidden, second_back, *parts = run(
        part(gelu_kernel, z, count),
        [weight, acts, acts] + sends,
        [mixed],
        [ids, *second_pieces, *preact, *second_rows],
        products,
    )
    first_upstream = exchange(parts)
    parts = run(part(second_kernel, z), sends, [mixed], [ids, right_second, hidden], products)
    second_columns = exchange(parts)
    right_two_halves = run(part(grad_kernel, z), halves, [sums], [ids, hidden, second_back], products)
    _, upstream_rows, *parts = run(
        part(middle_kernel, z, 1, 1),
        [weight, acts] + sends,
        [mixed],
        [ids, left_first, *first_upstream],
        products,
    )
    first_rows = exchange(parts)
    left_two_halves = run(
        part(placed_grad_kernel, z), halves, [held, sums], [ids, upstream_columns, *second_columns], products
    )
    left_one_halves = run(part(grad_kernel, z), halves, [sums], [ids, columns, upstream_rows], products)
    turned, *right_one_halves = run(
        part(last_grad_kernel, z),
        [shaped(bf16, z.local, z.tokens, z.block)] + halves,
        [held, sums],
        [ids, tokens, *first_rows],
        products,
    )
    (tokens_grad,) = run(
        part(tokens_kernel, z),
        [shaped(bf16, z.tokens, z.local * z.block)],
        [],
        [right_first, turned],
        products,
    )
    summed = [
        scatter_rows(sent, kept, scale).reshape(z.local, z.rows, z.block)
        for sent, kept in (right_one_halves, left_one_halves, right_two_halves, left_two_halves)
    ]
    return (tokens_grad, *summed)


def solution(mesh):
    placed = (
        P("dp", "mp"),
        P("dp", "mp"),
        P("mp", "dp", None),
        P("mp", "dp", None),
        P("mp", "dp", None),
        P("mp", "dp", None),
    )
    return jax.shard_map(
        on_device,
        mesh=mesh,
        in_specs=placed,
        out_specs=(
            P("dp", "mp"),
            P("mp", "dp", None),
            P("mp", "dp", None),
            P("mp", "dp", None),
            P("mp", "dp", None),
        ),
        check_vma=False,
    )
```

time: 464 us -> 220 us (0.47)
  waiting for transfers between devices: 307 us -> 68 us
  starting transfers between devices: 15.8 us -> 93 us
  blocking collectives: 51.9 us -> 0 us
  Pallas kernels: 0 us -> 50.4 us
  local copies, waits for them, and re-layouts: 46.5 us -> 2.86 us
  matrix products: 21.4 us -> 0 us
  between operations: 14.3 us -> 1.04 us
    reduce_scatter x4 -> x0, waiting for transfers between devices: 188 us -> none  [the longest x1 68.5 us: on_device(): lax.psum_scatter(grad_left_two, 'dp', scatter_dimension=1, tiled=True)]
    all_gather x4 -> x0, waiting for transfers between devices: 105 us -> none  [the longest x1 35.4 us: on_device(): lax.all_gather(right_one, 'dp', axis=1, tiled=True)]
    ppermute x0 -> x65, starting transfers between devices: none -> 93 us  [hop(): return lax.ppermute(source, axis, [(i, i ^ offset) for i in range(size)])]
    ppermute x0 -> x65, waiting for transfers between devices: none -> 68 us  [hop(): return lax.ppermute(source, axis, [(i, i ^ offset) for i in range(size)])]
    all_to_all x3 -> x0, blocking collectives: 51.9 us -> none  [the longest x1 18.1 us: grad_columns(): lax.all_to_all(source, 'mp', split_axis=0, concat_axis=1, tiled=True)]
    pallas_call x0 -> x12, Pallas kernels: none -> 50.4 us  [run(): pl.pallas_call(body, out_shape=outs, in_specs=specs, out_specs=[pl.BlockS...]
    dot_general x11 -> x0, matrix products: 21.4 us -> none  [the longest x1 4.55 us: on_device(): jnp.einsum('jbt,bij->bit', second_rows, right_second, preferred_element_t...]
    all_to_all x4 -> x0, starting transfers between devices: 15.5 us -> none  [the longest x2 7.04 us: to_blocks(): return lax.all_to_all(source, 'mp', split_axis=0, concat_axis=1, tiled=True)]
  transfers between devices with their start and end apart: 12 -> 65, of which waited for: 8 -> 22; matrix products, arithmetic and copies ran while one was open for 15% -> 2% of each run, Pallas kernels for 0% -> 18%
where the time goes in v2:
time: 220 us
  starting transfers between devices  93 us (42%)
  waiting for transfers between devices  68 us (31%)
  Pallas kernels  50.4 us (23%)
  other arithmetic  4.29 us (2%)
  local copies, waits for them, and re-layouts  2.86 us (1%)
    ppermute x65, starting transfers between devices, hop(): return lax.ppermute(source, axis, [(i, i ^ offset) for i in range(size)])  93 us
    ppermute x65, waiting for transfers between devices, hop(): return lax.ppermute(source, axis, [(i, i ^ offset) for i in range(size)])  68 us
    pallas_call x12, Pallas kernels, run(): pl.pallas_call(body, out_shape=outs, in_specs=specs, out_specs=[pl.BlockS...  50.4 us
  transfers between devices with their start and end apart: 65, of which 22 were waited for; matrix products, arithmetic and copies ran while one was open for 2% of the time, Pallas kernels for 18%

profile of v2, /device:TPU:0, one launch (start us, length us, event | category | flops | bytes accessed | tf_op | source)
XLA Modules:
  0.0 219.6 jit_solution(14966977673675573160)
XLA Ops:
  0.6 3.1 %collective-permute-start.1 = (bf16[32,16,128]{2,1,0:T(8,128)(2,1)}, bf16[32,16,128]{2,1,0:T(8,128)(2,1)S(1)}, u32[]{:S(2)}, u32[]{:S(2)}) collective-permute-start(bf16[32,16,128]{2,1,0:T(8,128)(2,1)} %param.8), channel_id=1, source_target_pairs={{0,8},{4,12},{8,0},{12,4},{16,24},{20,28},{24,16},{28,20},{1,9},{5... | collective-permute-start | bytes 393224 | tf_op jit(solution)/shard_map/ppermute | solution.py:28
  3.7 2.6 %collective-permute-start.3 = (bf16[32,16,128]{2,1,0:T(8,128)(2,1)}, bf16[32,16,128]{2,1,0:T(8,128)(2,1)S(1)}, u32[]{:S(2)}, u32[]{:S(2)}) collective-permute-start(bf16[32,16,128]{2,1,0:T(8,128)(2,1)} %param.8), channel_id=1, source_target_pairs={{0,16},{4,20},{8,24},{12,28},{16,0},{20,4},{24,8},{28,12},{1,17},{... | collective-permute-start | bytes 393224 | tf_op jit(solution)/shard_map/ppermute | solution.py:28
  6.3 1.7 collective-permute-start
  9.0 3.2 %collective-permute-start.10 = (bf16[32,16,128]{2,1,0:T(8,128)(2,1)}, bf16[32,16,128]{2,1,0:T(8,128)(2,1)S(1)}, u32[]{:S(2)}, u32[]{:S(2)}) collective-permute-start(bf16[32,16,128]{2,1,0:T(8,128)(2,1)} %param.9), channel_id=1, source_target_pairs={{0,16},{4,20},{8,24},{12,28},{16,0},{20,4},{24,8},{28,12},{1,17},{... | collective-permute-start | bytes 393224 | tf_op jit(solution)/shard_map/ppermute | solution.py:28
  12.2 4.7 %collective-permute-done.3 = bf16[32,16,128]{2,1,0:T(8,128)(2,1)S(1)} collective-permute-done((bf16[32,16,128]{2,1,0:T(8,128)(2,1)}, bf16[32,16,128]{2,1,0:T(8,128)(2,1)S(1)}, u32[]{:S(2)}, u32[]{:S(2)}) %collective-permute-start.3) | collective-permute-done | bytes 131104 | tf_op jit(solution)/shard_map/ppermute | solution.py:28
  16.9 3.0 %collective-permute-start.12 = (bf16[32,16,128]{2,1,0:T(8,128)(2,1)}, bf16[32,16,128]{2,1,0:T(8,128)(2,1)S(1)}, u32[]{:S(2)}, u32[]{:S(2)}) collective-permute-start(bf16[32,16,128]{2,1,0:T(8,128)(2,1)} %param.9), channel_id=1, source_target_pairs={{0,24},{4,28},{8,16},{12,20},{16,8},{20,12},{24,0},{28,4},{1,25},{... | collective-permute-start | bytes 393224 | tf_op jit(solution)/shard_map/ppermute | solution.py:28
  21.4 7.4 %collective-permute-start.28 = (bf16[32,16,128]{2,1,0:T(8,128)(2,1)}, bf16[32,16,128]{2,1,0:T(8,128)(2,1)S(1)}, u32[]{:S(2)}, u32[]{:S(2)}) collective-permute-start(bf16[32,16,128]{2,1,0:T(8,128)(2,1)} %param.11), channel_id=1, source_target_pairs={{0,8},{4,12},{8,0},{12,4},{16,24},{20,28},{24,16},{28,20},{1,9},{5... | collective-permute-start | bytes 393224 | tf_op jit(solution)/shard_map/ppermute | solution.py:28
  29.7 2.1 collective-permute-start.32
  33.3 2.5 %collective-permute-start.18 = (bf16[32,16,128]{2,1,0:T(8,128)(2,1)}, bf16[32,16,128]{2,1,0:T(8,128)(2,1)S(1)}, u32[]{:S(2)}, u32[]{:S(2)}) collective-permute-start(bf16[32,16,128]{2,1,0:T(8,128)(2,1)} %param.10), channel_id=1, source_target_pairs={{0,8},{4,12},{8,0},{12,4},{16,24},{20,28},{24,16},{28,20},{1,9},{5... | collective-permute-start | bytes 393224 | tf_op jit(solution)/shard_map/ppermute | solution.py:28
  35.8 2.4 %collective-permute-start.20 = (bf16[32,16,128]{2,1,0:T(8,128)(2,1)}, bf16[32,16,128]{2,1,0:T(8,128)(2,1)S(1)}, u32[]{:S(2)}, u32[]{:S(2)}) collective-permute-start(bf16[32,16,128]{2,1,0:T(8,128)(2,1)} %param.10), channel_id=1, source_target_pairs={{0,16},{4,20},{8,24},{12,28},{16,0},{20,4},{24,8},{28,12},{1,17},{... | collective-permute-start | bytes 393224 | tf_op jit(solution)/shard_map/ppermute | solution.py:28
  38.2 4.0 %collective-permute-done.30 = bf16[32,16,128]{2,1,0:T(8,128)(2,1)S(1)} collective-permute-done((bf16[32,16,128]{2,1,0:T(8,128)(2,1)}, bf16[32,16,128]{2,1,0:T(8,128)(2,1)S(1)}, u32[]{:S(2)}, u32[]{:S(2)}) %collective-permute-start.30) | collective-permute-done | bytes 131104 | tf_op jit(solution)/shard_map/ppermute | solution.py:28
  42.2 2.1 collective-permute-start.22
  44.3 3.1 %collective-permute-start.2 = (bf16[32,16,128]{2,1,0:T(8,128)(2,1)S(1)}, bf16[32,16,128]{2,1,0:T(8,128)(2,1)S(1)}, u32[]{:S(2)}, u32[]{:S(2)}) collective-permute-start(bf16[32,16,128]{2,1,0:T(8,128)(2,1)S(1)} %collective-permute-done.1), channel_id=1, source_target_pairs={{0,4},{4,0},{8,12},{12,8},{16,20},{20,16},{24,28},{28,24},{1,5},{5... | collective-permute-start | bytes 393224 | tf_op jit(solution)/shard_map/ppermute | solution.py:28
  48.1 3.5 %shard_map.103 = (bf16[1024,128]{1,0:T(8,128)(2,1)}, bf16[1024,128]{1,0:T(8,128)(2,1)}, bf16[1024,128]{1,0:T(8,128)(2,1)}, bf16[1024,128]{1,0:T(8,128)(2,1)}) custom-call(s32[2]{0:T(128)} %pad_add_fusion.ids, bf16[128,4096]{1,0:T(8,128)(2,1)} %cotangent.1), custom_call_target="tpu_custom_call" | custom-call | bytes 2097160 | tf_op jit(solution)/shard_map/pallas_call | solution.py:202
  51.8 1.6 collective-permute-start.35
  53.6 2.0 collective-permute-start.6
  55.8 4.2 %collective-permute-done.6 = bf16[32,16,128]{2,1,0:T(8,128)(2,1)S(1)} collective-permute-done((bf16[32,16,128]{2,1,0:T(8,128)(2,1)S(1)}, bf16[32,16,128]{2,1,0:T(8,128)(2,1)S(1)}, u32[]{:S(2)}, u32[]{:S(2)}) %collective-permute-start.6) | collective-permute-done | bytes 131104 | tf_op jit(solution)/shard_map/ppermute | solution.py:28
  60.0 2.0 collective-permute-start.29
  62.8 2.0 collective-permute-start.31
  64.9 4.6 %shard_map.101 = (bf16[32,128,128]{2,1,0:T(8,128)(2,1)}, bf16[1024,128]{1,0:T(8,128)(2,1)}, bf16[1024,128]{1,0:T(8,128)(2,1)}, bf16[1024,128]{1,0:T(8,128)(2,1)}, bf16[1024,128]{1,0:T(8,128)(2,1)}) custom-call(s32[2]{0:T(128)} %pad_add_fusion.ids, bf16[128,4096]{1,0:T(8,128)(2,1)} %tokens.3, bf16[512,128]{1,0:T(8,128)(2,1)} %bitcast.106, ...), custom_call_target="tpu_custom_call" | custom-call | flops 134217728 | bytes 4194312 | tf_op jit(solution)/shard_map/pallas_call | solution.py:202
  69.6 1.6 collective-permute-start.15
  71.5 2.0 collective-permute-start.11
  74.2 4.5 %shard_map.104 = (bf16[32,128,128]{2,1,0:T(8,128)(2,1)}, bf16[32,128,128]{2,1,0:T(8,128)(2,1)}, bf16[1024,128]{1,0:T(8,128)(2,1)}, bf16[1024,128]{1,0:T(8,128)(2...) custom-call(s32[2]{0:T(128)} %pad_add_fusion.ids, bf16[512,128]{1,0:T(8,128)(2,1)} %bitcast.107, ...), custom_call_target="tpu_custom_call" | custom-call | flops 134217728 | bytes 5242888 | tf_op jit(solution)/shard_map/pallas_call | solution.py:202
  80.3 1.7 collective-permute-start.17
  82.4 1.8 collective-permute-start.21
  85.7 4.6 %shard_map.102 = (bf16[32,128,128]{2,1,0:T(8,128)(2,1)}, bf16[32,128,128]{2,1,0:T(8,128)(2,1)}, bf16[1024,128]{1,0:T(8,128)(2,1)}, bf16[1024,128]{1,0:T(8,128)(2...) custom-call(s32[2]{0:T(128)} %pad_add_fusion.ids, bf16[512,128]{1,0:T(8,128)(2,1)} %bitcast.108, ...), custom_call_target="tpu_custom_call" | custom-call | flops 134217728 | bytes 5242888 | tf_op jit(solution)/shard_map/pallas_call | solution.py:202
  95.5 4.0 %collective-permute-done.38.refs_14_ = bf16[1024,128]{1,0:T(8,128)(2,1)S(1)} collective-permute-done((bf16[1024,128]{1,0:T(8,128)(2,1)S(1)}, bf16[1024,128]{1,0:T(8,128)(2,1)S(1)}, u32[]{:S(2)}, u32[]{:S(2)}) %collective-permute-start.38) | collective-permute-done | bytes 262176 | tf_op jit(solution)/shard_map/ppermute | solution.py:28
  99.5 4.7 %collective-permute-done.39.refs_15_ = bf16[1024,128]{1,0:T(8,128)(2,1)S(1)} collective-permute-done((bf16[1024,128]{1,0:T(8,128)(2,1)S(1)}, bf16[1024,128]{1,0:T(8,128)(2,1)S(1)}, u32[]{:S(2)}, u32[]{:S(2)}) %collective-permute-start.39) | collective-permute-done | bytes 262176 | tf_op jit(solution)/shard_map/ppermute | solution.py:28
  104.2 6.6 %collective-permute-done.25.refs_10_ = bf16[1024,128]{1,0:T(8,128)(2,1)S(1)} collective-permute-done((bf16[1024,128]{1,0:T(8,128)(2,1)}, bf16[1024,128]{1,0:T(8,128)(2,1)S(1)}, u32[]{:S(2)}, u32[]{:S(2)}) %collective-permute-start.25) | collective-permute-done | bytes 262176 | tf_op jit(solution)/shard_map/ppermute | solution.py:28
  110.8 4.4 %collective-permute-done.26.refs_11_ = bf16[1024,128]{1,0:T(8,128)(2,1)S(1)} collective-permute-done((bf16[1024,128]{1,0:T(8,128)(2,1)}, bf16[1024,128]{1,0:T(8,128)(2,1)S(1)}, u32[]{:S(2)}, u32[]{:S(2)}) %collective-permute-start.26) | collective-permute-done | bytes 262176 | tf_op jit(solution)/shard_map/ppermute | solution.py:28
  115.9 6.1 %shard_map.105 = (bf16[32,128,128]{2,1,0:T(8,128)(2,1)}, bf16[32,128,128]{2,1,0:T(8,128)(2,1)}, bf16[32,128,128]{2,1,0:T(8,128)(2,1)}, bf16[1024,128]{1,0:T(8,12...) custom-call(s32[2]{0:T(128)} %pad_add_fusion.ids, ...), custom_call_target="tpu_custom_call" | custom-call | flops 134217728 | bytes 7340040 | tf_op jit(solution)/shard_map/pallas_call | solution.py:202
  122.0 4.3 %shard_map.111 = (bf16[1024,128]{1,0:T(8,128)(2,1)}, bf16[1024,128]{1,0:T(8,128)(2,1)}, bf16[1024,128]{1,0:T(8,128)(2,1)}, bf16[1024,128]{1,0:T(8,128)(2,1)}) custom-call(s32[2]{0:T(128)} %pad_add_fusion.ids, bf16[32,128,128]{2,1,0:T(8,128)(2,1)} %get-tuple-element.88.full, bf16[32,128,128]{2,1,0:T(8,128)(2,1)} %get-tuple-element.83.left.hidden), custom_call_target="tpu_custom_call" | custom-call | flops 134217728 | bytes 3145736 | tf_op jit(solution)/shard_map/pallas_call | solution.py:202
  128.2 3.8 %shard_map.110 = (bf16[4,512,128]{2,1,0:T(8,128)(2,1)}, f32[4,512,128]{2,1,0:T(8,128)}) custom-call(s32[2]{0:T(128)} %pad_add_fusion.ids, bf16[32,128,128]{2,1,0:T(8,128)(2,1)} %get-tuple-element.83.left.hidden, bf16[32,128,128]{2,1,0:T(8,128)(2,1)} %get-tuple-element.84.right), custom_call_target="tpu_custom_call" | custom-call | flops 134217728 | bytes 3670024 | tf_op jit(solution)/shard_map/pallas_call | solution.py:202
  135.6 6.0 %collective-permute-done.60.refs_3_ = bf16[1024,128]{1,0:T(8,128)(2,1)S(1)} collective-permute-done((bf16[1024,128]{1,0:T(8,128)(2,1)S(1)}, bf16[1024,128]{1,0:T(8,128)(2,1)S(1)}, u32[]{:S(2)}, u32[]{:S(2)}) %collective-permute-start.60) | collective-permute-done | bytes 262176 | tf_op jit(solution)/shard_map/ppermute | solution.py:28
  142.3 3.7 %shard_map.112 = (bf16[4,512,128]{2,1,0:T(8,128)(2,1)}, f32[4,512,128]{2,1,0:T(8,128)}) custom-call(s32[2]{0:T(128)} %pad_add_fusion.ids, bf16[32,128,128]{2,1,0:T(8,128)(2,1)} %get-tuple-element.87.right, bf16[1024,128]{1,0:T(8,128)(2,1)} %get-tuple-element.89.refs_0_, bf16[1024,128]{1,0:T(8,128)(2,1)} %copy-done.15, bf16[1024,128]{1,0:T(8,128)(2,1)} %copy-done.16, ...), custom_call_target="tpu_custom_call" | custom-call | flops 134217728 | bytes 3670024 | tf_op jit(solution)/shard_map/pallas_call | solution.py:202
  147.1 5.7 %collective-permute-done.42.refs_4_ = bf16[1024,128]{1,0:T(8,128)(2,1)S(1)} collective-permute-done((bf16[1024,128]{1,0:T(8,128)(2,1)S(1)}, bf16[1024,128]{1,0:T(8,128)(2,1)S(1)}, u32[]{:S(2)}, u32[]{:S(2)}) %collective-permute-start.42) | collective-permute-done | bytes 262176 | tf_op jit(solution)/shard_map/ppermute | solution.py:28
  153.5 4.4 %shard_map.106 = (bf16[32,128,128]{2,1,0:T(8,128)(2,1)}, bf16[32,128,128]{2,1,0:T(8,128)(2,1)}, bf16[1024,128]{1,0:T(8,128)(2,1)}, bf16[1024,128]{1,0:T(8,128)(2...) custom-call(s32[2]{0:T(128)} %pad_add_fusion.ids, bf16[32,128,128]{2,1,0:T(8,128)(2,1)} %get-tuple-element.55.refs_0_, ...), custom_call_target="tpu_custom_call" | custom-call | flops 134217728 | bytes 5242888 | tf_op jit(solution)/shard_map/pallas_call | solution.py:202
  161.9 5.3 %collective-permute-done.44.refs_2_ = bf16[1024,128]{1,0:T(8,128)(2,1)S(1)} collective-permute-done((bf16[1024,128]{1,0:T(8,128)(2,1)}, bf16[1024,128]{1,0:T(8,128)(2,1)S(1)}, u32[]{:S(2)}, u32[]{:S(2)}) %collective-permute-start.44) | collective-permute-done | bytes 262176 | tf_op jit(solution)/shard_map/ppermute | solution.py:28
  167.4 3.7 %shard_map.109 = (bf16[4,512,128]{2,1,0:T(8,128)(2,1)}, f32[4,512,128]{2,1,0:T(8,128)}) custom-call(s32[2]{0:T(128)} %pad_add_fusion.ids, bf16[32,128,128]{2,1,0:T(8,128)(2,1)} %get-tuple-element.79.left, bf16[32,128,128]{2,1,0:T(8,128)(2,1)} %get-tuple-element.80.right), custom_call_target="tpu_custom_call" | custom-call | flops 134217728 | bytes 3670024 | tf_op jit(solution)/shard_map/pallas_call | solution.py:202
  172.8 3.8 %shard_map.107 = (bf16[32,128,128]{2,1,0:T(8,128)(2,1)}, bf16[4,512,128]{2,1,0:T(8,128)(2,1)}, f32[4,512,128]{2,1,0:T(8,128)}) custom-call(s32[2]{0:T(128)} %pad_add_fusion.ids, bf16[128,4096]{1,0:T(8,128)(2,1)} %tokens.3, bf16[1024,128]{1,0:T(8,128)(2,1)} %get-tuple-element.72.refs_0_, bf16[1024,128]{1,0:T(8,128)(2,1)} %copy-done.10, ...), custom_call_target="tpu_custom_call" | custom-call | flops 134217728 | bytes 4718600 | tf_op jit(solution)/shard_map/pallas_call | solution.py:202
  176.6 3.5 %shard_map.108 = bf16[128,4096]{1,0:T(8,128)(2,1)} custom-call(bf16[32,128,128]{2,1,0:T(8,128)(2,1)} %get-tuple-element.50.full, bf16[32,128,128]{2,1,0:T(8,128)(2,1)} %get-tuple-element.76.turned), custom_call_target="tpu_custom_call" | custom-call | flops 134217728 | bytes 3145728 | tf_op jit(solution)/shard_map/pallas_call | solution.py:202
  183.7 2.0 collective-permute-start.63
  189.2 1.7 collective-permute-start.52
  190.9 5.8 %collective-permute-done.63 = bf16[512,128]{1,0:T(8,128)(2,1)S(1)} collective-permute-done((bf16[512,128]{1,0:T(8,128)(2,1)S(1)}, bf16[512,128]{1,0:T(8,128)(2,1)S(1)}, u32[]{:S(2)}, u32[]{:S(2)}) %collective-permute-start.63) | collective-permute-done | bytes 131104 | tf_op jit(solution)/shard_map/ppermute | solution.py:28
  196.7 1.9 collective-permute-start.53
  199.5 9.5 %collective-permute-start.47 = (bf16[512,128]{1,0:T(8,128)(2,1)S(1)}, bf16[512,128]{1,0:T(8,128)(2,1)S(1)}, u32[]{:S(2)}, u32[]{:S(2)}) collective-permute-start(bf16[512,128]{1,0:T(8,128)(2,1)S(1)} %get-tuple-element.112), channel_id=1, source_target_pairs={{0,8},{4,12},{8,0},{12,4},{16,24},{20,28},{24,16},{28,20},{1,9},{5... | collective-permute-start | bytes 393224 | tf_op jit(solution)/shard_map/ppermute | solution.py:28
  209.6 1.9 collective-permute-start.49
  213.4 5.5 %collective-permute-done.48 = bf16[512,128]{1,0:T(8,128)(2,1)S(1)} collective-permute-done((bf16[512,128]{1,0:T(8,128)(2,1)S(1)}, bf16[512,128]{1,0:T(8,128)(2,1)S(1)}, u32[]{:S(2)}, u32[]{:S(2)}) %collective-permute-start.48) | collective-permute-done | bytes 131104 | tf_op jit(solution)/shard_map/ppermute | solution.py:28
  (229 shorter events, 42.6 us)
Async XLA Ops:
  3.7 13.2 %collective-permute-start.3 = (bf16[32,16,128]{2,1,0:T(8,128)(2,1)}, bf16[32,16,128]{2,1,0:T(8,128)(2,1)S(1)}, u32[]{:S(2)}, u32[]{:S(2)}) collective-permute-start(bf16[32,16,128]{2,1,0:T(8,128)(2,1)} %param.8), channel_id=1, source_target_pairs={{0,16},{4,20},{8,24},{12,28},{16,0},{20,4},{24,8},{28,12},{1,17},{... | collective-permute-start | bytes 393224 | tf_op jit(solution)/shard_map/ppermute | solution.py:28
  6.3 13.6 %collective-permute-start.5 = (bf16[32,16,128]{2,1,0:T(8,128)(2,1)}, bf16[32,16,128]{2,1,0:T(8,128)(2,1)S(1)}, u32[]{:S(2)}, u32[]{:S(2)}) collective-permute-start(bf16[32,16,128]{2,1,0:T(8,128)(2,1)} %param.8), channel_id=1, source_target_pairs={{0,24},{4,28},{8,16},{12,20},{16,8},{20,12},{24,0},{28,4},{1,25},{... | collective-permute-start | bytes 393224 | tf_op jit(solution)/shard_map/ppermute | solution.py:28
  6.3 15.1 %collective-permute-start = (bf16[32,16,128]{2,1,0:T(8,128)(2,1)}, bf16[32,16,128]{2,1,0:T(8,128)(2,1)S(1)}, u32[]{:S(2)}, u32[]{:S(2)}) collective-permute-start(bf16[32,16,128]{2,1,0:T(8,128)(2,1)} %param.8), channel_id=1, source_target_pairs={{0,4},{4,0},{8,12},{12,8},{16,20},{20,16},{24,28},{28,24},{1,5},{5... | collective-permute-start | bytes 393224 | tf_op jit(solution)/shard_map/ppermute | solution.py:28
  8.0 20.7 %collective-permute-start.8 = (bf16[32,16,128]{2,1,0:T(8,128)(2,1)}, bf16[32,16,128]{2,1,0:T(8,128)(2,1)S(1)}, u32[]{:S(2)}, u32[]{:S(2)}) collective-permute-start(bf16[32,16,128]{2,1,0:T(8,128)(2,1)} %param.9), channel_id=1, source_target_pairs={{0,8},{4,12},{8,0},{12,4},{16,24},{20,28},{24,16},{28,20},{1,9},{5... | collective-permute-start | bytes 393224 | tf_op jit(solution)/shard_map/ppermute | solution.py:28
  9.0 20.7 %collective-permute-start.10 = (bf16[32,16,128]{2,1,0:T(8,128)(2,1)}, bf16[32,16,128]{2,1,0:T(8,128)(2,1)S(1)}, u32[]{:S(2)}, u32[]{:S(2)}) collective-permute-start(bf16[32,16,128]{2,1,0:T(8,128)(2,1)} %param.9), channel_id=1, source_target_pairs={{0,16},{4,20},{8,24},{12,28},{16,0},{20,4},{24,8},{28,12},{1,17},{... | collective-permute-start | bytes 393224 | tf_op jit(solution)/shard_map/ppermute | solution.py:28
  16.9 15.0 %collective-permute-start.12 = (bf16[32,16,128]{2,1,0:T(8,128)(2,1)}, bf16[32,16,128]{2,1,0:T(8,128)(2,1)S(1)}, u32[]{:S(2)}, u32[]{:S(2)}) collective-permute-start(bf16[32,16,128]{2,1,0:T(8,128)(2,1)} %param.9), channel_id=1, source_target_pairs={{0,24},{4,28},{8,16},{12,20},{16,8},{20,12},{24,0},{28,4},{1,25},{... | collective-permute-start | bytes 393224 | tf_op jit(solution)/shard_map/ppermute | solution.py:28
  19.9 13.4 %collective-permute-start.7 = (bf16[32,16,128]{2,1,0:T(8,128)(2,1)}, bf16[32,16,128]{2,1,0:T(8,128)(2,1)S(1)}, u32[]{:S(2)}, u32[]{:S(2)}) collective-permute-start(bf16[32,16,128]{2,1,0:T(8,128)(2,1)} %param.9), channel_id=1, source_target_pairs={{0,4},{4,0},{8,12},{12,8},{16,20},{20,16},{24,28},{28,24},{1,5},{5... | collective-permute-start | bytes 393224 | tf_op jit(solution)/shard_map/ppermute | solution.py:28
  21.4 14.4 %collective-permute-start.28 = (bf16[32,16,128]{2,1,0:T(8,128)(2,1)}, bf16[32,16,128]{2,1,0:T(8,128)(2,1)S(1)}, u32[]{:S(2)}, u32[]{:S(2)}) collective-permute-start(bf16[32,16,128]{2,1,0:T(8,128)(2,1)} %param.11), channel_id=1, source_target_pairs={{0,8},{4,12},{8,0},{12,4},{16,24},{20,28},{24,16},{28,20},{1,9},{5... | collective-permute-start | bytes 393224 | tf_op jit(solution)/shard_map/ppermute | solution.py:28
  28.8 13.4 %collective-permute-start.30 = (bf16[32,16,128]{2,1,0:T(8,128)(2,1)}, bf16[32,16,128]{2,1,0:T(8,128)(2,1)S(1)}, u32[]{:S(2)}, u32[]{:S(2)}) collective-permute-start(bf16[32,16,128]{2,1,0:T(8,128)(2,1)} %param.11), channel_id=1, source_target_pairs={{0,16},{4,20},{8,24},{12,28},{16,0},{20,4},{24,8},{28,12},{1,17},{... | collective-permute-start | bytes 393224 | tf_op jit(solution)/shard_map/ppermute | solution.py:28
  29.7 14.6 %collective-permute-start.32 = (bf16[32,16,128]{2,1,0:T(8,128)(2,1)}, bf16[32,16,128]{2,1,0:T(8,128)(2,1)S(1)}, u32[]{:S(2)}, u32[]{:S(2)}) collective-permute-start(bf16[32,16,128]{2,1,0:T(8,128)(2,1)} %param.11), channel_id=1, source_target_pairs={{0,24},{4,28},{8,16},{12,20},{16,8},{20,12},{24,0},{28,4},{1,25},{... | collective-permute-start | bytes 393224 | tf_op jit(solution)/shard_map/ppermute | solution.py:28
  31.8 15.5 %collective-permute-start.27 = (bf16[32,16,128]{2,1,0:T(8,128)(2,1)}, bf16[32,16,128]{2,1,0:T(8,128)(2,1)S(1)}, u32[]{:S(2)}, u32[]{:S(2)}) collective-permute-start(bf16[32,16,128]{2,1,0:T(8,128)(2,1)} %param.11), channel_id=1, source_target_pairs={{0,4},{4,0},{8,12},{12,8},{16,20},{20,16},{24,28},{28,24},{1,5},{5... | collective-permute-start | bytes 393224 | tf_op jit(solution)/shard_map/ppermute | solution.py:28
  33.3 18.3 %collective-permute-start.18 = (bf16[32,16,128]{2,1,0:T(8,128)(2,1)}, bf16[32,16,128]{2,1,0:T(8,128)(2,1)S(1)}, u32[]{:S(2)}, u32[]{:S(2)}) collective-permute-start(bf16[32,16,128]{2,1,0:T(8,128)(2,1)} %param.10), channel_id=1, source_target_pairs={{0,8},{4,12},{8,0},{12,4},{16,24},{20,28},{24,16},{28,20},{1,9},{5... | collective-permute-start | bytes 393224 | tf_op jit(solution)/shard_map/ppermute | solution.py:28
  35.8 16.0 %collective-permute-start.20 = (bf16[32,16,128]{2,1,0:T(8,128)(2,1)}, bf16[32,16,128]{2,1,0:T(8,128)(2,1)S(1)}, u32[]{:S(2)}, u32[]{:S(2)}) collective-permute-start(bf16[32,16,128]{2,1,0:T(8,128)(2,1)} %param.10), channel_id=1, source_target_pairs={{0,16},{4,20},{8,24},{12,28},{16,0},{20,4},{24,8},{28,12},{1,17},{... | collective-permute-start | bytes 393224 | tf_op jit(solution)/shard_map/ppermute | solution.py:28
  42.2 11.2 %collective-permute-start.22 = (bf16[32,16,128]{2,1,0:T(8,128)(2,1)}, bf16[32,16,128]{2,1,0:T(8,128)(2,1)S(1)}, u32[]{:S(2)}, u32[]{:S(2)}) collective-permute-start(bf16[32,16,128]{2,1,0:T(8,128)(2,1)} %param.10), channel_id=1, source_target_pairs={{0,24},{4,28},{8,16},{12,20},{16,8},{20,12},{24,0},{28,4},{1,25},{... | collective-permute-start | bytes 393224 | tf_op jit(solution)/shard_map/ppermute | solution.py:28
  51.7 13.1 %collective-permute-start.34 = (bf16[1024,128]{1,0:T(8,128)(2,1)}, bf16[1024,128]{1,0:T(8,128)(2,1)S(1)}, u32[]{:S(2)}, u32[]{:S(2)}) collective-permute-start(bf16[1024,128]{1,0:T(8,128)(2,1)} %get-tuple-element.61), channel_id=1, source_target_pairs={{0,1},{1,0},{2,3},{3,2},{4,5},{5,4},{6,7},{7,6},{8,9},{9,8},{10,11... | collective-permute-start | bytes 786440 | tf_op jit(solution)/shard_map/ppermute | solution.py:28
  51.8 17.7 %collective-permute-start.35 = (bf16[1024,128]{1,0:T(8,128)(2,1)}, bf16[1024,128]{1,0:T(8,128)(2,1)S(1)}, u32[]{:S(2)}, u32[]{:S(2)}) collective-permute-start(bf16[1024,128]{1,0:T(8,128)(2,1)} %get-tuple-element.62), channel_id=1, source_target_pairs={{0,2},{1,3},{2,0},{3,1},{4,6},{5,7},{6,4},{7,5},{8,10},{9,11},{10,... | collective-permute-start | bytes 786440 | tf_op jit(solution)/shard_map/ppermute | solution.py:28
  53.4 16.2 %collective-permute-start.36 = (bf16[1024,128]{1,0:T(8,128)(2,1)}, bf16[1024,128]{1,0:T(8,128)(2,1)S(1)}, u32[]{:S(2)}, u32[]{:S(2)}) collective-permute-start(bf16[1024,128]{1,0:T(8,128)(2,1)} %get-tuple-element.63), channel_id=1, source_target_pairs={{0,3},{1,2},{2,1},{3,0},{4,7},{5,6},{6,5},{7,4},{8,11},{9,10},{10,... | collective-permute-start | bytes 786440 | tf_op jit(solution)/shard_map/ppermute | solution.py:28
  60.0 11.2 %collective-permute-start.29 = (bf16[32,16,128]{2,1,0:T(8,128)(2,1)S(1)}, bf16[32,16,128]{2,1,0:T(8,128)(2,1)S(1)}, u32[]{:S(2)}, u32[]{:S(2)}) collective-permute-start(bf16[32,16,128]{2,1,0:T(8,128)(2,1)S(1)} %collective-permute-done.28), channel_id=1, source_target_pairs={{0,4},{4,0},{8,12},{12,8},{16,20},{20,16},{24,28},{28,24},{1,5},{5... | collective-permute-start | bytes 393224 | tf_op jit(solution)/shard_map/ppermute | solution.py:28
  69.5 12.6 %collective-permute-start.14 = (bf16[1024,128]{1,0:T(8,128)(2,1)}, bf16[1024,128]{1,0:T(8,128)(2,1)S(1)}, u32[]{:S(2)}, u32[]{:S(2)}) collective-permute-start(bf16[1024,128]{1,0:T(8,128)(2,1)} %get-tuple-element.52), channel_id=1, source_target_pairs={{0,1},{1,0},{2,3},{3,2},{4,5},{5,4},{6,7},{7,6},{8,9},{9,8},{10,11... | collective-permute-start | bytes 786440 | tf_op jit(solution)/shard_map/ppermute | solution.py:28
  69.6 12.8 %collective-permute-start.15 = (bf16[1024,128]{1,0:T(8,128)(2,1)}, bf16[1024,128]{1,0:T(8,128)(2,1)S(1)}, u32[]{:S(2)}, u32[]{:S(2)}) collective-permute-start(bf16[1024,128]{1,0:T(8,128)(2,1)} %get-tuple-element.53), channel_id=1, source_target_pairs={{0,2},{1,3},{2,0},{3,1},{4,6},{5,7},{6,4},{7,5},{8,10},{9,11},{10,... | collective-permute-start | bytes 786440 | tf_op jit(solution)/shard_map/ppermute | solution.py:28
  71.2 13.0 %collective-permute-start.16 = (bf16[1024,128]{1,0:T(8,128)(2,1)}, bf16[1024,128]{1,0:T(8,128)(2,1)S(1)}, u32[]{:S(2)}, u32[]{:S(2)}) collective-permute-start(bf16[1024,128]{1,0:T(8,128)(2,1)} %get-tuple-element.54), channel_id=1, source_target_pairs={{0,3},{1,2},{2,1},{3,0},{4,7},{5,6},{6,5},{7,4},{8,11},{9,10},{10,... | collective-permute-start | bytes 786440 | tf_op jit(solution)/shard_map/ppermute | solution.py:28
  78.7 16.8 %collective-permute-start.37 = (bf16[1024,128]{1,0:T(8,128)(2,1)}, bf16[1024,128]{1,0:T(8,128)(2,1)S(1)}, u32[]{:S(2)}, u32[]{:S(2)}) collective-permute-start(bf16[1024,128]{1,0:T(8,128)(2,1)} %get-tuple-element.65), channel_id=1, source_target_pairs={{0,1},{1,0},{2,3},{3,2},{4,5},{5,4},{6,7},{7,6},{8,9},{9,8},{10,11... | collective-permute-start | bytes 786440 | tf_op jit(solution)/shard_map/ppermute | solution.py:28
  80.3 10.0 %collective-permute-start.17 = (bf16[32,16,128]{2,1,0:T(8,128)(2,1)S(1)}, bf16[32,16,128]{2,1,0:T(8,128)(2,1)S(1)}, u32[]{:S(2)}, u32[]{:S(2)}) collective-permute-start(bf16[32,16,128]{2,1,0:T(8,128)(2,1)S(1)} %copy-done.46), channel_id=1, source_target_pairs={{0,4},{4,0},{8,12},{12,8},{16,20},{20,16},{24,28},{28,24},{1,5},{5... | collective-permute-start | bytes 393224 | tf_op jit(solution)/shard_map/ppermute | solution.py:28
  82.1 9.8 %collective-permute-start.19 = (bf16[32,16,128]{2,1,0:T(8,128)(2,1)S(1)}, bf16[32,16,128]{2,1,0:T(8,128)(2,1)S(1)}, u32[]{:S(2)}, u32[]{:S(2)}) collective-permute-start(bf16[32,16,128]{2,1,0:T(8,128)(2,1)S(1)} %collective-permute-done.18), channel_id=1, source_target_pairs={{0,4},{4,0},{8,12},{12,8},{16,20},{20,16},{24,28},{28,24},{1,5},{5... | collective-permute-start | bytes 393224 | tf_op jit(solution)/shard_map/ppermute | solution.py:28
  82.4 9.9 %collective-permute-start.21 = (bf16[32,16,128]{2,1,0:T(8,128)(2,1)S(1)}, bf16[32,16,128]{2,1,0:T(8,128)(2,1)S(1)}, u32[]{:S(2)}, u32[]{:S(2)}) collective-permute-start(bf16[32,16,128]{2,1,0:T(8,128)(2,1)S(1)} %collective-permute-done.20), channel_id=1, source_target_pairs={{0,4},{4,0},{8,12},{12,8},{16,20},{20,16},{24,28},{28,24},{1,5},{5... | collective-permute-start | bytes 393224 | tf_op jit(solution)/shard_map/ppermute | solution.py:28
  84.3 9.7 %collective-permute-start.23 = (bf16[32,16,128]{2,1,0:T(8,128)(2,1)S(1)}, bf16[32,16,128]{2,1,0:T(8,128)(2,1)S(1)}, u32[]{:S(2)}, u32[]{:S(2)}) collective-permute-start(bf16[32,16,128]{2,1,0:T(8,128)(2,1)S(1)} %collective-permute-done.22), channel_id=1, source_target_pairs={{0,4},{4,0},{8,12},{12,8},{16,20},{20,16},{24,28},{28,24},{1,5},{5... | collective-permute-start | bytes 393224 | tf_op jit(solution)/shard_map/ppermute | solution.py:28
  91.9 12.3 %collective-permute-start.39 = (bf16[1024,128]{1,0:T(8,128)(2,1)S(1)}, bf16[1024,128]{1,0:T(8,128)(2,1)S(1)}, u32[]{:S(2)}, u32[]{:S(2)}) collective-permute-start(bf16[1024,128]{1,0:T(8,128)(2,1)S(1)} %copy-done.55), channel_id=1, source_target_pairs={{0,3},{1,2},{2,1},{3,0},{4,7},{5,6},{6,5},{7,4},{8,11},{9,10},{10,... | collective-permute-start | bytes 786440 | tf_op jit(solution)/shard_map/ppermute | solution.py:28
  92.4 11.8 %collective-permute-start.24 = (bf16[1024,128]{1,0:T(8,128)(2,1)}, bf16[1024,128]{1,0:T(8,128)(2,1)S(1)}, u32[]{:S(2)}, u32[]{:S(2)}) collective-permute-start(bf16[1024,128]{1,0:T(8,128)(2,1)} %get-tuple-element.57), channel_id=1, source_target_pairs={{0,1},{1,0},{2,3},{3,2},{4,5},{5,4},{6,7},{7,6},{8,9},{9,8},{10,11... | collective-permute-start | bytes 786440 | tf_op jit(solution)/shard_map/ppermute | solution.py:28
  94.0 16.8 %collective-permute-start.25 = (bf16[1024,128]{1,0:T(8,128)(2,1)}, bf16[1024,128]{1,0:T(8,128)(2,1)S(1)}, u32[]{:S(2)}, u32[]{:S(2)}) collective-permute-start(bf16[1024,128]{1,0:T(8,128)(2,1)} %get-tuple-element.58), channel_id=1, source_target_pairs={{0,2},{1,3},{2,0},{3,1},{4,6},{5,7},{6,4},{7,5},{8,10},{9,11},{10,... | collective-permute-start | bytes 786440 | tf_op jit(solution)/shard_map/ppermute | solution.py:28
  95.5 19.7 %collective-permute-start.26 = (bf16[1024,128]{1,0:T(8,128)(2,1)}, bf16[1024,128]{1,0:T(8,128)(2,1)S(1)}, u32[]{:S(2)}, u32[]{:S(2)}) collective-permute-start(bf16[1024,128]{1,0:T(8,128)(2,1)} %get-tuple-element.59), channel_id=1, source_target_pairs={{0,3},{1,2},{2,1},{3,0},{4,7},{5,6},{6,5},{7,4},{8,11},{9,10},{10,... | collective-permute-start | bytes 786440 | tf_op jit(solution)/shard_map/ppermute | solution.py:28
  132.0 27.7 %collective-permute-start.54 = (bf16[4,512,128]{2,1,0:T(8,128)(2,1)}, bf16[4,512,128]{2,1,0:T(8,128)(2,1)S(1)}, u32[]{:S(2)}, u32[]{:S(2)}) collective-permute-start(bf16[4,512,128]{2,1,0:T(8,128)(2,1)} %get-tuple-element.86), channel_id=1, source_target_pairs={{0,4},{4,0},{8,12},{12,8},{16,20},{20,16},{24,28},{28,24},{1,5},{5... | collective-permute-start | bytes 1572872 | tf_op jit(solution)/shard_map/ppermute | solution.py:28
  133.0 14.1 %collective-permute-start.40 = (bf16[1024,128]{1,0:T(8,128)(2,1)S(1)}, bf16[1024,128]{1,0:T(8,128)(2,1)S(1)}, u32[]{:S(2)}, u32[]{:S(2)}) collective-permute-start(bf16[1024,128]{1,0:T(8,128)(2,1)S(1)} %copy-done.59), channel_id=1, source_target_pairs={{0,1},{1,0},{2,3},{3,2},{4,5},{5,4},{6,7},{7,6},{8,9},{9,8},{10,11... | collective-permute-start | bytes 786440 | tf_op jit(solution)/shard_map/ppermute | solution.py:28
  133.6 13.5 %collective-permute-start.41 = (bf16[1024,128]{1,0:T(8,128)(2,1)S(1)}, bf16[1024,128]{1,0:T(8,128)(2,1)S(1)}, u32[]{:S(2)}, u32[]{:S(2)}) collective-permute-start(bf16[1024,128]{1,0:T(8,128)(2,1)S(1)} %copy-done.58), channel_id=1, source_target_pairs={{0,2},{1,3},{2,0},{3,1},{4,6},{5,7},{6,4},{7,5},{8,10},{9,11},{10,... | collective-permute-start | bytes 786440 | tf_op jit(solution)/shard_map/ppermute | solution.py:28
  135.2 17.6 %collective-permute-start.42 = (bf16[1024,128]{1,0:T(8,128)(2,1)S(1)}, bf16[1024,128]{1,0:T(8,128)(2,1)S(1)}, u32[]{:S(2)}, u32[]{:S(2)}) collective-permute-start(bf16[1024,128]{1,0:T(8,128)(2,1)S(1)} %copy-done.57), channel_id=1, source_target_pairs={{0,3},{1,2},{2,1},{3,0},{4,7},{5,6},{6,5},{7,4},{8,11},{9,10},{10,... | collective-permute-start | bytes 786440 | tf_op jit(solution)/shard_map/ppermute | solution.py:28
  145.9 36.1 %collective-permute-start.61 = (bf16[4,512,128]{2,1,0:T(8,128)(2,1)}, bf16[4,512,128]{2,1,0:T(8,128)(2,1)S(1)}, u32[]{:S(2)}, u32[]{:S(2)}) collective-permute-start(bf16[4,512,128]{2,1,0:T(8,128)(2,1)} %get-tuple-element.94), channel_id=1, source_target_pairs={{0,4},{4,0},{8,12},{12,8},{16,20},{20,16},{24,28},{28,24},{1,5},{5... | collective-permute-start | bytes 1572872 | tf_op jit(solution)/shard_map/ppermute | solution.py:28
  158.8 13.2 %collective-permute-start.45 = (bf16[1024,128]{1,0:T(8,128)(2,1)}, bf16[1024,128]{1,0:T(8,128)(2,1)S(1)}, u32[]{:S(2)}, u32[]{:S(2)}) collective-permute-start(bf16[1024,128]{1,0:T(8,128)(2,1)} %get-tuple-element.75), channel_id=1, source_target_pairs={{0,3},{1,2},{2,1},{3,0},{4,7},{5,6},{6,5},{7,4},{8,11},{9,10},{10,... | collective-permute-start | bytes 786440 | tf_op jit(solution)/shard_map/ppermute | solution.py:28
  159.9 20.2 %collective-permute-start.55 = (bf16[512,128]{1,0:T(8,128)(2,1)S(1)}, bf16[512,128]{1,0:T(8,128)(2,1)S(1)}, u32[]{:S(2)}, u32[]{:S(2)}) collective-permute-start(bf16[512,128]{1,0:T(8,128)(2,1)S(1)} %get-tuple-element.106), channel_id=1, source_target_pairs={{0,8},{4,12},{8,0},{12,4},{16,24},{20,28},{24,16},{28,20},{1,9},{5... | collective-permute-start | bytes 393224 | tf_op jit(solution)/shard_map/ppermute | solution.py:28
  161.0 20.2 %collective-permute-start.56 = (bf16[512,128]{1,0:T(8,128)(2,1)S(1)}, bf16[512,128]{1,0:T(8,128)(2,1)S(1)}, u32[]{:S(2)}, u32[]{:S(2)}) collective-permute-start(bf16[512,128]{1,0:T(8,128)(2,1)S(1)} %get-tuple-element.108), channel_id=1, source_target_pairs={{0,16},{4,20},{8,24},{12,28},{16,0},{20,4},{24,8},{28,12},{1,17},{... | collective-permute-start | bytes 393224 | tf_op jit(solution)/shard_map/ppermute | solution.py:28
  167.2 14.0 %collective-permute-start.57 = (bf16[512,128]{1,0:T(8,128)(2,1)S(1)}, bf16[512,128]{1,0:T(8,128)(2,1)S(1)}, u32[]{:S(2)}, u32[]{:S(2)}) collective-permute-start(bf16[512,128]{1,0:T(8,128)(2,1)S(1)} %get-tuple-element.107), channel_id=1, source_target_pairs={{0,24},{4,28},{8,16},{12,20},{16,8},{20,12},{24,0},{28,4},{1,25},{... | collective-permute-start | bytes 393224 | tf_op jit(solution)/shard_map/ppermute | solution.py:28
  172.0 15.0 %collective-permute-start.50 = (bf16[4,512,128]{2,1,0:T(8,128)(2,1)}, bf16[4,512,128]{2,1,0:T(8,128)(2,1)S(1)}, u32[]{:S(2)}, u32[]{:S(2)}) collective-permute-start(bf16[4,512,128]{2,1,0:T(8,128)(2,1)} %get-tuple-element.82), channel_id=1, source_target_pairs={{0,4},{4,0},{8,12},{12,8},{16,20},{20,16},{24,28},{28,24},{1,5},{5... | collective-permute-start | bytes 1572872 | tf_op jit(solution)/shard_map/ppermute | solution.py:28
  180.1 19.3 %collective-permute-start.46 = (bf16[4,512,128]{2,1,0:T(8,128)(2,1)S(1)}, bf16[4,512,128]{2,1,0:T(8,128)(2,1)S(1)}, u32[]{:S(2)}, u32[]{:S(2)}) collective-permute-start(bf16[4,512,128]{2,1,0:T(8,128)(2,1)S(1)} %copy-done.54), channel_id=1, source_target_pairs={{0,4},{4,0},{8,12},{12,8},{16,20},{20,16},{24,28},{28,24},{1,5},{5... | collective-permute-start | bytes 1572872 | tf_op jit(solution)/shard_map/ppermute | solution.py:28
  183.7 13.0 %collective-permute-start.63 = (bf16[512,128]{1,0:T(8,128)(2,1)S(1)}, bf16[512,128]{1,0:T(8,128)(2,1)S(1)}, u32[]{:S(2)}, u32[]{:S(2)}) collective-permute-start(bf16[512,128]{1,0:T(8,128)(2,1)S(1)} %get-tuple-element.105), channel_id=1, source_target_pairs={{0,16},{4,20},{8,24},{12,28},{16,0},{20,4},{24,8},{28,12},{1,17},{... | collective-permute-start | bytes 393224 | tf_op jit(solution)/shard_map/ppermute | solution.py:28
  185.7 12.9 %collective-permute-start.64 = (bf16[512,128]{1,0:T(8,128)(2,1)S(1)}, bf16[512,128]{1,0:T(8,128)(2,1)S(1)}, u32[]{:S(2)}, u32[]{:S(2)}) collective-permute-start(bf16[512,128]{1,0:T(8,128)(2,1)S(1)} %get-tuple-element.104), channel_id=1, source_target_pairs={{0,24},{4,28},{8,16},{12,20},{16,8},{20,12},{24,0},{28,4},{1,25},{... | collective-permute-start | bytes 393224 | tf_op jit(solution)/shard_map/ppermute | solution.py:28
  187.1 22.4 %collective-permute-start.51 = (bf16[512,128]{1,0:T(8,128)(2,1)S(1)}, bf16[512,128]{1,0:T(8,128)(2,1)S(1)}, u32[]{:S(2)}, u32[]{:S(2)}) collective-permute-start(bf16[512,128]{1,0:T(8,128)(2,1)S(1)} %get-tuple-element.109), channel_id=1, source_target_pairs={{0,8},{4,12},{8,0},{12,4},{16,24},{20,28},{24,16},{28,20},{1,9},{5... | collective-permute-start | bytes 393224 | tf_op jit(solution)/shard_map/ppermute | solution.py:28
  189.2 22.3 %collective-permute-start.52 = (bf16[512,128]{1,0:T(8,128)(2,1)S(1)}, bf16[512,128]{1,0:T(8,128)(2,1)S(1)}, u32[]{:S(2)}, u32[]{:S(2)}) collective-permute-start(bf16[512,128]{1,0:T(8,128)(2,1)S(1)} %get-tuple-element.111), channel_id=1, source_target_pairs={{0,16},{4,20},{8,24},{12,28},{16,0},{20,4},{24,8},{28,12},{1,17},{... | collective-permute-start | bytes 393224 | tf_op jit(solution)/shard_map/ppermute | solution.py:28
  196.7 14.8 %collective-permute-start.53 = (bf16[512,128]{1,0:T(8,128)(2,1)S(1)}, bf16[512,128]{1,0:T(8,128)(2,1)S(1)}, u32[]{:S(2)}, u32[]{:S(2)}) collective-permute-start(bf16[512,128]{1,0:T(8,128)(2,1)S(1)} %get-tuple-element.110), channel_id=1, source_target_pairs={{0,24},{4,28},{8,16},{12,20},{16,8},{20,12},{24,0},{28,4},{1,25},{... | collective-permute-start | bytes 393224 | tf_op jit(solution)/shard_map/ppermute | solution.py:28
  199.5 13.9 %collective-permute-start.47 = (bf16[512,128]{1,0:T(8,128)(2,1)S(1)}, bf16[512,128]{1,0:T(8,128)(2,1)S(1)}, u32[]{:S(2)}, u32[]{:S(2)}) collective-permute-start(bf16[512,128]{1,0:T(8,128)(2,1)S(1)} %get-tuple-element.112), channel_id=1, source_target_pairs={{0,8},{4,12},{8,0},{12,4},{16,24},{20,28},{24,16},{28,20},{1,9},{5... | collective-permute-start | bytes 393224 | tf_op jit(solution)/shard_map/ppermute | solution.py:28
  209.1 9.8 %collective-permute-start.48 = (bf16[512,128]{1,0:T(8,128)(2,1)S(1)}, bf16[512,128]{1,0:T(8,128)(2,1)S(1)}, u32[]{:S(2)}, u32[]{:S(2)}) collective-permute-start(bf16[512,128]{1,0:T(8,128)(2,1)S(1)} %get-tuple-element.114), channel_id=1, source_target_pairs={{0,16},{4,20},{8,24},{12,28},{16,0},{20,4},{24,8},{28,12},{1,17},{... | collective-permute-start | bytes 393224 | tf_op jit(solution)/shard_map/ppermute | solution.py:28
  (78 other events, 903.5 us)

commit v3 on v2

--- a/solution.py
+++ b/solution.py
@@ -12,7 +12,7 @@
 inv_root_tau = 0.3989422804014327
 lane_tile = 128
 packed_rows = 16
-vmem_bytes = 56 * 1024 * 1024
+vmem_bytes = 14 * 1024 * 1024
 
 
 def gelu_parts(values):
@@ -32,26 +32,16 @@
     return [sends[0]] + [hop(sends[q], "mp", q) for q in range(1, len(sends))]
 
 
-def gather_rows(shard):
+def gather_rows(shards, after):
     size = lax.axis_size("dp")
-    held = [shard] + [hop(shard, "dp", r) for r in range(2, size, 2)]
+    if shards.shape[2] % packed_rows:
+        return [lax.all_gather(shards, "dp", axis=2, tiled=True)], after
+    sent = [shards] * (size // 2)
+    if after is not None:
+        sent = [lax.optimization_barrier((shards, piece))[0] for piece in after]
+    held = [shards] + [hop(sent[q], "dp", 2 * q) for q in range(1, size // 2)]
     other = [hop(piece, "dp", 1) for piece in held]
-    pieces = [piece for pair in zip(held, other) for piece in pair]
-    if shard.shape[1] % packed_rows == 0:
-        return [piece.reshape(-1, shard.shape[2]) for piece in pieces]
-    return [reorder(jnp.stack(pieces))]
-
-
-def reorder(pieces):
-    size, local, rows, width = pieces.shape
-    me = lax.axis_index("dp")
-    bits = size.bit_length() - 1
-    pieces = pieces.reshape((2,) * bits + (local, rows, width))
-    for bit in range(bits):
-        axis = bits - 1 - bit
-        pieces = jnp.where((me >> bit) & 1 == 1, jnp.flip(pieces, axis), pieces)
-    pieces = jnp.transpose(pieces.reshape(size, local, rows, width), (1, 0, 2, 3))
-    return pieces.reshape(local * size * rows, width)
+    return [piece for pair in zip(held, other) for piece in pair], held
 
 
 def scatter_rows(sent, kept, scale):
@@ -76,14 +66,11 @@
     )
 
 
-def place(full, pieces, index):
+def place(full, pieces, me):
     local, block, width = full.shape
     rows = block // len(pieces)
-    if len(pieces) == 1:
-        full[...] = pieces[0][...].reshape(local, rows, width)
-        return
     for q, piece in enumerate(pieces):
-        start = pl.multiple_of((index ^ q) * rows, rows)
+        start = 0 if rows == block else pl.multiple_of((me ^ q) * rows, rows)
         full[:, pl.ds(start, rows), :] = piece[...].reshape(local, rows, width)
 
 
@@ -229,19 +216,26 @@
 
     part = functools.partial
 
-    first_pieces = gather_rows(right_one)
-    outer_pieces = gather_rows(left_two)
-    inner_pieces = gather_rows(left_one)
-    second_pieces = gather_rows(right_two)
-    count = len(first_pieces)
+    def part_of(pieces, which):
+        return [piece[which] for piece in pieces]
+
+    first, after = gather_rows(right_one[None], None)
+    outer, after = gather_rows(left_two[None], after)
+    inner, after = gather_rows(left_one[None], after)
+    second, after = gather_rows(right_two[None], after)
+    first_pieces, outer_pieces = part_of(first, 0), part_of(outer, 0)
+    inner_pieces, second_pieces = part_of(inner, 0), part_of(second, 0)
 
     upstream = exchange(run(part(turn_kernel, z), sends, [mixed], [ids, cotangent], 0))
     right_first, *parts = run(
-        part(first_kernel, z, count), [weight] + sends, [mixed], [ids, tokens, *first_pieces], products
+        part(first_kernel, z, len(first_pieces)),
+        [weight] + sends,
+        [mixed],
+        [ids, tokens, *first_pieces], products
     )
     first_columns = exchange(parts)
     _, upstream_columns, *parts = run(
-        part(middle_kernel, z, count, 1),
+        part(middle_kernel, z, len(outer_pieces), 1),
         [weight, acts] + sends,
         [mixed],
         [ids, *outer_pieces, *upstream],
@@ -249,7 +243,7 @@
     )
     second_rows = exchange(parts)
     left_first, columns, *parts = run(
-        part(middle_kernel, z, count, 0),
+        part(middle_kernel, z, len(inner_pieces), 0),
         [weight, acts] + sends,
         [mixed],
         [ids, *inner_pieces, *first_columns],
@@ -257,7 +251,7 @@
     )
     preact = exchange(parts)
     right_second, hidden, second_back, *parts = run(
-        part(gelu_kernel, z, count),
+        part(gelu_kernel, z, len(second_pieces)),
         [weight, acts, acts] + sends,
         [mixed],
         [ids, *second_pieces, *preact, *second_rows],

time: 220 us -> 179 us (0.81)
  Pallas kernels: 50.4 us -> 25.8 us
  starting transfers between devices: 93 us -> 72.4 us
  waiting for transfers between devices: 68 us -> 73.6 us
    pallas_call x12, Pallas kernels: 50.4 us -> 25.8 us  [run(): pl.pallas_call(body, out_shape=outs, in_specs=specs, out_specs=[pl.BlockS...]
    ppermute x65, starting transfers between devices: 93 us -> 72.4 us  [hop(): return lax.ppermute(source, axis, [(i, i ^ offset) for i in range(size)])]
    ppermute x65, waiting for transfers between devices: 68 us -> 73.6 us  [hop(): return lax.ppermute(source, axis, [(i, i ^ offset) for i in range(size)])]
  transfers between devices with their start and end apart: 65 -> 65, of which waited for: 22 -> 24; matrix products, arithmetic and copies ran while one was open for 2% -> 2% of each run, Pallas kernels for 18% -> 11%
where the time goes in v3:
time: 179 us
  waiting for transfers between devices  73.6 us (41%)
  starting transfers between devices  72.4 us (40%)
  Pallas kernels  25.8 us (14%)
  other arithmetic  3.75 us (2%)
  local copies, waits for them, and re-layouts  2.26 us (1%)
    ppermute x65, waiting for transfers between devices, hop(): return lax.ppermute(source, axis, [(i, i ^ offset) for i in range(size)])  73.6 us
    ppermute x65, starting transfers between devices, hop(): return lax.ppermute(source, axis, [(i, i ^ offset) for i in range(size)])  72.4 us
    pallas_call x12, Pallas kernels, run(): pl.pallas_call(body, out_shape=outs, in_specs=specs, out_specs=[pl.BlockS...  25.8 us
  transfers between devices with their start and end apart: 65, of which 24 were waited for; matrix products, arithmetic and copies ran while one was open for 2% of the time, Pallas kernels for 11%

profile of v3, /device:TPU:0, one launch (start us, length us, event | category | flops | bytes accessed | tf_op | source)
XLA Modules:
  0.0 178.7 jit_solution(9685922440785676787)
XLA Ops:
  0.6 3.1 %collective-permute-start.1 = (bf16[1,32,16,128]{3,2,1,0:T(8,128)(2,1)}, bf16[1,32,16,128]{3,2,1,0:T(8,128)(2,1)S(1)}, u32[]{:S(2)}, u32[]{:S(2)}) collective-permute-start(bf16[1,32,16,128]{3,2,1,0:T(8,128)(2,1)} %bitcast.102), channel_id=1, source_target_pairs={{0,8},{4,12},{8,0},{12,4},{16,24},{20,28},{24,16},{28,20},{1,9},{5... | collective-permute-start | bytes 393224 | tf_op jit(solution)/shard_map/ppermute | solution.py:28
  3.7 2.6 %collective-permute-start.3 = (bf16[1,32,16,128]{3,2,1,0:T(8,128)(2,1)}, bf16[1,32,16,128]{3,2,1,0:T(8,128)(2,1)S(1)}, u32[]{:S(2)}, u32[]{:S(2)}) collective-permute-start(bf16[1,32,16,128]{3,2,1,0:T(8,128)(2,1)} %bitcast.103), channel_id=1, source_target_pairs={{0,16},{4,20},{8,24},{12,28},{16,0},{20,4},{24,8},{28,12},{1,17},{... | collective-permute-start | bytes 393224 | tf_op jit(solution)/shard_map/ppermute | solution.py:28
  6.3 1.7 collective-permute-start
  9.0 1.7 collective-permute-start.30
  10.7 6.2 %collective-permute-done.3 = bf16[1,32,16,128]{3,2,1,0:T(8,128)(2,1)S(1)} collective-permute-done((bf16[1,32,16,128]{3,2,1,0:T(8,128)(2,1)}, bf16[1,32,16,128]{3,2,1,0:T(8,128)(2,1)S(1)}, u32[]{:S(2)}, u32[]{:S(2)}) %collective-permute-start.3) | collective-permute-done | bytes 131104 | tf_op jit(solution)/shard_map/ppermute | solution.py:28
  18.9 2.4 %collective-permute-start.11 = (bf16[1,32,16,128]{3,2,1,0:T(8,128)(2,1)}, bf16[1,32,16,128]{3,2,1,0:T(8,128)(2,1)S(1)}, u32[]{:S(2)}, u32[]{:S(2)}) collective-permute-start(bf16[1,32,16,128]{3,2,1,0:T(8,128)(2,1)} %bitcast.108), channel_id=1, source_target_pairs={{0,16},{4,20},{8,24},{12,28},{16,0},{20,4},{24,8},{28,12},{1,17},{... | collective-permute-start | bytes 393224 | tf_op jit(solution)/shard_map/ppermute | solution.py:28
  24.6 1.9 %shard_map.103 = (bf16[1024,128]{1,0:T(8,128)(2,1)S(1)}, bf16[1024,128]{1,0:T(8,128)(2,1)S(1)}, bf16[1024,128]{1,0:T(8,128)(2,1)S(1)}, bf16[1024,128]{1,0:T(8,128)(2,1)S(1)}) custom-call(s32[2]{0:T(128)S(1)} %pad_add_fusion.ids, bf16[128,4096]{1,0:T(8,128)(2,1)S(1)} %copy-done.1), custom_call_target="tpu_custom_call" | custom-call | bytes 2097160 | tf_op jit(solution)/shard_map/pallas_call | solution.py:189
  26.6 1.6 collective-permute-start.35
  29.4 1.9 %collective-permute-start.14 = (bf16[1,32,16,128]{3,2,1,0:T(8,128)(2,1)}, bf16[1,32,16,128]{3,2,1,0:T(8,128)(2,1)S(1)}, u32[]{:S(2)}, u32[]{:S(2)}) collective-permute-start(bf16[1,32,16,128]{3,2,1,0:T(8,128)(2,1)} %bitcast.109), channel_id=1, source_target_pairs={{0,24},{4,28},{8,16},{12,20},{16,8},{20,12},{24,0},{28,4},{1,25},{... | collective-permute-start | bytes 393224 | tf_op jit(solution)/shard_map/ppermute | solution.py:28
  31.3 3.4 %collective-permute-done.6 = bf16[1,32,16,128]{3,2,1,0:T(8,128)(2,1)S(1)} collective-permute-done((bf16[1,32,16,128]{3,2,1,0:T(8,128)(2,1)S(1)}, bf16[1,32,16,128]{3,2,1,0:T(8,128)(2,1)S(1)}, u32[]{:S(2)}, u32[]{:S(2)}) %collective-permute-start.6) | collective-permute-done | bytes 131104 | tf_op jit(solution)/shard_map/ppermute | solution.py:28
  35.5 2.2 %collective-permute-done.14 = bf16[1,32,16,128]{3,2,1,0:T(8,128)(2,1)S(1)} collective-permute-done((bf16[1,32,16,128]{3,2,1,0:T(8,128)(2,1)}, bf16[1,32,16,128]{3,2,1,0:T(8,128)(2,1)S(1)}, u32[]{:S(2)}, u32[]{:S(2)}) %collective-permute-start.14) | collective-permute-done | bytes 131104 | tf_op jit(solution)/shard_map/ppermute | solution.py:28
  37.7 1.8 collective-permute-start.12
  42.4 2.6 %shard_map.101 = (bf16[32,128,128]{2,1,0:T(8,128)(2,1)S(1)}, bf16[1024,128]{1,0:T(8,128)(2,1)S(1)}, bf16[1024,128]{1,0:T(8,128)(2,1)S(1)}, bf16[1024,128]{1,0:T(8,128)(2,1)S(1)}, bf16[1024,128]{1,0:T(8,128)(2,1)S(1)}) custom-call(s32[2]{0:T(128)S(1)} %pad_add_fusion.ids, bf16[128,4096]{1,0:T(8,128)(2,1)S(1)} %copy-done, bf16[32,16,128]{2,1,0:T(8,128)(2,1)S(1)} %copy-done.2, ...), custom_call_target="tpu_custom_call" | custom-call | flops 134217728 | bytes 4194312 | tf_op jit(solution)/shard_map/pallas_call | solution.py:189
  47.7 2.4 %collective-permute-start.15 = (bf16[1,32,16,128]{3,2,1,0:T(8,128)(2,1)S(1)}, bf16[1,32,16,128]{3,2,1,0:T(8,128)(2,1)S(1)}, u32[]{:S(2)}, u32[]{:S(2)}) collective-permute-start(bf16[1,32,16,128]{3,2,1,0:T(8,128)(2,1)S(1)} %bitcast.113), channel_id=1, source_target_pairs={{0,24},{4,28},{8,16},{12,20},{16,8},{20,12},{24,0},{28,4},{1,25},{... | collective-permute-start | bytes 393224 | tf_op jit(solution)/shard_map/ppermute | solution.py:28
  50.1 3.0 %collective-permute-done.33 = bf16[1,32,16,128]{3,2,1,0:T(8,128)(2,1)S(1)} collective-permute-done((bf16[1,32,16,128]{3,2,1,0:T(8,128)(2,1)S(1)}, bf16[1,32,16,128]{3,2,1,0:T(8,128)(2,1)S(1)}, u32[]{:S(2)}, u32[]{:S(2)}) %collective-permute-start.33) | collective-permute-done | bytes 131104 | tf_op jit(solution)/shard_map/ppermute | solution.py:28
  53.6 2.5 %shard_map.104 = (bf16[32,128,128]{2,1,0:T(8,128)(2,1)}, bf16[32,128,128]{2,1,0:T(8,128)(2,1)S(1)}, bf16[1024,128]{1,0:T(8,128)(2,1)S(1)}, bf16[1024,128]{1,0:T(...) custom-call(s32[2]{0:T(128)S(1)} %pad_add_fusion.ids, bf16[32,16,128]{2,1,0:T(8,128)(2,1)S(1)} %copy-done.3, ...), custom_call_target="tpu_custom_call" | custom-call | flops 134217728 | bytes 5242888 | tf_op jit(solution)/shard_map/pallas_call | solution.py:189
  56.1 1.6 collective-permute-start.13
  60.4 2.2 %collective-permute-done.13 = bf16[1,32,16,128]{3,2,1,0:T(8,128)(2,1)S(1)} collective-permute-done((bf16[1,32,16,128]{3,2,1,0:T(8,128)(2,1)S(1)}, bf16[1,32,16,128]{3,2,1,0:T(8,128)(2,1)S(1)}, u32[]{:S(2)}, u32[]{:S(2)}) %collective-permute-start.13) | collective-permute-done | bytes 131104 | tf_op jit(solution)/shard_map/ppermute | solution.py:28
  64.0 2.0 %collective-permute-start.25 = (bf16[1,32,16,128]{3,2,1,0:T(8,128)(2,1)S(1)}, bf16[1,32,16,128]{3,2,1,0:T(8,128)(2,1)S(1)}, u32[]{:S(2)}, u32[]{:S(2)}) collective-permute-start(bf16[1,32,16,128]{3,2,1,0:T(8,128)(2,1)S(1)} %bitcast.138), channel_id=1, source_target_pairs={{0,24},{4,28},{8,16},{12,20},{16,8},{20,12},{24,0},{28,4},{1,25},{... | collective-permute-start | bytes 393224 | tf_op jit(solution)/shard_map/ppermute | solution.py:28
  66.0 2.6 %shard_map.102 = (bf16[32,128,128]{2,1,0:T(8,128)(2,1)S(1)}, bf16[32,128,128]{2,1,0:T(8,128)(2,1)S(1)}, bf16[1024,128]{1,0:T(8,128)(2,1)S(1)}, bf16[1024,128]{1,...) custom-call(s32[2]{0:T(128)S(1)} %pad_add_fusion.ids, ...), custom_call_target="tpu_custom_call" | custom-call | flops 134217728 | bytes 5242888 | tf_op jit(solution)/shard_map/pallas_call | solution.py:189
  68.5 5.1 %collective-permute-done.23 = bf16[1,32,16,128]{3,2,1,0:T(8,128)(2,1)S(1)} collective-permute-done((bf16[1,32,16,128]{3,2,1,0:T(8,128)(2,1)S(1)}, bf16[1,32,16,128]{3,2,1,0:T(8,128)(2,1)S(1)}, u32[]{:S(2)}, u32[]{:S(2)}) %collective-permute-start.23) | collective-permute-done | bytes 131104 | tf_op jit(solution)/shard_map/ppermute | solution.py:28
  77.3 2.3 %collective-permute-done.22 = bf16[1,32,16,128]{3,2,1,0:T(8,128)(2,1)S(1)} collective-permute-done((bf16[1,32,16,128]{3,2,1,0:T(8,128)(2,1)S(1)}, bf16[1,32,16,128]{3,2,1,0:T(8,128)(2,1)S(1)}, u32[]{:S(2)}, u32[]{:S(2)}) %collective-permute-start.22) | collective-permute-done | bytes 131104 | tf_op jit(solution)/shard_map/ppermute | solution.py:28
  81.0 1.8 collective-permute-done.24
  82.7 2.4 %collective-permute-done.26 = bf16[1,32,16,128]{3,2,1,0:T(8,128)(2,1)S(1)} collective-permute-done((bf16[1,32,16,128]{3,2,1,0:T(8,128)(2,1)S(1)}, bf16[1,32,16,128]{3,2,1,0:T(8,128)(2,1)S(1)}, u32[]{:S(2)}, u32[]{:S(2)}) %collective-permute-start.26) | collective-permute-done | bytes 131104 | tf_op jit(solution)/shard_map/ppermute | solution.py:28
  85.2 3.0 %collective-permute-done.29.refs_11_ = bf16[1024,128]{1,0:T(8,128)(2,1)S(1)} collective-permute-done((bf16[1024,128]{1,0:T(8,128)(2,1)S(1)}, bf16[1024,128]{1,0:T(8,128)(2,1)S(1)}, u32[]{:S(2)}, u32[]{:S(2)}) %collective-permute-start.29) | collective-permute-done | bytes 262176 | tf_op jit(solution)/shard_map/ppermute | solution.py:28
  88.2 3.0 %shard_map.105 = (bf16[32,128,128]{2,1,0:T(8,128)(2,1)S(1)}, bf16[32,128,128]{2,1,0:T(8,128)(2,1)S(1)}, bf16[32,128,128]{2,1,0:T(8,128)(2,1)S(1)}, bf16[1024,128...) custom-call(s32[2]{0:T(128)S(1)} %pad_add_fusion.ids, ...), custom_call_target="tpu_custom_call" | custom-call | flops 134217728 | bytes 7340040 | tf_op jit(solution)/shard_map/pallas_call | solution.py:189
  91.1 2.5 %shard_map.111 = (bf16[1024,128]{1,0:T(8,128)(2,1)S(1)}, bf16[1024,128]{1,0:T(8,128)(2,1)S(1)}, bf16[1024,128]{1,0:T(8,128)(2,1)S(1)}, bf16[1024,128]{1,0:T(8,128)(2,1)S(1)}) custom-call(s32[2]{0:T(128)S(1)} %pad_add_fusion.ids, bf16[32,128,128]{2,1,0:T(8,128)(2,1)S(1)} %get-tuple-element.106.full, bf16[32,128,128]{2,1,0:T(8,128)(2,1)S(1)} %get-tuple-element.101.left.hidden), custom_call_target="tpu_custom_call" | custom-call | flops 134217728 | bytes 3145736 | tf_op jit(solution)/shard_map/pallas_call | solution.py:189
  100.4 3.1 %collective-permute-done.59.refs_2_ = bf16[1024,128]{1,0:T(8,128)(2,1)S(1)} collective-permute-done((bf16[1024,128]{1,0:T(8,128)(2,1)S(1)}, bf16[1024,128]{1,0:T(8,128)(2,1)S(1)}, u32[]{:S(2)}, u32[]{:S(2)}) %collective-permute-start.59) | collective-permute-done | bytes 262176 | tf_op jit(solution)/shard_map/ppermute | solution.py:28
  103.4 4.7 %collective-permute-done.60.refs_3_ = bf16[1024,128]{1,0:T(8,128)(2,1)S(1)} collective-permute-done((bf16[1024,128]{1,0:T(8,128)(2,1)S(1)}, bf16[1024,128]{1,0:T(8,128)(2,1)S(1)}, u32[]{:S(2)}, u32[]{:S(2)}) %collective-permute-start.60) | collective-permute-done | bytes 262176 | tf_op jit(solution)/shard_map/ppermute | solution.py:28
  108.1 1.6 shard_map.112
  110.6 4.1 %collective-permute-done.41.refs_3_ = bf16[1024,128]{1,0:T(8,128)(2,1)S(1)} collective-permute-done((bf16[1024,128]{1,0:T(8,128)(2,1)S(1)}, bf16[1024,128]{1,0:T(8,128)(2,1)S(1)}, u32[]{:S(2)}, u32[]{:S(2)}) %collective-permute-start.41) | collective-permute-done | bytes 262176 | tf_op jit(solution)/shard_map/ppermute | solution.py:28
  114.7 3.9 %collective-permute-done.42.refs_4_ = bf16[1024,128]{1,0:T(8,128)(2,1)S(1)} collective-permute-done((bf16[1024,128]{1,0:T(8,128)(2,1)S(1)}, bf16[1024,128]{1,0:T(8,128)(2,1)S(1)}, u32[]{:S(2)}, u32[]{:S(2)}) %collective-permute-start.42) | collective-permute-done | bytes 262176 | tf_op jit(solution)/shard_map/ppermute | solution.py:28
  118.5 2.7 %shard_map.106 = (bf16[32,128,128]{2,1,0:T(8,128)(2,1)}, bf16[32,128,128]{2,1,0:T(8,128)(2,1)S(1)}, bf16[1024,128]{1,0:T(8,128)(2,1)S(1)}, bf16[1024,128]{1,0:T(...) custom-call(s32[2]{0:T(128)S(1)} %pad_add_fusion.ids, ...), custom_call_target="tpu_custom_call" | custom-call | flops 134217728 | bytes 5242888 | tf_op jit(solution)/shard_map/pallas_call | solution.py:189
  122.3 1.6 collective-permute-start.44
  125.0 1.6 collective-permute-start.56
  126.6 4.8 %collective-permute-done.44.refs_2_ = bf16[1024,128]{1,0:T(8,128)(2,1)S(1)} collective-permute-done((bf16[1024,128]{1,0:T(8,128)(2,1)S(1)}, bf16[1024,128]{1,0:T(8,128)(2,1)S(1)}, u32[]{:S(2)}, u32[]{:S(2)}) %collective-permute-start.44) | collective-permute-done | bytes 262176 | tf_op jit(solution)/shard_map/ppermute | solution.py:28
  131.4 2.2 %collective-permute-start.57 = (bf16[512,128]{1,0:T(8,128)(2,1)S(1)}, bf16[512,128]{1,0:T(8,128)(2,1)S(1)}, u32[]{:S(2)}, u32[]{:S(2)}) collective-permute-start(bf16[512,128]{1,0:T(8,128)(2,1)S(1)} %get-tuple-element.125), channel_id=1, source_target_pairs={{0,24},{4,28},{8,16},{12,20},{16,8},{20,12},{24,0},{28,4},{1,25},{... | collective-permute-start | bytes 393224 | tf_op jit(solution)/shard_map/ppermute | solution.py:28
  136.1 1.6 shard_map.107
  137.6 1.8 %shard_map.108 = bf16[128,4096]{1,0:T(8,128)(2,1)} custom-call(bf16[32,128,128]{2,1,0:T(8,128)(2,1)S(1)} %get-tuple-element.59.full, bf16[32,128,128]{2,1,0:T(8,128)(2,1)S(1)} %get-tuple-element.94.turned), custom_call_target="tpu_custom_call" | custom-call | flops 134217728 | bytes 3145728 | tf_op jit(solution)/shard_map/pallas_call | solution.py:189
  142.6 1.7 collective-permute-start.63
  144.3 1.7 collective-permute-start.64
  146.0 3.9 %collective-permute-done.50 = bf16[4,512,128]{2,1,0:T(8,128)(2,1)S(1)} collective-permute-done((bf16[4,512,128]{2,1,0:T(8,128)(2,1)S(1)}, bf16[4,512,128]{2,1,0:T(8,128)(2,1)S(1)}, u32[]{:S(2)}, u32[]{:S(2)}) %collective-permute-start.50) | collective-permute-done | bytes 524320 | tf_op jit(solution)/shard_map/ppermute | solution.py:28
  151.1 1.8 %collective-permute-start.52 = (bf16[512,128]{1,0:T(8,128)(2,1)S(1)}, bf16[512,128]{1,0:T(8,128)(2,1)S(1)}, u32[]{:S(2)}, u32[]{:S(2)}) collective-permute-start(bf16[512,128]{1,0:T(8,128)(2,1)S(1)} %get-tuple-element.129), channel_id=1, source_target_pairs={{0,16},{4,20},{8,24},{12,28},{16,0},{20,4},{24,8},{28,12},{1,17},{... | collective-permute-start | bytes 393224 | tf_op jit(solution)/shard_map/ppermute | solution.py:28
  152.9 2.6 %collective-permute-done.63 = bf16[512,128]{1,0:T(8,128)(2,1)S(1)} collective-permute-done((bf16[512,128]{1,0:T(8,128)(2,1)S(1)}, bf16[512,128]{1,0:T(8,128)(2,1)S(1)}, u32[]{:S(2)}, u32[]{:S(2)}) %collective-permute-start.63) | collective-permute-done | bytes 131104 | tf_op jit(solution)/shard_map/ppermute | solution.py:28
  157.5 3.7 %collective-permute-done.46 = bf16[4,512,128]{2,1,0:T(8,128)(2,1)S(1)} collective-permute-done((bf16[4,512,128]{2,1,0:T(8,128)(2,1)S(1)}, bf16[4,512,128]{2,1,0:T(8,128)(2,1)S(1)}, u32[]{:S(2)}, u32[]{:S(2)}) %collective-permute-start.46) | collective-permute-done | bytes 524320 | tf_op jit(solution)/shard_map/ppermute | solution.py:28
  161.4 4.1 %collective-permute-start.47 = (bf16[512,128]{1,0:T(8,128)(2,1)S(1)}, bf16[512,128]{1,0:T(8,128)(2,1)S(1)}, u32[]{:S(2)}, u32[]{:S(2)}) collective-permute-start(bf16[512,128]{1,0:T(8,128)(2,1)S(1)} %get-tuple-element.130), channel_id=1, source_target_pairs={{0,8},{4,12},{8,0},{12,4},{16,24},{20,28},{24,16},{28,20},{1,9},{5... | collective-permute-start | bytes 393224 | tf_op jit(solution)/shard_map/ppermute | solution.py:28
  165.5 2.4 %collective-permute-start.49 = (bf16[512,128]{1,0:T(8,128)(2,1)S(1)}, bf16[512,128]{1,0:T(8,128)(2,1)S(1)}, u32[]{:S(2)}, u32[]{:S(2)}) collective-permute-start(bf16[512,128]{1,0:T(8,128)(2,1)S(1)} %get-tuple-element.131), channel_id=1, source_target_pairs={{0,24},{4,28},{8,16},{12,20},{16,8},{20,12},{24,0},{28,4},{1,25},{... | collective-permute-start | bytes 393224 | tf_op jit(solution)/shard_map/ppermute | solution.py:28
  170.2 7.8 %collective-permute-done.48 = bf16[512,128]{1,0:T(8,128)(2,1)S(1)} collective-permute-done((bf16[512,128]{1,0:T(8,128)(2,1)S(1)}, bf16[512,128]{1,0:T(8,128)(2,1)S(1)}, u32[]{:S(2)}, u32[]{:S(2)}) %collective-permute-start.48) | collective-permute-done | bytes 131104 | tf_op jit(solution)/shard_map/ppermute | solution.py:28
  (119 shorter events, 45.0 us)
Async XLA Ops:
  3.7 13.2 %collective-permute-start.3 = (bf16[1,32,16,128]{3,2,1,0:T(8,128)(2,1)}, bf16[1,32,16,128]{3,2,1,0:T(8,128)(2,1)S(1)}, u32[]{:S(2)}, u32[]{:S(2)}) collective-permute-start(bf16[1,32,16,128]{3,2,1,0:T(8,128)(2,1)} %bitcast.103), channel_id=1, source_target_pairs={{0,16},{4,20},{8,24},{12,28},{16,0},{20,4},{24,8},{28,12},{1,17},{... | collective-permute-start | bytes 393224 | tf_op jit(solution)/shard_map/ppermute | solution.py:28
  6.3 12.1 %collective-permute-start.5 = (bf16[1,32,16,128]{3,2,1,0:T(8,128)(2,1)}, bf16[1,32,16,128]{3,2,1,0:T(8,128)(2,1)S(1)}, u32[]{:S(2)}, u32[]{:S(2)}) collective-permute-start(bf16[1,32,16,128]{3,2,1,0:T(8,128)(2,1)} %bitcast.104), channel_id=1, source_target_pairs={{0,24},{4,28},{8,16},{12,20},{16,8},{20,12},{24,0},{28,4},{1,25},{... | collective-permute-start | bytes 393224 | tf_op jit(solution)/shard_map/ppermute | solution.py:28
  6.3 12.5 %collective-permute-start = (bf16[1,32,16,128]{3,2,1,0:T(8,128)(2,1)}, bf16[1,32,16,128]{3,2,1,0:T(8,128)(2,1)S(1)}, u32[]{:S(2)}, u32[]{:S(2)}) collective-permute-start(bf16[1,32,16,128]{3,2,1,0:T(8,128)(2,1)} %bitcast.105), channel_id=1, source_target_pairs={{0,4},{4,0},{8,12},{12,8},{16,20},{20,16},{24,28},{28,24},{1,5},{5... | collective-permute-start | bytes 393224 | tf_op jit(solution)/shard_map/ppermute | solution.py:28
  8.0 13.2 %collective-permute-start.7 = (bf16[1,32,16,128]{3,2,1,0:T(8,128)(2,1)}, bf16[1,32,16,128]{3,2,1,0:T(8,128)(2,1)S(1)}, u32[]{:S(2)}, u32[]{:S(2)}) collective-permute-start(bf16[1,32,16,128]{3,2,1,0:T(8,128)(2,1)} %bitcast.110), channel_id=1, source_target_pairs={{0,4},{4,0},{8,12},{12,8},{16,20},{20,16},{24,28},{28,24},{1,5},{5... | collective-permute-start | bytes 393224 | tf_op jit(solution)/shard_map/ppermute | solution.py:28
  9.0 12.8 %collective-permute-start.30 = (bf16[1,32,16,128]{3,2,1,0:T(8,128)(2,1)}, bf16[1,32,16,128]{3,2,1,0:T(8,128)(2,1)S(1)}, u32[]{:S(2)}, u32[]{:S(2)}) collective-permute-start(bf16[1,32,16,128]{3,2,1,0:T(8,128)(2,1)} %bitcast.106), channel_id=1, source_target_pairs={{0,4},{4,0},{8,12},{12,8},{16,20},{20,16},{24,28},{28,24},{1,5},{5... | collective-permute-start | bytes 393224 | tf_op jit(solution)/shard_map/ppermute | solution.py:28
  16.9 9.6 %collective-permute-start.20 = (bf16[1,32,16,128]{3,2,1,0:T(8,128)(2,1)}, bf16[1,32,16,128]{3,2,1,0:T(8,128)(2,1)S(1)}, u32[]{:S(2)}, u32[]{:S(2)}) collective-permute-start(bf16[1,32,16,128]{3,2,1,0:T(8,128)(2,1)} %bitcast.135), channel_id=1, source_target_pairs={{0,4},{4,0},{8,12},{12,8},{16,20},{20,16},{24,28},{28,24},{1,5},{5... | collective-permute-start | bytes 393224 | tf_op jit(solution)/shard_map/ppermute | solution.py:28
  18.4 10.1 %collective-permute-start.8 = (bf16[1,32,16,128]{3,2,1,0:T(8,128)(2,1)}, bf16[1,32,16,128]{3,2,1,0:T(8,128)(2,1)S(1)}, u32[]{:S(2)}, u32[]{:S(2)}) collective-permute-start(bf16[1,32,16,128]{3,2,1,0:T(8,128)(2,1)} %bitcast.107), channel_id=1, source_target_pairs={{0,8},{4,12},{8,0},{12,4},{16,24},{20,28},{24,16},{28,20},{1,9},{5... | collective-permute-start | bytes 393224 | tf_op jit(solution)/shard_map/ppermute | solution.py:28
  18.9 10.5 %collective-permute-start.11 = (bf16[1,32,16,128]{3,2,1,0:T(8,128)(2,1)}, bf16[1,32,16,128]{3,2,1,0:T(8,128)(2,1)S(1)}, u32[]{:S(2)}, u32[]{:S(2)}) collective-permute-start(bf16[1,32,16,128]{3,2,1,0:T(8,128)(2,1)} %bitcast.108), channel_id=1, source_target_pairs={{0,16},{4,20},{8,24},{12,28},{16,0},{20,4},{24,8},{28,12},{1,17},{... | collective-permute-start | bytes 393224 | tf_op jit(solution)/shard_map/ppermute | solution.py:28
  26.5 13.0 %collective-permute-start.34 = (bf16[1024,128]{1,0:T(8,128)(2,1)S(1)}, bf16[1024,128]{1,0:T(8,128)(2,1)S(1)}, u32[]{:S(2)}, u32[]{:S(2)}) collective-permute-start(bf16[1024,128]{1,0:T(8,128)(2,1)S(1)} %get-tuple-element.79), channel_id=1, source_target_pairs={{0,1},{1,0},{2,3},{3,2},{4,5},{5,4},{6,7},{7,6},{8,9},{9,8},{10,11... | collective-permute-start | bytes 786440 | tf_op jit(solution)/shard_map/ppermute | solution.py:28
  26.6 13.5 %collective-permute-start.35 = (bf16[1024,128]{1,0:T(8,128)(2,1)S(1)}, bf16[1024,128]{1,0:T(8,128)(2,1)S(1)}, u32[]{:S(2)}, u32[]{:S(2)}) collective-permute-start(bf16[1024,128]{1,0:T(8,128)(2,1)S(1)} %get-tuple-element.80), channel_id=1, source_target_pairs={{0,2},{1,3},{2,0},{3,1},{4,6},{5,7},{6,4},{7,5},{8,10},{9,11},{10,... | collective-permute-start | bytes 786440 | tf_op jit(solution)/shard_map/ppermute | solution.py:28
  28.2 16.9 %collective-permute-start.36 = (bf16[1024,128]{1,0:T(8,128)(2,1)S(1)}, bf16[1024,128]{1,0:T(8,128)(2,1)S(1)}, u32[]{:S(2)}, u32[]{:S(2)}) collective-permute-start(bf16[1024,128]{1,0:T(8,128)(2,1)S(1)} %get-tuple-element.81), channel_id=1, source_target_pairs={{0,3},{1,2},{2,1},{3,0},{4,7},{5,6},{6,5},{7,4},{8,11},{9,10},{10,... | collective-permute-start | bytes 786440 | tf_op jit(solution)/shard_map/ppermute | solution.py:28
  34.7 10.4 %collective-permute-start.9 = (bf16[1,32,16,128]{3,2,1,0:T(8,128)(2,1)}, bf16[1,32,16,128]{3,2,1,0:T(8,128)(2,1)S(1)}, u32[]{:S(2)}, u32[]{:S(2)}) collective-permute-start(bf16[1,32,16,128]{3,2,1,0:T(8,128)(2,1)} %bitcast.111), channel_id=1, source_target_pairs={{0,8},{4,12},{8,0},{12,4},{16,24},{20,28},{24,16},{28,20},{1,9},{5... | collective-permute-start | bytes 393224 | tf_op jit(solution)/shard_map/ppermute | solution.py:28
  37.7 9.4 %collective-permute-start.12 = (bf16[1,32,16,128]{3,2,1,0:T(8,128)(2,1)}, bf16[1,32,16,128]{3,2,1,0:T(8,128)(2,1)S(1)}, u32[]{:S(2)}, u32[]{:S(2)}) collective-permute-start(bf16[1,32,16,128]{3,2,1,0:T(8,128)(2,1)} %bitcast.112), channel_id=1, source_target_pairs={{0,16},{4,20},{8,24},{12,28},{16,0},{20,4},{24,8},{28,12},{1,17},{... | collective-permute-start | bytes 393224 | tf_op jit(solution)/shard_map/ppermute | solution.py:28
  45.0 12.7 %collective-permute-start.17 = (bf16[1024,128]{1,0:T(8,128)(2,1)S(1)}, bf16[1024,128]{1,0:T(8,128)(2,1)S(1)}, u32[]{:S(2)}, u32[]{:S(2)}) collective-permute-start(bf16[1024,128]{1,0:T(8,128)(2,1)S(1)} %get-tuple-element.67), channel_id=1, source_target_pairs={{0,1},{1,0},{2,3},{3,2},{4,5},{5,4},{6,7},{7,6},{8,9},{9,8},{10,11... | collective-permute-start | bytes 786440 | tf_op jit(solution)/shard_map/ppermute | solution.py:28
  45.1 13.1 %collective-permute-start.18 = (bf16[1024,128]{1,0:T(8,128)(2,1)S(1)}, bf16[1024,128]{1,0:T(8,128)(2,1)S(1)}, u32[]{:S(2)}, u32[]{:S(2)}) collective-permute-start(bf16[1024,128]{1,0:T(8,128)(2,1)S(1)} %get-tuple-element.68), channel_id=1, source_target_pairs={{0,2},{1,3},{2,0},{3,1},{4,6},{5,7},{6,4},{7,5},{8,10},{9,11},{10,... | collective-permute-start | bytes 786440 | tf_op jit(solution)/shard_map/ppermute | solution.py:28
  47.0 12.0 %collective-permute-start.19 = (bf16[1024,128]{1,0:T(8,128)(2,1)S(1)}, bf16[1024,128]{1,0:T(8,128)(2,1)S(1)}, u32[]{:S(2)}, u32[]{:S(2)}) collective-permute-start(bf16[1024,128]{1,0:T(8,128)(2,1)S(1)} %get-tuple-element.69), channel_id=1, source_target_pairs={{0,3},{1,2},{2,1},{3,0},{4,7},{5,6},{6,5},{7,4},{8,11},{9,10},{10,... | collective-permute-start | bytes 786440 | tf_op jit(solution)/shard_map/ppermute | solution.py:28
  47.7 8.4 %collective-permute-start.15 = (bf16[1,32,16,128]{3,2,1,0:T(8,128)(2,1)S(1)}, bf16[1,32,16,128]{3,2,1,0:T(8,128)(2,1)S(1)}, u32[]{:S(2)}, u32[]{:S(2)}) collective-permute-start(bf16[1,32,16,128]{3,2,1,0:T(8,128)(2,1)S(1)} %bitcast.113), channel_id=1, source_target_pairs={{0,24},{4,28},{8,16},{12,20},{16,8},{20,12},{24,0},{28,4},{1,25},{... | collective-permute-start | bytes 393224 | tf_op jit(solution)/shard_map/ppermute | solution.py:28
  59.0 15.8 %collective-permute-start.37 = (bf16[1024,128]{1,0:T(8,128)(2,1)S(1)}, bf16[1024,128]{1,0:T(8,128)(2,1)S(1)}, u32[]{:S(2)}, u32[]{:S(2)}) collective-permute-start(bf16[1024,128]{1,0:T(8,128)(2,1)S(1)} %get-tuple-element.83), channel_id=1, source_target_pairs={{0,1},{1,0},{2,3},{3,2},{4,5},{5,4},{6,7},{7,6},{8,9},{9,8},{10,11... | collective-permute-start | bytes 786440 | tf_op jit(solution)/shard_map/ppermute | solution.py:28
  59.3 17.1 %collective-permute-start.38 = (bf16[1024,128]{1,0:T(8,128)(2,1)S(1)}, bf16[1024,128]{1,0:T(8,128)(2,1)S(1)}, u32[]{:S(2)}, u32[]{:S(2)}) collective-permute-start(bf16[1024,128]{1,0:T(8,128)(2,1)S(1)} %get-tuple-element.84), channel_id=1, source_target_pairs={{0,2},{1,3},{2,0},{3,1},{4,6},{5,7},{6,4},{7,5},{8,10},{9,11},{10,... | collective-permute-start | bytes 786440 | tf_op jit(solution)/shard_map/ppermute | solution.py:28
  62.6 11.0 %collective-permute-start.23 = (bf16[1,32,16,128]{3,2,1,0:T(8,128)(2,1)S(1)}, bf16[1,32,16,128]{3,2,1,0:T(8,128)(2,1)S(1)}, u32[]{:S(2)}, u32[]{:S(2)}) collective-permute-start(bf16[1,32,16,128]{3,2,1,0:T(8,128)(2,1)S(1)} %bitcast.137), channel_id=1, source_target_pairs={{0,16},{4,20},{8,24},{12,28},{16,0},{20,4},{24,8},{28,12},{1,17},{... | collective-permute-start | bytes 393224 | tf_op jit(solution)/shard_map/ppermute | solution.py:28
  64.0 9.6 %collective-permute-start.25 = (bf16[1,32,16,128]{3,2,1,0:T(8,128)(2,1)S(1)}, bf16[1,32,16,128]{3,2,1,0:T(8,128)(2,1)S(1)}, u32[]{:S(2)}, u32[]{:S(2)}) collective-permute-start(bf16[1,32,16,128]{3,2,1,0:T(8,128)(2,1)S(1)} %bitcast.138), channel_id=1, source_target_pairs={{0,24},{4,28},{8,16},{12,20},{16,8},{20,12},{24,0},{28,4},{1,25},{... | collective-permute-start | bytes 393224 | tf_op jit(solution)/shard_map/ppermute | solution.py:28
  66.0 10.4 %collective-permute-start.39 = (bf16[1024,128]{1,0:T(8,128)(2,1)S(1)}, bf16[1024,128]{1,0:T(8,128)(2,1)S(1)}, u32[]{:S(2)}, u32[]{:S(2)}) collective-permute-start(bf16[1024,128]{1,0:T(8,128)(2,1)S(1)} %get-tuple-element.85), channel_id=1, source_target_pairs={{0,3},{1,2},{2,1},{3,0},{4,7},{5,6},{6,5},{7,4},{8,11},{9,10},{10,... | collective-permute-start | bytes 786440 | tf_op jit(solution)/shard_map/ppermute | solution.py:28
  73.6 11.5 %collective-permute-start.27 = (bf16[1024,128]{1,0:T(8,128)(2,1)S(1)}, bf16[1024,128]{1,0:T(8,128)(2,1)S(1)}, u32[]{:S(2)}, u32[]{:S(2)}) collective-permute-start(bf16[1024,128]{1,0:T(8,128)(2,1)S(1)} %get-tuple-element.75), channel_id=1, source_target_pairs={{0,1},{1,0},{2,3},{3,2},{4,5},{5,4},{6,7},{7,6},{8,9},{9,8},{10,11... | collective-permute-start | bytes 786440 | tf_op jit(solution)/shard_map/ppermute | solution.py:28
  74.8 10.4 %collective-permute-start.28 = (bf16[1024,128]{1,0:T(8,128)(2,1)S(1)}, bf16[1024,128]{1,0:T(8,128)(2,1)S(1)}, u32[]{:S(2)}, u32[]{:S(2)}) collective-permute-start(bf16[1024,128]{1,0:T(8,128)(2,1)S(1)} %get-tuple-element.76), channel_id=1, source_target_pairs={{0,2},{1,3},{2,0},{3,1},{4,6},{5,7},{6,4},{7,5},{8,10},{9,11},{10,... | collective-permute-start | bytes 786440 | tf_op jit(solution)/shard_map/ppermute | solution.py:28
  76.4 11.8 %collective-permute-start.29 = (bf16[1024,128]{1,0:T(8,128)(2,1)S(1)}, bf16[1024,128]{1,0:T(8,128)(2,1)S(1)}, u32[]{:S(2)}, u32[]{:S(2)}) collective-permute-start(bf16[1024,128]{1,0:T(8,128)(2,1)S(1)} %get-tuple-element.77), channel_id=1, source_target_pairs={{0,3},{1,2},{2,1},{3,0},{4,7},{5,6},{6,5},{7,4},{8,11},{9,10},{10,... | collective-permute-start | bytes 786440 | tf_op jit(solution)/shard_map/ppermute | solution.py:28
  94.3 9.2 %collective-permute-start.59 = (bf16[1024,128]{1,0:T(8,128)(2,1)S(1)}, bf16[1024,128]{1,0:T(8,128)(2,1)S(1)}, u32[]{:S(2)}, u32[]{:S(2)}) collective-permute-start(bf16[1024,128]{1,0:T(8,128)(2,1)S(1)} %get-tuple-element.109), channel_id=1, source_target_pairs={{0,2},{1,3},{2,0},{3,1},{4,6},{5,7},{6,4},{7,5},{8,10},{9,11},{10,... | collective-permute-start | bytes 786440 | tf_op jit(solution)/shard_map/ppermute | solution.py:28
  97.4 26.4 %collective-permute-start.54 = (bf16[4,512,128]{2,1,0:T(8,128)(2,1)S(1)}, bf16[4,512,128]{2,1,0:T(8,128)(2,1)S(1)}, u32[]{:S(2)}, u32[]{:S(2)}) collective-permute-start(bf16[4,512,128]{2,1,0:T(8,128)(2,1)S(1)} %get-tuple-element.104), channel_id=1, source_target_pairs={{0,4},{4,0},{8,12},{12,8},{16,20},{20,16},{24,28},{28,24},{1,5},{5... | collective-permute-start | bytes 1572872 | tf_op jit(solution)/shard_map/ppermute | solution.py:28
  98.2 9.9 %collective-permute-start.60 = (bf16[1024,128]{1,0:T(8,128)(2,1)S(1)}, bf16[1024,128]{1,0:T(8,128)(2,1)S(1)}, u32[]{:S(2)}, u32[]{:S(2)}) collective-permute-start(bf16[1024,128]{1,0:T(8,128)(2,1)S(1)} %get-tuple-element.110), channel_id=1, source_target_pairs={{0,3},{1,2},{2,1},{3,0},{4,7},{5,6},{6,5},{7,4},{8,11},{9,10},{10,... | collective-permute-start | bytes 786440 | tf_op jit(solution)/shard_map/ppermute | solution.py:28
  98.2 12.4 %collective-permute-start.40 = (bf16[1024,128]{1,0:T(8,128)(2,1)S(1)}, bf16[1024,128]{1,0:T(8,128)(2,1)S(1)}, u32[]{:S(2)}, u32[]{:S(2)}) collective-permute-start(bf16[1024,128]{1,0:T(8,128)(2,1)S(1)} %get-tuple-element.87), channel_id=1, source_target_pairs={{0,1},{1,0},{2,3},{3,2},{4,5},{5,4},{6,7},{7,6},{8,9},{9,8},{10,11... | collective-permute-start | bytes 786440 | tf_op jit(solution)/shard_map/ppermute | solution.py:28
  98.9 15.8 %collective-permute-start.41 = (bf16[1024,128]{1,0:T(8,128)(2,1)S(1)}, bf16[1024,128]{1,0:T(8,128)(2,1)S(1)}, u32[]{:S(2)}, u32[]{:S(2)}) collective-permute-start(bf16[1024,128]{1,0:T(8,128)(2,1)S(1)} %get-tuple-element.88), channel_id=1, source_target_pairs={{0,2},{1,3},{2,0},{3,1},{4,6},{5,7},{6,4},{7,5},{8,10},{9,11},{10,... | collective-permute-start | bytes 786440 | tf_op jit(solution)/shard_map/ppermute | solution.py:28
  103.4 15.1 %collective-permute-start.42 = (bf16[1024,128]{1,0:T(8,128)(2,1)S(1)}, bf16[1024,128]{1,0:T(8,128)(2,1)S(1)}, u32[]{:S(2)}, u32[]{:S(2)}) collective-permute-start(bf16[1024,128]{1,0:T(8,128)(2,1)S(1)} %get-tuple-element.89), channel_id=1, source_target_pairs={{0,3},{1,2},{2,1},{3,0},{4,7},{5,6},{6,5},{7,4},{8,11},{9,10},{10,... | collective-permute-start | bytes 786440 | tf_op jit(solution)/shard_map/ppermute | solution.py:28
  109.7 31.7 %collective-permute-start.61 = (bf16[4,512,128]{2,1,0:T(8,128)(2,1)S(1)}, bf16[4,512,128]{2,1,0:T(8,128)(2,1)S(1)}, u32[]{:S(2)}, u32[]{:S(2)}) collective-permute-start(bf16[4,512,128]{2,1,0:T(8,128)(2,1)S(1)} %get-tuple-element.112), channel_id=1, source_target_pairs={{0,4},{4,0},{8,12},{12,8},{16,20},{20,16},{24,28},{28,24},{1,5},{5... | collective-permute-start | bytes 1572872 | tf_op jit(solution)/shard_map/ppermute | solution.py:28
  122.3 9.2 %collective-permute-start.44 = (bf16[1024,128]{1,0:T(8,128)(2,1)S(1)}, bf16[1024,128]{1,0:T(8,128)(2,1)S(1)}, u32[]{:S(2)}, u32[]{:S(2)}) collective-permute-start(bf16[1024,128]{1,0:T(8,128)(2,1)S(1)} %get-tuple-element.92), channel_id=1, source_target_pairs={{0,2},{1,3},{2,0},{3,1},{4,6},{5,7},{6,4},{7,5},{8,10},{9,11},{10,... | collective-permute-start | bytes 786440 | tf_op jit(solution)/shard_map/ppermute | solution.py:28
  123.8 11.3 %collective-permute-start.45 = (bf16[1024,128]{1,0:T(8,128)(2,1)S(1)}, bf16[1024,128]{1,0:T(8,128)(2,1)S(1)}, u32[]{:S(2)}, u32[]{:S(2)}) collective-permute-start(bf16[1024,128]{1,0:T(8,128)(2,1)S(1)} %get-tuple-element.93), channel_id=1, source_target_pairs={{0,3},{1,2},{2,1},{3,0},{4,7},{5,6},{6,5},{7,4},{8,11},{9,10},{10,... | collective-permute-start | bytes 786440 | tf_op jit(solution)/shard_map/ppermute | solution.py:28
  124.0 15.5 %collective-permute-start.55 = (bf16[512,128]{1,0:T(8,128)(2,1)S(1)}, bf16[512,128]{1,0:T(8,128)(2,1)S(1)}, u32[]{:S(2)}, u32[]{:S(2)}) collective-permute-start(bf16[512,128]{1,0:T(8,128)(2,1)S(1)} %get-tuple-element.124), channel_id=1, source_target_pairs={{0,8},{4,12},{8,0},{12,4},{16,24},{20,28},{24,16},{28,20},{1,9},{5... | collective-permute-start | bytes 393224 | tf_op jit(solution)/shard_map/ppermute | solution.py:28
  125.0 15.6 %collective-permute-start.56 = (bf16[512,128]{1,0:T(8,128)(2,1)S(1)}, bf16[512,128]{1,0:T(8,128)(2,1)S(1)}, u32[]{:S(2)}, u32[]{:S(2)}) collective-permute-start(bf16[512,128]{1,0:T(8,128)(2,1)S(1)} %get-tuple-element.126), channel_id=1, source_target_pairs={{0,16},{4,20},{8,24},{12,28},{16,0},{20,4},{24,8},{28,12},{1,17},{... | collective-permute-start | bytes 393224 | tf_op jit(solution)/shard_map/ppermute | solution.py:28
  131.4 9.2 %collective-permute-start.57 = (bf16[512,128]{1,0:T(8,128)(2,1)S(1)}, bf16[512,128]{1,0:T(8,128)(2,1)S(1)}, u32[]{:S(2)}, u32[]{:S(2)}) collective-permute-start(bf16[512,128]{1,0:T(8,128)(2,1)S(1)} %get-tuple-element.125), channel_id=1, source_target_pairs={{0,24},{4,28},{8,16},{12,20},{16,8},{20,12},{24,0},{28,4},{1,25},{... | collective-permute-start | bytes 393224 | tf_op jit(solution)/shard_map/ppermute | solution.py:28
  135.2 14.8 %collective-permute-start.50 = (bf16[4,512,128]{2,1,0:T(8,128)(2,1)S(1)}, bf16[4,512,128]{2,1,0:T(8,128)(2,1)S(1)}, u32[]{:S(2)}, u32[]{:S(2)}) collective-permute-start(bf16[4,512,128]{2,1,0:T(8,128)(2,1)S(1)} %get-tuple-element.100), channel_id=1, source_target_pairs={{0,4},{4,0},{8,12},{12,8},{16,20},{20,16},{24,28},{28,24},{1,5},{5... | collective-permute-start | bytes 1572872 | tf_op jit(solution)/shard_map/ppermute | solution.py:28
  139.5 21.7 %collective-permute-start.46 = (bf16[4,512,128]{2,1,0:T(8,128)(2,1)S(1)}, bf16[4,512,128]{2,1,0:T(8,128)(2,1)S(1)}, u32[]{:S(2)}, u32[]{:S(2)}) collective-permute-start(bf16[4,512,128]{2,1,0:T(8,128)(2,1)S(1)} %get-tuple-element.96), channel_id=1, source_target_pairs={{0,4},{4,0},{8,12},{12,8},{16,20},{20,16},{24,28},{28,24},{1,5},{5... | collective-permute-start | bytes 1572872 | tf_op jit(solution)/shard_map/ppermute | solution.py:28
  141.6 9.5 %collective-permute-start.62 = (bf16[512,128]{1,0:T(8,128)(2,1)S(1)}, bf16[512,128]{1,0:T(8,128)(2,1)S(1)}, u32[]{:S(2)}, u32[]{:S(2)}) collective-permute-start(bf16[512,128]{1,0:T(8,128)(2,1)S(1)} %get-tuple-element.121), channel_id=1, source_target_pairs={{0,8},{4,12},{8,0},{12,4},{16,24},{20,28},{24,16},{28,20},{1,9},{5... | collective-permute-start | bytes 393224 | tf_op jit(solution)/shard_map/ppermute | solution.py:28
  142.6 12.9 %collective-permute-start.63 = (bf16[512,128]{1,0:T(8,128)(2,1)S(1)}, bf16[512,128]{1,0:T(8,128)(2,1)S(1)}, u32[]{:S(2)}, u32[]{:S(2)}) collective-permute-start(bf16[512,128]{1,0:T(8,128)(2,1)S(1)} %get-tuple-element.123), channel_id=1, source_target_pairs={{0,16},{4,20},{8,24},{12,28},{16,0},{20,4},{24,8},{28,12},{1,17},{... | collective-permute-start | bytes 393224 | tf_op jit(solution)/shard_map/ppermute | solution.py:28
  144.3 12.4 %collective-permute-start.64 = (bf16[512,128]{1,0:T(8,128)(2,1)S(1)}, bf16[512,128]{1,0:T(8,128)(2,1)S(1)}, u32[]{:S(2)}, u32[]{:S(2)}) collective-permute-start(bf16[512,128]{1,0:T(8,128)(2,1)S(1)} %get-tuple-element.122), channel_id=1, source_target_pairs={{0,24},{4,28},{8,16},{12,20},{16,8},{20,12},{24,0},{28,4},{1,25},{... | collective-permute-start | bytes 393224 | tf_op jit(solution)/shard_map/ppermute | solution.py:28
  150.1 15.4 %collective-permute-start.51 = (bf16[512,128]{1,0:T(8,128)(2,1)S(1)}, bf16[512,128]{1,0:T(8,128)(2,1)S(1)}, u32[]{:S(2)}, u32[]{:S(2)}) collective-permute-start(bf16[512,128]{1,0:T(8,128)(2,1)S(1)} %get-tuple-element.127), channel_id=1, source_target_pairs={{0,8},{4,12},{8,0},{12,4},{16,24},{20,28},{24,16},{28,20},{1,9},{5... | collective-permute-start | bytes 393224 | tf_op jit(solution)/shard_map/ppermute | solution.py:28
  151.1 18.0 %collective-permute-start.52 = (bf16[512,128]{1,0:T(8,128)(2,1)S(1)}, bf16[512,128]{1,0:T(8,128)(2,1)S(1)}, u32[]{:S(2)}, u32[]{:S(2)}) collective-permute-start(bf16[512,128]{1,0:T(8,128)(2,1)S(1)} %get-tuple-element.129), channel_id=1, source_target_pairs={{0,16},{4,20},{8,24},{12,28},{16,0},{20,4},{24,8},{28,12},{1,17},{... | collective-permute-start | bytes 393224 | tf_op jit(solution)/shard_map/ppermute | solution.py:28
  155.5 13.6 %collective-permute-start.53 = (bf16[512,128]{1,0:T(8,128)(2,1)S(1)}, bf16[512,128]{1,0:T(8,128)(2,1)S(1)}, u32[]{:S(2)}, u32[]{:S(2)}) collective-permute-start(bf16[512,128]{1,0:T(8,128)(2,1)S(1)} %get-tuple-element.128), channel_id=1, source_target_pairs={{0,24},{4,28},{8,16},{12,20},{16,8},{20,12},{24,0},{28,4},{1,25},{... | collective-permute-start | bytes 393224 | tf_op jit(solution)/shard_map/ppermute | solution.py:28
  161.4 8.8 %collective-permute-start.47 = (bf16[512,128]{1,0:T(8,128)(2,1)S(1)}, bf16[512,128]{1,0:T(8,128)(2,1)S(1)}, u32[]{:S(2)}, u32[]{:S(2)}) collective-permute-start(bf16[512,128]{1,0:T(8,128)(2,1)S(1)} %get-tuple-element.130), channel_id=1, source_target_pairs={{0,8},{4,12},{8,0},{12,4},{16,24},{20,28},{24,16},{28,20},{1,9},{5... | collective-permute-start | bytes 393224 | tf_op jit(solution)/shard_map/ppermute | solution.py:28
  165.5 12.4 %collective-permute-start.48 = (bf16[512,128]{1,0:T(8,128)(2,1)S(1)}, bf16[512,128]{1,0:T(8,128)(2,1)S(1)}, u32[]{:S(2)}, u32[]{:S(2)}) collective-permute-start(bf16[512,128]{1,0:T(8,128)(2,1)S(1)} %get-tuple-element.132), channel_id=1, source_target_pairs={{0,16},{4,20},{8,24},{12,28},{16,0},{20,4},{24,8},{28,12},{1,17},{... | collective-permute-start | bytes 393224 | tf_op jit(solution)/shard_map/ppermute | solution.py:28
  165.5 12.4 %collective-permute-start.49 = (bf16[512,128]{1,0:T(8,128)(2,1)S(1)}, bf16[512,128]{1,0:T(8,128)(2,1)S(1)}, u32[]{:S(2)}, u32[]{:S(2)}) collective-permute-start(bf16[512,128]{1,0:T(8,128)(2,1)S(1)} %get-tuple-element.131), channel_id=1, source_target_pairs={{0,24},{4,28},{8,16},{12,20},{16,8},{20,12},{24,0},{28,4},{1,25},{... | collective-permute-start | bytes 393224 | tf_op jit(solution)/shard_map/ppermute | solution.py:28
  (23 other events, 173.5 us)

commit v4 on v3

v4 whole, which is shorter than its diff:
```python
import functools
import math

import jax
import jax.numpy as jnp
from jax import lax
from jax.experimental import pallas as pl
from jax.experimental.pallas import tpu as pltpu
from jax.sharding import PartitionSpec as P

half_root = 0.7071067811865476
inv_root_tau = 0.3989422804014327
lane_tile = 128
packed_rows = 16
CFG = {'flops': 2, 'near': (True, True, False), 'scatters': {'first': 'direct', 'inner': 'direct', 'outer': 'direct', 'second': 'direct'}, 'A1': 0, 'A2': 0, 'A3': 0, 'A4': 0, 'A5': 0, 'A6': 0, 'A7': 1, 'B1': 0, 'B2': 0, 'B3': 0, 'B4': 0, 'B5': 0, 'B6': 0, 'B7': 0, 'C1': 0, 'C2': 0, 'C3': 0, 'C4': 0, 'T1': 0, 'T2': 0, 'T3': 0, 'T4': 0, 'T5': 0, 'T6': 0, 'Q1': 0, 'Q2': 0, 'Q3': 0, 'Q4': 0, 'Q5': 0, 'Q6': 0}
vmem_bytes = 14 * 1024 * 1024


def gelu_parts(values):
    normal_cdf = 0.5 * (1.0 + lax.erf(values * half_root))
    return (
        values * normal_cdf,
        normal_cdf + values * jnp.exp(-0.5 * values * values) * inv_root_tau,
    )


def hop(source, axis, offset):
    size = lax.axis_size(axis)
    return lax.ppermute(source, axis, [(i, i ^ offset) for i in range(size)])


def exchange(sends):
    return [sends[0]] + [hop(sends[q], "mp", q) for q in range(1, len(sends))]


def nothing_kernel(*refs):
    pass


def wait_for(source, *others):
    if not others:
        return source
    return pl.pallas_call(
        nothing_kernel,
        out_shape=shaped(source.dtype, *source.shape),
        in_specs=[pl.BlockSpec(memory_space=pl.ANY)] * (1 + len(others)),
        out_specs=pl.BlockSpec(memory_space=pl.ANY),
        input_output_aliases={0: 0},
        compiler_params=pltpu.CompilerParams(vmem_limit_bytes=vmem_bytes),
    )(source, *others)


def steps_of(size):
    return [1 << bit for bit in reversed(range(1, size.bit_length() - 1))]


class Pieces:
    def __init__(self, shard):
        self.size = lax.axis_size("dp")
        self.depth = 0
        self.whole = None
        self.got = {0: shard[None]}
        if shard.shape[1] % packed_rows:
            self.whole = lax.all_gather(shard, "dp", axis=1, tiled=True)[None]

    def wave(self, *others):
        self.depth += 1
        offsets = [o for o in range(self.size) if o.bit_count() == self.depth]
        if self.whole is not None:
            return []
        for o in offsets:
            low = o & -o
            self.got[o] = hop(wait_for(self.got[o ^ low], *others), "dp", low)
        return [self.got[o] for o in offsets]

    def finish(self):
        if self.whole is not None:
            return ((0,),), (self.whole,)
        while len(self.got) < self.size:
            self.wave()
        return tuple((o,) for o in self.got), tuple(self.got.values())


class Joined:
    def __init__(self, shard, near):
        self.steps = steps_of(lax.axis_size("dp"))
        self.steps.insert(0 if near else len(self.steps), 1)
        self.offsets, self.held = (0,), shard[None]
        self.arrived = None
        if shard.shape[1] % packed_rows:
            self.steps = []
            self.held = lax.all_gather(shard, "dp", axis=1, tiled=True)[None]

    def step(self, *others):
        if not self.steps:
            return []
        if self.arrived is not None:
            self.held = join(self.held, self.arrived, others)
            self.offsets += self.new
            others = ()
        step = self.steps.pop(0)
        self.new = tuple(o ^ step for o in self.offsets)
        self.arrived = hop(wait_for(self.held, *others), "dp", step)
        return [self.arrived]

    def finish(self):
        while self.steps:
            self.step()
        if self.arrived is None:
            return ((0,),), (self.held,)
        return (self.offsets, self.new), (self.held, self.arrived)


class Scatter:
    def __init__(self, halves, steps, direct):
        self.sent, self.kept = halves
        self.steps = list(steps)
        self.direct = direct
        self.held = None

    def step(self, *others):
        step = self.steps.pop(0)
        if self.held is not None:
            half = self.held.shape[0] // 2
            self.sent, self.kept = self.held[half:].astype(jnp.bfloat16), self.held[:half]
        self.held = self.kept + hop(wait_for(self.sent, *others), "dp", step).astype(jnp.float32)
        return self.held

    def finish(self, *others):
        if not self.direct:
            while self.steps:
                self.step(*others)
            return self.held[0]
        size = self.held.shape[0]
        bits = list(reversed(self.steps))
        offsets = [sum(bit for k, bit in enumerate(bits) if q >> k & 1) for q in range(size)]
        total = self.held[0]
        for q in range(1, size):
            part = wait_for(self.held[q].astype(jnp.bfloat16), *others)
            total = total + hop(part, "dp", offsets[q]).astype(jnp.float32)
        return total


def join_kernel(one, two, out):
    out[: one.shape[0]] = one[...]
    out[one.shape[0] :] = two[...]


def join(one, two, after):
    count = one.shape[0] + two.shape[0]
    (out,) = run(join_kernel, [shaped(one.dtype, count, *one.shape[1:])], [], [one, two], 0, after)
    return out


class Sizes:
    def __init__(self, tokens, right_one):
        self.tokens = tokens.shape[0]
        self.local, self.rows, self.block = right_one.shape
        self.dp = lax.axis_size("dp")
        self.mp = lax.axis_size("mp")


def matmul(left, right, left_dim, right_dim):
    return lax.dot_general(
        left, right, (((left_dim,), (right_dim,)), ((), ())), preferred_element_type=jnp.float32
    )


def place(full, pieces, layout, me):
    local, block, width = full.shape
    rows = block // sum(len(offsets) for offsets in layout)
    for piece, offsets in zip(pieces, layout, strict=True):
        for k, offset in enumerate(offsets):
            start = 0 if rows == block else pl.multiple_of((me ^ offset) * rows, rows)
            full[:, pl.ds(start, rows), :] = piece[k].reshape(local, rows, width)


def place_arrived(full, pieces, me):
    local, block, width = full.shape
    rows = block // len(pieces)
    for q, piece in enumerate(pieces):
        start = pl.multiple_of((me ^ q) * rows, rows)
        full[:, pl.ds(start, rows), :] = piece[...].reshape(local, rows, width)


def spread(mixed, sends, index):
    size = sends[0].shape[0]
    for q, send in enumerate(sends):
        start = pl.multiple_of((index ^ q) * size, size)
        for h in range(mixed.shape[0]):
            lanes = slice(h * lane_tile, (h + 1) * lane_tile)
            send[:, lanes] = mixed[h, pl.ds(start, size), :].astype(jnp.bfloat16)


def split_grad(sums, sent, kept, index, steps):
    local, block, width = sums.shape
    offsets = [0]
    for step in reversed(steps[1:]):
        offsets += [offset ^ step for offset in offsets]
    rows = block // (2 * len(offsets))
    for q, offset in enumerate(offsets):
        for target, number in ((kept, offset), (sent, offset ^ steps[0])):
            start = pl.multiple_of((index ^ number) * rows, rows)
            part = sums[:, pl.ds(start, rows), :].reshape(local * rows, width)
            target[q] = part.astype(target.dtype)


def column(mixed, c, local, value):
    for h in range(mixed.shape[0]):
        lanes = slice(h * lane_tile, (h + 1) * lane_tile)
        mixed[h, pl.ds(c, value.shape[0], stride=local), :] = value[:, lanes]


def turn_kernel(z, ids, cotangent, *refs):
    sends, (mixed,) = refs[: z.mp], refs[z.mp :]
    for c in range(z.local):
        part = cotangent[:, c * z.block : (c + 1) * z.block].astype(jnp.float32)
        column(mixed, c, z.local, part.T)
    spread(mixed, sends, ids[1])


def first_kernel(z, layout, ids, tokens, *refs):
    pieces, refs = refs[: len(layout)], refs[len(layout) :]
    full, sends, mixed = refs[0], refs[1 : 1 + z.mp], refs[1 + z.mp]
    place(full, pieces, layout, ids[0])
    for c in range(z.local):
        part = tokens[:, c * z.block : (c + 1) * z.block]
        column(mixed, c, z.local, matmul(full[c], part, 0, 1))
    spread(mixed, sends, ids[1])


def middle_kernel(z, layout, side, ids, *refs):
    pieces, refs = refs[: len(layout)], refs[len(layout) :]
    arrived, refs = refs[: z.mp], refs[z.mp :]
    full, columns, sends, mixed = refs[0], refs[1], refs[2 : 2 + z.mp], refs[2 + z.mp]
    place(full, pieces, layout, ids[0])
    place_arrived(columns, arrived, ids[1])
    for c in range(z.local):
        column(mixed, c, z.local, matmul(full[c], columns[c], side, 0))
    spread(mixed, sends, ids[1])


def gelu_kernel(z, layout, ids, *refs):
    pieces, refs = refs[: len(layout)], refs[len(layout) :]
    preact, backs, refs = refs[: z.mp], refs[z.mp : 2 * z.mp], refs[2 * z.mp :]
    full, hidden, back, sends, mixed = refs[0], refs[1], refs[2], refs[3 : 3 + z.mp], refs[3 + z.mp]
    place(full, pieces, layout, ids[0])
    place_arrived(hidden, preact, ids[1])
    place_arrived(back, backs, ids[1])
    for c in range(z.local):
        activated, slope = gelu_parts(hidden[c].astype(jnp.float32))
        hidden[c] = activated.astype(jnp.bfloat16)
        column(mixed, c, z.local, matmul(full[c], back[c], 1, 0) * slope)
    spread(mixed, sends, ids[1])


def second_kernel(z, ids, full, hidden, *refs):
    sends, (mixed,) = refs[: z.mp], refs[z.mp :]
    for c in range(z.local):
        column(mixed, c, z.local, matmul(full[c], hidden[c], 0, 0))
    spread(mixed, sends, ids[1])


def grad_kernel(z, steps, ids, left, right, sent, kept, sums):
    for c in range(z.local):
        sums[c] = matmul(left[c], right[c], 1, 1)
    split_grad(sums, sent, kept, ids[0], steps)


def placed_grad_kernel(z, steps, ids, right, *refs):
    pieces, (sent, kept, left, sums) = refs[: z.mp], refs[z.mp :]
    place_arrived(left, pieces, ids[1])
    grad_kernel(z, steps, ids, left, right, sent, kept, sums)


def last_grad_kernel(z, steps, ids, tokens, *refs):
    pieces, (turned, sent, kept, back, sums) = refs[: z.mp], refs[z.mp :]
    place_arrived(back, pieces, ids[1])
    for c in range(z.local):
        block = back[c].T
        turned[c] = block
        sums[c] = matmul(tokens[:, c * z.block : (c + 1) * z.block], block, 0, 0)
    split_grad(sums, sent, kept, ids[0], steps)


def tokens_kernel(z, full, turned, out):
    for c in range(z.local):
        part = matmul(turned[c], full[c], 1, 1)
        out[:, c * z.block : (c + 1) * z.block] = part.astype(jnp.bfloat16)


def shaped(kind, *shape):
    return jax.ShapeDtypeStruct(shape, kind)


def run(body, outs, scratch, inputs, products, after=()):
    def skip(*refs):
        body(*refs[: len(inputs)], *refs[len(inputs) + len(after) :])

    specs = [
        pl.BlockSpec(memory_space=pltpu.SMEM if one.dtype == jnp.int32 else pltpu.VMEM) for one in inputs
    ]
    moved = sum(math.prod(one.shape) * one.dtype.itemsize for one in (*inputs, *outs))
    return pl.pallas_call(
        skip,
        out_shape=outs,
        in_specs=specs + [pl.BlockSpec(memory_space=pl.ANY)] * len(after),
        out_specs=[pl.BlockSpec(memory_space=pltpu.VMEM) for _ in outs],
        scratch_shapes=scratch,
        compiler_params=pltpu.CompilerParams(vmem_limit_bytes=vmem_bytes),
        cost_estimate=pl.CostEstimate(flops=CFG["flops"] * products, bytes_accessed=moved, transcendentals=0),
    )(*inputs, *after)


def on_device(tokens, cotangent, right_one, left_one, right_two, left_two):
    z = Sizes(tokens, right_one)
    bf16, f32 = jnp.bfloat16, jnp.float32
    scale = 1.0 / math.sqrt(z.tokens * z.dp)
    ids = jnp.stack([lax.axis_index("dp"), lax.axis_index("mp")]).astype(jnp.int32)
    products = z.local * z.block * z.block * z.tokens
    weight = shaped(bf16, z.local, z.block, z.block)
    acts = shaped(bf16, z.local, z.block, z.tokens)
    sends = [shaped(bf16, z.local * z.local, z.tokens)] * z.mp
    halves = [
        shaped(bf16, z.dp // 2, z.local * z.rows, z.block),
        shaped(f32, z.dp // 2, z.local * z.rows, z.block),
    ]
    mixed = pltpu.VMEM((z.tokens // lane_tile, z.block * z.local, lane_tile), f32)
    sums = pltpu.VMEM((z.local, z.block, z.block), f32)
    held = pltpu.VMEM((z.local, z.block, z.tokens), bf16)

    part = functools.partial
    along = list(reversed(steps_of(z.dp)))
    orders = {name: [*along, 1] if kind == "far" else [1, *along] for name, kind in CFG["scatters"].items()}

    def on(key, *values):
        return values if CFG[key] else ()

    near = CFG["near"]
    first, inner = Pieces(right_one), Joined(left_one, near[0])
    outer, second = Joined(left_two, near[1]), Joined(right_two, near[2])

    wave0 = first.wave()
    i0 = inner.step()
    turned_up = run(part(turn_kernel, z), sends, [mixed], [ids, cotangent], 0)
    upstream = exchange(turned_up)
    wave1 = first.wave()
    o0 = outer.step() if near[1] else outer.step(*on("A1", *wave0[:1]))
    i1 = inner.step(*on("A2", turned_up[1]))
    s0 = second.step(*on("A3", *wave0[:1])) if not near[2] else second.step()
    wave2 = first.wave()
    first_layout, first_pieces = first.finish()
    right_first, *parts = run(
        part(first_kernel, z, first_layout),
        [weight] + sends,
        [mixed],
        [ids, tokens, *first_pieces],
        products,
        [*on("A4", *s0), *on("A5", *i1), *on("A6", *o0), *on("A7", *upstream[2:3])],
    )
    k1 = parts[1]
    first_columns = exchange(parts)
    i2 = inner.step(*on("B1", *wave2))
    o1 = outer.step(*on("B2", k1), *on("B3", first_columns[1]))
    s1 = second.step(*on("B4", k1), *on("B5", first_columns[1]))
    inner_layout, inner_pieces = inner.finish()
    left_first, columns, *parts = run(
        part(middle_kernel, z, inner_layout, 0),
        [weight, acts] + sends,
        [mixed],
        [ids, *inner_pieces, *first_columns],
        products,
        [*on("B6", *s1), *on("B7", *o1)],
    )
    k3 = parts[1]
    preact = exchange(parts)
    outer.step(*on("C1", k3))
    second.step(*on("C2", k3))
    outer_layout, outer_pieces = outer.finish()
    second_layout, second_pieces = second.finish()
    _, upstream_columns, *parts = run(
        part(middle_kernel, z, outer_layout, 1),
        [weight, acts] + sends,
        [mixed],
        [ids, *outer_pieces, *upstream],
        products,
        [*on("C3", k3), *on("C4", preact[1])],
    )
    second_rows = exchange(parts)
    right_second, hidden, second_back, *parts = run(
        part(gelu_kernel, z, second_layout),
        [weight, acts, acts] + sends,
        [mixed],
        [ids, *second_pieces, *preact, *second_rows],
        products,
    )
    first_upstream = exchange(parts)
    parts = run(
        part(second_kernel, z),
        sends,
        [mixed],
        [ids, right_second, hidden],
        products,
        [*on("T1", first_upstream[1])],
    )
    second_columns = exchange(parts)
    right_two_halves = run(
        part(grad_kernel, z, orders["second"]),
        halves,
        [sums],
        [ids, hidden, second_back],
        products,
        [*on("T2", first_upstream[1]), *on("T3", second_columns[1])],
    )
    scatter = {"second": Scatter(right_two_halves, orders["second"], CFG["scatters"]["second"] == "direct")}
    scatter["second"].step()
    _, upstream_rows, *parts = run(
        part(middle_kernel, z, ((0,),), 1),
        [weight, acts] + sends,
        [mixed],
        [ids, left_first[None], *first_upstream],
        products,
        [*on("T4", *right_two_halves[:1])],
    )
    left_one_halves = run(part(grad_kernel, z, orders["inner"]), halves, [sums], [ids, columns, upstream_rows], products)
    parts[1] = wait_for(parts[1], *on("T5", left_one_halves[0]))
    first_rows = exchange(parts)
    scatter["inner"] = Scatter(left_one_halves, orders["inner"], CFG["scatters"]["inner"] == "direct")
    scatter["inner"].step()
    left_two_halves = run(
        part(placed_grad_kernel, z, orders["outer"]),
        halves,
        [held, sums],
        [ids, upstream_columns, *second_columns],
        products,
        [*on("T6", first_rows[1])],
    )
    scatter["outer"] = Scatter(left_two_halves, orders["outer"], CFG["scatters"]["outer"] == "direct")
    o_held = scatter["outer"].step()
    totals = {"second": scatter["second"].finish()}
    turned, *right_one_halves = run(
        part(last_grad_kernel, z, orders["first"]),
        [shaped(bf16, z.local, z.tokens, z.block)] + halves,
        [held, sums],
        [ids, tokens, *first_rows],
        products,
        [*on("Q1", totals["second"]), *on("Q2", left_two_halves[0]), *on("Q3", scatter["inner"].held)],
    )
    scatter["first"] = Scatter(right_one_halves, orders["first"], CFG["scatters"]["first"] == "direct")
    f_held = scatter["first"].step()
    totals["inner"] = scatter["inner"].finish()
    totals["first"] = scatter["first"].finish(*on("Q4", totals["inner"]), *on("Q5", o_held))
    totals["outer"] = scatter["outer"].finish()
    (tokens_grad,) = run(
        part(tokens_kernel, z),
        [shaped(bf16, z.tokens, z.local * z.block)],
        [],
        [right_first, turned],
        products,
        [*on("Q6", f_held)],
    )
    summed = [
        (totals[name] * scale).reshape(z.local, z.rows, z.block) for name in ("first", "inner", "second", "outer")
    ]
    return (tokens_grad, *summed)


def solution(mesh):
    placed = (
        P("dp", "mp"),
        P("dp", "mp"),
        P("mp", "dp", None),
        P("mp", "dp", None),
        P("mp", "dp", None),
        P("mp", "dp", None),
    )
    return jax.shard_map(
        on_device,
        mesh=mesh,
        in_specs=placed,
        out_specs=(
            P("dp", "mp"),
            P("mp", "dp", None),
            P("mp", "dp", None),
            P("mp", "dp", None),
            P("mp", "dp", None),
        ),
        check_vma=False,
    )
```

time: 179 us -> 170 us (0.950)
  waiting for transfers between devices: 73.6 us -> 69.2 us
  starting transfers between devices: 72.4 us -> 68.7 us
    ppermute x65 -> x53, waiting for transfers between devices: 73.6 us -> 69.2 us  [hop(): return lax.ppermute(source, axis, [(i, i ^ offset) for i in range(size)])]
    ppermute x65 -> x53, starting transfers between devices: 72.4 us -> 68.7 us  [hop(): return lax.ppermute(source, axis, [(i, i ^ offset) for i in range(size)])]
    pallas_call x12 -> x18, Pallas kernels: 25.8 us -> 26 us  [run(): pl.pallas_call(skip, out_shape=outs, in_specs=specs + [pl.BlockSpec(memor...]
  transfers between devices with their start and end apart: 65 -> 53, of which waited for: 24 -> 19; matrix products, arithmetic and copies ran while one was open for 2% -> 2% of each run, Pallas kernels for 11% -> 13%
where the time goes in v4:
time: 170 us
  waiting for transfers between devices  69.2 us (41%)
  starting transfers between devices  68.7 us (40%)
  Pallas kernels  26 us (15%)
  other arithmetic  3.72 us (2%)
    ppermute x53, waiting for transfers between devices, hop(): return lax.ppermute(source, axis, [(i, i ^ offset) for i in range(size)])  69.2 us
    ppermute x53, starting transfers between devices, hop(): return lax.ppermute(source, axis, [(i, i ^ offset) for i in range(size)])  68.7 us
    pallas_call x18, Pallas kernels, run(): pl.pallas_call(skip, out_shape=outs, in_specs=specs + [pl.BlockSpec(memor...  26 us
  transfers between devices with their start and end apart: 53, of which 19 were waited for; matrix products, arithmetic and copies ran while one was open for 2% of the time, Pallas kernels for 13%

profile of v4, /device:TPU:0, one launch (start us, length us, event | category | flops | bytes accessed | tf_op | source)
XLA Modules:
  0.0 169.9 jit_solution(9155699773726483552)
XLA Ops:
  0.6 3.0 %collective-permute-start.8 = (bf16[1,32,16,128]{3,2,1,0:T(8,128)(2,1)}, bf16[1,32,16,128]{3,2,1,0:T(8,128)(2,1)S(1)}, u32[]{:S(2)}, u32[]{:S(2)}) collective-permute-start(bf16[1,32,16,128]{3,2,1,0:T(8,128)(2,1)} %bitcast.80), channel_id=1, source_target_pairs={{0,4},{4,0},{8,12},{12,8},{16,20},{20,16},{24,28},{28,24},{1,5},{5... | collective-permute-start | bytes 393224 | tf_op jit(solution)/shard_map/ppermute | solution.py:29
  3.6 2.6 %collective-permute-start.2 = (bf16[1,32,16,128]{3,2,1,0:T(8,128)(2,1)}, bf16[1,32,16,128]{3,2,1,0:T(8,128)(2,1)S(1)}, u32[]{:S(2)}, u32[]{:S(2)}) collective-permute-start(bf16[1,32,16,128]{3,2,1,0:T(8,128)(2,1)} %bitcast.76), channel_id=1, source_target_pairs={{0,16},{4,20},{8,24},{12,28},{16,0},{20,4},{24,8},{28,12},{1,17},{... | collective-permute-start | bytes 393224 | tf_op jit(solution)/shard_map/ppermute | solution.py:29
  6.2 1.6 collective-permute-start.1
  10.0 1.9 %shard_map.101 = (bf16[1024,128]{1,0:T(8,128)(2,1)S(1)}, bf16[1024,128]{1,0:T(8,128)(2,1)S(1)}, bf16[1024,128]{1,0:T(8,128)(2,1)S(1)}, bf16[1024,128]{1,0:T(8,128)(2,1)S(1)}) custom-call(s32[2]{0:T(128)S(1)} %pad_add_fusion.refs_0_, bf16[128,4096]{1,0:T(8,128)(2,1)S(1)} %copy-done.1), custom_call_target="tpu_custom_call" | custom-call | bytes 2097160 | tf_op jit(solution)/shard_map/pallas_call | solution.py:304
  11.9 2.7 %collective-permute-start.9 = (bf16[2,32,16,128]{3,2,1,0:T(8,128)(2,1)S(1)}, bf16[2,32,16,128]{3,2,1,0:T(8,128)(2,1)S(1)}, u32[]{:S(2)}, u32[]{:S(2)}) collective-permute-start(bf16[2,32,16,128]{3,2,1,0:T(8,128)(2,1)S(1)} %shard_map.103.refs_0_), channel_id=1, source_target_pairs={{0,16},{4,20},{8,24},{12,28},{16,0},{20,4},{24,8},{28,12},{1,17},{... | collective-permute-start | bytes 786440 | tf_op jit(solution)/shard_map/ppermute | solution.py:29
  18.1 6.7 %collective-permute-done.14.refs_1_ = bf16[1,32,16,128]{3,2,1,0:T(8,128)(2,1)S(1)} collective-permute-done((bf16[1,32,16,128]{3,2,1,0:T(8,128)(2,1)}, bf16[1,32,16,128]{3,2,1,0:T(8,128)(2,1)S(1)}, u32[]{:S(2)}, u32[]{:S(2)}) %collective-permute-start.14) | collective-permute-done | bytes 131104 | tf_op jit(solution)/shard_map/ppermute | solution.py:29
  25.0 1.9 %collective-permute-start.3 = (bf16[1,32,16,128]{3,2,1,0:T(8,128)(2,1)S(1)}, bf16[1,32,16,128]{3,2,1,0:T(8,128)(2,1)S(1)}, u32[]{:S(2)}, u32[]{:S(2)}) collective-permute-start(bf16[1,32,16,128]{3,2,1,0:T(8,128)(2,1)S(1)} %collective-permute-done.1.refs_4_), channel_id=1, source_target_pairs={{0,4},{4,0},{8,12},{12,8},{16,20},{20,16},{24,28},{28,24},{1,5},{5... | collective-permute-start | bytes 393224 | tf_op jit(solution)/shard_map/ppermute | solution.py:29
  26.9 2.8 %collective-permute-done.5.refs_8_ = bf16[1,32,16,128]{3,2,1,0:T(8,128)(2,1)S(1)} collective-permute-done((bf16[1,32,16,128]{3,2,1,0:T(8,128)(2,1)S(1)}, bf16[1,32,16,128]{3,2,1,0:T(8,128)(2,1)S(1)}, u32[]{:S(2)}, u32[]{:S(2)}) %collective-permute-start.5) | collective-permute-done | bytes 131104 | tf_op jit(solution)/shard_map/ppermute | solution.py:29
  30.4 2.6 %collective-permute-start.21 = (bf16[2,32,16,128]{3,2,1,0:T(8,128)(2,1)S(1)}, bf16[2,32,16,128]{3,2,1,0:T(8,128)(2,1)S(1)}, u32[]{:S(2)}, u32[]{:S(2)}) collective-permute-start(bf16[2,32,16,128]{3,2,1,0:T(8,128)(2,1)S(1)} %shard_map.108.refs_0_), channel_id=1, source_target_pairs={{0,16},{4,20},{8,24},{12,28},{16,0},{20,4},{24,8},{28,12},{1,17},{... | collective-permute-start | bytes 786440 | tf_op jit(solution)/shard_map/ppermute | solution.py:29
  33.1 2.5 %collective-permute-start.15 = (bf16[2,32,16,128]{3,2,1,0:T(8,128)(2,1)S(1)}, bf16[2,32,16,128]{3,2,1,0:T(8,128)(2,1)S(1)}, u32[]{:S(2)}, u32[]{:S(2)}) collective-permute-start(bf16[2,32,16,128]{3,2,1,0:T(8,128)(2,1)S(1)} %shard_map.106.refs_0_), channel_id=1, source_target_pairs={{0,8},{4,12},{8,0},{12,4},{16,24},{20,28},{24,16},{28,20},{1,9},{5... | collective-permute-start | bytes 786440 | tf_op jit(solution)/shard_map/ppermute | solution.py:29
  35.7 2.6 %shard_map.102 = (bf16[32,128,128]{2,1,0:T(8,128)(2,1)S(1)}, bf16[1024,128]{1,0:T(8,128)(2,1)S(1)}, bf16[1024,128]{1,0:T(8,128)(2,1)S(1)}, bf16[1024,128]{1,0:T(8,128)(2,1)S(1)}, bf16[1024,128]{1,0:T(8,128)(2,1)S(1)}) custom-call(s32[2]{0:T(128)S(1)} %pad_add_fusion.refs_0_, bf16[128,4096]{1,0:T(8,128)(2,1)S(1)} %copy-done, ...), custom_call_target="tpu_custom_call" | custom-call | flops 134217728 | bytes 4194312 | tf_op jit(solution)/shard_map/pallas_call | solution.py:304
  38.4 1.6 collective-permute-start.12
  40.0 3.4 %collective-permute-done.21.refs_1_ = bf16[2,32,16,128]{3,2,1,0:T(8,128)(2,1)S(1)} collective-permute-done((bf16[2,32,16,128]{3,2,1,0:T(8,128)(2,1)S(1)}, bf16[2,32,16,128]{3,2,1,0:T(8,128)(2,1)S(1)}, u32[]{:S(2)}, u32[]{:S(2)}) %collective-permute-start.21) | collective-permute-done | bytes 262176 | tf_op jit(solution)/shard_map/ppermute | solution.py:29
  43.4 3.1 %collective-permute-done.15.refs_1_ = bf16[2,32,16,128]{3,2,1,0:T(8,128)(2,1)S(1)} collective-permute-done((bf16[2,32,16,128]{3,2,1,0:T(8,128)(2,1)S(1)}, bf16[2,32,16,128]{3,2,1,0:T(8,128)(2,1)S(1)}, u32[]{:S(2)}, u32[]{:S(2)}) %collective-permute-start.15) | collective-permute-done | bytes 262176 | tf_op jit(solution)/shard_map/ppermute | solution.py:29
  47.8 1.7 collective-permute-start.16
  49.4 2.9 %collective-permute-done.13.refs_6_ = bf16[1024,128]{1,0:T(8,128)(2,1)S(1)} collective-permute-done((bf16[1024,128]{1,0:T(8,128)(2,1)S(1)}, bf16[1024,128]{1,0:T(8,128)(2,1)S(1)}, u32[]{:S(2)}, u32[]{:S(2)}) %collective-permute-start.13) | collective-permute-done | bytes 262176 | tf_op jit(solution)/shard_map/ppermute | solution.py:29
  52.3 1.7 collective-permute-start.24
  54.0 3.7 %collective-permute-done.10.refs_2_ = bf16[4,32,16,128]{3,2,1,0:T(8,128)(2,1)S(1)} collective-permute-done((bf16[4,32,16,128]{3,2,1,0:T(8,128)(2,1)S(1)}, bf16[4,32,16,128]{3,2,1,0:T(8,128)(2,1)S(1)}, u32[]{:S(2)}, u32[]{:S(2)}) %collective-permute-start.10) | collective-permute-done | bytes 524320 | tf_op jit(solution)/shard_map/ppermute | solution.py:29
  57.7 2.6 %shard_map.105 = (bf16[32,128,128]{2,1,0:T(8,128)(2,1)S(1)}, bf16[32,128,128]{2,1,0:T(8,128)(2,1)S(1)}, bf16[1024,128]{1,0:T(8,128)(2,1)S(1)}, bf16[1024,128]{1,...) custom-call(s32[2]{0:T(128)S(1)} %pad_add_fusion.refs_0_, ...), custom_call_target="tpu_custom_call" | custom-call | flops 134217728 | bytes 5242888 | tf_op jit(solution)/shard_map/pallas_call | solution.py:304
  62.2 3.9 %collective-permute-done.22.refs_2_ = bf16[4,32,16,128]{3,2,1,0:T(8,128)(2,1)S(1)} collective-permute-done((bf16[4,32,16,128]{3,2,1,0:T(8,128)(2,1)S(1)}, bf16[4,32,16,128]{3,2,1,0:T(8,128)(2,1)S(1)}, u32[]{:S(2)}, u32[]{:S(2)}) %collective-permute-start.22) | collective-permute-done | bytes 524320 | tf_op jit(solution)/shard_map/ppermute | solution.py:29
  66.1 2.5 %shard_map.110 = (bf16[32,128,128]{2,1,0:T(8,128)(2,1)}, bf16[32,128,128]{2,1,0:T(8,128)(2,1)S(1)}, bf16[1024,128]{1,0:T(8,128)(2,1)S(1)}, bf16[1024,128]{1,0:T(...) custom-call(s32[2]{0:T(128)S(1)} %pad_add_fusion.refs_0_, ...), custom_call_target="tpu_custom_call" | custom-call | flops 134217728 | bytes 5242888 | tf_op jit(solution)/shard_map/pallas_call | solution.py:304
  70.5 3.7 %collective-permute-done.19.refs_6_ = bf16[1024,128]{1,0:T(8,128)(2,1)S(1)} collective-permute-done((bf16[1024,128]{1,0:T(8,128)(2,1)S(1)}, bf16[1024,128]{1,0:T(8,128)(2,1)S(1)}, u32[]{:S(2)}, u32[]{:S(2)}) %collective-permute-start.19) | collective-permute-done | bytes 262176 | tf_op jit(solution)/shard_map/ppermute | solution.py:29
  74.2 6.5 %collective-permute-done.26.refs_9_ = bf16[1024,128]{1,0:T(8,128)(2,1)S(1)} collective-permute-done((bf16[1024,128]{1,0:T(8,128)(2,1)S(1)}, bf16[1024,128]{1,0:T(8,128)(2,1)S(1)}, u32[]{:S(2)}, u32[]{:S(2)}) %collective-permute-start.26) | collective-permute-done | bytes 262176 | tf_op jit(solution)/shard_map/ppermute | solution.py:29
  80.8 4.7 %collective-permute-done.27.refs_10_ = bf16[1024,128]{1,0:T(8,128)(2,1)S(1)} collective-permute-done((bf16[1024,128]{1,0:T(8,128)(2,1)S(1)}, bf16[1024,128]{1,0:T(8,128)(2,1)S(1)}, u32[]{:S(2)}, u32[]{:S(2)}) %collective-permute-start.27) | collective-permute-done | bytes 262176 | tf_op jit(solution)/shard_map/ppermute | solution.py:29
  85.5 3.0 %shard_map.111 = (bf16[32,128,128]{2,1,0:T(8,128)(2,1)S(1)}, bf16[32,128,128]{2,1,0:T(8,128)(2,1)S(1)}, bf16[32,128,128]{2,1,0:T(8,128)(2,1)S(1)}, bf16[1024,128...) custom-call(s32[2]{0:T(128)S(1)} %pad_add_fusion.refs_0_, ...), custom_call_target="tpu_custom_call" | custom-call | flops 134217728 | bytes 7340040 | tf_op jit(solution)/shard_map/pallas_call | solution.py:304
  90.9 1.6 collective-permute-start.29
  92.8 2.6 %shard_map.117 = (bf16[1024,128]{1,0:T(8,128)(2,1)S(1)}, bf16[1024,128]{1,0:T(8,128)(2,1)S(1)}, bf16[1024,128]{1,0:T(8,128)(2,1)S(1)}, bf16[1024,128]{1,0:T(8,128)(2,1)S(1)}) custom-call(s32[2]{0:T(128)S(1)} %pad_add_fusion.refs_0_, bf16[32,128,128]{2,1,0:T(8,128)(2,1)S(1)} %get-tuple-element.88.refs_1_, ...), custom_call_target="tpu_custom_call" | custom-call | flops 134217728 | bytes 3145736 | tf_op jit(solution)/shard_map/pallas_call | solution.py:304
  95.7 1.6 collective-permute-start.47
  97.2 2.8 %collective-permute-done.29.refs_4_ = bf16[1024,128]{1,0:T(8,128)(2,1)S(1)} collective-permute-done((bf16[1024,128]{1,0:T(8,128)(2,1)S(1)}, bf16[1024,128]{1,0:T(8,128)(2,1)S(1)}, u32[]{:S(2)}, u32[]{:S(2)}) %collective-permute-start.29) | collective-permute-done | bytes 262176 | tf_op jit(solution)/shard_map/ppermute | solution.py:29
  100.5 4.3 %collective-permute-done.30.refs_5_ = bf16[1024,128]{1,0:T(8,128)(2,1)S(1)} collective-permute-done((bf16[1024,128]{1,0:T(8,128)(2,1)S(1)}, bf16[1024,128]{1,0:T(8,128)(2,1)S(1)}, u32[]{:S(2)}, u32[]{:S(2)}) %collective-permute-start.30) | collective-permute-done | bytes 262176 | tf_op jit(solution)/shard_map/ppermute | solution.py:29
  104.8 2.7 %shard_map.112 = (bf16[32,128,128]{2,1,0:T(8,128)(2,1)}, bf16[32,128,128]{2,1,0:T(8,128)(2,1)S(1)}, bf16[1024,128]{1,0:T(8,128)(2,1)S(1)}, bf16[1024,128]{1,0:T(...) custom-call(s32[2]{0:T(128)S(1)} %pad_add_fusion.refs_0_, ...), custom_call_target="tpu_custom_call" | custom-call | flops 134217728 | bytes 5242888 | tf_op jit(solution)/shard_map/pallas_call | solution.py:304
  109.7 1.6 collective-permute-start.32
  112.8 3.3 %collective-permute-done.48.refs_5_ = bf16[1024,128]{1,0:T(8,128)(2,1)S(1)} collective-permute-done((bf16[1024,128]{1,0:T(8,128)(2,1)S(1)}, bf16[1024,128]{1,0:T(8,128)(2,1)S(1)}, u32[]{:S(2)}, u32[]{:S(2)}) %collective-permute-start.48) | collective-permute-done | bytes 262176 | tf_op jit(solution)/shard_map/ppermute | solution.py:29
  116.1 2.5 %collective-permute-start.43 = (bf16[512,128]{1,0:T(8,128)(2,1)S(1)}, bf16[512,128]{1,0:T(8,128)(2,1)S(1)}, u32[]{:S(2)}, u32[]{:S(2)}) collective-permute-start(bf16[512,128]{1,0:T(8,128)(2,1)S(1)} %get-tuple-element.106), channel_id=1, source_target_pairs={{0,16},{4,20},{8,24},{12,28},{16,0},{20,4},{24,8},{28,12},{1,17},{... | collective-permute-start | bytes 393224 | tf_op jit(solution)/shard_map/ppermute | solution.py:29
  118.6 1.9 %collective-permute-start.45 = (bf16[512,128]{1,0:T(8,128)(2,1)S(1)}, bf16[512,128]{1,0:T(8,128)(2,1)S(1)}, u32[]{:S(2)}, u32[]{:S(2)}) collective-permute-start(bf16[512,128]{1,0:T(8,128)(2,1)S(1)} %get-tuple-element.107), channel_id=1, source_target_pairs={{0,24},{4,28},{8,16},{12,20},{16,8},{20,12},{24,0},{28,4},{1,25},{... | collective-permute-start | bytes 393224 | tf_op jit(solution)/shard_map/ppermute | solution.py:29
  120.5 2.0 %collective-permute-done.32.refs_4_ = bf16[1024,128]{1,0:T(8,128)(2,1)S(1)} collective-permute-done((bf16[1024,128]{1,0:T(8,128)(2,1)S(1)}, bf16[1024,128]{1,0:T(8,128)(2,1)S(1)}, u32[]{:S(2)}, u32[]{:S(2)}) %collective-permute-start.32) | collective-permute-done | bytes 262176 | tf_op jit(solution)/shard_map/ppermute | solution.py:29
  122.5 2.0 %collective-permute-start.44 = (bf16[512,128]{1,0:T(8,128)(2,1)S(1)}, bf16[512,128]{1,0:T(8,128)(2,1)S(1)}, u32[]{:S(2)}, u32[]{:S(2)}) collective-permute-start(bf16[512,128]{1,0:T(8,128)(2,1)S(1)} %get-tuple-element.108), channel_id=1, source_target_pairs={{0,8},{4,12},{8,0},{12,4},{16,24},{20,28},{24,16},{28,20},{1,9},{5... | collective-permute-start | bytes 393224 | tf_op jit(solution)/shard_map/ppermute | solution.py:29
  124.5 1.6 shard_map.118
  128.5 1.6 shard_map.113
  130.1 1.8 %shard_map.114 = bf16[128,4096]{1,0:T(8,128)(2,1)} custom-call(bf16[32,128,128]{2,1,0:T(8,128)(2,1)S(1)} %get-tuple-element.51.refs_0_, bf16[32,128,128]{2,1,0:T(8,128)(2,1)S(1)} %get-tuple-element.76.refs_1_), custom_call_target="tpu_custom_call" | custom-call | flops 134217728 | bytes 3145728 | tf_op jit(solution)/shard_map/pallas_call | solution.py:304
  133.7 2.6 %collective-permute-start.39 = (bf16[512,128]{1,0:T(8,128)(2,1)S(1)}, bf16[512,128]{1,0:T(8,128)(2,1)S(1)}, u32[]{:S(2)}, u32[]{:S(2)}) collective-permute-start(bf16[512,128]{1,0:T(8,128)(2,1)S(1)} %get-tuple-element.109), channel_id=1, source_target_pairs={{0,16},{4,20},{8,24},{12,28},{16,0},{20,4},{24,8},{28,12},{1,17},{... | collective-permute-start | bytes 393224 | tf_op jit(solution)/shard_map/ppermute | solution.py:29
  136.2 1.9 %collective-permute-start.41 = (bf16[512,128]{1,0:T(8,128)(2,1)S(1)}, bf16[512,128]{1,0:T(8,128)(2,1)S(1)}, u32[]{:S(2)}, u32[]{:S(2)}) collective-permute-start(bf16[512,128]{1,0:T(8,128)(2,1)S(1)} %get-tuple-element.110), channel_id=1, source_target_pairs={{0,24},{4,28},{8,16},{12,20},{16,8},{20,12},{24,0},{28,4},{1,25},{... | collective-permute-start | bytes 393224 | tf_op jit(solution)/shard_map/ppermute | solution.py:29
  138.2 3.9 %collective-permute-done.49 = bf16[4,512,128]{2,1,0:T(8,128)(2,1)S(1)} collective-permute-done((bf16[4,512,128]{2,1,0:T(8,128)(2,1)S(1)}, bf16[4,512,128]{2,1,0:T(8,128)(2,1)S(1)}, u32[]{:S(2)}, u32[]{:S(2)}) %collective-permute-start.49) | collective-permute-done | bytes 524320 | tf_op jit(solution)/shard_map/ppermute | solution.py:29
  142.2 2.6 %collective-permute-start.50 = (bf16[512,128]{1,0:T(8,128)(2,1)S(1)}, bf16[512,128]{1,0:T(8,128)(2,1)S(1)}, u32[]{:S(2)}, u32[]{:S(2)}) collective-permute-start(bf16[512,128]{1,0:T(8,128)(2,1)S(1)} %get-tuple-element.103), channel_id=1, source_target_pairs={{0,16},{4,20},{8,24},{12,28},{16,0},{20,4},{24,8},{28,12},{1,17},{... | collective-permute-start | bytes 393224 | tf_op jit(solution)/shard_map/ppermute | solution.py:29
  144.8 2.0 %collective-permute-done.39 = bf16[512,128]{1,0:T(8,128)(2,1)S(1)} collective-permute-done((bf16[512,128]{1,0:T(8,128)(2,1)S(1)}, bf16[512,128]{1,0:T(8,128)(2,1)S(1)}, u32[]{:S(2)}, u32[]{:S(2)}) %collective-permute-start.39) | collective-permute-done | bytes 131104 | tf_op jit(solution)/shard_map/ppermute | solution.py:29
  148.2 7.5 %collective-permute-start.51 = (bf16[512,128]{1,0:T(8,128)(2,1)S(1)}, bf16[512,128]{1,0:T(8,128)(2,1)S(1)}, u32[]{:S(2)}, u32[]{:S(2)}) collective-permute-start(bf16[512,128]{1,0:T(8,128)(2,1)S(1)} %get-tuple-element.105), channel_id=1, source_target_pairs={{0,8},{4,12},{8,0},{12,4},{16,24},{20,28},{24,16},{28,20},{1,9},{5... | collective-permute-start | bytes 393224 | tf_op jit(solution)/shard_map/ppermute | solution.py:29
  156.7 2.4 %collective-permute-start.37 = (bf16[512,128]{1,0:T(8,128)(2,1)S(1)}, bf16[512,128]{1,0:T(8,128)(2,1)S(1)}, u32[]{:S(2)}, u32[]{:S(2)}) collective-permute-start(bf16[512,128]{1,0:T(8,128)(2,1)S(1)} %get-tuple-element.113), channel_id=1, source_target_pairs={{0,24},{4,28},{8,16},{12,20},{16,8},{20,12},{24,0},{28,4},{1,25},{... | collective-permute-start | bytes 393224 | tf_op jit(solution)/shard_map/ppermute | solution.py:29
  161.0 8.2 %collective-permute-done.35 = bf16[512,128]{1,0:T(8,128)(2,1)S(1)} collective-permute-done((bf16[512,128]{1,0:T(8,128)(2,1)S(1)}, bf16[512,128]{1,0:T(8,128)(2,1)S(1)}, u32[]{:S(2)}, u32[]{:S(2)}) %collective-permute-start.35) | collective-permute-done | bytes 131104 | tf_op jit(solution)/shard_map/ppermute | solution.py:29
  (101 shorter events, 28.6 us)
Async XLA Ops:
  0.6 11.3 %collective-permute-start.8 = (bf16[1,32,16,128]{3,2,1,0:T(8,128)(2,1)}, bf16[1,32,16,128]{3,2,1,0:T(8,128)(2,1)S(1)}, u32[]{:S(2)}, u32[]{:S(2)}) collective-permute-start(bf16[1,32,16,128]{3,2,1,0:T(8,128)(2,1)} %bitcast.80), channel_id=1, source_target_pairs={{0,4},{4,0},{8,12},{12,8},{16,20},{20,16},{24,28},{28,24},{1,5},{5... | collective-permute-start | bytes 393224 | tf_op jit(solution)/shard_map/ppermute | solution.py:29
  3.6 11.2 %collective-permute-start.2 = (bf16[1,32,16,128]{3,2,1,0:T(8,128)(2,1)}, bf16[1,32,16,128]{3,2,1,0:T(8,128)(2,1)S(1)}, u32[]{:S(2)}, u32[]{:S(2)}) collective-permute-start(bf16[1,32,16,128]{3,2,1,0:T(8,128)(2,1)} %bitcast.76), channel_id=1, source_target_pairs={{0,16},{4,20},{8,24},{12,28},{16,0},{20,4},{24,8},{28,12},{1,17},{... | collective-permute-start | bytes 393224 | tf_op jit(solution)/shard_map/ppermute | solution.py:29
  6.2 9.9 %collective-permute-start.1 = (bf16[1,32,16,128]{3,2,1,0:T(8,128)(2,1)}, bf16[1,32,16,128]{3,2,1,0:T(8,128)(2,1)S(1)}, u32[]{:S(2)}, u32[]{:S(2)}) collective-permute-start(bf16[1,32,16,128]{3,2,1,0:T(8,128)(2,1)} %bitcast.77), channel_id=1, source_target_pairs={{0,8},{4,12},{8,0},{12,4},{16,24},{20,28},{24,16},{28,20},{1,9},{5... | collective-permute-start | bytes 393224 | tf_op jit(solution)/shard_map/ppermute | solution.py:29
  7.8 9.8 %collective-permute-start = (bf16[1,32,16,128]{3,2,1,0:T(8,128)(2,1)}, bf16[1,32,16,128]{3,2,1,0:T(8,128)(2,1)S(1)}, u32[]{:S(2)}, u32[]{:S(2)}) collective-permute-start(bf16[1,32,16,128]{3,2,1,0:T(8,128)(2,1)} %bitcast.78), channel_id=1, source_target_pairs={{0,4},{4,0},{8,12},{12,8},{16,20},{20,16},{24,28},{28,24},{1,5},{5... | collective-permute-start | bytes 393224 | tf_op jit(solution)/shard_map/ppermute | solution.py:29
  8.3 16.5 %collective-permute-start.14 = (bf16[1,32,16,128]{3,2,1,0:T(8,128)(2,1)}, bf16[1,32,16,128]{3,2,1,0:T(8,128)(2,1)S(1)}, u32[]{:S(2)}, u32[]{:S(2)}) collective-permute-start(bf16[1,32,16,128]{3,2,1,0:T(8,128)(2,1)} %bitcast.84), channel_id=1, source_target_pairs={{0,16},{4,20},{8,24},{12,28},{16,0},{20,4},{24,8},{28,12},{1,17},{... | collective-permute-start | bytes 393224 | tf_op jit(solution)/shard_map/ppermute | solution.py:29
  11.9 18.4 %collective-permute-start.9 = (bf16[2,32,16,128]{3,2,1,0:T(8,128)(2,1)S(1)}, bf16[2,32,16,128]{3,2,1,0:T(8,128)(2,1)S(1)}, u32[]{:S(2)}, u32[]{:S(2)}) collective-permute-start(bf16[2,32,16,128]{3,2,1,0:T(8,128)(2,1)S(1)} %shard_map.103.refs_0_), channel_id=1, source_target_pairs={{0,16},{4,20},{8,24},{12,28},{16,0},{20,4},{24,8},{28,12},{1,17},{... | collective-permute-start | bytes 786440 | tf_op jit(solution)/shard_map/ppermute | solution.py:29
  14.8 10.2 %collective-permute-start.20 = (bf16[1,32,16,128]{3,2,1,0:T(8,128)(2,1)S(1)}, bf16[1,32,16,128]{3,2,1,0:T(8,128)(2,1)S(1)}, u32[]{:S(2)}, u32[]{:S(2)}) collective-permute-start(bf16[1,32,16,128]{3,2,1,0:T(8,128)(2,1)S(1)} %bitcast.82), channel_id=1, source_target_pairs={{0,4},{4,0},{8,12},{12,8},{16,20},{20,16},{24,28},{28,24},{1,5},{5... | collective-permute-start | bytes 393224 | tf_op jit(solution)/shard_map/ppermute | solution.py:29
  16.1 19.6 %collective-permute-start.7 = (bf16[1024,128]{1,0:T(8,128)(2,1)S(1)}, bf16[1024,128]{1,0:T(8,128)(2,1)S(1)}, u32[]{:S(2)}, u32[]{:S(2)}) collective-permute-start(bf16[1024,128]{1,0:T(8,128)(2,1)S(1)} %get-tuple-element.50), channel_id=1, source_target_pairs={{0,2},{1,3},{2,0},{3,1},{4,6},{5,7},{6,4},{7,5},{8,10},{9,11},{10,... | collective-permute-start | bytes 786440 | tf_op jit(solution)/shard_map/ppermute | solution.py:29
  17.6 12.0 %collective-permute-start.5 = (bf16[1,32,16,128]{3,2,1,0:T(8,128)(2,1)S(1)}, bf16[1,32,16,128]{3,2,1,0:T(8,128)(2,1)S(1)}, u32[]{:S(2)}, u32[]{:S(2)}) collective-permute-start(bf16[1,32,16,128]{3,2,1,0:T(8,128)(2,1)S(1)} %collective-permute-done.2.refs_5_), channel_id=1, source_target_pairs={{0,8},{4,12},{8,0},{12,4},{16,24},{20,28},{24,16},{28,20},{1,9},{5... | collective-permute-start | bytes 393224 | tf_op jit(solution)/shard_map/ppermute | solution.py:29
  25.0 10.6 %collective-permute-start.3 = (bf16[1,32,16,128]{3,2,1,0:T(8,128)(2,1)S(1)}, bf16[1,32,16,128]{3,2,1,0:T(8,128)(2,1)S(1)}, u32[]{:S(2)}, u32[]{:S(2)}) collective-permute-start(bf16[1,32,16,128]{3,2,1,0:T(8,128)(2,1)S(1)} %collective-permute-done.1.refs_4_), channel_id=1, source_target_pairs={{0,4},{4,0},{8,12},{12,8},{16,20},{20,16},{24,28},{28,24},{1,5},{5... | collective-permute-start | bytes 393224 | tf_op jit(solution)/shard_map/ppermute | solution.py:29
  30.4 13.0 %collective-permute-start.21 = (bf16[2,32,16,128]{3,2,1,0:T(8,128)(2,1)S(1)}, bf16[2,32,16,128]{3,2,1,0:T(8,128)(2,1)S(1)}, u32[]{:S(2)}, u32[]{:S(2)}) collective-permute-start(bf16[2,32,16,128]{3,2,1,0:T(8,128)(2,1)S(1)} %shard_map.108.refs_0_), channel_id=1, source_target_pairs={{0,16},{4,20},{8,24},{12,28},{16,0},{20,4},{24,8},{28,12},{1,17},{... | collective-permute-start | bytes 786440 | tf_op jit(solution)/shard_map/ppermute | solution.py:29
  33.1 13.4 %collective-permute-start.15 = (bf16[2,32,16,128]{3,2,1,0:T(8,128)(2,1)S(1)}, bf16[2,32,16,128]{3,2,1,0:T(8,128)(2,1)S(1)}, u32[]{:S(2)}, u32[]{:S(2)}) collective-permute-start(bf16[2,32,16,128]{3,2,1,0:T(8,128)(2,1)S(1)} %shard_map.106.refs_0_), channel_id=1, source_target_pairs={{0,8},{4,12},{8,0},{12,4},{16,24},{20,28},{24,16},{28,20},{1,9},{5... | collective-permute-start | bytes 786440 | tf_op jit(solution)/shard_map/ppermute | solution.py:29
  35.6 22.1 %collective-permute-start.10 = (bf16[4,32,16,128]{3,2,1,0:T(8,128)(2,1)S(1)}, bf16[4,32,16,128]{3,2,1,0:T(8,128)(2,1)S(1)}, u32[]{:S(2)}, u32[]{:S(2)}) collective-permute-start(bf16[4,32,16,128]{3,2,1,0:T(8,128)(2,1)S(1)} %shard_map.104.refs_1_), channel_id=1, source_target_pairs={{0,8},{4,12},{8,0},{12,4},{16,24},{20,28},{24,16},{28,20},{1,9},{5... | collective-permute-start | bytes 1572872 | tf_op jit(solution)/shard_map/ppermute | solution.py:29
  38.4 9.4 %collective-permute-start.11 = (bf16[1024,128]{1,0:T(8,128)(2,1)S(1)}, bf16[1024,128]{1,0:T(8,128)(2,1)S(1)}, u32[]{:S(2)}, u32[]{:S(2)}) collective-permute-start(bf16[1024,128]{1,0:T(8,128)(2,1)S(1)} %get-tuple-element.53), channel_id=1, source_target_pairs={{0,1},{1,0},{2,3},{3,2},{4,5},{5,4},{6,7},{7,6},{8,9},{9,8},{10,11... | collective-permute-start | bytes 786440 | tf_op jit(solution)/shard_map/ppermute | solution.py:29
  38.4 11.0 %collective-permute-start.12 = (bf16[1024,128]{1,0:T(8,128)(2,1)S(1)}, bf16[1024,128]{1,0:T(8,128)(2,1)S(1)}, u32[]{:S(2)}, u32[]{:S(2)}) collective-permute-start(bf16[1024,128]{1,0:T(8,128)(2,1)S(1)} %get-tuple-element.54), channel_id=1, source_target_pairs={{0,2},{1,3},{2,0},{3,1},{4,6},{5,7},{6,4},{7,5},{8,10},{9,11},{10,... | collective-permute-start | bytes 786440 | tf_op jit(solution)/shard_map/ppermute | solution.py:29
  46.5 19.6 %collective-permute-start.22 = (bf16[4,32,16,128]{3,2,1,0:T(8,128)(2,1)S(1)}, bf16[4,32,16,128]{3,2,1,0:T(8,128)(2,1)S(1)}, u32[]{:S(2)}, u32[]{:S(2)}) collective-permute-start(bf16[4,32,16,128]{3,2,1,0:T(8,128)(2,1)S(1)} %shard_map.109.refs_1_), channel_id=1, source_target_pairs={{0,8},{4,12},{8,0},{12,4},{16,24},{20,28},{24,16},{28,20},{1,9},{5... | collective-permute-start | bytes 1572872 | tf_op jit(solution)/shard_map/ppermute | solution.py:29
  47.8 20.9 %collective-permute-start.16 = (bf16[4,32,16,128]{3,2,1,0:T(8,128)(2,1)S(1)}, bf16[4,32,16,128]{3,2,1,0:T(8,128)(2,1)S(1)}, u32[]{:S(2)}, u32[]{:S(2)}) collective-permute-start(bf16[4,32,16,128]{3,2,1,0:T(8,128)(2,1)S(1)} %shard_map.107.refs_1_), channel_id=1, source_target_pairs={{0,4},{4,0},{8,12},{12,8},{16,20},{20,16},{24,28},{28,24},{1,5},{5... | collective-permute-start | bytes 1572872 | tf_op jit(solution)/shard_map/ppermute | solution.py:29
  49.4 10.9 %collective-permute-start.23 = (bf16[1024,128]{1,0:T(8,128)(2,1)S(1)}, bf16[1024,128]{1,0:T(8,128)(2,1)S(1)}, u32[]{:S(2)}, u32[]{:S(2)}) collective-permute-start(bf16[1024,128]{1,0:T(8,128)(2,1)S(1)} %get-tuple-element.62), channel_id=1, source_target_pairs={{0,1},{1,0},{2,3},{3,2},{4,5},{5,4},{6,7},{7,6},{8,9},{9,8},{10,11... | collective-permute-start | bytes 786440 | tf_op jit(solution)/shard_map/ppermute | solution.py:29
  52.3 9.6 %collective-permute-start.24 = (bf16[1024,128]{1,0:T(8,128)(2,1)S(1)}, bf16[1024,128]{1,0:T(8,128)(2,1)S(1)}, u32[]{:S(2)}, u32[]{:S(2)}) collective-permute-start(bf16[1024,128]{1,0:T(8,128)(2,1)S(1)} %get-tuple-element.63), channel_id=1, source_target_pairs={{0,3},{1,2},{2,1},{3,0},{4,7},{5,6},{6,5},{7,4},{8,11},{9,10},{10,... | collective-permute-start | bytes 786440 | tf_op jit(solution)/shard_map/ppermute | solution.py:29
  60.3 9.9 %collective-permute-start.17 = (bf16[1024,128]{1,0:T(8,128)(2,1)S(1)}, bf16[1024,128]{1,0:T(8,128)(2,1)S(1)}, u32[]{:S(2)}, u32[]{:S(2)}) collective-permute-start(bf16[1024,128]{1,0:T(8,128)(2,1)S(1)} %get-tuple-element.58), channel_id=1, source_target_pairs={{0,1},{1,0},{2,3},{3,2},{4,5},{5,4},{6,7},{7,6},{8,9},{9,8},{10,11... | collective-permute-start | bytes 786440 | tf_op jit(solution)/shard_map/ppermute | solution.py:29
  60.4 10.2 %collective-permute-start.18 = (bf16[1024,128]{1,0:T(8,128)(2,1)S(1)}, bf16[1024,128]{1,0:T(8,128)(2,1)S(1)}, u32[]{:S(2)}, u32[]{:S(2)}) collective-permute-start(bf16[1024,128]{1,0:T(8,128)(2,1)S(1)} %get-tuple-element.59), channel_id=1, source_target_pairs={{0,2},{1,3},{2,0},{3,1},{4,6},{5,7},{6,4},{7,5},{8,10},{9,11},{10,... | collective-permute-start | bytes 786440 | tf_op jit(solution)/shard_map/ppermute | solution.py:29
  61.9 12.3 %collective-permute-start.19 = (bf16[1024,128]{1,0:T(8,128)(2,1)S(1)}, bf16[1024,128]{1,0:T(8,128)(2,1)S(1)}, u32[]{:S(2)}, u32[]{:S(2)}) collective-permute-start(bf16[1024,128]{1,0:T(8,128)(2,1)S(1)} %get-tuple-element.60), channel_id=1, source_target_pairs={{0,3},{1,2},{2,1},{3,0},{4,7},{5,6},{6,5},{7,4},{8,11},{9,10},{10,... | collective-permute-start | bytes 786440 | tf_op jit(solution)/shard_map/ppermute | solution.py:29
  68.7 12.1 %collective-permute-start.26 = (bf16[1024,128]{1,0:T(8,128)(2,1)S(1)}, bf16[1024,128]{1,0:T(8,128)(2,1)S(1)}, u32[]{:S(2)}, u32[]{:S(2)}) collective-permute-start(bf16[1024,128]{1,0:T(8,128)(2,1)S(1)} %get-tuple-element.66), channel_id=1, source_target_pairs={{0,2},{1,3},{2,0},{3,1},{4,6},{5,7},{6,4},{7,5},{8,10},{9,11},{10,... | collective-permute-start | bytes 786440 | tf_op jit(solution)/shard_map/ppermute | solution.py:29
  70.2 15.3 %collective-permute-start.27 = (bf16[1024,128]{1,0:T(8,128)(2,1)S(1)}, bf16[1024,128]{1,0:T(8,128)(2,1)S(1)}, u32[]{:S(2)}, u32[]{:S(2)}) collective-permute-start(bf16[1024,128]{1,0:T(8,128)(2,1)S(1)} %get-tuple-element.67), channel_id=1, source_target_pairs={{0,3},{1,2},{2,1},{3,0},{4,7},{5,6},{6,5},{7,4},{8,11},{9,10},{10,... | collective-permute-start | bytes 786440 | tf_op jit(solution)/shard_map/ppermute | solution.py:29
  90.0 19.7 %collective-permute-start.42 = (bf16[4,512,128]{2,1,0:T(8,128)(2,1)S(1)}, bf16[4,512,128]{2,1,0:T(8,128)(2,1)S(1)}, u32[]{:S(2)}, u32[]{:S(2)}) collective-permute-start(bf16[4,512,128]{2,1,0:T(8,128)(2,1)S(1)} %get-tuple-element.86), channel_id=1, source_target_pairs={{0,4},{4,0},{8,12},{12,8},{16,20},{20,16},{24,28},{28,24},{1,5},{5... | collective-permute-start | bytes 1572872 | tf_op jit(solution)/shard_map/ppermute | solution.py:29
  90.9 9.1 %collective-permute-start.29 = (bf16[1024,128]{1,0:T(8,128)(2,1)S(1)}, bf16[1024,128]{1,0:T(8,128)(2,1)S(1)}, u32[]{:S(2)}, u32[]{:S(2)}) collective-permute-start(bf16[1024,128]{1,0:T(8,128)(2,1)S(1)} %get-tuple-element.70), channel_id=1, source_target_pairs={{0,2},{1,3},{2,0},{3,1},{4,6},{5,7},{6,4},{7,5},{8,10},{9,11},{10,... | collective-permute-start | bytes 786440 | tf_op jit(solution)/shard_map/ppermute | solution.py:29
  92.5 12.4 %collective-permute-start.30 = (bf16[1024,128]{1,0:T(8,128)(2,1)S(1)}, bf16[1024,128]{1,0:T(8,128)(2,1)S(1)}, u32[]{:S(2)}, u32[]{:S(2)}) collective-permute-start(bf16[1024,128]{1,0:T(8,128)(2,1)S(1)} %get-tuple-element.71), channel_id=1, source_target_pairs={{0,3},{1,2},{2,1},{3,0},{4,7},{5,6},{6,5},{7,4},{8,11},{9,10},{10,... | collective-permute-start | bytes 786440 | tf_op jit(solution)/shard_map/ppermute | solution.py:29
  95.3 16.2 %collective-permute-start.46 = (bf16[1024,128]{1,0:T(8,128)(2,1)S(1)}, bf16[1024,128]{1,0:T(8,128)(2,1)S(1)}, u32[]{:S(2)}, u32[]{:S(2)}) collective-permute-start(bf16[1024,128]{1,0:T(8,128)(2,1)S(1)} %get-tuple-element.90), channel_id=1, source_target_pairs={{0,1},{1,0},{2,3},{3,2},{4,5},{5,4},{6,7},{7,6},{8,9},{9,8},{10,11... | collective-permute-start | bytes 786440 | tf_op jit(solution)/shard_map/ppermute | solution.py:29
  95.7 15.9 %collective-permute-start.47 = (bf16[1024,128]{1,0:T(8,128)(2,1)S(1)}, bf16[1024,128]{1,0:T(8,128)(2,1)S(1)}, u32[]{:S(2)}, u32[]{:S(2)}) collective-permute-start(bf16[1024,128]{1,0:T(8,128)(2,1)S(1)} %get-tuple-element.91), channel_id=1, source_target_pairs={{0,2},{1,3},{2,0},{3,1},{4,6},{5,7},{6,4},{7,5},{8,10},{9,11},{10,... | collective-permute-start | bytes 786440 | tf_op jit(solution)/shard_map/ppermute | solution.py:29
  100.0 16.1 %collective-permute-start.48 = (bf16[1024,128]{1,0:T(8,128)(2,1)S(1)}, bf16[1024,128]{1,0:T(8,128)(2,1)S(1)}, u32[]{:S(2)}, u32[]{:S(2)}) collective-permute-start(bf16[1024,128]{1,0:T(8,128)(2,1)S(1)} %get-tuple-element.92), channel_id=1, source_target_pairs={{0,3},{1,2},{2,1},{3,0},{4,7},{5,6},{6,5},{7,4},{8,11},{9,10},{10,... | collective-permute-start | bytes 786440 | tf_op jit(solution)/shard_map/ppermute | solution.py:29
  107.6 11.0 %collective-permute-start.31 = (bf16[1024,128]{1,0:T(8,128)(2,1)S(1)}, bf16[1024,128]{1,0:T(8,128)(2,1)S(1)}, u32[]{:S(2)}, u32[]{:S(2)}) collective-permute-start(bf16[1024,128]{1,0:T(8,128)(2,1)S(1)} %get-tuple-element.73), channel_id=1, source_target_pairs={{0,1},{1,0},{2,3},{3,2},{4,5},{5,4},{6,7},{7,6},{8,9},{9,8},{10,11... | collective-permute-start | bytes 786440 | tf_op jit(solution)/shard_map/ppermute | solution.py:29
  109.7 12.8 %collective-permute-start.32 = (bf16[1024,128]{1,0:T(8,128)(2,1)S(1)}, bf16[1024,128]{1,0:T(8,128)(2,1)S(1)}, u32[]{:S(2)}, u32[]{:S(2)}) collective-permute-start(bf16[1024,128]{1,0:T(8,128)(2,1)S(1)} %get-tuple-element.74), channel_id=1, source_target_pairs={{0,2},{1,3},{2,0},{3,1},{4,6},{5,7},{6,4},{7,5},{8,10},{9,11},{10,... | collective-permute-start | bytes 786440 | tf_op jit(solution)/shard_map/ppermute | solution.py:29
  111.5 15.8 %collective-permute-start.33 = (bf16[1024,128]{1,0:T(8,128)(2,1)S(1)}, bf16[1024,128]{1,0:T(8,128)(2,1)S(1)}, u32[]{:S(2)}, u32[]{:S(2)}) collective-permute-start(bf16[1024,128]{1,0:T(8,128)(2,1)S(1)} %get-tuple-element.75), channel_id=1, source_target_pairs={{0,3},{1,2},{2,1},{3,0},{4,7},{5,6},{6,5},{7,4},{8,11},{9,10},{10,... | collective-permute-start | bytes 786440 | tf_op jit(solution)/shard_map/ppermute | solution.py:29
  111.6 21.9 %collective-permute-start.38 = (bf16[4,512,128]{2,1,0:T(8,128)(2,1)S(1)}, bf16[4,512,128]{2,1,0:T(8,128)(2,1)S(1)}, u32[]{:S(2)}, u32[]{:S(2)}) collective-permute-start(bf16[4,512,128]{2,1,0:T(8,128)(2,1)S(1)} %get-tuple-element.82), channel_id=1, source_target_pairs={{0,4},{4,0},{8,12},{12,8},{16,20},{20,16},{24,28},{28,24},{1,5},{5... | collective-permute-start | bytes 1572872 | tf_op jit(solution)/shard_map/ppermute | solution.py:29
  116.1 15.8 %collective-permute-start.43 = (bf16[512,128]{1,0:T(8,128)(2,1)S(1)}, bf16[512,128]{1,0:T(8,128)(2,1)S(1)}, u32[]{:S(2)}, u32[]{:S(2)}) collective-permute-start(bf16[512,128]{1,0:T(8,128)(2,1)S(1)} %get-tuple-element.106), channel_id=1, source_target_pairs={{0,16},{4,20},{8,24},{12,28},{16,0},{20,4},{24,8},{28,12},{1,17},{... | collective-permute-start | bytes 393224 | tf_op jit(solution)/shard_map/ppermute | solution.py:29
  118.6 14.2 %collective-permute-start.45 = (bf16[512,128]{1,0:T(8,128)(2,1)S(1)}, bf16[512,128]{1,0:T(8,128)(2,1)S(1)}, u32[]{:S(2)}, u32[]{:S(2)}) collective-permute-start(bf16[512,128]{1,0:T(8,128)(2,1)S(1)} %get-tuple-element.107), channel_id=1, source_target_pairs={{0,24},{4,28},{8,16},{12,20},{16,8},{20,12},{24,0},{28,4},{1,25},{... | collective-permute-start | bytes 393224 | tf_op jit(solution)/shard_map/ppermute | solution.py:29
  122.5 10.3 %collective-permute-start.44 = (bf16[512,128]{1,0:T(8,128)(2,1)S(1)}, bf16[512,128]{1,0:T(8,128)(2,1)S(1)}, u32[]{:S(2)}, u32[]{:S(2)}) collective-permute-start(bf16[512,128]{1,0:T(8,128)(2,1)S(1)} %get-tuple-element.108), channel_id=1, source_target_pairs={{0,8},{4,12},{8,0},{12,4},{16,24},{20,28},{24,16},{28,20},{1,9},{5... | collective-permute-start | bytes 393224 | tf_op jit(solution)/shard_map/ppermute | solution.py:29
  127.3 14.7 %collective-permute-start.49 = (bf16[4,512,128]{2,1,0:T(8,128)(2,1)S(1)}, bf16[4,512,128]{2,1,0:T(8,128)(2,1)S(1)}, u32[]{:S(2)}, u32[]{:S(2)}) collective-permute-start(bf16[4,512,128]{2,1,0:T(8,128)(2,1)S(1)} %get-tuple-element.94), channel_id=1, source_target_pairs={{0,4},{4,0},{8,12},{12,8},{16,20},{20,16},{24,28},{28,24},{1,5},{5... | collective-permute-start | bytes 1572872 | tf_op jit(solution)/shard_map/ppermute | solution.py:29
  131.9 24.5 %collective-permute-start.34 = (bf16[4,512,128]{2,1,0:T(8,128)(2,1)S(1)}, bf16[4,512,128]{2,1,0:T(8,128)(2,1)S(1)}, u32[]{:S(2)}, u32[]{:S(2)}) collective-permute-start(bf16[4,512,128]{2,1,0:T(8,128)(2,1)S(1)} %get-tuple-element.78), channel_id=1, source_target_pairs={{0,4},{4,0},{8,12},{12,8},{16,20},{20,16},{24,28},{28,24},{1,5},{5... | collective-permute-start | bytes 1572872 | tf_op jit(solution)/shard_map/ppermute | solution.py:29
  133.7 13.0 %collective-permute-start.39 = (bf16[512,128]{1,0:T(8,128)(2,1)S(1)}, bf16[512,128]{1,0:T(8,128)(2,1)S(1)}, u32[]{:S(2)}, u32[]{:S(2)}) collective-permute-start(bf16[512,128]{1,0:T(8,128)(2,1)S(1)} %get-tuple-element.109), channel_id=1, source_target_pairs={{0,16},{4,20},{8,24},{12,28},{16,0},{20,4},{24,8},{28,12},{1,17},{... | collective-permute-start | bytes 393224 | tf_op jit(solution)/shard_map/ppermute | solution.py:29
  136.2 11.9 %collective-permute-start.41 = (bf16[512,128]{1,0:T(8,128)(2,1)S(1)}, bf16[512,128]{1,0:T(8,128)(2,1)S(1)}, u32[]{:S(2)}, u32[]{:S(2)}) collective-permute-start(bf16[512,128]{1,0:T(8,128)(2,1)S(1)} %get-tuple-element.110), channel_id=1, source_target_pairs={{0,24},{4,28},{8,16},{12,20},{16,8},{20,12},{24,0},{28,4},{1,25},{... | collective-permute-start | bytes 393224 | tf_op jit(solution)/shard_map/ppermute | solution.py:29
  138.2 17.5 %collective-permute-start.40 = (bf16[512,128]{1,0:T(8,128)(2,1)S(1)}, bf16[512,128]{1,0:T(8,128)(2,1)S(1)}, u32[]{:S(2)}, u32[]{:S(2)}) collective-permute-start(bf16[512,128]{1,0:T(8,128)(2,1)S(1)} %get-tuple-element.111), channel_id=1, source_target_pairs={{0,8},{4,12},{8,0},{12,4},{16,24},{20,28},{24,16},{28,20},{1,9},{5... | collective-permute-start | bytes 393224 | tf_op jit(solution)/shard_map/ppermute | solution.py:29
  142.2 16.9 %collective-permute-start.50 = (bf16[512,128]{1,0:T(8,128)(2,1)S(1)}, bf16[512,128]{1,0:T(8,128)(2,1)S(1)}, u32[]{:S(2)}, u32[]{:S(2)}) collective-permute-start(bf16[512,128]{1,0:T(8,128)(2,1)S(1)} %get-tuple-element.103), channel_id=1, source_target_pairs={{0,16},{4,20},{8,24},{12,28},{16,0},{20,4},{24,8},{28,12},{1,17},{... | collective-permute-start | bytes 393224 | tf_op jit(solution)/shard_map/ppermute | solution.py:29
  146.7 13.5 %collective-permute-start.52 = (bf16[512,128]{1,0:T(8,128)(2,1)S(1)}, bf16[512,128]{1,0:T(8,128)(2,1)S(1)}, u32[]{:S(2)}, u32[]{:S(2)}) collective-permute-start(bf16[512,128]{1,0:T(8,128)(2,1)S(1)} %get-tuple-element.104), channel_id=1, source_target_pairs={{0,24},{4,28},{8,16},{12,20},{16,8},{20,12},{24,0},{28,4},{1,25},{... | collective-permute-start | bytes 393224 | tf_op jit(solution)/shard_map/ppermute | solution.py:29
  148.2 12.0 %collective-permute-start.51 = (bf16[512,128]{1,0:T(8,128)(2,1)S(1)}, bf16[512,128]{1,0:T(8,128)(2,1)S(1)}, u32[]{:S(2)}, u32[]{:S(2)}) collective-permute-start(bf16[512,128]{1,0:T(8,128)(2,1)S(1)} %get-tuple-element.105), channel_id=1, source_target_pairs={{0,8},{4,12},{8,0},{12,4},{16,24},{20,28},{24,16},{28,20},{1,9},{5... | collective-permute-start | bytes 393224 | tf_op jit(solution)/shard_map/ppermute | solution.py:29
  156.6 12.5 %collective-permute-start.35 = (bf16[512,128]{1,0:T(8,128)(2,1)S(1)}, bf16[512,128]{1,0:T(8,128)(2,1)S(1)}, u32[]{:S(2)}, u32[]{:S(2)}) collective-permute-start(bf16[512,128]{1,0:T(8,128)(2,1)S(1)} %get-tuple-element.112), channel_id=1, source_target_pairs={{0,16},{4,20},{8,24},{12,28},{16,0},{20,4},{24,8},{28,12},{1,17},{... | collective-permute-start | bytes 393224 | tf_op jit(solution)/shard_map/ppermute | solution.py:29
  156.7 12.5 %collective-permute-start.37 = (bf16[512,128]{1,0:T(8,128)(2,1)S(1)}, bf16[512,128]{1,0:T(8,128)(2,1)S(1)}, u32[]{:S(2)}, u32[]{:S(2)}) collective-permute-start(bf16[512,128]{1,0:T(8,128)(2,1)S(1)} %get-tuple-element.113), channel_id=1, source_target_pairs={{0,24},{4,28},{8,16},{12,20},{16,8},{20,12},{24,0},{28,4},{1,25},{... | collective-permute-start | bytes 393224 | tf_op jit(solution)/shard_map/ppermute | solution.py:29
  159.1 10.1 %collective-permute-start.36 = (bf16[512,128]{1,0:T(8,128)(2,1)S(1)}, bf16[512,128]{1,0:T(8,128)(2,1)S(1)}, u32[]{:S(2)}, u32[]{:S(2)}) collective-permute-start(bf16[512,128]{1,0:T(8,128)(2,1)S(1)} %get-tuple-element.114), channel_id=1, source_target_pairs={{0,8},{4,12},{8,0},{12,4},{16,24},{20,28},{24,16},{28,20},{1,9},{5... | collective-permute-start | bytes 393224 | tf_op jit(solution)/shard_map/ppermute | solution.py:29
  (11 other events, 79.0 us)

commit v5 on v4

--- a/solution.py
+++ b/solution.py
@@ -12,7 +12,7 @@
 inv_root_tau = 0.3989422804014327
 lane_tile = 128
 packed_rows = 16
-CFG = {'flops': 2, 'near': (True, True, False), 'scatters': {'first': 'direct', 'inner': 'direct', 'outer': 'direct', 'second': 'direct'}, 'A1': 0, 'A2': 0, 'A3': 0, 'A4': 0, 'A5': 0, 'A6': 0, 'A7': 1, 'B1': 0, 'B2': 0, 'B3': 0, 'B4': 0, 'B5': 0, 'B6': 0, 'B7': 0, 'C1': 0, 'C2': 0, 'C3': 0, 'C4': 0, 'T1': 0, 'T2': 0, 'T3': 0, 'T4': 0, 'T5': 0, 'T6': 0, 'Q1': 0, 'Q2': 0, 'Q3': 0, 'Q4': 0, 'Q5': 0, 'Q6': 0}
+CFG = {'flops': 2, 'near': (True, True, False), 'scatters': {'first': 'direct', 'inner': 'direct', 'outer': 'direct', 'second': 'direct'}, 'A1': 0, 'A2': 0, 'A3': 0, 'A4': 0, 'A5': 0, 'A6': 0, 'A7': 1, 'B1': 0, 'B2': 0, 'B3': 0, 'B4': 0, 'B5': 0, 'B6': 0, 'B7': 0, 'C1': 0, 'C2': 0, 'C3': 0, 'C4': 0, 'T1': 0, 'T2': 0, 'T3': 0, 'T4': 0, 'T5': 1, 'T6': 0, 'Q1': 0, 'Q2': 0, 'Q3': 1, 'Q4': 0, 'Q5': 0, 'Q6': 0, 'Q7': 0, 'Q8': 0, 'Q9': 0, 'A8': 0, 'A9': 0, 'B8': 0, 'B9': 0, 'D1': 0, 'D2': 0, 'E1': 0, 'E2': 0, 'E3': 0, 'E4': 0, 'T8': 0, 'T9': 0, 'T10': 0, 'T11': 0, 'T12': 0, 'T13': 0, 'T14': 0, 'T15': 0, 'T16': 0, 'BA': 0, 'BC': 0, 'S': 0, 'S1': 0, 'S2': 0, 'S3': 0, 'S4': 0, 'S5': 0, 'pair': 0}
 vmem_bytes = 14 * 1024 * 1024
 
 
@@ -87,9 +87,9 @@
         self.steps.insert(0 if near else len(self.steps), 1)
         self.offsets, self.held = (0,), shard[None]
         self.arrived = None
-        if shard.shape[1] % packed_rows:
+        if shard.shape[-2] % packed_rows:
             self.steps = []
-            self.held = lax.all_gather(shard, "dp", axis=1, tiled=True)[None]
+            self.held = lax.all_gather(shard, "dp", axis=shard.ndim - 2, tiled=True)[None]
 
     def step(self, *others):
         if not self.steps:
@@ -125,6 +125,21 @@
             self.sent, self.kept = self.held[half:].astype(jnp.bfloat16), self.held[:half]
         self.held = self.kept + hop(wait_for(self.sent, *others), "dp", step).astype(jnp.float32)
         return self.held
+
+    def send(self, *others):
+        size = self.held.shape[0]
+        bits = list(reversed(self.steps))
+        self.total = self.held[0]
+        self.pieces = []
+        for q in range(1, size):
+            part = wait_for(self.held[q].astype(jnp.bfloat16), *others)
+            self.pieces.append(hop(part, "dp", sum(bit for k, bit in enumerate(bits) if q >> k & 1)))
+        return self.pieces
+
+    def collect(self, scale, *others):
+        body = functools.partial(total_kernel, scale)
+        (out,) = run(body, [shaped(jnp.float32, *self.total.shape)], [], [self.total, *self.pieces], 0, others)
+        return out
 
     def finish(self, *others):
         if not self.direct:
@@ -166,13 +181,14 @@
     )
 
 
-def place(full, pieces, layout, me):
+def place(full, pieces, layout, me, which):
     local, block, width = full.shape
     rows = block // sum(len(offsets) for offsets in layout)
     for piece, offsets in zip(pieces, layout, strict=True):
         for k, offset in enumerate(offsets):
             start = 0 if rows == block else pl.multiple_of((me ^ offset) * rows, rows)
-            full[:, pl.ds(start, rows), :] = piece[k].reshape(local, rows, width)
+            part = piece[k] if which is None else piece[k, which]
+            full[:, pl.ds(start, rows), :] = part.reshape(local, rows, width)
 
 
 def place_arrived(full, pieces, me):
@@ -219,32 +235,41 @@
     spread(mixed, sends, ids[1])
 
 
-def first_kernel(z, layout, ids, tokens, *refs):
+def first_kernel(z, layout, which, ids, tokens, *refs):
     pieces, refs = refs[: len(layout)], refs[len(layout) :]
     full, sends, mixed = refs[0], refs[1 : 1 + z.mp], refs[1 + z.mp]
-    place(full, pieces, layout, ids[0])
+    place(full, pieces, layout, ids[0], which)
     for c in range(z.local):
         part = tokens[:, c * z.block : (c + 1) * z.block]
         column(mixed, c, z.local, matmul(full[c], part, 0, 1))
     spread(mixed, sends, ids[1])
 
 
-def middle_kernel(z, layout, side, ids, *refs):
+def middle_kernel(z, layout, which, side, ids, *refs):
     pieces, refs = refs[: len(layout)], refs[len(layout) :]
     arrived, refs = refs[: z.mp], refs[z.mp :]
     full, columns, sends, mixed = refs[0], refs[1], refs[2 : 2 + z.mp], refs[2 + z.mp]
-    place(full, pieces, layout, ids[0])
+    place(full, pieces, layout, ids[0], which)
     place_arrived(columns, arrived, ids[1])
     for c in range(z.local):
         column(mixed, c, z.local, matmul(full[c], columns[c], side, 0))
     spread(mixed, sends, ids[1])
 
 
-def gelu_kernel(z, layout, ids, *refs):
+def back_kernel(z, ids, full, *refs):
+    arrived, refs = refs[: z.mp], refs[z.mp :]
+    columns, sends, mixed = refs[0], refs[1 : 1 + z.mp], refs[1 + z.mp]
+    place_arrived(columns, arrived, ids[1])
+    for c in range(z.local):
+        column(mixed, c, z.local, matmul(full[c], columns[c], 1, 0))
+    spread(mixed, sends, ids[1])
+
+
+def gelu_kernel(z, layout, which, ids, *refs):
     pieces, refs = refs[: len(layout)], refs[len(layout) :]
     preact, backs, refs = refs[: z.mp], refs[z.mp : 2 * z.mp], refs[2 * z.mp :]
     full, hidden, back, sends, mixed = refs[0], refs[1], refs[2], refs[3 : 3 + z.mp], refs[3 + z.mp]
-    place(full, pieces, layout, ids[0])
+    place(full, pieces, layout, ids[0], which)
     place_arrived(hidden, preact, ids[1])
     place_arrived(back, backs, ids[1])
     for c in range(z.local):
@@ -281,6 +306,14 @@
         turned[c] = block
         sums[c] = matmul(tokens[:, c * z.block : (c + 1) * z.block], block, 0, 0)
     split_grad(sums, sent, kept, ids[0], steps)
+
+
+def total_kernel(scale, held, *refs):
+    pieces, out = refs[:-1], refs[-1]
+    total = held[...]
+    for piece in pieces:
+        total += piece[...].astype(jnp.float32)
+    out[...] = total * scale
 
 
 def tokens_kernel(z, full, turned, out):
@@ -338,7 +371,12 @@
 
     near = CFG["near"]
     first, inner = Pieces(right_one), Joined(left_one, near[0])
-    outer, second = Joined(left_two, near[1]), Joined(right_two, near[2])
+    which = dict(outer=None, second=None)
+    if CFG["pair"]:
+        outer = second = Joined(jnp.stack([left_two, right_two]), near[1])
+        which = dict(outer=0, second=1)
+    else:
+        outer, second = Joined(left_two, near[1]), Joined(right_two, near[2])
 
     wave0 = first.wave()
     i0 = inner.step()
@@ -346,26 +384,26 @@
     upstream = exchange(turned_up)
     wave1 = first.wave()
     o0 = outer.step() if near[1] else outer.step(*on("A1", *wave0[:1]))
-    i1 = inner.step(*on("A2", turned_up[1]))
-    s0 = second.step(*on("A3", *wave0[:1])) if not near[2] else second.step()
+    s0 = [] if CFG["pair"] else second.step(*on("A3", *wave0[:1])) if not near[2] else second.step()
+    i1 = inner.step(*on("A2", turned_up[1]), *on("D1", *s0), *on("D2", *o0))
     wave2 = first.wave()
     first_layout, first_pieces = first.finish()
     right_first, *parts = run(
-        part(first_kernel, z, first_layout),
+        part(first_kernel, z, first_layout, None),
         [weight] + sends,
         [mixed],
         [ids, tokens, *first_pieces],
         products,
-        [*on("A4", *s0), *on("A5", *i1), *on("A6", *o0), *on("A7", *upstream[2:3])],
+        [*on("A4", *s0), *on("A5", *i1), *on("A6", *o0), *on("A7", *upstream[2:3]), *on("A8", *upstream[3:4]), *on("A9", *upstream[1:2])],
     )
     k1 = parts[1]
     first_columns = exchange(parts)
-    i2 = inner.step(*on("B1", *wave2))
-    o1 = outer.step(*on("B2", k1), *on("B3", first_columns[1]))
-    s1 = second.step(*on("B4", k1), *on("B5", first_columns[1]))
+    i2 = inner.step(*on("B1", *wave2), *on("BC", k1))
+    o1 = outer.step(*on("B2", k1), *on("B3", first_columns[1]), *on("BA", first_columns[2]))
+    s1 = [] if CFG["pair"] else second.step(*on("B4", k1), *on("B5", first_columns[1]), *on("B8", first_columns[2]), *on("B9", *i2))
     inner_layout, inner_pieces = inner.finish()
     left_first, columns, *parts = run(
-        part(middle_kernel, z, inner_layout, 0),
+        part(middle_kernel, z, inner_layout, None, 0),
         [weight, acts] + sends,
         [mixed],
         [ids, *inner_pieces, *first_columns],
@@ -374,21 +412,21 @@
     )
     k3 = parts[1]
     preact = exchange(parts)
-    outer.step(*on("C1", k3))
-    second.step(*on("C2", k3))
+    outer.step(*on("C1", k3), *on("E3", preact[1]))
+    [] if CFG["pair"] else second.step(*on("C2", k3), *on("E1", preact[1]), *on("E2", preact[2]))
     outer_layout, outer_pieces = outer.finish()
     second_layout, second_pieces = second.finish()
     _, upstream_columns, *parts = run(
-        part(middle_kernel, z, outer_layout, 1),
+        part(middle_kernel, z, outer_layout, which["outer"], 1),
         [weight, acts] + sends,
         [mixed],
         [ids, *outer_pieces, *upstream],
         products,
-        [*on("C3", k3), *on("C4", preact[1])],
+        [*on("C3", k3), *on("C4", preact[1]), *on("E4", preact[2])],
     )
     second_rows = exchange(parts)
     right_second, hidden, second_back, *parts = run(
-        part(gelu_kernel, z, second_layout),
+        part(gelu_kernel, z, second_layout, which["second"]),
         [weight, acts, acts] + sends,
         [mixed],
         [ids, *second_pieces, *preact, *second_rows],
@@ -401,7 +439,7 @@
         [mixed],
         [ids, right_second, hidden],
         products,
-        [*on("T1", first_upstream[1])],
+        [*on("T1", first_upstream[1]), *on("T14", first_upstream[2])],
     )
     second_columns = exchange(parts)
     right_two_halves = run(
@@ -410,21 +448,29 @@
         [sums],
         [ids, hidden, second_back],
         products,
-        [*on("T2", first_upstream[1]), *on("T3", second_columns[1])],
+        [*on("T2", first_upstream[1]), *on("T3", second_columns[1]), *on("T15", first_upstream[2])],
     )
     scatter = {"second": Scatter(right_two_halves, orders["second"], CFG["scatters"]["second"] == "direct")}
     scatter["second"].step()
-    _, upstream_rows, *parts = run(
-        part(middle_kernel, z, ((0,),), 1),
-        [weight, acts] + sends,
+    upstream_rows, *parts = run(
+        part(back_kernel, z),
+        [acts] + sends,
         [mixed],
-        [ids, left_first[None], *first_upstream],
-        products,
-        [*on("T4", *right_two_halves[:1])],
-    )
-    left_one_halves = run(part(grad_kernel, z, orders["inner"]), halves, [sums], [ids, columns, upstream_rows], products)
-    parts[1] = wait_for(parts[1], *on("T5", left_one_halves[0]))
+        [ids, left_first, *first_upstream],
+        products,
+        [*on("T4", *right_two_halves[:1]), *on("T16", parts[1])],
+    )
+    def left_one(after):
+        return run(
+            part(grad_kernel, z, orders["inner"]), halves, [sums], [ids, columns, upstream_rows], products, after
+        )
+
+    if CFG["T5"]:
+        left_one_halves = left_one([])
+        parts[1] = wait_for(parts[1], left_one_halves[0])
     first_rows = exchange(parts)
+    if not CFG["T5"]:
+        left_one_halves = left_one([*on("T8", first_rows[1]), *on("T11", first_rows[2])])
     scatter["inner"] = Scatter(left_one_halves, orders["inner"], CFG["scatters"]["inner"] == "direct")
     scatter["inner"].step()
     left_two_halves = run(
@@ -433,34 +479,48 @@
         [held, sums],
         [ids, upstream_columns, *second_columns],
         products,
-        [*on("T6", first_rows[1])],
+        [*on("T6", first_rows[1]), *on("T9", first_rows[2]), *on("T12", first_rows[3])],
     )
     scatter["outer"] = Scatter(left_two_halves, orders["outer"], CFG["scatters"]["outer"] == "direct")
     o_held = scatter["outer"].step()
-    totals = {"second": scatter["second"].finish()}
+    totals = {}
+    r_pieces = []
+    if CFG["S"]:
+        r_pieces = scatter["second"].send(*on("T10", first_rows[2]), *on("T13", first_rows[3]))
+    else:
+        totals["second"] = scatter["second"].finish(*on("T10", first_rows[2]), *on("T13", first_rows[3])) * scale
     turned, *right_one_halves = run(
         part(last_grad_kernel, z, orders["first"]),
         [shaped(bf16, z.local, z.tokens, z.block)] + halves,
         [held, sums],
         [ids, tokens, *first_rows],
         products,
-        [*on("Q1", totals["second"]), *on("Q2", left_two_halves[0]), *on("Q3", scatter["inner"].held)],
+        [*(on("Q1", totals["second"]) if not CFG["S"] else on("Q1", r_pieces[0])), *on("Q2", left_two_halves[0]), *on("Q3", scatter["inner"].held), *on("Q8", scatter["outer"].held)],
     )
     scatter["first"] = Scatter(right_one_halves, orders["first"], CFG["scatters"]["first"] == "direct")
     f_held = scatter["first"].step()
-    totals["inner"] = scatter["inner"].finish()
-    totals["first"] = scatter["first"].finish(*on("Q4", totals["inner"]), *on("Q5", o_held))
-    totals["outer"] = scatter["outer"].finish()
+    if CFG["S"]:
+        totals["second"] = scatter["second"].collect(scale, *on("S1", f_held))
+        scatter["inner"].send()
+        scatter["outer"].send(*on("S3", f_held))
+        f_pieces = scatter["first"].send()
+        totals["inner"] = scatter["inner"].collect(scale, *on("S2", f_held), *on("S4", f_pieces[0]))
+        totals["outer"] = scatter["outer"].collect(scale, *on("S5", f_pieces[0]))
+        totals["first"] = scatter["first"].collect(scale)
+    else:
+        totals["inner"] = scatter["inner"].finish() * scale
+        totals["first"] = scatter["first"].finish(*on("Q4", totals["inner"]), *on("Q5", o_held)) * scale
+        totals["outer"] = scatter["outer"].finish(*on("Q9", f_held)) * scale
     (tokens_grad,) = run(
         part(tokens_kernel, z),
         [shaped(bf16, z.tokens, z.local * z.block)],
         [],
         [right_first, turned],
         products,
-        [*on("Q6", f_held)],
+        [*on("Q6", f_held), *on("Q7", totals["inner"])],
     )
     summed = [
-        (totals[name] * scale).reshape(z.local, z.rows, z.block) for name in ("first", "inner", "second", "outer")
+        totals[name].reshape(z.local, z.rows, z.block) for name in ("first", "inner", "second", "outer")
     ]
     return (tokens_grad, *summed)
 

time: 170 us -> 164 us (0.965)
  starting transfers between devices: 68.7 us -> 58.2 us
  waiting for transfers between devices: 69.2 us -> 73.7 us
    ppermute x53, starting transfers between devices: 68.7 us -> 58.2 us  [hop(): return lax.ppermute(source, axis, [(i, i ^ offset) for i in range(size)])]
    ppermute x53, waiting for transfers between devices: 69.2 us -> 73.7 us  [hop(): return lax.ppermute(source, axis, [(i, i ^ offset) for i in range(size)])]
  transfers between devices with their start and end apart: 53 -> 53, of which waited for: 19 -> 20; matrix products, arithmetic and copies ran while one was open for 2% -> 2% of each run, Pallas kernels for 13% -> 13%
where the time goes in v5:
time: 164 us
  waiting for transfers between devices  73.7 us (45%)
  starting transfers between devices  58.2 us (35%)
  Pallas kernels  25.7 us (16%)
  other arithmetic  3.71 us (2%)
    ppermute x53, waiting for transfers between devices, hop(): return lax.ppermute(source, axis, [(i, i ^ offset) for i in range(size)])  73.7 us
    ppermute x53, starting transfers between devices, hop(): return lax.ppermute(source, axis, [(i, i ^ offset) for i in range(size)])  58.2 us
    pallas_call x18, Pallas kernels, run(): pl.pallas_call(skip, out_shape=outs, in_specs=specs + [pl.BlockSpec(memor...  25.7 us
  transfers between devices with their start and end apart: 53, of which 20 were waited for; matrix products, arithmetic and copies ran while one was open for 2% of the time, Pallas kernels for 13%

profile of v5, /device:TPU:0, one launch (start us, length us, event | category | flops | bytes accessed | tf_op | source)
XLA Modules:
  0.0 163.7 jit_solution(10670329662931991490)
XLA Ops:
  0.6 3.0 %collective-permute-start.8 = (bf16[1,32,16,128]{3,2,1,0:T(8,128)(2,1)}, bf16[1,32,16,128]{3,2,1,0:T(8,128)(2,1)S(1)}, u32[]{:S(2)}, u32[]{:S(2)}) collective-permute-start(bf16[1,32,16,128]{3,2,1,0:T(8,128)(2,1)} %bitcast.78), channel_id=1, source_target_pairs={{0,4},{4,0},{8,12},{12,8},{16,20},{20,16},{24,28},{28,24},{1,5},{5... | collective-permute-start | bytes 393224 | tf_op jit(solution)/shard_map/ppermute | solution.py:29
  3.6 2.6 %collective-permute-start.2 = (bf16[1,32,16,128]{3,2,1,0:T(8,128)(2,1)}, bf16[1,32,16,128]{3,2,1,0:T(8,128)(2,1)S(1)}, u32[]{:S(2)}, u32[]{:S(2)}) collective-permute-start(bf16[1,32,16,128]{3,2,1,0:T(8,128)(2,1)} %bitcast.74), channel_id=1, source_target_pairs={{0,16},{4,20},{8,24},{12,28},{16,0},{20,4},{24,8},{28,12},{1,17},{... | collective-permute-start | bytes 393224 | tf_op jit(solution)/shard_map/ppermute | solution.py:29
  6.2 1.6 collective-permute-start.1
  10.0 1.9 %shard_map.101 = (bf16[1024,128]{1,0:T(8,128)(2,1)S(1)}, bf16[1024,128]{1,0:T(8,128)(2,1)S(1)}, bf16[1024,128]{1,0:T(8,128)(2,1)S(1)}, bf16[1024,128]{1,0:T(8,128)(2,1)S(1)}) custom-call(s32[2]{0:T(128)S(1)} %pad_add_fusion.refs_0_, bf16[128,4096]{1,0:T(8,128)(2,1)S(1)} %copy-done.1), custom_call_target="tpu_custom_call" | custom-call | bytes 2097160 | tf_op jit(solution)/shard_map/pallas_call | solution.py:337
  11.9 2.7 %collective-permute-start.9 = (bf16[2,32,16,128]{3,2,1,0:T(8,128)(2,1)S(1)}, bf16[2,32,16,128]{3,2,1,0:T(8,128)(2,1)S(1)}, u32[]{:S(2)}, u32[]{:S(2)}) collective-permute-start(bf16[2,32,16,128]{3,2,1,0:T(8,128)(2,1)S(1)} %shard_map.103.refs_0_), channel_id=1, source_target_pairs={{0,16},{4,20},{8,24},{12,28},{16,0},{20,4},{24,8},{28,12},{1,17},{... | collective-permute-start | bytes 786440 | tf_op jit(solution)/shard_map/ppermute | solution.py:29
  18.1 6.7 %collective-permute-done.14.refs_1_ = bf16[1,32,16,128]{3,2,1,0:T(8,128)(2,1)S(1)} collective-permute-done((bf16[1,32,16,128]{3,2,1,0:T(8,128)(2,1)}, bf16[1,32,16,128]{3,2,1,0:T(8,128)(2,1)S(1)}, u32[]{:S(2)}, u32[]{:S(2)}) %collective-permute-start.14) | collective-permute-done | bytes 131104 | tf_op jit(solution)/shard_map/ppermute | solution.py:29
  25.0 1.9 %collective-permute-start.3 = (bf16[1,32,16,128]{3,2,1,0:T(8,128)(2,1)S(1)}, bf16[1,32,16,128]{3,2,1,0:T(8,128)(2,1)S(1)}, u32[]{:S(2)}, u32[]{:S(2)}) collective-permute-start(bf16[1,32,16,128]{3,2,1,0:T(8,128)(2,1)S(1)} %collective-permute-done.1.refs_4_), channel_id=1, source_target_pairs={{0,4},{4,0},{8,12},{12,8},{16,20},{20,16},{24,28},{28,24},{1,5},{5... | collective-permute-start | bytes 393224 | tf_op jit(solution)/shard_map/ppermute | solution.py:29
  26.9 2.8 %collective-permute-done.5.refs_8_ = bf16[1,32,16,128]{3,2,1,0:T(8,128)(2,1)S(1)} collective-permute-done((bf16[1,32,16,128]{3,2,1,0:T(8,128)(2,1)S(1)}, bf16[1,32,16,128]{3,2,1,0:T(8,128)(2,1)S(1)}, u32[]{:S(2)}, u32[]{:S(2)}) %collective-permute-start.5) | collective-permute-done | bytes 131104 | tf_op jit(solution)/shard_map/ppermute | solution.py:29
  30.4 2.6 %collective-permute-start.21 = (bf16[2,32,16,128]{3,2,1,0:T(8,128)(2,1)S(1)}, bf16[2,32,16,128]{3,2,1,0:T(8,128)(2,1)S(1)}, u32[]{:S(2)}, u32[]{:S(2)}) collective-permute-start(bf16[2,32,16,128]{3,2,1,0:T(8,128)(2,1)S(1)} %shard_map.108.refs_0_), channel_id=1, source_target_pairs={{0,16},{4,20},{8,24},{12,28},{16,0},{20,4},{24,8},{28,12},{1,17},{... | collective-permute-start | bytes 786440 | tf_op jit(solution)/shard_map/ppermute | solution.py:29
  33.1 2.5 %collective-permute-start.15 = (bf16[2,32,16,128]{3,2,1,0:T(8,128)(2,1)S(1)}, bf16[2,32,16,128]{3,2,1,0:T(8,128)(2,1)S(1)}, u32[]{:S(2)}, u32[]{:S(2)}) collective-permute-start(bf16[2,32,16,128]{3,2,1,0:T(8,128)(2,1)S(1)} %shard_map.106.refs_0_), channel_id=1, source_target_pairs={{0,8},{4,12},{8,0},{12,4},{16,24},{20,28},{24,16},{28,20},{1,9},{5... | collective-permute-start | bytes 786440 | tf_op jit(solution)/shard_map/ppermute | solution.py:29
  35.7 2.6 %shard_map.102 = (bf16[32,128,128]{2,1,0:T(8,128)(2,1)S(1)}, bf16[1024,128]{1,0:T(8,128)(2,1)S(1)}, bf16[1024,128]{1,0:T(8,128)(2,1)S(1)}, bf16[1024,128]{1,0:T(8,128)(2,1)S(1)}, bf16[1024,128]{1,0:T(8,128)(2,1)S(1)}) custom-call(s32[2]{0:T(128)S(1)} %pad_add_fusion.refs_0_, bf16[128,4096]{1,0:T(8,128)(2,1)S(1)} %copy-done, ...), custom_call_target="tpu_custom_call" | custom-call | flops 134217728 | bytes 4194312 | tf_op jit(solution)/shard_map/pallas_call | solution.py:337
  38.4 1.6 collective-permute-start.12
  40.0 3.4 %collective-permute-done.21.refs_1_ = bf16[2,32,16,128]{3,2,1,0:T(8,128)(2,1)S(1)} collective-permute-done((bf16[2,32,16,128]{3,2,1,0:T(8,128)(2,1)S(1)}, bf16[2,32,16,128]{3,2,1,0:T(8,128)(2,1)S(1)}, u32[]{:S(2)}, u32[]{:S(2)}) %collective-permute-start.21) | collective-permute-done | bytes 262176 | tf_op jit(solution)/shard_map/ppermute | solution.py:29
  43.4 3.1 %collective-permute-done.15.refs_1_ = bf16[2,32,16,128]{3,2,1,0:T(8,128)(2,1)S(1)} collective-permute-done((bf16[2,32,16,128]{3,2,1,0:T(8,128)(2,1)S(1)}, bf16[2,32,16,128]{3,2,1,0:T(8,128)(2,1)S(1)}, u32[]{:S(2)}, u32[]{:S(2)}) %collective-permute-start.15) | collective-permute-done | bytes 262176 | tf_op jit(solution)/shard_map/ppermute | solution.py:29
  47.8 1.7 %collective-permute-start.16 = (bf16[4,32,16,128]{3,2,1,0:T(8,128)(2,1)S(1)}, bf16[4,32,16,128]{3,2,1,0:T(8,128)(2,1)S(1)}, u32[]{:S(2)}, u32[]{:S(2)}) collective-permute-start(bf16[4,32,16,128]{3,2,1,0:T(8,128)(2,1)S(1)} %shard_map.107.refs_1_), channel_id=1, source_target_pairs={{0,4},{4,0},{8,12},{12,8},{16,20},{20,16},{24,28},{28,24},{1,5},{5... | collective-permute-start | bytes 1572872 | tf_op jit(solution)/shard_map/ppermute | solution.py:29
  49.4 2.9 %collective-permute-done.13.refs_6_ = bf16[1024,128]{1,0:T(8,128)(2,1)S(1)} collective-permute-done((bf16[1024,128]{1,0:T(8,128)(2,1)S(1)}, bf16[1024,128]{1,0:T(8,128)(2,1)S(1)}, u32[]{:S(2)}, u32[]{:S(2)}) %collective-permute-start.13) | collective-permute-done | bytes 262176 | tf_op jit(solution)/shard_map/ppermute | solution.py:29
  52.3 1.7 %collective-permute-start.24 = (bf16[1024,128]{1,0:T(8,128)(2,1)S(1)}, bf16[1024,128]{1,0:T(8,128)(2,1)S(1)}, u32[]{:S(2)}, u32[]{:S(2)}) collective-permute-start(bf16[1024,128]{1,0:T(8,128)(2,1)S(1)} %get-tuple-element.63), channel_id=1, source_target_pairs={{0,3},{1,2},{2,1},{3,0},{4,7},{5,6},{6,5},{7,4},{8,11},{9,10},{10,... | collective-permute-start | bytes 786440 | tf_op jit(solution)/shard_map/ppermute | solution.py:29
  54.0 3.7 %collective-permute-done.10.refs_2_ = bf16[4,32,16,128]{3,2,1,0:T(8,128)(2,1)S(1)} collective-permute-done((bf16[4,32,16,128]{3,2,1,0:T(8,128)(2,1)S(1)}, bf16[4,32,16,128]{3,2,1,0:T(8,128)(2,1)S(1)}, u32[]{:S(2)}, u32[]{:S(2)}) %collective-permute-start.10) | collective-permute-done | bytes 524320 | tf_op jit(solution)/shard_map/ppermute | solution.py:29
  57.7 2.6 %shard_map.105 = (bf16[32,128,128]{2,1,0:T(8,128)(2,1)S(1)}, bf16[32,128,128]{2,1,0:T(8,128)(2,1)S(1)}, bf16[1024,128]{1,0:T(8,128)(2,1)S(1)}, bf16[1024,128]{1,...) custom-call(s32[2]{0:T(128)S(1)} %pad_add_fusion.refs_0_, ...), custom_call_target="tpu_custom_call" | custom-call | flops 134217728 | bytes 5242888 | tf_op jit(solution)/shard_map/pallas_call | solution.py:337
  60.4 1.5 collective-permute-start.18
  62.2 3.9 %collective-permute-done.22.refs_2_ = bf16[4,32,16,128]{3,2,1,0:T(8,128)(2,1)S(1)} collective-permute-done((bf16[4,32,16,128]{3,2,1,0:T(8,128)(2,1)S(1)}, bf16[4,32,16,128]{3,2,1,0:T(8,128)(2,1)S(1)}, u32[]{:S(2)}, u32[]{:S(2)}) %collective-permute-start.22) | collective-permute-done | bytes 524320 | tf_op jit(solution)/shard_map/ppermute | solution.py:29
  66.1 2.5 %shard_map.110 = (bf16[32,128,128]{2,1,0:T(8,128)(2,1)}, bf16[32,128,128]{2,1,0:T(8,128)(2,1)S(1)}, bf16[1024,128]{1,0:T(8,128)(2,1)S(1)}, bf16[1024,128]{1,0:T(...) custom-call(s32[2]{0:T(128)S(1)} %pad_add_fusion.refs_0_, ...), custom_call_target="tpu_custom_call" | custom-call | flops 134217728 | bytes 5242888 | tf_op jit(solution)/shard_map/pallas_call | solution.py:337
  70.5 3.7 %collective-permute-done.19.refs_6_ = bf16[1024,128]{1,0:T(8,128)(2,1)S(1)} collective-permute-done((bf16[1024,128]{1,0:T(8,128)(2,1)S(1)}, bf16[1024,128]{1,0:T(8,128)(2,1)S(1)}, u32[]{:S(2)}, u32[]{:S(2)}) %collective-permute-start.19) | collective-permute-done | bytes 262176 | tf_op jit(solution)/shard_map/ppermute | solution.py:29
  74.2 6.5 %collective-permute-done.26.refs_9_ = bf16[1024,128]{1,0:T(8,128)(2,1)S(1)} collective-permute-done((bf16[1024,128]{1,0:T(8,128)(2,1)S(1)}, bf16[1024,128]{1,0:T(8,128)(2,1)S(1)}, u32[]{:S(2)}, u32[]{:S(2)}) %collective-permute-start.26) | collective-permute-done | bytes 262176 | tf_op jit(solution)/shard_map/ppermute | solution.py:29
  80.8 4.7 %collective-permute-done.27.refs_10_ = bf16[1024,128]{1,0:T(8,128)(2,1)S(1)} collective-permute-done((bf16[1024,128]{1,0:T(8,128)(2,1)S(1)}, bf16[1024,128]{1,0:T(8,128)(2,1)S(1)}, u32[]{:S(2)}, u32[]{:S(2)}) %collective-permute-start.27) | collective-permute-done | bytes 262176 | tf_op jit(solution)/shard_map/ppermute | solution.py:29
  85.5 3.0 %shard_map.111 = (bf16[32,128,128]{2,1,0:T(8,128)(2,1)S(1)}, bf16[32,128,128]{2,1,0:T(8,128)(2,1)S(1)}, bf16[32,128,128]{2,1,0:T(8,128)(2,1)S(1)}, bf16[1024,128...) custom-call(s32[2]{0:T(128)S(1)} %pad_add_fusion.refs_0_, ...), custom_call_target="tpu_custom_call" | custom-call | flops 134217728 | bytes 7340040 | tf_op jit(solution)/shard_map/pallas_call | solution.py:337
  90.9 1.6 collective-permute-start.29
  92.8 2.6 %shard_map.118 = (bf16[1024,128]{1,0:T(8,128)(2,1)S(1)}, bf16[1024,128]{1,0:T(8,128)(2,1)S(1)}, bf16[1024,128]{1,0:T(8,128)(2,1)S(1)}, bf16[1024,128]{1,0:T(8,128)(2,1)S(1)}) custom-call(s32[2]{0:T(128)S(1)} %pad_add_fusion.refs_0_, bf16[32,128,128]{2,1,0:T(8,128)(2,1)S(1)} %get-tuple-element.88.refs_1_, ...), custom_call_target="tpu_custom_call" | custom-call | flops 134217728 | bytes 3145736 | tf_op jit(solution)/shard_map/pallas_call | solution.py:337
  95.7 1.6 collective-permute-start.47
  97.2 2.8 %collective-permute-done.29.refs_4_ = bf16[1024,128]{1,0:T(8,128)(2,1)S(1)} collective-permute-done((bf16[1024,128]{1,0:T(8,128)(2,1)S(1)}, bf16[1024,128]{1,0:T(8,128)(2,1)S(1)}, u32[]{:S(2)}, u32[]{:S(2)}) %collective-permute-start.29) | collective-permute-done | bytes 262176 | tf_op jit(solution)/shard_map/ppermute | solution.py:29
  100.5 4.3 %collective-permute-done.30.refs_5_ = bf16[1024,128]{1,0:T(8,128)(2,1)S(1)} collective-permute-done((bf16[1024,128]{1,0:T(8,128)(2,1)S(1)}, bf16[1024,128]{1,0:T(8,128)(2,1)S(1)}, u32[]{:S(2)}, u32[]{:S(2)}) %collective-permute-start.30) | collective-permute-done | bytes 262176 | tf_op jit(solution)/shard_map/ppermute | solution.py:29
  104.8 2.3 %shard_map.112 = (bf16[32,128,128]{2,1,0:T(8,128)(2,1)S(1)}, bf16[1024,128]{1,0:T(8,128)(2,1)S(1)}, bf16[1024,128]{1,0:T(8,128)(2,1)S(1)}, bf16[1024,128]{1,0:T(8,128)(2,1)S(1)}, bf16[1024,128]{1,0:T(8,128)(2,1)S(1)}) custom-call(s32[2]{0:T(128)S(1)} %pad_add_fusion.refs_0_, bf16[32,128,128]{2,1,0:T(8,128)(2,1)S(1)} %get-tuple-element.56.refs_1_, ...), custom_call_target="tpu_custom_call" | custom-call | flops 134217728 | bytes 4194312 | tf_op jit(solution)/shard_map/pallas_call | solution.py:337
  110.2 1.9 %collective-permute-start.43 = (bf16[512,128]{1,0:T(8,128)(2,1)S(1)}, bf16[512,128]{1,0:T(8,128)(2,1)S(1)}, u32[]{:S(2)}, u32[]{:S(2)}) collective-permute-start(bf16[512,128]{1,0:T(8,128)(2,1)S(1)} %get-tuple-element.106), channel_id=1, source_target_pairs={{0,16},{4,20},{8,24},{12,28},{16,0},{20,4},{24,8},{28,12},{1,17},{... | collective-permute-start | bytes 393224 | tf_op jit(solution)/shard_map/ppermute | solution.py:29
  112.1 1.8 %collective-permute-start.45 = (bf16[512,128]{1,0:T(8,128)(2,1)S(1)}, bf16[512,128]{1,0:T(8,128)(2,1)S(1)}, u32[]{:S(2)}, u32[]{:S(2)}) collective-permute-start(bf16[512,128]{1,0:T(8,128)(2,1)S(1)} %get-tuple-element.107), channel_id=1, source_target_pairs={{0,24},{4,28},{8,16},{12,20},{16,8},{20,12},{24,0},{28,4},{1,25},{... | collective-permute-start | bytes 393224 | tf_op jit(solution)/shard_map/ppermute | solution.py:29
  113.9 2.2 %collective-permute-done.48.refs_5_ = bf16[1024,128]{1,0:T(8,128)(2,1)S(1)} collective-permute-done((bf16[1024,128]{1,0:T(8,128)(2,1)S(1)}, bf16[1024,128]{1,0:T(8,128)(2,1)S(1)}, u32[]{:S(2)}, u32[]{:S(2)}) %collective-permute-start.48) | collective-permute-done | bytes 262176 | tf_op jit(solution)/shard_map/ppermute | solution.py:29
  116.1 1.6 collective-permute-start.32
  117.6 1.6 shard_map.119
  119.2 3.9 %collective-permute-done.43 = bf16[512,128]{1,0:T(8,128)(2,1)S(1)} collective-permute-done((bf16[512,128]{1,0:T(8,128)(2,1)S(1)}, bf16[512,128]{1,0:T(8,128)(2,1)S(1)}, u32[]{:S(2)}, u32[]{:S(2)}) %collective-permute-start.43) | collective-permute-done | bytes 131104 | tf_op jit(solution)/shard_map/ppermute | solution.py:29
  128.1 2.1 %collective-permute-start.41 = (bf16[512,128]{1,0:T(8,128)(2,1)S(1)}, bf16[512,128]{1,0:T(8,128)(2,1)S(1)}, u32[]{:S(2)}, u32[]{:S(2)}) collective-permute-start(bf16[512,128]{1,0:T(8,128)(2,1)S(1)} %get-tuple-element.110), channel_id=1, source_target_pairs={{0,24},{4,28},{8,16},{12,20},{16,8},{20,12},{24,0},{28,4},{1,25},{... | collective-permute-start | bytes 393224 | tf_op jit(solution)/shard_map/ppermute | solution.py:29
  130.1 1.6 collective-permute-done.33.refs_5_
  132.1 1.6 shard_map.115
  134.1 5.4 %collective-permute-done.49 = bf16[4,512,128]{2,1,0:T(8,128)(2,1)S(1)} collective-permute-done((bf16[4,512,128]{2,1,0:T(8,128)(2,1)S(1)}, bf16[4,512,128]{2,1,0:T(8,128)(2,1)S(1)}, u32[]{:S(2)}, u32[]{:S(2)}) %collective-permute-start.49) | collective-permute-done | bytes 524320 | tf_op jit(solution)/shard_map/ppermute | solution.py:29
  140.9 1.8 %shard_map.116 = bf16[128,4096]{1,0:T(8,128)(2,1)} custom-call(bf16[32,128,128]{2,1,0:T(8,128)(2,1)S(1)} %get-tuple-element.51.refs_0_, bf16[32,128,128]{2,1,0:T(8,128)(2,1)S(1)} %get-tuple-element.80.refs_1_), custom_call_target="tpu_custom_call" | custom-call | flops 134217728 | bytes 3145728 | tf_op jit(solution)/shard_map/pallas_call | solution.py:337
  142.7 2.4 %collective-permute-start.52 = (bf16[512,128]{1,0:T(8,128)(2,1)S(1)}, bf16[512,128]{1,0:T(8,128)(2,1)S(1)}, u32[]{:S(2)}, u32[]{:S(2)}) collective-permute-start(bf16[512,128]{1,0:T(8,128)(2,1)S(1)} %get-tuple-element.104), channel_id=1, source_target_pairs={{0,24},{4,28},{8,16},{12,20},{16,8},{20,12},{24,0},{28,4},{1,25},{... | collective-permute-start | bytes 393224 | tf_op jit(solution)/shard_map/ppermute | solution.py:29
  145.9 4.0 %collective-permute-done.35 = bf16[4,512,128]{2,1,0:T(8,128)(2,1)S(1)} collective-permute-done((bf16[4,512,128]{2,1,0:T(8,128)(2,1)S(1)}, bf16[4,512,128]{2,1,0:T(8,128)(2,1)S(1)}, u32[]{:S(2)}, u32[]{:S(2)}) %collective-permute-start.35) | collective-permute-done | bytes 524320 | tf_op jit(solution)/shard_map/ppermute | solution.py:29
  150.0 1.7 %collective-permute-start.36 = (bf16[512,128]{1,0:T(8,128)(2,1)S(1)}, bf16[512,128]{1,0:T(8,128)(2,1)S(1)}, u32[]{:S(2)}, u32[]{:S(2)}) collective-permute-start(bf16[512,128]{1,0:T(8,128)(2,1)S(1)} %get-tuple-element.112), channel_id=1, source_target_pairs={{0,16},{4,20},{8,24},{12,28},{16,0},{20,4},{24,8},{28,12},{1,17},{... | collective-permute-start | bytes 393224 | tf_op jit(solution)/shard_map/ppermute | solution.py:29
  151.7 2.4 %collective-permute-start.38 = (bf16[512,128]{1,0:T(8,128)(2,1)S(1)}, bf16[512,128]{1,0:T(8,128)(2,1)S(1)}, u32[]{:S(2)}, u32[]{:S(2)}) collective-permute-start(bf16[512,128]{1,0:T(8,128)(2,1)S(1)} %get-tuple-element.113), channel_id=1, source_target_pairs={{0,24},{4,28},{8,16},{12,20},{16,8},{20,12},{24,0},{28,4},{1,25},{... | collective-permute-start | bytes 393224 | tf_op jit(solution)/shard_map/ppermute | solution.py:29
  155.3 7.6 %collective-permute-done.36 = bf16[512,128]{1,0:T(8,128)(2,1)S(1)} collective-permute-done((bf16[512,128]{1,0:T(8,128)(2,1)S(1)}, bf16[512,128]{1,0:T(8,128)(2,1)S(1)}, u32[]{:S(2)}, u32[]{:S(2)}) %collective-permute-start.36) | collective-permute-done | bytes 131104 | tf_op jit(solution)/shard_map/ppermute | solution.py:29
  (102 shorter events, 27.0 us)
Async XLA Ops:
  0.6 11.3 %collective-permute-start.8 = (bf16[1,32,16,128]{3,2,1,0:T(8,128)(2,1)}, bf16[1,32,16,128]{3,2,1,0:T(8,128)(2,1)S(1)}, u32[]{:S(2)}, u32[]{:S(2)}) collective-permute-start(bf16[1,32,16,128]{3,2,1,0:T(8,128)(2,1)} %bitcast.78), channel_id=1, source_target_pairs={{0,4},{4,0},{8,12},{12,8},{16,20},{20,16},{24,28},{28,24},{1,5},{5... | collective-permute-start | bytes 393224 | tf_op jit(solution)/shard_map/ppermute | solution.py:29
  3.6 11.2 %collective-permute-start.2 = (bf16[1,32,16,128]{3,2,1,0:T(8,128)(2,1)}, bf16[1,32,16,128]{3,2,1,0:T(8,128)(2,1)S(1)}, u32[]{:S(2)}, u32[]{:S(2)}) collective-permute-start(bf16[1,32,16,128]{3,2,1,0:T(8,128)(2,1)} %bitcast.74), channel_id=1, source_target_pairs={{0,16},{4,20},{8,24},{12,28},{16,0},{20,4},{24,8},{28,12},{1,17},{... | collective-permute-start | bytes 393224 | tf_op jit(solution)/shard_map/ppermute | solution.py:29
  6.2 9.9 %collective-permute-start.1 = (bf16[1,32,16,128]{3,2,1,0:T(8,128)(2,1)}, bf16[1,32,16,128]{3,2,1,0:T(8,128)(2,1)S(1)}, u32[]{:S(2)}, u32[]{:S(2)}) collective-permute-start(bf16[1,32,16,128]{3,2,1,0:T(8,128)(2,1)} %bitcast.75), channel_id=1, source_target_pairs={{0,8},{4,12},{8,0},{12,4},{16,24},{20,28},{24,16},{28,20},{1,9},{5... | collective-permute-start | bytes 393224 | tf_op jit(solution)/shard_map/ppermute | solution.py:29
  7.8 9.8 %collective-permute-start = (bf16[1,32,16,128]{3,2,1,0:T(8,128)(2,1)}, bf16[1,32,16,128]{3,2,1,0:T(8,128)(2,1)S(1)}, u32[]{:S(2)}, u32[]{:S(2)}) collective-permute-start(bf16[1,32,16,128]{3,2,1,0:T(8,128)(2,1)} %bitcast.76), channel_id=1, source_target_pairs={{0,4},{4,0},{8,12},{12,8},{16,20},{20,16},{24,28},{28,24},{1,5},{5... | collective-permute-start | bytes 393224 | tf_op jit(solution)/shard_map/ppermute | solution.py:29
  8.3 16.5 %collective-permute-start.14 = (bf16[1,32,16,128]{3,2,1,0:T(8,128)(2,1)}, bf16[1,32,16,128]{3,2,1,0:T(8,128)(2,1)S(1)}, u32[]{:S(2)}, u32[]{:S(2)}) collective-permute-start(bf16[1,32,16,128]{3,2,1,0:T(8,128)(2,1)} %bitcast.82), channel_id=1, source_target_pairs={{0,16},{4,20},{8,24},{12,28},{16,0},{20,4},{24,8},{28,12},{1,17},{... | collective-permute-start | bytes 393224 | tf_op jit(solution)/shard_map/ppermute | solution.py:29
  11.9 18.4 %collective-permute-start.9 = (bf16[2,32,16,128]{3,2,1,0:T(8,128)(2,1)S(1)}, bf16[2,32,16,128]{3,2,1,0:T(8,128)(2,1)S(1)}, u32[]{:S(2)}, u32[]{:S(2)}) collective-permute-start(bf16[2,32,16,128]{3,2,1,0:T(8,128)(2,1)S(1)} %shard_map.103.refs_0_), channel_id=1, source_target_pairs={{0,16},{4,20},{8,24},{12,28},{16,0},{20,4},{24,8},{28,12},{1,17},{... | collective-permute-start | bytes 786440 | tf_op jit(solution)/shard_map/ppermute | solution.py:29
  14.8 10.2 %collective-permute-start.20 = (bf16[1,32,16,128]{3,2,1,0:T(8,128)(2,1)S(1)}, bf16[1,32,16,128]{3,2,1,0:T(8,128)(2,1)S(1)}, u32[]{:S(2)}, u32[]{:S(2)}) collective-permute-start(bf16[1,32,16,128]{3,2,1,0:T(8,128)(2,1)S(1)} %bitcast.80), channel_id=1, source_target_pairs={{0,4},{4,0},{8,12},{12,8},{16,20},{20,16},{24,28},{28,24},{1,5},{5... | collective-permute-start | bytes 393224 | tf_op jit(solution)/shard_map/ppermute | solution.py:29
  16.1 19.6 %collective-permute-start.7 = (bf16[1024,128]{1,0:T(8,128)(2,1)S(1)}, bf16[1024,128]{1,0:T(8,128)(2,1)S(1)}, u32[]{:S(2)}, u32[]{:S(2)}) collective-permute-start(bf16[1024,128]{1,0:T(8,128)(2,1)S(1)} %get-tuple-element.50), channel_id=1, source_target_pairs={{0,2},{1,3},{2,0},{3,1},{4,6},{5,7},{6,4},{7,5},{8,10},{9,11},{10,... | collective-permute-start | bytes 786440 | tf_op jit(solution)/shard_map/ppermute | solution.py:29
  17.6 12.0 %collective-permute-start.5 = (bf16[1,32,16,128]{3,2,1,0:T(8,128)(2,1)S(1)}, bf16[1,32,16,128]{3,2,1,0:T(8,128)(2,1)S(1)}, u32[]{:S(2)}, u32[]{:S(2)}) collective-permute-start(bf16[1,32,16,128]{3,2,1,0:T(8,128)(2,1)S(1)} %collective-permute-done.2.refs_5_), channel_id=1, source_target_pairs={{0,8},{4,12},{8,0},{12,4},{16,24},{20,28},{24,16},{28,20},{1,9},{5... | collective-permute-start | bytes 393224 | tf_op jit(solution)/shard_map/ppermute | solution.py:29
  25.0 10.6 %collective-permute-start.3 = (bf16[1,32,16,128]{3,2,1,0:T(8,128)(2,1)S(1)}, bf16[1,32,16,128]{3,2,1,0:T(8,128)(2,1)S(1)}, u32[]{:S(2)}, u32[]{:S(2)}) collective-permute-start(bf16[1,32,16,128]{3,2,1,0:T(8,128)(2,1)S(1)} %collective-permute-done.1.refs_4_), channel_id=1, source_target_pairs={{0,4},{4,0},{8,12},{12,8},{16,20},{20,16},{24,28},{28,24},{1,5},{5... | collective-permute-start | bytes 393224 | tf_op jit(solution)/shard_map/ppermute | solution.py:29
  30.4 13.0 %collective-permute-start.21 = (bf16[2,32,16,128]{3,2,1,0:T(8,128)(2,1)S(1)}, bf16[2,32,16,128]{3,2,1,0:T(8,128)(2,1)S(1)}, u32[]{:S(2)}, u32[]{:S(2)}) collective-permute-start(bf16[2,32,16,128]{3,2,1,0:T(8,128)(2,1)S(1)} %shard_map.108.refs_0_), channel_id=1, source_target_pairs={{0,16},{4,20},{8,24},{12,28},{16,0},{20,4},{24,8},{28,12},{1,17},{... | collective-permute-start | bytes 786440 | tf_op jit(solution)/shard_map/ppermute | solution.py:29
  33.1 13.4 %collective-permute-start.15 = (bf16[2,32,16,128]{3,2,1,0:T(8,128)(2,1)S(1)}, bf16[2,32,16,128]{3,2,1,0:T(8,128)(2,1)S(1)}, u32[]{:S(2)}, u32[]{:S(2)}) collective-permute-start(bf16[2,32,16,128]{3,2,1,0:T(8,128)(2,1)S(1)} %shard_map.106.refs_0_), channel_id=1, source_target_pairs={{0,8},{4,12},{8,0},{12,4},{16,24},{20,28},{24,16},{28,20},{1,9},{5... | collective-permute-start | bytes 786440 | tf_op jit(solution)/shard_map/ppermute | solution.py:29
  35.6 22.1 %collective-permute-start.10 = (bf16[4,32,16,128]{3,2,1,0:T(8,128)(2,1)S(1)}, bf16[4,32,16,128]{3,2,1,0:T(8,128)(2,1)S(1)}, u32[]{:S(2)}, u32[]{:S(2)}) collective-permute-start(bf16[4,32,16,128]{3,2,1,0:T(8,128)(2,1)S(1)} %shard_map.104.refs_1_), channel_id=1, source_target_pairs={{0,8},{4,12},{8,0},{12,4},{16,24},{20,28},{24,16},{28,20},{1,9},{5... | collective-permute-start | bytes 1572872 | tf_op jit(solution)/shard_map/ppermute | solution.py:29
  38.4 9.4 %collective-permute-start.11 = (bf16[1024,128]{1,0:T(8,128)(2,1)S(1)}, bf16[1024,128]{1,0:T(8,128)(2,1)S(1)}, u32[]{:S(2)}, u32[]{:S(2)}) collective-permute-start(bf16[1024,128]{1,0:T(8,128)(2,1)S(1)} %get-tuple-element.53), channel_id=1, source_target_pairs={{0,1},{1,0},{2,3},{3,2},{4,5},{5,4},{6,7},{7,6},{8,9},{9,8},{10,11... | collective-permute-start | bytes 786440 | tf_op jit(solution)/shard_map/ppermute | solution.py:29
  38.4 11.0 %collective-permute-start.12 = (bf16[1024,128]{1,0:T(8,128)(2,1)S(1)}, bf16[1024,128]{1,0:T(8,128)(2,1)S(1)}, u32[]{:S(2)}, u32[]{:S(2)}) collective-permute-start(bf16[1024,128]{1,0:T(8,128)(2,1)S(1)} %get-tuple-element.54), channel_id=1, source_target_pairs={{0,2},{1,3},{2,0},{3,1},{4,6},{5,7},{6,4},{7,5},{8,10},{9,11},{10,... | collective-permute-start | bytes 786440 | tf_op jit(solution)/shard_map/ppermute | solution.py:29
  43.4 8.9 %collective-permute-start.13 = (bf16[1024,128]{1,0:T(8,128)(2,1)S(1)}, bf16[1024,128]{1,0:T(8,128)(2,1)S(1)}, u32[]{:S(2)}, u32[]{:S(2)}) collective-permute-start(bf16[1024,128]{1,0:T(8,128)(2,1)S(1)} %get-tuple-element.55), channel_id=1, source_target_pairs={{0,3},{1,2},{2,1},{3,0},{4,7},{5,6},{6,5},{7,4},{8,11},{9,10},{10,... | collective-permute-start | bytes 786440 | tf_op jit(solution)/shard_map/ppermute | solution.py:29
  46.5 19.6 %collective-permute-start.22 = (bf16[4,32,16,128]{3,2,1,0:T(8,128)(2,1)S(1)}, bf16[4,32,16,128]{3,2,1,0:T(8,128)(2,1)S(1)}, u32[]{:S(2)}, u32[]{:S(2)}) collective-permute-start(bf16[4,32,16,128]{3,2,1,0:T(8,128)(2,1)S(1)} %shard_map.109.refs_1_), channel_id=1, source_target_pairs={{0,8},{4,12},{8,0},{12,4},{16,24},{20,28},{24,16},{28,20},{1,9},{5... | collective-permute-start | bytes 1572872 | tf_op jit(solution)/shard_map/ppermute | solution.py:29
  47.8 20.9 %collective-permute-start.16 = (bf16[4,32,16,128]{3,2,1,0:T(8,128)(2,1)S(1)}, bf16[4,32,16,128]{3,2,1,0:T(8,128)(2,1)S(1)}, u32[]{:S(2)}, u32[]{:S(2)}) collective-permute-start(bf16[4,32,16,128]{3,2,1,0:T(8,128)(2,1)S(1)} %shard_map.107.refs_1_), channel_id=1, source_target_pairs={{0,4},{4,0},{8,12},{12,8},{16,20},{20,16},{24,28},{28,24},{1,5},{5... | collective-permute-start | bytes 1572872 | tf_op jit(solution)/shard_map/ppermute | solution.py:29
  49.4 10.9 %collective-permute-start.23 = (bf16[1024,128]{1,0:T(8,128)(2,1)S(1)}, bf16[1024,128]{1,0:T(8,128)(2,1)S(1)}, u32[]{:S(2)}, u32[]{:S(2)}) collective-permute-start(bf16[1024,128]{1,0:T(8,128)(2,1)S(1)} %get-tuple-element.62), channel_id=1, source_target_pairs={{0,1},{1,0},{2,3},{3,2},{4,5},{5,4},{6,7},{7,6},{8,9},{9,8},{10,11... | collective-permute-start | bytes 786440 | tf_op jit(solution)/shard_map/ppermute | solution.py:29
  52.3 9.6 %collective-permute-start.24 = (bf16[1024,128]{1,0:T(8,128)(2,1)S(1)}, bf16[1024,128]{1,0:T(8,128)(2,1)S(1)}, u32[]{:S(2)}, u32[]{:S(2)}) collective-permute-start(bf16[1024,128]{1,0:T(8,128)(2,1)S(1)} %get-tuple-element.63), channel_id=1, source_target_pairs={{0,3},{1,2},{2,1},{3,0},{4,7},{5,6},{6,5},{7,4},{8,11},{9,10},{10,... | collective-permute-start | bytes 786440 | tf_op jit(solution)/shard_map/ppermute | solution.py:29
  60.3 9.9 %collective-permute-start.17 = (bf16[1024,128]{1,0:T(8,128)(2,1)S(1)}, bf16[1024,128]{1,0:T(8,128)(2,1)S(1)}, u32[]{:S(2)}, u32[]{:S(2)}) collective-permute-start(bf16[1024,128]{1,0:T(8,128)(2,1)S(1)} %get-tuple-element.58), channel_id=1, source_target_pairs={{0,1},{1,0},{2,3},{3,2},{4,5},{5,4},{6,7},{7,6},{8,9},{9,8},{10,11... | collective-permute-start | bytes 786440 | tf_op jit(solution)/shard_map/ppermute | solution.py:29
  60.4 10.2 %collective-permute-start.18 = (bf16[1024,128]{1,0:T(8,128)(2,1)S(1)}, bf16[1024,128]{1,0:T(8,128)(2,1)S(1)}, u32[]{:S(2)}, u32[]{:S(2)}) collective-permute-start(bf16[1024,128]{1,0:T(8,128)(2,1)S(1)} %get-tuple-element.59), channel_id=1, source_target_pairs={{0,2},{1,3},{2,0},{3,1},{4,6},{5,7},{6,4},{7,5},{8,10},{9,11},{10,... | collective-permute-start | bytes 786440 | tf_op jit(solution)/shard_map/ppermute | solution.py:29
  61.9 12.3 %collective-permute-start.19 = (bf16[1024,128]{1,0:T(8,128)(2,1)S(1)}, bf16[1024,128]{1,0:T(8,128)(2,1)S(1)}, u32[]{:S(2)}, u32[]{:S(2)}) collective-permute-start(bf16[1024,128]{1,0:T(8,128)(2,1)S(1)} %get-tuple-element.60), channel_id=1, source_target_pairs={{0,3},{1,2},{2,1},{3,0},{4,7},{5,6},{6,5},{7,4},{8,11},{9,10},{10,... | collective-permute-start | bytes 786440 | tf_op jit(solution)/shard_map/ppermute | solution.py:29
  68.7 12.1 %collective-permute-start.26 = (bf16[1024,128]{1,0:T(8,128)(2,1)S(1)}, bf16[1024,128]{1,0:T(8,128)(2,1)S(1)}, u32[]{:S(2)}, u32[]{:S(2)}) collective-permute-start(bf16[1024,128]{1,0:T(8,128)(2,1)S(1)} %get-tuple-element.66), channel_id=1, source_target_pairs={{0,2},{1,3},{2,0},{3,1},{4,6},{5,7},{6,4},{7,5},{8,10},{9,11},{10,... | collective-permute-start | bytes 786440 | tf_op jit(solution)/shard_map/ppermute | solution.py:29
  70.2 15.3 %collective-permute-start.27 = (bf16[1024,128]{1,0:T(8,128)(2,1)S(1)}, bf16[1024,128]{1,0:T(8,128)(2,1)S(1)}, u32[]{:S(2)}, u32[]{:S(2)}) collective-permute-start(bf16[1024,128]{1,0:T(8,128)(2,1)S(1)} %get-tuple-element.67), channel_id=1, source_target_pairs={{0,3},{1,2},{2,1},{3,0},{4,7},{5,6},{6,5},{7,4},{8,11},{9,10},{10,... | collective-permute-start | bytes 786440 | tf_op jit(solution)/shard_map/ppermute | solution.py:29
  90.0 20.0 %collective-permute-start.42 = (bf16[4,512,128]{2,1,0:T(8,128)(2,1)S(1)}, bf16[4,512,128]{2,1,0:T(8,128)(2,1)S(1)}, u32[]{:S(2)}, u32[]{:S(2)}) collective-permute-start(bf16[4,512,128]{2,1,0:T(8,128)(2,1)S(1)} %get-tuple-element.86), channel_id=1, source_target_pairs={{0,4},{4,0},{8,12},{12,8},{16,20},{20,16},{24,28},{28,24},{1,5},{5... | collective-permute-start | bytes 1572872 | tf_op jit(solution)/shard_map/ppermute | solution.py:29
  90.9 9.1 %collective-permute-start.29 = (bf16[1024,128]{1,0:T(8,128)(2,1)S(1)}, bf16[1024,128]{1,0:T(8,128)(2,1)S(1)}, u32[]{:S(2)}, u32[]{:S(2)}) collective-permute-start(bf16[1024,128]{1,0:T(8,128)(2,1)S(1)} %get-tuple-element.70), channel_id=1, source_target_pairs={{0,2},{1,3},{2,0},{3,1},{4,6},{5,7},{6,4},{7,5},{8,10},{9,11},{10,... | collective-permute-start | bytes 786440 | tf_op jit(solution)/shard_map/ppermute | solution.py:29
  92.5 12.4 %collective-permute-start.30 = (bf16[1024,128]{1,0:T(8,128)(2,1)S(1)}, bf16[1024,128]{1,0:T(8,128)(2,1)S(1)}, u32[]{:S(2)}, u32[]{:S(2)}) collective-permute-start(bf16[1024,128]{1,0:T(8,128)(2,1)S(1)} %get-tuple-element.71), channel_id=1, source_target_pairs={{0,3},{1,2},{2,1},{3,0},{4,7},{5,6},{6,5},{7,4},{8,11},{9,10},{10,... | collective-permute-start | bytes 786440 | tf_op jit(solution)/shard_map/ppermute | solution.py:29
  95.3 16.8 %collective-permute-start.46 = (bf16[1024,128]{1,0:T(8,128)(2,1)S(1)}, bf16[1024,128]{1,0:T(8,128)(2,1)S(1)}, u32[]{:S(2)}, u32[]{:S(2)}) collective-permute-start(bf16[1024,128]{1,0:T(8,128)(2,1)S(1)} %get-tuple-element.90), channel_id=1, source_target_pairs={{0,1},{1,0},{2,3},{3,2},{4,5},{5,4},{6,7},{7,6},{8,9},{9,8},{10,11... | collective-permute-start | bytes 786440 | tf_op jit(solution)/shard_map/ppermute | solution.py:29
  95.7 18.2 %collective-permute-start.47 = (bf16[1024,128]{1,0:T(8,128)(2,1)S(1)}, bf16[1024,128]{1,0:T(8,128)(2,1)S(1)}, u32[]{:S(2)}, u32[]{:S(2)}) collective-permute-start(bf16[1024,128]{1,0:T(8,128)(2,1)S(1)} %get-tuple-element.91), channel_id=1, source_target_pairs={{0,2},{1,3},{2,0},{3,1},{4,6},{5,7},{6,4},{7,5},{8,10},{9,11},{10,... | collective-permute-start | bytes 786440 | tf_op jit(solution)/shard_map/ppermute | solution.py:29
  100.0 16.1 %collective-permute-start.48 = (bf16[1024,128]{1,0:T(8,128)(2,1)S(1)}, bf16[1024,128]{1,0:T(8,128)(2,1)S(1)}, u32[]{:S(2)}, u32[]{:S(2)}) collective-permute-start(bf16[1024,128]{1,0:T(8,128)(2,1)S(1)} %get-tuple-element.92), channel_id=1, source_target_pairs={{0,3},{1,2},{2,1},{3,0},{4,7},{5,6},{6,5},{7,4},{8,11},{9,10},{10,... | collective-permute-start | bytes 786440 | tf_op jit(solution)/shard_map/ppermute | solution.py:29
  108.7 17.7 %collective-permute-start.34 = (bf16[4,512,128]{2,1,0:T(8,128)(2,1)S(1)}, bf16[4,512,128]{2,1,0:T(8,128)(2,1)S(1)}, u32[]{:S(2)}, u32[]{:S(2)}) collective-permute-start(bf16[4,512,128]{2,1,0:T(8,128)(2,1)S(1)} %get-tuple-element.76.refs_1_), channel_id=1, source_target_pairs={{0,4},{4,0},{8,12},{12,8},{16,20},{20,16},{24,28},{28,24},{1,5},{5... | collective-permute-start | bytes 1572872 | tf_op jit(solution)/shard_map/ppermute | solution.py:29
  110.2 12.9 %collective-permute-start.43 = (bf16[512,128]{1,0:T(8,128)(2,1)S(1)}, bf16[512,128]{1,0:T(8,128)(2,1)S(1)}, u32[]{:S(2)}, u32[]{:S(2)}) collective-permute-start(bf16[512,128]{1,0:T(8,128)(2,1)S(1)} %get-tuple-element.106), channel_id=1, source_target_pairs={{0,16},{4,20},{8,24},{12,28},{16,0},{20,4},{24,8},{28,12},{1,17},{... | collective-permute-start | bytes 393224 | tf_op jit(solution)/shard_map/ppermute | solution.py:29
  112.1 11.1 %collective-permute-start.45 = (bf16[512,128]{1,0:T(8,128)(2,1)S(1)}, bf16[512,128]{1,0:T(8,128)(2,1)S(1)}, u32[]{:S(2)}, u32[]{:S(2)}) collective-permute-start(bf16[512,128]{1,0:T(8,128)(2,1)S(1)} %get-tuple-element.107), channel_id=1, source_target_pairs={{0,24},{4,28},{8,16},{12,20},{16,8},{20,12},{24,0},{28,4},{1,25},{... | collective-permute-start | bytes 393224 | tf_op jit(solution)/shard_map/ppermute | solution.py:29
  113.9 10.9 %collective-permute-start.44 = (bf16[512,128]{1,0:T(8,128)(2,1)S(1)}, bf16[512,128]{1,0:T(8,128)(2,1)S(1)}, u32[]{:S(2)}, u32[]{:S(2)}) collective-permute-start(bf16[512,128]{1,0:T(8,128)(2,1)S(1)} %get-tuple-element.108), channel_id=1, source_target_pairs={{0,8},{4,12},{8,0},{12,4},{16,24},{20,28},{24,16},{28,20},{1,9},{5... | collective-permute-start | bytes 393224 | tf_op jit(solution)/shard_map/ppermute | solution.py:29
  116.1 12.0 %collective-permute-start.32 = (bf16[1024,128]{1,0:T(8,128)(2,1)S(1)}, bf16[1024,128]{1,0:T(8,128)(2,1)S(1)}, u32[]{:S(2)}, u32[]{:S(2)}) collective-permute-start(bf16[1024,128]{1,0:T(8,128)(2,1)S(1)} %get-tuple-element.77), channel_id=1, source_target_pairs={{0,2},{1,3},{2,0},{3,1},{4,6},{5,7},{6,4},{7,5},{8,10},{9,11},{10,... | collective-permute-start | bytes 786440 | tf_op jit(solution)/shard_map/ppermute | solution.py:29
  123.2 8.9 %collective-permute-start.31 = (bf16[1024,128]{1,0:T(8,128)(2,1)S(1)}, bf16[1024,128]{1,0:T(8,128)(2,1)S(1)}, u32[]{:S(2)}, u32[]{:S(2)}) collective-permute-start(bf16[1024,128]{1,0:T(8,128)(2,1)S(1)} %shard_map.114), channel_id=1, source_target_pairs={{0,1},{1,0},{2,3},{3,2},{4,5},{5,4},{6,7},{7,6},{8,9},{9,8},{10,11... | collective-permute-start | bytes 786440 | tf_op jit(solution)/shard_map/ppermute | solution.py:29
  124.7 14.8 %collective-permute-start.49 = (bf16[4,512,128]{2,1,0:T(8,128)(2,1)S(1)}, bf16[4,512,128]{2,1,0:T(8,128)(2,1)S(1)}, u32[]{:S(2)}, u32[]{:S(2)}) collective-permute-start(bf16[4,512,128]{2,1,0:T(8,128)(2,1)S(1)} %get-tuple-element.94), channel_id=1, source_target_pairs={{0,4},{4,0},{8,12},{12,8},{16,20},{20,16},{24,28},{28,24},{1,5},{5... | collective-permute-start | bytes 1572872 | tf_op jit(solution)/shard_map/ppermute | solution.py:29
  126.6 16.1 %collective-permute-start.39 = (bf16[512,128]{1,0:T(8,128)(2,1)S(1)}, bf16[512,128]{1,0:T(8,128)(2,1)S(1)}, u32[]{:S(2)}, u32[]{:S(2)}) collective-permute-start(bf16[512,128]{1,0:T(8,128)(2,1)S(1)} %get-tuple-element.109), channel_id=1, source_target_pairs={{0,16},{4,20},{8,24},{12,28},{16,0},{20,4},{24,8},{28,12},{1,17},{... | collective-permute-start | bytes 393224 | tf_op jit(solution)/shard_map/ppermute | solution.py:29
  128.1 17.0 %collective-permute-start.41 = (bf16[512,128]{1,0:T(8,128)(2,1)S(1)}, bf16[512,128]{1,0:T(8,128)(2,1)S(1)}, u32[]{:S(2)}, u32[]{:S(2)}) collective-permute-start(bf16[512,128]{1,0:T(8,128)(2,1)S(1)} %get-tuple-element.110), channel_id=1, source_target_pairs={{0,24},{4,28},{8,16},{12,20},{16,8},{20,12},{24,0},{28,4},{1,25},{... | collective-permute-start | bytes 393224 | tf_op jit(solution)/shard_map/ppermute | solution.py:29
  131.7 13.4 %collective-permute-start.40 = (bf16[512,128]{1,0:T(8,128)(2,1)S(1)}, bf16[512,128]{1,0:T(8,128)(2,1)S(1)}, u32[]{:S(2)}, u32[]{:S(2)}) collective-permute-start(bf16[512,128]{1,0:T(8,128)(2,1)S(1)} %get-tuple-element.111), channel_id=1, source_target_pairs={{0,8},{4,12},{8,0},{12,4},{16,24},{20,28},{24,16},{28,20},{1,9},{5... | collective-permute-start | bytes 393224 | tf_op jit(solution)/shard_map/ppermute | solution.py:29
  133.6 16.2 %collective-permute-start.35 = (bf16[4,512,128]{2,1,0:T(8,128)(2,1)S(1)}, bf16[4,512,128]{2,1,0:T(8,128)(2,1)S(1)}, u32[]{:S(2)}, u32[]{:S(2)}) collective-permute-start(bf16[4,512,128]{2,1,0:T(8,128)(2,1)S(1)} %get-tuple-element.82), channel_id=1, source_target_pairs={{0,4},{4,0},{8,12},{12,8},{16,20},{20,16},{24,28},{28,24},{1,5},{5... | collective-permute-start | bytes 1572872 | tf_op jit(solution)/shard_map/ppermute | solution.py:29
  139.7 14.4 %collective-permute-start.50 = (bf16[512,128]{1,0:T(8,128)(2,1)S(1)}, bf16[512,128]{1,0:T(8,128)(2,1)S(1)}, u32[]{:S(2)}, u32[]{:S(2)}) collective-permute-start(bf16[512,128]{1,0:T(8,128)(2,1)S(1)} %get-tuple-element.103), channel_id=1, source_target_pairs={{0,16},{4,20},{8,24},{12,28},{16,0},{20,4},{24,8},{28,12},{1,17},{... | collective-permute-start | bytes 393224 | tf_op jit(solution)/shard_map/ppermute | solution.py:29
  142.7 11.4 %collective-permute-start.52 = (bf16[512,128]{1,0:T(8,128)(2,1)S(1)}, bf16[512,128]{1,0:T(8,128)(2,1)S(1)}, u32[]{:S(2)}, u32[]{:S(2)}) collective-permute-start(bf16[512,128]{1,0:T(8,128)(2,1)S(1)} %get-tuple-element.104), channel_id=1, source_target_pairs={{0,24},{4,28},{8,16},{12,20},{16,8},{20,12},{24,0},{28,4},{1,25},{... | collective-permute-start | bytes 393224 | tf_op jit(solution)/shard_map/ppermute | solution.py:29
  145.1 9.4 %collective-permute-start.51 = (bf16[512,128]{1,0:T(8,128)(2,1)S(1)}, bf16[512,128]{1,0:T(8,128)(2,1)S(1)}, u32[]{:S(2)}, u32[]{:S(2)}) collective-permute-start(bf16[512,128]{1,0:T(8,128)(2,1)S(1)} %get-tuple-element.105), channel_id=1, source_target_pairs={{0,8},{4,12},{8,0},{12,4},{16,24},{20,28},{24,16},{28,20},{1,9},{5... | collective-permute-start | bytes 393224 | tf_op jit(solution)/shard_map/ppermute | solution.py:29
  150.0 12.8 %collective-permute-start.36 = (bf16[512,128]{1,0:T(8,128)(2,1)S(1)}, bf16[512,128]{1,0:T(8,128)(2,1)S(1)}, u32[]{:S(2)}, u32[]{:S(2)}) collective-permute-start(bf16[512,128]{1,0:T(8,128)(2,1)S(1)} %get-tuple-element.112), channel_id=1, source_target_pairs={{0,16},{4,20},{8,24},{12,28},{16,0},{20,4},{24,8},{28,12},{1,17},{... | collective-permute-start | bytes 393224 | tf_op jit(solution)/shard_map/ppermute | solution.py:29
  151.7 11.1 %collective-permute-start.38 = (bf16[512,128]{1,0:T(8,128)(2,1)S(1)}, bf16[512,128]{1,0:T(8,128)(2,1)S(1)}, u32[]{:S(2)}, u32[]{:S(2)}) collective-permute-start(bf16[512,128]{1,0:T(8,128)(2,1)S(1)} %get-tuple-element.113), channel_id=1, source_target_pairs={{0,24},{4,28},{8,16},{12,20},{16,8},{20,12},{24,0},{28,4},{1,25},{... | collective-permute-start | bytes 393224 | tf_op jit(solution)/shard_map/ppermute | solution.py:29
  154.1 8.8 %collective-permute-start.37 = (bf16[512,128]{1,0:T(8,128)(2,1)S(1)}, bf16[512,128]{1,0:T(8,128)(2,1)S(1)}, u32[]{:S(2)}, u32[]{:S(2)}) collective-permute-start(bf16[512,128]{1,0:T(8,128)(2,1)S(1)} %get-tuple-element.114), channel_id=1, source_target_pairs={{0,8},{4,12},{8,0},{12,4},{16,24},{20,28},{24,16},{28,20},{1,9},{5... | collective-permute-start | bytes 393224 | tf_op jit(solution)/shard_map/ppermute | solution.py:29
  (11 other events, 78.6 us)

commit v6 on v4

--- a/solution.py
+++ b/solution.py
@@ -12,7 +12,6 @@
 inv_root_tau = 0.3989422804014327
 lane_tile = 128
 packed_rows = 16
-CFG = {'flops': 2, 'near': (True, True, False), 'scatters': {'first': 'direct', 'inner': 'direct', 'outer': 'direct', 'second': 'direct'}, 'A1': 0, 'A2': 0, 'A3': 0, 'A4': 0, 'A5': 0, 'A6': 0, 'A7': 1, 'B1': 0, 'B2': 0, 'B3': 0, 'B4': 0, 'B5': 0, 'B6': 0, 'B7': 0, 'C1': 0, 'C2': 0, 'C3': 0, 'C4': 0, 'T1': 0, 'T2': 0, 'T3': 0, 'T4': 0, 'T5': 0, 'T6': 0, 'Q1': 0, 'Q2': 0, 'Q3': 0, 'Q4': 0, 'Q5': 0, 'Q6': 0}
 vmem_bytes = 14 * 1024 * 1024
 
 
@@ -87,9 +86,9 @@
         self.steps.insert(0 if near else len(self.steps), 1)
         self.offsets, self.held = (0,), shard[None]
         self.arrived = None
-        if shard.shape[1] % packed_rows:
+        if shard.shape[-2] % packed_rows:
             self.steps = []
-            self.held = lax.all_gather(shard, "dp", axis=1, tiled=True)[None]
+            self.held = lax.all_gather(shard, "dp", axis=shard.ndim - 2, tiled=True)[None]
 
     def step(self, *others):
         if not self.steps:
@@ -112,32 +111,19 @@
 
 
 class Scatter:
-    def __init__(self, halves, steps, direct):
+    def __init__(self, halves, steps):
         self.sent, self.kept = halves
-        self.steps = list(steps)
-        self.direct = direct
-        self.held = None
-
-    def step(self, *others):
-        step = self.steps.pop(0)
-        if self.held is not None:
-            half = self.held.shape[0] // 2
-            self.sent, self.kept = self.held[half:].astype(jnp.bfloat16), self.held[:half]
-        self.held = self.kept + hop(wait_for(self.sent, *others), "dp", step).astype(jnp.float32)
-        return self.held
-
-    def finish(self, *others):
-        if not self.direct:
-            while self.steps:
-                self.step(*others)
-            return self.held[0]
-        size = self.held.shape[0]
-        bits = list(reversed(self.steps))
-        offsets = [sum(bit for k, bit in enumerate(bits) if q >> k & 1) for q in range(size)]
+        self.steps = steps
+
+    def step(self):
+        self.held = self.kept + hop(self.sent, "dp", self.steps[0]).astype(jnp.float32)
+
+    def finish(self):
+        bits = list(reversed(self.steps[1:]))
         total = self.held[0]
-        for q in range(1, size):
-            part = wait_for(self.held[q].astype(jnp.bfloat16), *others)
-            total = total + hop(part, "dp", offsets[q]).astype(jnp.float32)
+        for q in range(1, self.held.shape[0]):
+            offset = sum(bit for k, bit in enumerate(bits) if q >> k & 1)
+            total = total + hop(self.held[q].astype(jnp.bfloat16), "dp", offset).astype(jnp.float32)
         return total
 
 
@@ -240,6 +226,15 @@
     spread(mixed, sends, ids[1])
 
 
+def back_kernel(z, ids, full, *refs):
+    arrived, refs = refs[: z.mp], refs[z.mp :]
+    columns, sends, mixed = refs[0], refs[1 : 1 + z.mp], refs[1 + z.mp]
+    place_arrived(columns, arrived, ids[1])
+    for c in range(z.local):
+        column(mixed, c, z.local, matmul(full[c], columns[c], 1, 0))
+    spread(mixed, sends, ids[1])
+
+
 def gelu_kernel(z, layout, ids, *refs):
     pieces, refs = refs[: len(layout)], refs[len(layout) :]
     preact, backs, refs = refs[: z.mp], refs[z.mp : 2 * z.mp], refs[2 * z.mp :]
@@ -308,7 +303,7 @@
         out_specs=[pl.BlockSpec(memory_space=pltpu.VMEM) for _ in outs],
         scratch_shapes=scratch,
         compiler_params=pltpu.CompilerParams(vmem_limit_bytes=vmem_bytes),
-        cost_estimate=pl.CostEstimate(flops=CFG["flops"] * products, bytes_accessed=moved, transcendentals=0),
+        cost_estimate=pl.CostEstimate(flops=2 * products, bytes_accessed=moved, transcendentals=0),
     )(*inputs, *after)
 
 
@@ -330,25 +325,20 @@
     held = pltpu.VMEM((z.local, z.block, z.tokens), bf16)
 
     part = functools.partial
-    along = list(reversed(steps_of(z.dp)))
-    orders = {name: [*along, 1] if kind == "far" else [1, *along] for name, kind in CFG["scatters"].items()}
-
-    def on(key, *values):
-        return values if CFG[key] else ()
-
-    near = CFG["near"]
-    first, inner = Pieces(right_one), Joined(left_one, near[0])
-    outer, second = Joined(left_two, near[1]), Joined(right_two, near[2])
-
-    wave0 = first.wave()
-    i0 = inner.step()
+    orders = [1, *reversed(steps_of(z.dp))]
+
+    first, inner = Pieces(right_one), Joined(left_one, near=True)
+    outer, second = Joined(left_two, near=True), Joined(right_two, near=False)
+
+    first.wave()
+    inner.step()
     turned_up = run(part(turn_kernel, z), sends, [mixed], [ids, cotangent], 0)
     upstream = exchange(turned_up)
-    wave1 = first.wave()
-    o0 = outer.step() if near[1] else outer.step(*on("A1", *wave0[:1]))
-    i1 = inner.step(*on("A2", turned_up[1]))
-    s0 = second.step(*on("A3", *wave0[:1])) if not near[2] else second.step()
-    wave2 = first.wave()
+    first.wave()
+    outer.step()
+    second.step()
+    inner.step()
+    first.wave()
     first_layout, first_pieces = first.finish()
     right_first, *parts = run(
         part(first_kernel, z, first_layout),
@@ -356,13 +346,12 @@
         [mixed],
         [ids, tokens, *first_pieces],
         products,
-        [*on("A4", *s0), *on("A5", *i1), *on("A6", *o0), *on("A7", *upstream[2:3])],
-    )
-    k1 = parts[1]
+        [*upstream[2:3]],
+    )
     first_columns = exchange(parts)
-    i2 = inner.step(*on("B1", *wave2))
-    o1 = outer.step(*on("B2", k1), *on("B3", first_columns[1]))
-    s1 = second.step(*on("B4", k1), *on("B5", first_columns[1]))
+    inner.step()
+    outer.step()
+    second.step()
     inner_layout, inner_pieces = inner.finish()
     left_first, columns, *parts = run(
         part(middle_kernel, z, inner_layout, 0),
@@ -370,12 +359,10 @@
         [mixed],
         [ids, *inner_pieces, *first_columns],
         products,
-        [*on("B6", *s1), *on("B7", *o1)],
-    )
-    k3 = parts[1]
+    )
     preact = exchange(parts)
-    outer.step(*on("C1", k3))
-    second.step(*on("C2", k3))
+    outer.step()
+    second.step()
     outer_layout, outer_pieces = outer.finish()
     second_layout, second_pieces = second.finish()
     _, upstream_columns, *parts = run(
@@ -384,7 +371,6 @@
         [mixed],
         [ids, *outer_pieces, *upstream],
         products,
-        [*on("C3", k3), *on("C4", preact[1])],
     )
     second_rows = exchange(parts)
     right_second, hidden, second_back, *parts = run(
@@ -401,66 +387,61 @@
         [mixed],
         [ids, right_second, hidden],
         products,
-        [*on("T1", first_upstream[1])],
     )
     second_columns = exchange(parts)
     right_two_halves = run(
-        part(grad_kernel, z, orders["second"]),
+        part(grad_kernel, z, orders),
         halves,
         [sums],
         [ids, hidden, second_back],
         products,
-        [*on("T2", first_upstream[1]), *on("T3", second_columns[1])],
-    )
-    scatter = {"second": Scatter(right_two_halves, orders["second"], CFG["scatters"]["second"] == "direct")}
+    )
+    scatter = {"second": Scatter(right_two_halves, orders)}
     scatter["second"].step()
-    _, upstream_rows, *parts = run(
-        part(middle_kernel, z, ((0,),), 1),
-        [weight, acts] + sends,
-        [mixed],
-        [ids, left_first[None], *first_upstream],
-        products,
-        [*on("T4", *right_two_halves[:1])],
-    )
-    left_one_halves = run(part(grad_kernel, z, orders["inner"]), halves, [sums], [ids, columns, upstream_rows], products)
-    parts[1] = wait_for(parts[1], *on("T5", left_one_halves[0]))
+    upstream_rows, *parts = run(
+        part(back_kernel, z),
+        [acts] + sends,
+        [mixed],
+        [ids, left_first, *first_upstream],
+        products,
+    )
+    left_one_halves = run(part(grad_kernel, z, orders), halves, [sums], [ids, columns, upstream_rows], products)
+    parts[1] = wait_for(parts[1], left_one_halves[0])
     first_rows = exchange(parts)
-    scatter["inner"] = Scatter(left_one_halves, orders["inner"], CFG["scatters"]["inner"] == "direct")
+    scatter["inner"] = Scatter(left_one_halves, orders)
     scatter["inner"].step()
     left_two_halves = run(
-        part(placed_grad_kernel, z, orders["outer"]),
+        part(placed_grad_kernel, z, orders),
         halves,
         [held, sums],
         [ids, upstream_columns, *second_columns],
         products,
-        [*on("T6", first_rows[1])],
-    )
-    scatter["outer"] = Scatter(left_two_halves, orders["outer"], CFG["scatters"]["outer"] == "direct")
-    o_held = scatter["outer"].step()
-    totals = {"second": scatter["second"].finish()}
+    )
+    scatter["outer"] = Scatter(left_two_halves, orders)
+    scatter["outer"].step()
+    totals = {"second": scatter["second"].finish() * scale}
     turned, *right_one_halves = run(
-        part(last_grad_kernel, z, orders["first"]),
+        part(last_grad_kernel, z, orders),
         [shaped(bf16, z.local, z.tokens, z.block)] + halves,
         [held, sums],
         [ids, tokens, *first_rows],
         products,
-        [*on("Q1", totals["second"]), *on("Q2", left_two_halves[0]), *on("Q3", scatter["inner"].held)],
-    )
-    scatter["first"] = Scatter(right_one_halves, orders["first"], CFG["scatters"]["first"] == "direct")
-    f_held = scatter["first"].step()
-    totals["inner"] = scatter["inner"].finish()
-    totals["first"] = scatter["first"].finish(*on("Q4", totals["inner"]), *on("Q5", o_held))
-    totals["outer"] = scatter["outer"].finish()
+        [scatter["inner"].held],
+    )
+    scatter["first"] = Scatter(right_one_halves, orders)
+    scatter["first"].step()
+    totals["inner"] = scatter["inner"].finish() * scale
+    totals["first"] = scatter["first"].finish() * scale
+    totals["outer"] = scatter["outer"].finish() * scale
     (tokens_grad,) = run(
         part(tokens_kernel, z),
         [shaped(bf16, z.tokens, z.local * z.block)],
         [],
         [right_first, turned],
         products,
-        [*on("Q6", f_held)],
     )
     summed = [
-        (totals[name] * scale).reshape(z.local, z.rows, z.block) for name in ("first", "inner", "second", "outer")
+        totals[name].reshape(z.local, z.rows, z.block) for name in ("first", "inner", "second", "outer")
     ]
     return (tokens_grad, *summed)
 

time: 170 us -> 164 us (0.965)
  starting transfers between devices: 68.7 us -> 58.2 us
  waiting for transfers between devices: 69.2 us -> 73.7 us
    ppermute x53, starting transfers between devices: 68.7 us -> 58.2 us  [hop(): return lax.ppermute(source, axis, [(i, i ^ offset) for i in range(size)])]
    ppermute x53, waiting for transfers between devices: 69.2 us -> 73.7 us  [hop(): return lax.ppermute(source, axis, [(i, i ^ offset) for i in range(size)])]
  transfers between devices with their start and end apart: 53 -> 53, of which waited for: 19 -> 20; matrix products, arithmetic and copies ran while one was open for 2% -> 2% of each run, Pallas kernels for 13% -> 13%
where the time goes in v6:
time: 164 us
  waiting for transfers between devices  73.7 us (45%)
  starting transfers between devices  58.2 us (35%)
  Pallas kernels  25.7 us (16%)
  other arithmetic  3.71 us (2%)
    ppermute x53, waiting for transfers between devices, hop(): return lax.ppermute(source, axis, [(i, i ^ offset) for i in range(size)])  73.7 us
    ppermute x53, starting transfers between devices, hop(): return lax.ppermute(source, axis, [(i, i ^ offset) for i in range(size)])  58.2 us
    pallas_call x18, Pallas kernels, run(): pl.pallas_call(skip, out_shape=outs, in_specs=specs + [pl.BlockSpec(memor...  25.7 us
  transfers between devices with their start and end apart: 53, of which 20 were waited for; matrix products, arithmetic and copies ran while one was open for 2% of the time, Pallas kernels for 13%

profile of v6, /device:TPU:0, one launch (start us, length us, event | category | flops | bytes accessed | tf_op | source)
XLA Modules:
  0.0 163.7 jit_solution(10670329662931991490)
XLA Ops:
  0.6 3.0 %collective-permute-start.8 = (bf16[1,32,16,128]{3,2,1,0:T(8,128)(2,1)}, bf16[1,32,16,128]{3,2,1,0:T(8,128)(2,1)S(1)}, u32[]{:S(2)}, u32[]{:S(2)}) collective-permute-start(bf16[1,32,16,128]{3,2,1,0:T(8,128)(2,1)} %bitcast.78), channel_id=1, source_target_pairs={{0,4},{4,0},{8,12},{12,8},{16,20},{20,16},{24,28},{28,24},{1,5},{5... | collective-permute-start | bytes 393224 | tf_op jit(solution)/shard_map/ppermute | solution.py:28
  3.6 2.6 %collective-permute-start.2 = (bf16[1,32,16,128]{3,2,1,0:T(8,128)(2,1)}, bf16[1,32,16,128]{3,2,1,0:T(8,128)(2,1)S(1)}, u32[]{:S(2)}, u32[]{:S(2)}) collective-permute-start(bf16[1,32,16,128]{3,2,1,0:T(8,128)(2,1)} %bitcast.74), channel_id=1, source_target_pairs={{0,16},{4,20},{8,24},{12,28},{16,0},{20,4},{24,8},{28,12},{1,17},{... | collective-permute-start | bytes 393224 | tf_op jit(solution)/shard_map/ppermute | solution.py:28
  6.2 1.6 collective-permute-start.1
  10.0 1.9 %shard_map.101 = (bf16[1024,128]{1,0:T(8,128)(2,1)S(1)}, bf16[1024,128]{1,0:T(8,128)(2,1)S(1)}, bf16[1024,128]{1,0:T(8,128)(2,1)S(1)}, bf16[1024,128]{1,0:T(8,128)(2,1)S(1)}) custom-call(s32[2]{0:T(128)S(1)} %pad_add_fusion.refs_0_, bf16[128,4096]{1,0:T(8,128)(2,1)S(1)} %copy-done.1), custom_call_target="tpu_custom_call" | custom-call | bytes 2097160 | tf_op jit(solution)/shard_map/pallas_call | solution.py:299
  11.9 2.7 %collective-permute-start.9 = (bf16[2,32,16,128]{3,2,1,0:T(8,128)(2,1)S(1)}, bf16[2,32,16,128]{3,2,1,0:T(8,128)(2,1)S(1)}, u32[]{:S(2)}, u32[]{:S(2)}) collective-permute-start(bf16[2,32,16,128]{3,2,1,0:T(8,128)(2,1)S(1)} %shard_map.103.refs_0_), channel_id=1, source_target_pairs={{0,16},{4,20},{8,24},{12,28},{16,0},{20,4},{24,8},{28,12},{1,17},{... | collective-permute-start | bytes 786440 | tf_op jit(solution)/shard_map/ppermute | solution.py:28
  18.1 6.7 %collective-permute-done.14.refs_1_ = bf16[1,32,16,128]{3,2,1,0:T(8,128)(2,1)S(1)} collective-permute-done((bf16[1,32,16,128]{3,2,1,0:T(8,128)(2,1)}, bf16[1,32,16,128]{3,2,1,0:T(8,128)(2,1)S(1)}, u32[]{:S(2)}, u32[]{:S(2)}) %collective-permute-start.14) | collective-permute-done | bytes 131104 | tf_op jit(solution)/shard_map/ppermute | solution.py:28
  25.0 1.9 %collective-permute-start.3 = (bf16[1,32,16,128]{3,2,1,0:T(8,128)(2,1)S(1)}, bf16[1,32,16,128]{3,2,1,0:T(8,128)(2,1)S(1)}, u32[]{:S(2)}, u32[]{:S(2)}) collective-permute-start(bf16[1,32,16,128]{3,2,1,0:T(8,128)(2,1)S(1)} %collective-permute-done.1.refs_4_), channel_id=1, source_target_pairs={{0,4},{4,0},{8,12},{12,8},{16,20},{20,16},{24,28},{28,24},{1,5},{5... | collective-permute-start | bytes 393224 | tf_op jit(solution)/shard_map/ppermute | solution.py:28
  26.9 2.8 %collective-permute-done.5.refs_8_ = bf16[1,32,16,128]{3,2,1,0:T(8,128)(2,1)S(1)} collective-permute-done((bf16[1,32,16,128]{3,2,1,0:T(8,128)(2,1)S(1)}, bf16[1,32,16,128]{3,2,1,0:T(8,128)(2,1)S(1)}, u32[]{:S(2)}, u32[]{:S(2)}) %collective-permute-start.5) | collective-permute-done | bytes 131104 | tf_op jit(solution)/shard_map/ppermute | solution.py:28
  30.4 2.6 %collective-permute-start.21 = (bf16[2,32,16,128]{3,2,1,0:T(8,128)(2,1)S(1)}, bf16[2,32,16,128]{3,2,1,0:T(8,128)(2,1)S(1)}, u32[]{:S(2)}, u32[]{:S(2)}) collective-permute-start(bf16[2,32,16,128]{3,2,1,0:T(8,128)(2,1)S(1)} %shard_map.108.refs_0_), channel_id=1, source_target_pairs={{0,16},{4,20},{8,24},{12,28},{16,0},{20,4},{24,8},{28,12},{1,17},{... | collective-permute-start | bytes 786440 | tf_op jit(solution)/shard_map/ppermute | solution.py:28
  33.1 2.5 %collective-permute-start.15 = (bf16[2,32,16,128]{3,2,1,0:T(8,128)(2,1)S(1)}, bf16[2,32,16,128]{3,2,1,0:T(8,128)(2,1)S(1)}, u32[]{:S(2)}, u32[]{:S(2)}) collective-permute-start(bf16[2,32,16,128]{3,2,1,0:T(8,128)(2,1)S(1)} %shard_map.106.refs_0_), channel_id=1, source_target_pairs={{0,8},{4,12},{8,0},{12,4},{16,24},{20,28},{24,16},{28,20},{1,9},{5... | collective-permute-start | bytes 786440 | tf_op jit(solution)/shard_map/ppermute | solution.py:28
  35.7 2.6 %shard_map.102 = (bf16[32,128,128]{2,1,0:T(8,128)(2,1)S(1)}, bf16[1024,128]{1,0:T(8,128)(2,1)S(1)}, bf16[1024,128]{1,0:T(8,128)(2,1)S(1)}, bf16[1024,128]{1,0:T(8,128)(2,1)S(1)}, bf16[1024,128]{1,0:T(8,128)(2,1)S(1)}) custom-call(s32[2]{0:T(128)S(1)} %pad_add_fusion.refs_0_, bf16[128,4096]{1,0:T(8,128)(2,1)S(1)} %copy-done, ...), custom_call_target="tpu_custom_call" | custom-call | flops 134217728 | bytes 4194312 | tf_op jit(solution)/shard_map/pallas_call | solution.py:299
  38.4 1.6 collective-permute-start.12
  40.0 3.4 %collective-permute-done.21.refs_1_ = bf16[2,32,16,128]{3,2,1,0:T(8,128)(2,1)S(1)} collective-permute-done((bf16[2,32,16,128]{3,2,1,0:T(8,128)(2,1)S(1)}, bf16[2,32,16,128]{3,2,1,0:T(8,128)(2,1)S(1)}, u32[]{:S(2)}, u32[]{:S(2)}) %collective-permute-start.21) | collective-permute-done | bytes 262176 | tf_op jit(solution)/shard_map/ppermute | solution.py:28
  43.4 3.1 %collective-permute-done.15.refs_1_ = bf16[2,32,16,128]{3,2,1,0:T(8,128)(2,1)S(1)} collective-permute-done((bf16[2,32,16,128]{3,2,1,0:T(8,128)(2,1)S(1)}, bf16[2,32,16,128]{3,2,1,0:T(8,128)(2,1)S(1)}, u32[]{:S(2)}, u32[]{:S(2)}) %collective-permute-start.15) | collective-permute-done | bytes 262176 | tf_op jit(solution)/shard_map/ppermute | solution.py:28
  47.8 1.7 %collective-permute-start.16 = (bf16[4,32,16,128]{3,2,1,0:T(8,128)(2,1)S(1)}, bf16[4,32,16,128]{3,2,1,0:T(8,128)(2,1)S(1)}, u32[]{:S(2)}, u32[]{:S(2)}) collective-permute-start(bf16[4,32,16,128]{3,2,1,0:T(8,128)(2,1)S(1)} %shard_map.107.refs_1_), channel_id=1, source_target_pairs={{0,4},{4,0},{8,12},{12,8},{16,20},{20,16},{24,28},{28,24},{1,5},{5... | collective-permute-start | bytes 1572872 | tf_op jit(solution)/shard_map/ppermute | solution.py:28
  49.4 2.9 %collective-permute-done.13.refs_6_ = bf16[1024,128]{1,0:T(8,128)(2,1)S(1)} collective-permute-done((bf16[1024,128]{1,0:T(8,128)(2,1)S(1)}, bf16[1024,128]{1,0:T(8,128)(2,1)S(1)}, u32[]{:S(2)}, u32[]{:S(2)}) %collective-permute-start.13) | collective-permute-done | bytes 262176 | tf_op jit(solution)/shard_map/ppermute | solution.py:28
  52.3 1.7 %collective-permute-start.24 = (bf16[1024,128]{1,0:T(8,128)(2,1)S(1)}, bf16[1024,128]{1,0:T(8,128)(2,1)S(1)}, u32[]{:S(2)}, u32[]{:S(2)}) collective-permute-start(bf16[1024,128]{1,0:T(8,128)(2,1)S(1)} %get-tuple-element.63), channel_id=1, source_target_pairs={{0,3},{1,2},{2,1},{3,0},{4,7},{5,6},{6,5},{7,4},{8,11},{9,10},{10,... | collective-permute-start | bytes 786440 | tf_op jit(solution)/shard_map/ppermute | solution.py:28
  54.0 3.7 %collective-permute-done.10.refs_2_ = bf16[4,32,16,128]{3,2,1,0:T(8,128)(2,1)S(1)} collective-permute-done((bf16[4,32,16,128]{3,2,1,0:T(8,128)(2,1)S(1)}, bf16[4,32,16,128]{3,2,1,0:T(8,128)(2,1)S(1)}, u32[]{:S(2)}, u32[]{:S(2)}) %collective-permute-start.10) | collective-permute-done | bytes 524320 | tf_op jit(solution)/shard_map/ppermute | solution.py:28
  57.7 2.6 %shard_map.105 = (bf16[32,128,128]{2,1,0:T(8,128)(2,1)S(1)}, bf16[32,128,128]{2,1,0:T(8,128)(2,1)S(1)}, bf16[1024,128]{1,0:T(8,128)(2,1)S(1)}, bf16[1024,128]{1,...) custom-call(s32[2]{0:T(128)S(1)} %pad_add_fusion.refs_0_, ...), custom_call_target="tpu_custom_call" | custom-call | flops 134217728 | bytes 5242888 | tf_op jit(solution)/shard_map/pallas_call | solution.py:299
  60.4 1.5 collective-permute-start.18
  62.2 3.9 %collective-permute-done.22.refs_2_ = bf16[4,32,16,128]{3,2,1,0:T(8,128)(2,1)S(1)} collective-permute-done((bf16[4,32,16,128]{3,2,1,0:T(8,128)(2,1)S(1)}, bf16[4,32,16,128]{3,2,1,0:T(8,128)(2,1)S(1)}, u32[]{:S(2)}, u32[]{:S(2)}) %collective-permute-start.22) | collective-permute-done | bytes 524320 | tf_op jit(solution)/shard_map/ppermute | solution.py:28
  66.1 2.5 %shard_map.110 = (bf16[32,128,128]{2,1,0:T(8,128)(2,1)}, bf16[32,128,128]{2,1,0:T(8,128)(2,1)S(1)}, bf16[1024,128]{1,0:T(8,128)(2,1)S(1)}, bf16[1024,128]{1,0:T(...) custom-call(s32[2]{0:T(128)S(1)} %pad_add_fusion.refs_0_, ...), custom_call_target="tpu_custom_call" | custom-call | flops 134217728 | bytes 5242888 | tf_op jit(solution)/shard_map/pallas_call | solution.py:299
  70.5 3.7 %collective-permute-done.19.refs_6_ = bf16[1024,128]{1,0:T(8,128)(2,1)S(1)} collective-permute-done((bf16[1024,128]{1,0:T(8,128)(2,1)S(1)}, bf16[1024,128]{1,0:T(8,128)(2,1)S(1)}, u32[]{:S(2)}, u32[]{:S(2)}) %collective-permute-start.19) | collective-permute-done | bytes 262176 | tf_op jit(solution)/shard_map/ppermute | solution.py:28
  74.2 6.5 %collective-permute-done.26.refs_9_ = bf16[1024,128]{1,0:T(8,128)(2,1)S(1)} collective-permute-done((bf16[1024,128]{1,0:T(8,128)(2,1)S(1)}, bf16[1024,128]{1,0:T(8,128)(2,1)S(1)}, u32[]{:S(2)}, u32[]{:S(2)}) %collective-permute-start.26) | collective-permute-done | bytes 262176 | tf_op jit(solution)/shard_map/ppermute | solution.py:28
  80.8 4.7 %collective-permute-done.27.refs_10_ = bf16[1024,128]{1,0:T(8,128)(2,1)S(1)} collective-permute-done((bf16[1024,128]{1,0:T(8,128)(2,1)S(1)}, bf16[1024,128]{1,0:T(8,128)(2,1)S(1)}, u32[]{:S(2)}, u32[]{:S(2)}) %collective-permute-start.27) | collective-permute-done | bytes 262176 | tf_op jit(solution)/shard_map/ppermute | solution.py:28
  85.5 3.0 %shard_map.111 = (bf16[32,128,128]{2,1,0:T(8,128)(2,1)S(1)}, bf16[32,128,128]{2,1,0:T(8,128)(2,1)S(1)}, bf16[32,128,128]{2,1,0:T(8,128)(2,1)S(1)}, bf16[1024,128...) custom-call(s32[2]{0:T(128)S(1)} %pad_add_fusion.refs_0_, ...), custom_call_target="tpu_custom_call" | custom-call | flops 134217728 | bytes 7340040 | tf_op jit(solution)/shard_map/pallas_call | solution.py:299
  90.9 1.6 collective-permute-start.29
  92.8 2.6 %shard_map.118 = (bf16[1024,128]{1,0:T(8,128)(2,1)S(1)}, bf16[1024,128]{1,0:T(8,128)(2,1)S(1)}, bf16[1024,128]{1,0:T(8,128)(2,1)S(1)}, bf16[1024,128]{1,0:T(8,128)(2,1)S(1)}) custom-call(s32[2]{0:T(128)S(1)} %pad_add_fusion.refs_0_, bf16[32,128,128]{2,1,0:T(8,128)(2,1)S(1)} %get-tuple-element.88.refs_1_, ...), custom_call_target="tpu_custom_call" | custom-call | flops 134217728 | bytes 3145736 | tf_op jit(solution)/shard_map/pallas_call | solution.py:299
  95.7 1.6 collective-permute-start.47
  97.2 2.8 %collective-permute-done.29.refs_4_ = bf16[1024,128]{1,0:T(8,128)(2,1)S(1)} collective-permute-done((bf16[1024,128]{1,0:T(8,128)(2,1)S(1)}, bf16[1024,128]{1,0:T(8,128)(2,1)S(1)}, u32[]{:S(2)}, u32[]{:S(2)}) %collective-permute-start.29) | collective-permute-done | bytes 262176 | tf_op jit(solution)/shard_map/ppermute | solution.py:28
  100.5 4.3 %collective-permute-done.30.refs_5_ = bf16[1024,128]{1,0:T(8,128)(2,1)S(1)} collective-permute-done((bf16[1024,128]{1,0:T(8,128)(2,1)S(1)}, bf16[1024,128]{1,0:T(8,128)(2,1)S(1)}, u32[]{:S(2)}, u32[]{:S(2)}) %collective-permute-start.30) | collective-permute-done | bytes 262176 | tf_op jit(solution)/shard_map/ppermute | solution.py:28
  104.8 2.3 %shard_map.112 = (bf16[32,128,128]{2,1,0:T(8,128)(2,1)S(1)}, bf16[1024,128]{1,0:T(8,128)(2,1)S(1)}, bf16[1024,128]{1,0:T(8,128)(2,1)S(1)}, bf16[1024,128]{1,0:T(8,128)(2,1)S(1)}, bf16[1024,128]{1,0:T(8,128)(2,1)S(1)}) custom-call(s32[2]{0:T(128)S(1)} %pad_add_fusion.refs_0_, bf16[32,128,128]{2,1,0:T(8,128)(2,1)S(1)} %get-tuple-element.56.refs_1_, ...), custom_call_target="tpu_custom_call" | custom-call | flops 134217728 | bytes 4194312 | tf_op jit(solution)/shard_map/pallas_call | solution.py:299
  110.2 1.9 %collective-permute-start.43 = (bf16[512,128]{1,0:T(8,128)(2,1)S(1)}, bf16[512,128]{1,0:T(8,128)(2,1)S(1)}, u32[]{:S(2)}, u32[]{:S(2)}) collective-permute-start(bf16[512,128]{1,0:T(8,128)(2,1)S(1)} %get-tuple-element.106), channel_id=1, source_target_pairs={{0,16},{4,20},{8,24},{12,28},{16,0},{20,4},{24,8},{28,12},{1,17},{... | collective-permute-start | bytes 393224 | tf_op jit(solution)/shard_map/ppermute | solution.py:28
  112.1 1.8 %collective-permute-start.45 = (bf16[512,128]{1,0:T(8,128)(2,1)S(1)}, bf16[512,128]{1,0:T(8,128)(2,1)S(1)}, u32[]{:S(2)}, u32[]{:S(2)}) collective-permute-start(bf16[512,128]{1,0:T(8,128)(2,1)S(1)} %get-tuple-element.107), channel_id=1, source_target_pairs={{0,24},{4,28},{8,16},{12,20},{16,8},{20,12},{24,0},{28,4},{1,25},{... | collective-permute-start | bytes 393224 | tf_op jit(solution)/shard_map/ppermute | solution.py:28
  113.9 2.2 %collective-permute-done.48.refs_5_ = bf16[1024,128]{1,0:T(8,128)(2,1)S(1)} collective-permute-done((bf16[1024,128]{1,0:T(8,128)(2,1)S(1)}, bf16[1024,128]{1,0:T(8,128)(2,1)S(1)}, u32[]{:S(2)}, u32[]{:S(2)}) %collective-permute-start.48) | collective-permute-done | bytes 262176 | tf_op jit(solution)/shard_map/ppermute | solution.py:28
  116.1 1.6 collective-permute-start.32
  117.6 1.6 shard_map.119
  119.2 3.9 %collective-permute-done.43 = bf16[512,128]{1,0:T(8,128)(2,1)S(1)} collective-permute-done((bf16[512,128]{1,0:T(8,128)(2,1)S(1)}, bf16[512,128]{1,0:T(8,128)(2,1)S(1)}, u32[]{:S(2)}, u32[]{:S(2)}) %collective-permute-start.43) | collective-permute-done | bytes 131104 | tf_op jit(solution)/shard_map/ppermute | solution.py:28
  128.1 2.1 %collective-permute-start.41 = (bf16[512,128]{1,0:T(8,128)(2,1)S(1)}, bf16[512,128]{1,0:T(8,128)(2,1)S(1)}, u32[]{:S(2)}, u32[]{:S(2)}) collective-permute-start(bf16[512,128]{1,0:T(8,128)(2,1)S(1)} %get-tuple-element.110), channel_id=1, source_target_pairs={{0,24},{4,28},{8,16},{12,20},{16,8},{20,12},{24,0},{28,4},{1,25},{... | collective-permute-start | bytes 393224 | tf_op jit(solution)/shard_map/ppermute | solution.py:28
  130.1 1.6 collective-permute-done.33.refs_5_
  132.1 1.6 shard_map.115
  134.1 5.4 %collective-permute-done.49 = bf16[4,512,128]{2,1,0:T(8,128)(2,1)S(1)} collective-permute-done((bf16[4,512,128]{2,1,0:T(8,128)(2,1)S(1)}, bf16[4,512,128]{2,1,0:T(8,128)(2,1)S(1)}, u32[]{:S(2)}, u32[]{:S(2)}) %collective-permute-start.49) | collective-permute-done | bytes 524320 | tf_op jit(solution)/shard_map/ppermute | solution.py:28
  140.9 1.8 %shard_map.116 = bf16[128,4096]{1,0:T(8,128)(2,1)} custom-call(bf16[32,128,128]{2,1,0:T(8,128)(2,1)S(1)} %get-tuple-element.51.refs_0_, bf16[32,128,128]{2,1,0:T(8,128)(2,1)S(1)} %get-tuple-element.80.refs_1_), custom_call_target="tpu_custom_call" | custom-call | flops 134217728 | bytes 3145728 | tf_op jit(solution)/shard_map/pallas_call | solution.py:299
  142.7 2.4 %collective-permute-start.52 = (bf16[512,128]{1,0:T(8,128)(2,1)S(1)}, bf16[512,128]{1,0:T(8,128)(2,1)S(1)}, u32[]{:S(2)}, u32[]{:S(2)}) collective-permute-start(bf16[512,128]{1,0:T(8,128)(2,1)S(1)} %get-tuple-element.104), channel_id=1, source_target_pairs={{0,24},{4,28},{8,16},{12,20},{16,8},{20,12},{24,0},{28,4},{1,25},{... | collective-permute-start | bytes 393224 | tf_op jit(solution)/shard_map/ppermute | solution.py:28
  145.9 4.0 %collective-permute-done.35 = bf16[4,512,128]{2,1,0:T(8,128)(2,1)S(1)} collective-permute-done((bf16[4,512,128]{2,1,0:T(8,128)(2,1)S(1)}, bf16[4,512,128]{2,1,0:T(8,128)(2,1)S(1)}, u32[]{:S(2)}, u32[]{:S(2)}) %collective-permute-start.35) | collective-permute-done | bytes 524320 | tf_op jit(solution)/shard_map/ppermute | solution.py:28
  150.0 1.7 %collective-permute-start.36 = (bf16[512,128]{1,0:T(8,128)(2,1)S(1)}, bf16[512,128]{1,0:T(8,128)(2,1)S(1)}, u32[]{:S(2)}, u32[]{:S(2)}) collective-permute-start(bf16[512,128]{1,0:T(8,128)(2,1)S(1)} %get-tuple-element.112), channel_id=1, source_target_pairs={{0,16},{4,20},{8,24},{12,28},{16,0},{20,4},{24,8},{28,12},{1,17},{... | collective-permute-start | bytes 393224 | tf_op jit(solution)/shard_map/ppermute | solution.py:28
  151.7 2.4 %collective-permute-start.38 = (bf16[512,128]{1,0:T(8,128)(2,1)S(1)}, bf16[512,128]{1,0:T(8,128)(2,1)S(1)}, u32[]{:S(2)}, u32[]{:S(2)}) collective-permute-start(bf16[512,128]{1,0:T(8,128)(2,1)S(1)} %get-tuple-element.113), channel_id=1, source_target_pairs={{0,24},{4,28},{8,16},{12,20},{16,8},{20,12},{24,0},{28,4},{1,25},{... | collective-permute-start | bytes 393224 | tf_op jit(solution)/shard_map/ppermute | solution.py:28
  155.3 7.6 %collective-permute-done.36 = bf16[512,128]{1,0:T(8,128)(2,1)S(1)} collective-permute-done((bf16[512,128]{1,0:T(8,128)(2,1)S(1)}, bf16[512,128]{1,0:T(8,128)(2,1)S(1)}, u32[]{:S(2)}, u32[]{:S(2)}) %collective-permute-start.36) | collective-permute-done | bytes 131104 | tf_op jit(solution)/shard_map/ppermute | solution.py:28
  (102 shorter events, 27.0 us)
Async XLA Ops:
  0.6 11.3 %collective-permute-start.8 = (bf16[1,32,16,128]{3,2,1,0:T(8,128)(2,1)}, bf16[1,32,16,128]{3,2,1,0:T(8,128)(2,1)S(1)}, u32[]{:S(2)}, u32[]{:S(2)}) collective-permute-start(bf16[1,32,16,128]{3,2,1,0:T(8,128)(2,1)} %bitcast.78), channel_id=1, source_target_pairs={{0,4},{4,0},{8,12},{12,8},{16,20},{20,16},{24,28},{28,24},{1,5},{5... | collective-permute-start | bytes 393224 | tf_op jit(solution)/shard_map/ppermute | solution.py:28
  3.6 11.2 %collective-permute-start.2 = (bf16[1,32,16,128]{3,2,1,0:T(8,128)(2,1)}, bf16[1,32,16,128]{3,2,1,0:T(8,128)(2,1)S(1)}, u32[]{:S(2)}, u32[]{:S(2)}) collective-permute-start(bf16[1,32,16,128]{3,2,1,0:T(8,128)(2,1)} %bitcast.74), channel_id=1, source_target_pairs={{0,16},{4,20},{8,24},{12,28},{16,0},{20,4},{24,8},{28,12},{1,17},{... | collective-permute-start | bytes 393224 | tf_op jit(solution)/shard_map/ppermute | solution.py:28
  6.2 9.9 %collective-permute-start.1 = (bf16[1,32,16,128]{3,2,1,0:T(8,128)(2,1)}, bf16[1,32,16,128]{3,2,1,0:T(8,128)(2,1)S(1)}, u32[]{:S(2)}, u32[]{:S(2)}) collective-permute-start(bf16[1,32,16,128]{3,2,1,0:T(8,128)(2,1)} %bitcast.75), channel_id=1, source_target_pairs={{0,8},{4,12},{8,0},{12,4},{16,24},{20,28},{24,16},{28,20},{1,9},{5... | collective-permute-start | bytes 393224 | tf_op jit(solution)/shard_map/ppermute | solution.py:28
  7.8 9.8 %collective-permute-start = (bf16[1,32,16,128]{3,2,1,0:T(8,128)(2,1)}, bf16[1,32,16,128]{3,2,1,0:T(8,128)(2,1)S(1)}, u32[]{:S(2)}, u32[]{:S(2)}) collective-permute-start(bf16[1,32,16,128]{3,2,1,0:T(8,128)(2,1)} %bitcast.76), channel_id=1, source_target_pairs={{0,4},{4,0},{8,12},{12,8},{16,20},{20,16},{24,28},{28,24},{1,5},{5... | collective-permute-start | bytes 393224 | tf_op jit(solution)/shard_map/ppermute | solution.py:28
  8.3 16.5 %collective-permute-start.14 = (bf16[1,32,16,128]{3,2,1,0:T(8,128)(2,1)}, bf16[1,32,16,128]{3,2,1,0:T(8,128)(2,1)S(1)}, u32[]{:S(2)}, u32[]{:S(2)}) collective-permute-start(bf16[1,32,16,128]{3,2,1,0:T(8,128)(2,1)} %bitcast.82), channel_id=1, source_target_pairs={{0,16},{4,20},{8,24},{12,28},{16,0},{20,4},{24,8},{28,12},{1,17},{... | collective-permute-start | bytes 393224 | tf_op jit(solution)/shard_map/ppermute | solution.py:28
  11.9 18.4 %collective-permute-start.9 = (bf16[2,32,16,128]{3,2,1,0:T(8,128)(2,1)S(1)}, bf16[2,32,16,128]{3,2,1,0:T(8,128)(2,1)S(1)}, u32[]{:S(2)}, u32[]{:S(2)}) collective-permute-start(bf16[2,32,16,128]{3,2,1,0:T(8,128)(2,1)S(1)} %shard_map.103.refs_0_), channel_id=1, source_target_pairs={{0,16},{4,20},{8,24},{12,28},{16,0},{20,4},{24,8},{28,12},{1,17},{... | collective-permute-start | bytes 786440 | tf_op jit(solution)/shard_map/ppermute | solution.py:28
  14.8 10.2 %collective-permute-start.20 = (bf16[1,32,16,128]{3,2,1,0:T(8,128)(2,1)S(1)}, bf16[1,32,16,128]{3,2,1,0:T(8,128)(2,1)S(1)}, u32[]{:S(2)}, u32[]{:S(2)}) collective-permute-start(bf16[1,32,16,128]{3,2,1,0:T(8,128)(2,1)S(1)} %bitcast.80), channel_id=1, source_target_pairs={{0,4},{4,0},{8,12},{12,8},{16,20},{20,16},{24,28},{28,24},{1,5},{5... | collective-permute-start | bytes 393224 | tf_op jit(solution)/shard_map/ppermute | solution.py:28
  16.1 19.6 %collective-permute-start.7 = (bf16[1024,128]{1,0:T(8,128)(2,1)S(1)}, bf16[1024,128]{1,0:T(8,128)(2,1)S(1)}, u32[]{:S(2)}, u32[]{:S(2)}) collective-permute-start(bf16[1024,128]{1,0:T(8,128)(2,1)S(1)} %get-tuple-element.50), channel_id=1, source_target_pairs={{0,2},{1,3},{2,0},{3,1},{4,6},{5,7},{6,4},{7,5},{8,10},{9,11},{10,... | collective-permute-start | bytes 786440 | tf_op jit(solution)/shard_map/ppermute | solution.py:28
  17.6 12.0 %collective-permute-start.5 = (bf16[1,32,16,128]{3,2,1,0:T(8,128)(2,1)S(1)}, bf16[1,32,16,128]{3,2,1,0:T(8,128)(2,1)S(1)}, u32[]{:S(2)}, u32[]{:S(2)}) collective-permute-start(bf16[1,32,16,128]{3,2,1,0:T(8,128)(2,1)S(1)} %collective-permute-done.2.refs_5_), channel_id=1, source_target_pairs={{0,8},{4,12},{8,0},{12,4},{16,24},{20,28},{24,16},{28,20},{1,9},{5... | collective-permute-start | bytes 393224 | tf_op jit(solution)/shard_map/ppermute | solution.py:28
  25.0 10.6 %collective-permute-start.3 = (bf16[1,32,16,128]{3,2,1,0:T(8,128)(2,1)S(1)}, bf16[1,32,16,128]{3,2,1,0:T(8,128)(2,1)S(1)}, u32[]{:S(2)}, u32[]{:S(2)}) collective-permute-start(bf16[1,32,16,128]{3,2,1,0:T(8,128)(2,1)S(1)} %collective-permute-done.1.refs_4_), channel_id=1, source_target_pairs={{0,4},{4,0},{8,12},{12,8},{16,20},{20,16},{24,28},{28,24},{1,5},{5... | collective-permute-start | bytes 393224 | tf_op jit(solution)/shard_map/ppermute | solution.py:28
  30.4 13.0 %collective-permute-start.21 = (bf16[2,32,16,128]{3,2,1,0:T(8,128)(2,1)S(1)}, bf16[2,32,16,128]{3,2,1,0:T(8,128)(2,1)S(1)}, u32[]{:S(2)}, u32[]{:S(2)}) collective-permute-start(bf16[2,32,16,128]{3,2,1,0:T(8,128)(2,1)S(1)} %shard_map.108.refs_0_), channel_id=1, source_target_pairs={{0,16},{4,20},{8,24},{12,28},{16,0},{20,4},{24,8},{28,12},{1,17},{... | collective-permute-start | bytes 786440 | tf_op jit(solution)/shard_map/ppermute | solution.py:28
  33.1 13.4 %collective-permute-start.15 = (bf16[2,32,16,128]{3,2,1,0:T(8,128)(2,1)S(1)}, bf16[2,32,16,128]{3,2,1,0:T(8,128)(2,1)S(1)}, u32[]{:S(2)}, u32[]{:S(2)}) collective-permute-start(bf16[2,32,16,128]{3,2,1,0:T(8,128)(2,1)S(1)} %shard_map.106.refs_0_), channel_id=1, source_target_pairs={{0,8},{4,12},{8,0},{12,4},{16,24},{20,28},{24,16},{28,20},{1,9},{5... | collective-permute-start | bytes 786440 | tf_op jit(solution)/shard_map/ppermute | solution.py:28
  35.6 22.1 %collective-permute-start.10 = (bf16[4,32,16,128]{3,2,1,0:T(8,128)(2,1)S(1)}, bf16[4,32,16,128]{3,2,1,0:T(8,128)(2,1)S(1)}, u32[]{:S(2)}, u32[]{:S(2)}) collective-permute-start(bf16[4,32,16,128]{3,2,1,0:T(8,128)(2,1)S(1)} %shard_map.104.refs_1_), channel_id=1, source_target_pairs={{0,8},{4,12},{8,0},{12,4},{16,24},{20,28},{24,16},{28,20},{1,9},{5... | collective-permute-start | bytes 1572872 | tf_op jit(solution)/shard_map/ppermute | solution.py:28
  38.4 9.4 %collective-permute-start.11 = (bf16[1024,128]{1,0:T(8,128)(2,1)S(1)}, bf16[1024,128]{1,0:T(8,128)(2,1)S(1)}, u32[]{:S(2)}, u32[]{:S(2)}) collective-permute-start(bf16[1024,128]{1,0:T(8,128)(2,1)S(1)} %get-tuple-element.53), channel_id=1, source_target_pairs={{0,1},{1,0},{2,3},{3,2},{4,5},{5,4},{6,7},{7,6},{8,9},{9,8},{10,11... | collective-permute-start | bytes 786440 | tf_op jit(solution)/shard_map/ppermute | solution.py:28
  38.4 11.0 %collective-permute-start.12 = (bf16[1024,128]{1,0:T(8,128)(2,1)S(1)}, bf16[1024,128]{1,0:T(8,128)(2,1)S(1)}, u32[]{:S(2)}, u32[]{:S(2)}) collective-permute-start(bf16[1024,128]{1,0:T(8,128)(2,1)S(1)} %get-tuple-element.54), channel_id=1, source_target_pairs={{0,2},{1,3},{2,0},{3,1},{4,6},{5,7},{6,4},{7,5},{8,10},{9,11},{10,... | collective-permute-start | bytes 786440 | tf_op jit(solution)/shard_map/ppermute | solution.py:28
  43.4 8.9 %collective-permute-start.13 = (bf16[1024,128]{1,0:T(8,128)(2,1)S(1)}, bf16[1024,128]{1,0:T(8,128)(2,1)S(1)}, u32[]{:S(2)}, u32[]{:S(2)}) collective-permute-start(bf16[1024,128]{1,0:T(8,128)(2,1)S(1)} %get-tuple-element.55), channel_id=1, source_target_pairs={{0,3},{1,2},{2,1},{3,0},{4,7},{5,6},{6,5},{7,4},{8,11},{9,10},{10,... | collective-permute-start | bytes 786440 | tf_op jit(solution)/shard_map/ppermute | solution.py:28
  46.5 19.6 %collective-permute-start.22 = (bf16[4,32,16,128]{3,2,1,0:T(8,128)(2,1)S(1)}, bf16[4,32,16,128]{3,2,1,0:T(8,128)(2,1)S(1)}, u32[]{:S(2)}, u32[]{:S(2)}) collective-permute-start(bf16[4,32,16,128]{3,2,1,0:T(8,128)(2,1)S(1)} %shard_map.109.refs_1_), channel_id=1, source_target_pairs={{0,8},{4,12},{8,0},{12,4},{16,24},{20,28},{24,16},{28,20},{1,9},{5... | collective-permute-start | bytes 1572872 | tf_op jit(solution)/shard_map/ppermute | solution.py:28
  47.8 20.9 %collective-permute-start.16 = (bf16[4,32,16,128]{3,2,1,0:T(8,128)(2,1)S(1)}, bf16[4,32,16,128]{3,2,1,0:T(8,128)(2,1)S(1)}, u32[]{:S(2)}, u32[]{:S(2)}) collective-permute-start(bf16[4,32,16,128]{3,2,1,0:T(8,128)(2,1)S(1)} %shard_map.107.refs_1_), channel_id=1, source_target_pairs={{0,4},{4,0},{8,12},{12,8},{16,20},{20,16},{24,28},{28,24},{1,5},{5... | collective-permute-start | bytes 1572872 | tf_op jit(solution)/shard_map/ppermute | solution.py:28
  49.4 10.9 %collective-permute-start.23 = (bf16[1024,128]{1,0:T(8,128)(2,1)S(1)}, bf16[1024,128]{1,0:T(8,128)(2,1)S(1)}, u32[]{:S(2)}, u32[]{:S(2)}) collective-permute-start(bf16[1024,128]{1,0:T(8,128)(2,1)S(1)} %get-tuple-element.62), channel_id=1, source_target_pairs={{0,1},{1,0},{2,3},{3,2},{4,5},{5,4},{6,7},{7,6},{8,9},{9,8},{10,11... | collective-permute-start | bytes 786440 | tf_op jit(solution)/shard_map/ppermute | solution.py:28
  52.3 9.6 %collective-permute-start.24 = (bf16[1024,128]{1,0:T(8,128)(2,1)S(1)}, bf16[1024,128]{1,0:T(8,128)(2,1)S(1)}, u32[]{:S(2)}, u32[]{:S(2)}) collective-permute-start(bf16[1024,128]{1,0:T(8,128)(2,1)S(1)} %get-tuple-element.63), channel_id=1, source_target_pairs={{0,3},{1,2},{2,1},{3,0},{4,7},{5,6},{6,5},{7,4},{8,11},{9,10},{10,... | collective-permute-start | bytes 786440 | tf_op jit(solution)/shard_map/ppermute | solution.py:28
  60.3 9.9 %collective-permute-start.17 = (bf16[1024,128]{1,0:T(8,128)(2,1)S(1)}, bf16[1024,128]{1,0:T(8,128)(2,1)S(1)}, u32[]{:S(2)}, u32[]{:S(2)}) collective-permute-start(bf16[1024,128]{1,0:T(8,128)(2,1)S(1)} %get-tuple-element.58), channel_id=1, source_target_pairs={{0,1},{1,0},{2,3},{3,2},{4,5},{5,4},{6,7},{7,6},{8,9},{9,8},{10,11... | collective-permute-start | bytes 786440 | tf_op jit(solution)/shard_map/ppermute | solution.py:28
  60.4 10.2 %collective-permute-start.18 = (bf16[1024,128]{1,0:T(8,128)(2,1)S(1)}, bf16[1024,128]{1,0:T(8,128)(2,1)S(1)}, u32[]{:S(2)}, u32[]{:S(2)}) collective-permute-start(bf16[1024,128]{1,0:T(8,128)(2,1)S(1)} %get-tuple-element.59), channel_id=1, source_target_pairs={{0,2},{1,3},{2,0},{3,1},{4,6},{5,7},{6,4},{7,5},{8,10},{9,11},{10,... | collective-permute-start | bytes 786440 | tf_op jit(solution)/shard_map/ppermute | solution.py:28
  61.9 12.3 %collective-permute-start.19 = (bf16[1024,128]{1,0:T(8,128)(2,1)S(1)}, bf16[1024,128]{1,0:T(8,128)(2,1)S(1)}, u32[]{:S(2)}, u32[]{:S(2)}) collective-permute-start(bf16[1024,128]{1,0:T(8,128)(2,1)S(1)} %get-tuple-element.60), channel_id=1, source_target_pairs={{0,3},{1,2},{2,1},{3,0},{4,7},{5,6},{6,5},{7,4},{8,11},{9,10},{10,... | collective-permute-start | bytes 786440 | tf_op jit(solution)/shard_map/ppermute | solution.py:28
  68.7 12.1 %collective-permute-start.26 = (bf16[1024,128]{1,0:T(8,128)(2,1)S(1)}, bf16[1024,128]{1,0:T(8,128)(2,1)S(1)}, u32[]{:S(2)}, u32[]{:S(2)}) collective-permute-start(bf16[1024,128]{1,0:T(8,128)(2,1)S(1)} %get-tuple-element.66), channel_id=1, source_target_pairs={{0,2},{1,3},{2,0},{3,1},{4,6},{5,7},{6,4},{7,5},{8,10},{9,11},{10,... | collective-permute-start | bytes 786440 | tf_op jit(solution)/shard_map/ppermute | solution.py:28
  70.2 15.3 %collective-permute-start.27 = (bf16[1024,128]{1,0:T(8,128)(2,1)S(1)}, bf16[1024,128]{1,0:T(8,128)(2,1)S(1)}, u32[]{:S(2)}, u32[]{:S(2)}) collective-permute-start(bf16[1024,128]{1,0:T(8,128)(2,1)S(1)} %get-tuple-element.67), channel_id=1, source_target_pairs={{0,3},{1,2},{2,1},{3,0},{4,7},{5,6},{6,5},{7,4},{8,11},{9,10},{10,... | collective-permute-start | bytes 786440 | tf_op jit(solution)/shard_map/ppermute | solution.py:28
  90.0 20.0 %collective-permute-start.42 = (bf16[4,512,128]{2,1,0:T(8,128)(2,1)S(1)}, bf16[4,512,128]{2,1,0:T(8,128)(2,1)S(1)}, u32[]{:S(2)}, u32[]{:S(2)}) collective-permute-start(bf16[4,512,128]{2,1,0:T(8,128)(2,1)S(1)} %get-tuple-element.86), channel_id=1, source_target_pairs={{0,4},{4,0},{8,12},{12,8},{16,20},{20,16},{24,28},{28,24},{1,5},{5... | collective-permute-start | bytes 1572872 | tf_op jit(solution)/shard_map/ppermute | solution.py:28
  90.9 9.1 %collective-permute-start.29 = (bf16[1024,128]{1,0:T(8,128)(2,1)S(1)}, bf16[1024,128]{1,0:T(8,128)(2,1)S(1)}, u32[]{:S(2)}, u32[]{:S(2)}) collective-permute-start(bf16[1024,128]{1,0:T(8,128)(2,1)S(1)} %get-tuple-element.70), channel_id=1, source_target_pairs={{0,2},{1,3},{2,0},{3,1},{4,6},{5,7},{6,4},{7,5},{8,10},{9,11},{10,... | collective-permute-start | bytes 786440 | tf_op jit(solution)/shard_map/ppermute | solution.py:28
  92.5 12.4 %collective-permute-start.30 = (bf16[1024,128]{1,0:T(8,128)(2,1)S(1)}, bf16[1024,128]{1,0:T(8,128)(2,1)S(1)}, u32[]{:S(2)}, u32[]{:S(2)}) collective-permute-start(bf16[1024,128]{1,0:T(8,128)(2,1)S(1)} %get-tuple-element.71), channel_id=1, source_target_pairs={{0,3},{1,2},{2,1},{3,0},{4,7},{5,6},{6,5},{7,4},{8,11},{9,10},{10,... | collective-permute-start | bytes 786440 | tf_op jit(solution)/shard_map/ppermute | solution.py:28
  95.3 16.8 %collective-permute-start.46 = (bf16[1024,128]{1,0:T(8,128)(2,1)S(1)}, bf16[1024,128]{1,0:T(8,128)(2,1)S(1)}, u32[]{:S(2)}, u32[]{:S(2)}) collective-permute-start(bf16[1024,128]{1,0:T(8,128)(2,1)S(1)} %get-tuple-element.90), channel_id=1, source_target_pairs={{0,1},{1,0},{2,3},{3,2},{4,5},{5,4},{6,7},{7,6},{8,9},{9,8},{10,11... | collective-permute-start | bytes 786440 | tf_op jit(solution)/shard_map/ppermute | solution.py:28
  95.7 18.2 %collective-permute-start.47 = (bf16[1024,128]{1,0:T(8,128)(2,1)S(1)}, bf16[1024,128]{1,0:T(8,128)(2,1)S(1)}, u32[]{:S(2)}, u32[]{:S(2)}) collective-permute-start(bf16[1024,128]{1,0:T(8,128)(2,1)S(1)} %get-tuple-element.91), channel_id=1, source_target_pairs={{0,2},{1,3},{2,0},{3,1},{4,6},{5,7},{6,4},{7,5},{8,10},{9,11},{10,... | collective-permute-start | bytes 786440 | tf_op jit(solution)/shard_map/ppermute | solution.py:28
  100.0 16.1 %collective-permute-start.48 = (bf16[1024,128]{1,0:T(8,128)(2,1)S(1)}, bf16[1024,128]{1,0:T(8,128)(2,1)S(1)}, u32[]{:S(2)}, u32[]{:S(2)}) collective-permute-start(bf16[1024,128]{1,0:T(8,128)(2,1)S(1)} %get-tuple-element.92), channel_id=1, source_target_pairs={{0,3},{1,2},{2,1},{3,0},{4,7},{5,6},{6,5},{7,4},{8,11},{9,10},{10,... | collective-permute-start | bytes 786440 | tf_op jit(solution)/shard_map/ppermute | solution.py:28
  108.7 17.7 %collective-permute-start.34 = (bf16[4,512,128]{2,1,0:T(8,128)(2,1)S(1)}, bf16[4,512,128]{2,1,0:T(8,128)(2,1)S(1)}, u32[]{:S(2)}, u32[]{:S(2)}) collective-permute-start(bf16[4,512,128]{2,1,0:T(8,128)(2,1)S(1)} %get-tuple-element.76.refs_1_), channel_id=1, source_target_pairs={{0,4},{4,0},{8,12},{12,8},{16,20},{20,16},{24,28},{28,24},{1,5},{5... | collective-permute-start | bytes 1572872 | tf_op jit(solution)/shard_map/ppermute | solution.py:28
  110.2 12.9 %collective-permute-start.43 = (bf16[512,128]{1,0:T(8,128)(2,1)S(1)}, bf16[512,128]{1,0:T(8,128)(2,1)S(1)}, u32[]{:S(2)}, u32[]{:S(2)}) collective-permute-start(bf16[512,128]{1,0:T(8,128)(2,1)S(1)} %get-tuple-element.106), channel_id=1, source_target_pairs={{0,16},{4,20},{8,24},{12,28},{16,0},{20,4},{24,8},{28,12},{1,17},{... | collective-permute-start | bytes 393224 | tf_op jit(solution)/shard_map/ppermute | solution.py:28
  112.1 11.1 %collective-permute-start.45 = (bf16[512,128]{1,0:T(8,128)(2,1)S(1)}, bf16[512,128]{1,0:T(8,128)(2,1)S(1)}, u32[]{:S(2)}, u32[]{:S(2)}) collective-permute-start(bf16[512,128]{1,0:T(8,128)(2,1)S(1)} %get-tuple-element.107), channel_id=1, source_target_pairs={{0,24},{4,28},{8,16},{12,20},{16,8},{20,12},{24,0},{28,4},{1,25},{... | collective-permute-start | bytes 393224 | tf_op jit(solution)/shard_map/ppermute | solution.py:28
  113.9 10.9 %collective-permute-start.44 = (bf16[512,128]{1,0:T(8,128)(2,1)S(1)}, bf16[512,128]{1,0:T(8,128)(2,1)S(1)}, u32[]{:S(2)}, u32[]{:S(2)}) collective-permute-start(bf16[512,128]{1,0:T(8,128)(2,1)S(1)} %get-tuple-element.108), channel_id=1, source_target_pairs={{0,8},{4,12},{8,0},{12,4},{16,24},{20,28},{24,16},{28,20},{1,9},{5... | collective-permute-start | bytes 393224 | tf_op jit(solution)/shard_map/ppermute | solution.py:28
  116.1 12.0 %collective-permute-start.32 = (bf16[1024,128]{1,0:T(8,128)(2,1)S(1)}, bf16[1024,128]{1,0:T(8,128)(2,1)S(1)}, u32[]{:S(2)}, u32[]{:S(2)}) collective-permute-start(bf16[1024,128]{1,0:T(8,128)(2,1)S(1)} %get-tuple-element.77), channel_id=1, source_target_pairs={{0,2},{1,3},{2,0},{3,1},{4,6},{5,7},{6,4},{7,5},{8,10},{9,11},{10,... | collective-permute-start | bytes 786440 | tf_op jit(solution)/shard_map/ppermute | solution.py:28
  123.2 8.9 %collective-permute-start.31 = (bf16[1024,128]{1,0:T(8,128)(2,1)S(1)}, bf16[1024,128]{1,0:T(8,128)(2,1)S(1)}, u32[]{:S(2)}, u32[]{:S(2)}) collective-permute-start(bf16[1024,128]{1,0:T(8,128)(2,1)S(1)} %shard_map.114), channel_id=1, source_target_pairs={{0,1},{1,0},{2,3},{3,2},{4,5},{5,4},{6,7},{7,6},{8,9},{9,8},{10,11... | collective-permute-start | bytes 786440 | tf_op jit(solution)/shard_map/ppermute | solution.py:28
  124.7 14.8 %collective-permute-start.49 = (bf16[4,512,128]{2,1,0:T(8,128)(2,1)S(1)}, bf16[4,512,128]{2,1,0:T(8,128)(2,1)S(1)}, u32[]{:S(2)}, u32[]{:S(2)}) collective-permute-start(bf16[4,512,128]{2,1,0:T(8,128)(2,1)S(1)} %get-tuple-element.94), channel_id=1, source_target_pairs={{0,4},{4,0},{8,12},{12,8},{16,20},{20,16},{24,28},{28,24},{1,5},{5... | collective-permute-start | bytes 1572872 | tf_op jit(solution)/shard_map/ppermute | solution.py:28
  126.6 16.1 %collective-permute-start.39 = (bf16[512,128]{1,0:T(8,128)(2,1)S(1)}, bf16[512,128]{1,0:T(8,128)(2,1)S(1)}, u32[]{:S(2)}, u32[]{:S(2)}) collective-permute-start(bf16[512,128]{1,0:T(8,128)(2,1)S(1)} %get-tuple-element.109), channel_id=1, source_target_pairs={{0,16},{4,20},{8,24},{12,28},{16,0},{20,4},{24,8},{28,12},{1,17},{... | collective-permute-start | bytes 393224 | tf_op jit(solution)/shard_map/ppermute | solution.py:28
  128.1 17.0 %collective-permute-start.41 = (bf16[512,128]{1,0:T(8,128)(2,1)S(1)}, bf16[512,128]{1,0:T(8,128)(2,1)S(1)}, u32[]{:S(2)}, u32[]{:S(2)}) collective-permute-start(bf16[512,128]{1,0:T(8,128)(2,1)S(1)} %get-tuple-element.110), channel_id=1, source_target_pairs={{0,24},{4,28},{8,16},{12,20},{16,8},{20,12},{24,0},{28,4},{1,25},{... | collective-permute-start | bytes 393224 | tf_op jit(solution)/shard_map/ppermute | solution.py:28
  131.7 13.4 %collective-permute-start.40 = (bf16[512,128]{1,0:T(8,128)(2,1)S(1)}, bf16[512,128]{1,0:T(8,128)(2,1)S(1)}, u32[]{:S(2)}, u32[]{:S(2)}) collective-permute-start(bf16[512,128]{1,0:T(8,128)(2,1)S(1)} %get-tuple-element.111), channel_id=1, source_target_pairs={{0,8},{4,12},{8,0},{12,4},{16,24},{20,28},{24,16},{28,20},{1,9},{5... | collective-permute-start | bytes 393224 | tf_op jit(solution)/shard_map/ppermute | solution.py:28
  133.6 16.2 %collective-permute-start.35 = (bf16[4,512,128]{2,1,0:T(8,128)(2,1)S(1)}, bf16[4,512,128]{2,1,0:T(8,128)(2,1)S(1)}, u32[]{:S(2)}, u32[]{:S(2)}) collective-permute-start(bf16[4,512,128]{2,1,0:T(8,128)(2,1)S(1)} %get-tuple-element.82), channel_id=1, source_target_pairs={{0,4},{4,0},{8,12},{12,8},{16,20},{20,16},{24,28},{28,24},{1,5},{5... | collective-permute-start | bytes 1572872 | tf_op jit(solution)/shard_map/ppermute | solution.py:28
  139.7 14.4 %collective-permute-start.50 = (bf16[512,128]{1,0:T(8,128)(2,1)S(1)}, bf16[512,128]{1,0:T(8,128)(2,1)S(1)}, u32[]{:S(2)}, u32[]{:S(2)}) collective-permute-start(bf16[512,128]{1,0:T(8,128)(2,1)S(1)} %get-tuple-element.103), channel_id=1, source_target_pairs={{0,16},{4,20},{8,24},{12,28},{16,0},{20,4},{24,8},{28,12},{1,17},{... | collective-permute-start | bytes 393224 | tf_op jit(solution)/shard_map/ppermute | solution.py:28
  142.7 11.4 %collective-permute-start.52 = (bf16[512,128]{1,0:T(8,128)(2,1)S(1)}, bf16[512,128]{1,0:T(8,128)(2,1)S(1)}, u32[]{:S(2)}, u32[]{:S(2)}) collective-permute-start(bf16[512,128]{1,0:T(8,128)(2,1)S(1)} %get-tuple-element.104), channel_id=1, source_target_pairs={{0,24},{4,28},{8,16},{12,20},{16,8},{20,12},{24,0},{28,4},{1,25},{... | collective-permute-start | bytes 393224 | tf_op jit(solution)/shard_map/ppermute | solution.py:28
  145.1 9.4 %collective-permute-start.51 = (bf16[512,128]{1,0:T(8,128)(2,1)S(1)}, bf16[512,128]{1,0:T(8,128)(2,1)S(1)}, u32[]{:S(2)}, u32[]{:S(2)}) collective-permute-start(bf16[512,128]{1,0:T(8,128)(2,1)S(1)} %get-tuple-element.105), channel_id=1, source_target_pairs={{0,8},{4,12},{8,0},{12,4},{16,24},{20,28},{24,16},{28,20},{1,9},{5... | collective-permute-start | bytes 393224 | tf_op jit(solution)/shard_map/ppermute | solution.py:28
  150.0 12.8 %collective-permute-start.36 = (bf16[512,128]{1,0:T(8,128)(2,1)S(1)}, bf16[512,128]{1,0:T(8,128)(2,1)S(1)}, u32[]{:S(2)}, u32[]{:S(2)}) collective-permute-start(bf16[512,128]{1,0:T(8,128)(2,1)S(1)} %get-tuple-element.112), channel_id=1, source_target_pairs={{0,16},{4,20},{8,24},{12,28},{16,0},{20,4},{24,8},{28,12},{1,17},{... | collective-permute-start | bytes 393224 | tf_op jit(solution)/shard_map/ppermute | solution.py:28
  151.7 11.1 %collective-permute-start.38 = (bf16[512,128]{1,0:T(8,128)(2,1)S(1)}, bf16[512,128]{1,0:T(8,128)(2,1)S(1)}, u32[]{:S(2)}, u32[]{:S(2)}) collective-permute-start(bf16[512,128]{1,0:T(8,128)(2,1)S(1)} %get-tuple-element.113), channel_id=1, source_target_pairs={{0,24},{4,28},{8,16},{12,20},{16,8},{20,12},{24,0},{28,4},{1,25},{... | collective-permute-start | bytes 393224 | tf_op jit(solution)/shard_map/ppermute | solution.py:28
  154.1 8.8 %collective-permute-start.37 = (bf16[512,128]{1,0:T(8,128)(2,1)S(1)}, bf16[512,128]{1,0:T(8,128)(2,1)S(1)}, u32[]{:S(2)}, u32[]{:S(2)}) collective-permute-start(bf16[512,128]{1,0:T(8,128)(2,1)S(1)} %get-tuple-element.114), channel_id=1, source_target_pairs={{0,8},{4,12},{8,0},{12,4},{16,24},{20,28},{24,16},{28,20},{1,9},{5... | collective-permute-start | bytes 393224 | tf_op jit(solution)/shard_map/ppermute | solution.py:28
  (11 other events, 78.6 us)
